TPU v7x, 32 devices: a whole 2x2x4 slice. The times are simulated.
32 devices in a mesh: expert: 16 (over z, x, core), tensor: 2 (over y).
Axes of the slice: x: 2, y: 2, z: 4, core: 2. Of those that a mesh axis runs over, the one named last changes fastest.
Arguments:
- tokens_in: bfloat16 [4096, 2048], P('expert'), may hold values from -6 to 6
- cotangent: bfloat16 [4096, 2048], P('expert'), may hold values from -6 to 6
- norm_gains: bfloat16 [2, 2048], P(None, 'expert'), may hold values from 0.5 to 1.5
- qkv_weight: bfloat16 [2048, 3, 2048], P('expert', None, 'tensor'), may hold values from -0.125 to 0.125
- qkv_bias: bfloat16 [3, 16, 128], P(None, 'tensor', 'expert'), may hold values from -4 to 4
- out_weight: bfloat16 [2048, 2048], P('tensor', 'expert'), may hold values from -1.5 to 1.5
- router_weight: bfloat16 [2048, 16], P('expert'), may hold values from -0.0625 to 0.0625
- shared_gate: bfloat16 [2048], P('expert'), may hold values from -0.125 to 0.125
- shared_in: bfloat16 [2048, 2, 5632], P('expert', None, 'tensor'), may hold values from -0.125 to 0.125
- shared_out: bfloat16 [5632, 2048], P('tensor', 'expert'), may hold values from -0.078125 to 0.078125
- expert_in: bfloat16 [16, 2048, 2, 1408], P('expert', None, None, 'tensor'), may hold values from -0.375 to 0.375
- expert_out: bfloat16 [16, 1408, 2048], P('expert', 'tensor'), may hold values from -0.0546875 to 0.0546875
- expert_ids: int32 [4096, 4], P('expert'), may hold values from 0 to 15, all different within a row; in each aligned block of 256 rows (0 to 255, 256 to 511, ...) at most 96 rows name the same one
- prefix_len: int32 [16], P('expert'), may hold values from 25 to 128
Outputs:
- output: bfloat16 [4096, 2048], P('expert')
- input_grad: bfloat16 [4096, 2048], P('expert')
- gains_grad: float32 [2, 2048], P(None, 'expert')
- qkv_weight_grad: float32 [2048, 3, 2048], P('expert', None, 'tensor')
- qkv_bias_grad: float32 [3, 16, 128], P(None, 'tensor', 'expert')
- out_weight_grad: float32 [2048, 2048], P('tensor', 'expert')
- router_grad: float32 [2048, 16], P('expert')
- shared_gate_grad: float32 [2048], P('expert')
- shared_in_grad: float32 [2048, 2, 5632], P('expert', None, 'tensor')
- shared_out_grad: float32 [5632, 2048], P('tensor', 'expert')
- expert_in_grad: float32 [16, 2048, 2, 1408], P('expert', None, None, 'tensor')
- expert_out_grad: float32 [16, 1408, 2048], P('expert', 'tensor')
Inputs may be any that keep to these rules, and one draw needn't show every extreme that they name: `expert_ids`: each token names 4 different experts; among the tokens of one sequence no expert is named more than 96 times, a bound that some block reaches.
All inputs are finite; a program needn't handle non-finite values.
Results may differ from a plain program's by a relative error of at most 0.02.
Values may be sent and summed in bfloat16 or wider, within the bound.
No kernel may reach another device: no remote copies, remote signals or barrier semaphores. Data moves between devices by JAX's collectives and lax.ppermute only.
A program may use at most 384 MiB of HBM per device.

v0:
```python
import jax
import jax.numpy as jnp
from jax import lax
from jax.sharding import PartitionSpec as P

eps = 1e-06
theta_base = 1000000.0
neg_large = -1e30


def rms_norm(values, gain_row):
    factor = lax.rsqrt(jnp.mean(values * values, axis=-1, keepdims=True) + eps)
    return values * factor * gain_row


def rotary(values):
    length, head_count, head_size = values.shape
    half_size = head_size // 2
    frequency = theta_base ** (-(jnp.arange(half_size, dtype=jnp.float32) * 2.0) / head_size)
    angles = jnp.arange(length, dtype=jnp.float32)[:, None] * frequency[None, :]
    cosine = jnp.concatenate([jnp.cos(angles), jnp.cos(angles)], axis=-1)[:, None, :]
    sine_table = jnp.concatenate([jnp.sin(angles), jnp.sin(angles)], axis=-1)[:, None, :]
    turned = jnp.concatenate([-values[..., half_size:], values[..., :half_size]], axis=-1)
    return values * cosine + turned * sine_table


def silu_product(gate_part, up_part):
    return jax.nn.silu(gate_part) * up_part


def masked_scores(query_block, key_heads, block_start, prefix_cut, score_scale):
    block_rows = query_block.shape[0]
    length = key_heads.shape[0]
    scores = (
        jnp.einsum("qhd,khd->hqk", query_block, key_heads, preferred_element_type=jnp.float32)
        * score_scale
    )
    row_index = block_start + jnp.arange(block_rows, dtype=jnp.int32)[:, None]
    col_index = jnp.arange(length, dtype=jnp.int32)[None, :]
    allowed = (col_index <= row_index) | (col_index < prefix_cut)
    return jnp.where(allowed[None], scores, neg_large)


def local(
    tokens_in,
    cotangent,
    norm_gains,
    qkv_weight,
    qkv_bias,
    out_weight,
    router_weight,
    shared_gate,
    shared_in,
    shared_out,
    expert_in,
    expert_out,
    expert_ids,
    prefix_len,
):
    length, model_width = tokens_in.shape
    top_count = expert_ids.shape[1]
    experts = router_weight.shape[1]
    capacity = length * top_count * 3 // (2 * experts)
    gathered = (
        lax.all_gather(norm_gains, "expert", axis=1, tiled=True),
        lax.all_gather(qkv_weight, "expert", axis=0, tiled=True),
        lax.all_gather(qkv_bias, "expert", axis=2, tiled=True),
        lax.all_gather(out_weight, "expert", axis=1, tiled=True),
        lax.all_gather(router_weight, "expert", axis=0, tiled=True),
        lax.all_gather(shared_gate, "expert", axis=0, tiled=True),
        lax.all_gather(shared_in, "expert", axis=0, tiled=True),
        lax.all_gather(shared_out, "expert", axis=1, tiled=True),
    )
    gains, qkv_w, qkv_b, out_w, router_w, gate_vec, sh_in, sh_out = gathered
    gains_f = gains.astype(jnp.float32)
    heads_local = qkv_b.shape[1]
    head_size = qkv_b.shape[2]
    score_scale = head_size ** (-0.5)
    prefix_cut = prefix_len[0]
    block_rows = min(512, length)
    inputs = tokens_in.astype(jnp.float32)
    first_b = rms_norm(inputs, gains_f[0]).astype(jnp.bfloat16)
    projected = jnp.dot(first_b, qkv_w.reshape(model_width, -1), preferred_element_type=jnp.float32)
    projected = (
        projected.reshape(length, 3, heads_local, head_size) + qkv_b.astype(jnp.float32)[None]
    )
    query_heads = rotary(projected[:, 0]).astype(jnp.bfloat16)
    key_heads = rotary(projected[:, 1]).astype(jnp.bfloat16)
    value_heads = projected[:, 2].astype(jnp.bfloat16)
    block_start = 0
    scores = masked_scores(query_heads, key_heads, block_start, prefix_cut, score_scale)
    row_max = jnp.max(scores, axis=-1, keepdims=True)
    weights = jnp.exp(scores - row_max)
    row_total = jnp.sum(weights, axis=-1, keepdims=True)
    probs_low = (weights / row_total).astype(jnp.bfloat16)
    lse_blocks = [row_max + jnp.log(row_total)]
    mixed_blocks = jnp.einsum(
        "hqk,khd->qhd", probs_low, value_heads, preferred_element_type=jnp.float32
    )
    mixed_heads = mixed_blocks.reshape(length, -1).astype(jnp.bfloat16)
    attn_part = jnp.dot(mixed_heads, out_w, preferred_element_type=jnp.float32)
    attn_out = lax.psum(attn_part, "tensor")
    residual = inputs + attn_out
    second_b = rms_norm(residual, gains_f[1]).astype(jnp.bfloat16)
    logits = jnp.dot(second_b, router_w, preferred_element_type=jnp.float32)
    route_match = expert_ids[:, :, None] == jnp.arange(experts, dtype=jnp.int32)[None, None, :]
    chosen = jnp.sum(jnp.where(route_match, logits[:, None, :], 0.0), axis=-1)
    gate_weights = jax.nn.softmax(chosen, axis=-1)
    shared_sigma = jax.nn.sigmoid(jnp.dot(second_b, gate_vec, preferred_element_type=jnp.float32))
    shared_gu = jnp.dot(
        second_b, sh_in.reshape(model_width, -1), preferred_element_type=jnp.float32
    ).reshape(length, 2, -1)
    shared_hidden = silu_product(shared_gu[:, 0], shared_gu[:, 1]).astype(jnp.bfloat16)
    shared_part = jnp.dot(shared_hidden, sh_out, preferred_element_type=jnp.float32)
    flat_ids = expert_ids.reshape(-1)
    onehot = (flat_ids[:, None] == jnp.arange(experts, dtype=jnp.int32)[None, :]).astype(jnp.int32)
    slot_rank = jnp.sum(jnp.cumsum(onehot, axis=0) * onehot, axis=-1) - 1
    places = flat_ids * capacity + slot_rank
    entries = (
        jnp.full((experts * capacity,), length * top_count, jnp.int32)
        .at[places]
        .set(jnp.arange(length * top_count, dtype=jnp.int32))
    )
    token_of = entries // top_count
    padded_rows = jnp.concatenate([second_b, jnp.zeros((1, model_width), jnp.bfloat16)], axis=0)
    send_rows = padded_rows[token_of].reshape(experts, capacity, model_width)
    ex_in_local = expert_in[0].reshape(model_width, -1)
    ex_out_local = expert_out[0]
    part_units = ex_out_local.shape[0]
    received_rows = lax.all_to_all(send_rows, "expert", split_axis=0, concat_axis=0, tiled=True)
    flat_rows = received_rows.reshape(-1, model_width)
    gate_up = jnp.dot(flat_rows, ex_in_local, preferred_element_type=jnp.float32).reshape(
        -1, 2, part_units
    )
    hidden = silu_product(gate_up[:, 0], gate_up[:, 1]).astype(jnp.bfloat16)
    produced = jnp.dot(hidden, ex_out_local, preferred_element_type=jnp.float32).astype(
        jnp.bfloat16
    )
    returned_rows = lax.all_to_all(
        produced.reshape(received_rows.shape), "expert", split_axis=0, concat_axis=0, tiled=True
    )
    returned_rows, received = (returned_rows, received_rows)
    back_rows = returned_rows.reshape(-1, model_width)[places].reshape(
        length, top_count, model_width
    )
    routed_part = jnp.zeros((length, model_width), jnp.float32)
    for slot_index in range(top_count):
        routed_part = routed_part + gate_weights[:, slot_index, None] * back_rows[
            :, slot_index
        ].astype(jnp.float32)
    moe_part = routed_part + shared_sigma[:, None] * shared_part
    moe_out = lax.psum(moe_part, "tensor")
    output = (residual + moe_out).astype(jnp.bfloat16)
    regathered = (
        lax.all_gather(norm_gains, "expert", axis=1, tiled=True),
        lax.all_gather(qkv_weight, "expert", axis=0, tiled=True),
        lax.all_gather(qkv_bias, "expert", axis=2, tiled=True),
        lax.all_gather(out_weight, "expert", axis=1, tiled=True),
        lax.all_gather(router_weight, "expert", axis=0, tiled=True),
        lax.all_gather(shared_gate, "expert", axis=0, tiled=True),
        lax.all_gather(shared_in, "expert", axis=0, tiled=True),
        lax.all_gather(shared_out, "expert", axis=1, tiled=True),
    )
    gains, qkv_w, qkv_b, out_w, router_w, gate_vec, sh_in, sh_out = regathered
    gains_f = gains.astype(jnp.float32)
    upstream = cotangent.astype(jnp.float32)
    gate_dots = jnp.stack(
        [
            jnp.sum(upstream * back_rows[:, slot_index].astype(jnp.float32), axis=-1)
            for slot_index in range(top_count)
        ],
        axis=1,
    )
    sigma_dot = jnp.sum(upstream * shared_part, axis=-1)
    gate_grad, sigma_grad = lax.psum((gate_dots, sigma_dot), "tensor")
    padded_grad = jnp.concatenate([upstream, jnp.zeros((1, model_width), jnp.float32)], axis=0)
    padded_gates = jnp.concatenate([gate_weights.reshape(-1), jnp.zeros((1,), jnp.float32)], axis=0)
    slot_grad = (
        (padded_gates[entries][:, None] * padded_grad[token_of])
        .astype(jnp.bfloat16)
        .reshape(experts, capacity, model_width)
    )
    grad_received = lax.all_to_all(slot_grad, "expert", split_axis=0, concat_axis=0, tiled=True)
    flat_in = received.reshape(-1, model_width)
    flat_grad = grad_received.reshape(-1, model_width)
    gate_up = jnp.dot(flat_in, ex_in_local, preferred_element_type=jnp.float32).reshape(
        -1, 2, part_units
    )
    hidden_b = silu_product(gate_up[:, 0], gate_up[:, 1]).astype(jnp.bfloat16)
    hidden_grad = jnp.dot(flat_grad, ex_out_local.T, preferred_element_type=jnp.float32)
    gate_pre_grad, up_pre_grad = jax.vjp(silu_product, gate_up[:, 0], gate_up[:, 1])[1](hidden_grad)
    gu_grad = (
        jnp.stack([gate_pre_grad, up_pre_grad], axis=1)
        .astype(jnp.bfloat16)
        .reshape(-1, 2 * part_units)
    )
    expert_out_grad = jnp.dot(hidden_b.T, flat_grad, preferred_element_type=jnp.float32)[None]
    expert_in_grad = jnp.dot(flat_in.T, gu_grad, preferred_element_type=jnp.float32).reshape(
        1, model_width, 2, part_units
    )
    entry_grad = jnp.dot(gu_grad, ex_in_local.T, preferred_element_type=jnp.float32).astype(
        jnp.bfloat16
    )
    returned_grad = lax.all_to_all(
        entry_grad.reshape(experts, capacity, model_width),
        "expert",
        split_axis=0,
        concat_axis=0,
        tiled=True,
    )
    grad_rows = returned_grad.reshape(-1, model_width)[places].reshape(
        length, top_count, model_width
    )
    second_part = jnp.zeros((length, model_width), jnp.float32)
    for slot_index in range(top_count):
        second_part = second_part + grad_rows[:, slot_index].astype(jnp.float32)
    shared_y_grad = (shared_sigma[:, None] * upstream).astype(jnp.bfloat16)
    shared_hidden_grad = jnp.dot(shared_y_grad, sh_out.T, preferred_element_type=jnp.float32)
    shared_gate_pre, shared_up_pre = jax.vjp(silu_product, shared_gu[:, 0], shared_gu[:, 1])[1](
        shared_hidden_grad
    )
    shared_gu_grad = (
        jnp.stack([shared_gate_pre, shared_up_pre], axis=1).astype(jnp.bfloat16).reshape(length, -1)
    )
    shared_out_grad = jnp.dot(shared_hidden.T, shared_y_grad, preferred_element_type=jnp.float32)
    shared_in_grad = jnp.dot(
        second_b.T, shared_gu_grad, preferred_element_type=jnp.float32
    ).reshape(model_width, 2, -1)
    second_part = second_part + jnp.dot(
        shared_gu_grad, sh_in.reshape(model_width, -1).T, preferred_element_type=jnp.float32
    )
    second_grad = lax.psum(second_part, "tensor")
    chosen_grad = gate_weights * (
        gate_grad - jnp.sum(gate_weights * gate_grad, axis=-1, keepdims=True)
    )
    logit_grad = jnp.sum(jnp.where(route_match, chosen_grad[:, :, None], 0.0), axis=1).astype(
        jnp.bfloat16
    )
    router_grad = jnp.dot(second_b.T, logit_grad, preferred_element_type=jnp.float32)
    second_grad = second_grad + jnp.dot(logit_grad, router_w.T, preferred_element_type=jnp.float32)
    gate_logit_grad = sigma_grad * shared_sigma * (1.0 - shared_sigma)
    shared_gate_grad = jnp.dot(
        gate_logit_grad,
        second_b.astype(jnp.float32),
        precision=lax.Precision.HIGHEST,
        preferred_element_type=jnp.float32,
    )
    second_grad = second_grad + gate_logit_grad[:, None] * gate_vec.astype(jnp.float32)[None]
    norm_two_back = jax.vjp(rms_norm, residual, gains_f[1])[1]
    residual_norm_grad, gain_two_grad = norm_two_back(second_grad)
    residual_grad = upstream + residual_norm_grad
    attn_grad = residual_grad.astype(jnp.bfloat16)
    out_weight_grad = jnp.dot(mixed_heads.T, attn_grad, preferred_element_type=jnp.float32)
    mixed_grad = (
        jnp.dot(attn_grad, out_w.T, preferred_element_type=jnp.float32)
        .astype(jnp.bfloat16)
        .reshape(length, heads_local, head_size)
    )
    query_blocks = []
    key_grad = jnp.zeros((length, heads_local, head_size), jnp.float32)
    value_grad = jnp.zeros((length, heads_local, head_size), jnp.float32)
    for block_number, block_start in enumerate(range(0, length, block_rows)):
        scores = masked_scores(query_heads, key_heads, block_start, prefix_cut, score_scale)
        probs = jnp.exp(scores - lse_blocks[block_number])
        probs_low = probs.astype(jnp.bfloat16)
        prob_grad = jnp.einsum(
            "qhd,khd->hqk", mixed_grad, value_heads, preferred_element_type=jnp.float32
        )
        row_term = jnp.sum(probs * prob_grad, axis=-1, keepdims=True)
        score_grad = (probs * (prob_grad - row_term)).astype(jnp.bfloat16)
        query_blocks.append(
            jnp.einsum("hqk,khd->qhd", score_grad, key_heads, preferred_element_type=jnp.float32)
            * score_scale
        )
        key_grad = (
            jnp.einsum("hqk,qhd->khd", score_grad, query_heads, preferred_element_type=jnp.float32)
            * score_scale
        )
        value_grad = jnp.einsum(
            "hqk,qhd->khd", probs_low, mixed_grad, preferred_element_type=jnp.float32
        )
    query_grad = query_blocks[0]
    pre_query_grad = jax.vjp(rotary, projected[:, 0])[1](query_grad)[0]
    pre_key_grad = jax.vjp(rotary, projected[:, 1])[1](key_grad)[0]
    proj_grad = jnp.stack([pre_query_grad, pre_key_grad, value_grad], axis=1).astype(jnp.bfloat16)
    qkv_bias_grad = jnp.sum(proj_grad.astype(jnp.float32), axis=0)
    flat_proj_grad = proj_grad.reshape(length, -1)
    qkv_weight_grad = jnp.dot(
        first_b.T, flat_proj_grad, preferred_element_type=jnp.float32
    ).reshape(model_width, 3, -1)
    first_part = jnp.dot(
        flat_proj_grad, qkv_w.reshape(model_width, -1).T, preferred_element_type=jnp.float32
    )
    first_grad = lax.psum(first_part, "tensor")
    norm_one_back = jax.vjp(rms_norm, inputs, gains_f[0])[1]
    input_norm_grad, gain_one_grad = norm_one_back(first_grad)
    input_grad = (residual_grad + input_norm_grad).astype(jnp.bfloat16)
    gains_grad = jnp.stack([gain_one_grad, gain_two_grad], axis=0)
    weight_grads = (
        lax.psum_scatter(gains_grad, "expert", scatter_dimension=1, tiled=True),
        lax.psum_scatter(qkv_weight_grad, "expert", scatter_dimension=0, tiled=True),
        lax.psum_scatter(qkv_bias_grad, "expert", scatter_dimension=2, tiled=True),
        lax.psum_scatter(out_weight_grad, "expert", scatter_dimension=1, tiled=True),
        lax.psum_scatter(router_grad, "expert", scatter_dimension=0, tiled=True),
        lax.psum_scatter(shared_gate_grad, "expert", scatter_dimension=0, tiled=True),
        lax.psum_scatter(shared_in_grad, "expert", scatter_dimension=0, tiled=True),
        lax.psum_scatter(shared_out_grad, "expert", scatter_dimension=1, tiled=True),
    )
    return (
        output,
        input_grad,
        weight_grads[0],
        weight_grads[1],
        weight_grads[2],
        weight_grads[3],
        weight_grads[4],
        weight_grads[5],
        weight_grads[6],
        weight_grads[7],
        expert_in_grad,
        expert_out_grad,
    )


def solution(mesh):
    return jax.shard_map(
        local,
        mesh=mesh,
        in_specs=(
            P("expert", None),
            P("expert", None),
            P(None, "expert"),
            P("expert", None, "tensor"),
            P(None, "tensor", "expert"),
            P("tensor", "expert"),
            P("expert", None),
            P("expert"),
            P("expert", None, "tensor"),
            P("tensor", "expert"),
            P("expert", None, None, "tensor"),
            P("expert", "tensor", None),
            P("expert", None),
            P("expert"),
        ),
        out_specs=(
            P("expert", None),
            P("expert", None),
            P(None, "expert"),
            P("expert", None, "tensor"),
            P(None, "tensor", "expert"),
            P("tensor", "expert"),
            P("expert", None),
            P("expert"),
            P("expert", None, "tensor"),
            P("tensor", "expert"),
            P("expert", None, None, "tensor"),
            P("expert", "tensor", None),
        ),
        check_vma=False,
    )
```

profile of v0, /device:TPU:0, one launch (start us, length us, event | category | flops | bytes accessed | tf_op | source)
XLA Modules:
  0.0 2560.8 jit_solution(13416080525370766545)
XLA Ops:
  10.6 23.9 all_gather.33
  35.3 17.6 all_gather.31
  56.2 61.8 %all-gather.6.cloned.1.call-done = bf16[2048,3,1024]{0,2,1:T(8,128)(2,1)} async-done(((bf16[128,3,1024]{0,2,1:T(8,128)(2,1)}), bf16[2048,3,1024]{0,2,1:T(8,128)(2,1)}) %all-gather.6.cloned.1.call-update) | async-done | bytes 12582928 | tf_op jit(solution)/shard_map/all_gather | solution.py:66
  128.9 42.6 %all-gather.8.cloned.1.call-done = bf16[1024,2048]{1,0:T(8,128)(2,1)} async-done(((bf16[1024,128]{1,0:T(8,128)(2,1)}), bf16[1024,2048]{1,0:T(8,128)(2,1)}) %all-gather.8.cloned.1.call-update) | async-done | bytes 4194320 | tf_op jit(solution)/shard_map/all_gather | solution.py:68
  189.1 48.5 %all-reduce.15.cloned.1.call-done = f32[256,2048]{1,0:T(8,128)} async-done(((f32[256,2048]{1,0:T(8,128)}), f32[256,2048]{1,0:T(8,128)}) %all-reduce.15.cloned.1.call-update) | async-done | bytes 2097168 | tf_op jit(solution)/shard_map/psum | solution.py:102
  242.4 14.1 gather_fusion
  262.7 185.2 %all-to-all-done = bf16[16,96,2048]{2,1,0:T(8,128)(2,1)} async-done(((bf16[16,96,2048]{2,1,0:T(8,128)(2,1)}), bf16[16,96,2048]{2,1,0:T(8,128)(2,1)}, u32[]{:S(2)}, u32[]{:S(2)}) %all-to-all-start) | async-done | bytes 6291488 | tf_op jit(solution)/shard_map/all_to_all | solution.py:130
  447.9 13.2 fusion.2
  471.7 24.1 all-to-all-start.1
  498.6 14.2 gather_fusion.3
  512.8 139.2 %all_gather.35 = bf16[2048,16]{0,1:T(8,128)(2,1)S(1)} all-gather(bf16[128,16]{0,1:T(8,128)(2,1)S(1)} %copy-done.51), channel_id=1, replica_groups=mesh['expert'=16,'tensor'=2] {'expert'}, dimensions={0}, use_global_device_ids=true | all-gather | bytes 69632 | tf_op jit(solution)/shard_map/all_gather | solution.py:69
  653.7 29.0 %copy.159 = bf16[2048,2,2816]{0,2,1:T(8,128)(2,1)} copy(bf16[2048,2,2816]{2,0,1:T(8,128)(2,1)} %all-gather.10.cloned.1.call-done) | data formatting | bytes 46137344 | tf_op jit(solution)/shard_map/all_gather | solution.py:71
  682.7 12.6 fusion
  719.5 15.5 fusion.91
  735.1 14.4 fusion.37
  771.2 202.4 %all_to_all.20 = bf16[16,96,2048]{2,1,0:T(8,128)(2,1)S(1)} all-to-all(bf16[16,96,2048]{2,1,0:T(8,128)(2,1)} %multiply_convert_fusion), channel_id=1, replica_groups=mesh['expert'=16,'tensor'=2] {'expert'}, dimensions={0} | all-to-all | bytes 12582912 | tf_op jit(solution)/shard_map/all_to_all | solution.py:183
  1004.0 117.5 %all-gather = bf16[16,1,128]{2,1,0:T(2,128)(2,1)S(1)} all-gather(bf16[1,1,128]{2,1,0:T(2,128)(2,1)S(1)} %bitcast.314), channel_id=1, replica_groups=mesh['expert'=16,'tensor'=2] {'expert'}, dimensions={0}, use_global_device_ids=true | all-gather | bytes 4352 | tf_op jit(solution)/shard_map/all_gather | solution.py:70
  1122.0 15.1 fusion.15
  1137.1 12.4 gather_fusion.4
  1156.6 15.4 fusion.90
  1172.0 16.3 fusion.23
  1199.3 80.7 %all-reduce.17.cloned.1.call-done = f32[256,2048]{1,0:T(8,128)} async-done(((f32[256,2048]{1,0:T(8,128)}), f32[256,2048]{1,0:T(8,128)}) %all-reduce.17.cloned.1.call-update) | async-done | bytes 2097168 | tf_op jit(solution)/shard_map/psum | solution.py:232
  1312.4 99.0 %all-reduce.19.cloned.1.call-done = (f32[256,2048]{1,0:T(8,128)}, f32[256,2048]{1,0:T(8,128)}) async-done(((f32[256,2048]{1,0:T(8,128)}, f32[256,2048]{1,0:T(8,128)}), (f32[256,2048]{1,0:T(8,128)}, f32[256,2048]{1,0:T(8,128)})) %all-reduce.19.cloned.1.call-update) | async-done | bytes 4194320 | tf_op jit(solution)/shard_map/psum | solution.py:152
  1415.1 20.3 fusion.16
  1436.5 12.7 fusion.61
  1482.6 15.0 convolution_bitcast_fusion
  1497.5 62.3 %all-reduce.8 = (f32[3,8,128]{2,1,0:T(8,128)S(1)}, f32[2048]{0:T(1024)S(1)}) all-reduce(f32[3,8,128]{2,1,0:T(8,128)S(1)} %get-tuple-element.87, f32[2048]{0:T(1024)S(1)} %bitcast.297), channel_id=4, replica_groups=mesh['expert'=16,'tensor'=2] {'expert'}, use_global_device_ids=true, to_apply=%region_32.33.clone | all-reduce | flops 5120 | bytes 40960
  1567.9 341.8 %reduce-scatter.16.cloned.1.call-done = f32[128,2,2816]{2,0,1:T(8,128)} async-done(((f32[2048,2,2816]{2,0,1:T(8,128)}), f32[128,2,2816]{2,0,1:T(8,128)}) %reduce-scatter.16.cloned.1.call-update) | async-done | bytes 2883600 | tf_op jit(solution)/shard_map/reduce_scatter | solution.py:306
  1915.4 49.6 %reduce-scatter.14.cloned.1.call-done = f32[128,16]{0,1:T(8,128)} async-done(((f32[2048,16]{0,1:T(8,128)}), f32[128,16]{0,1:T(8,128)}) %reduce-scatter.14.cloned.1.call-update) | async-done | bytes 8208 | tf_op jit(solution)/shard_map/reduce_scatter | solution.py:304
  1965.0 231.2 %reduce-scatter.18.cloned.1.call-done = f32[2816,128]{1,0:T(8,128)} async-done(((f32[2816,2048]{1,0:T(8,128)}), f32[2816,128]{1,0:T(8,128)}) %reduce-scatter.18.cloned.1.call-update) | async-done | bytes 1441808 | tf_op jit(solution)/shard_map/reduce_scatter | solution.py:307
  2196.2 109.1 %reduce-scatter.12.cloned.1.call-done = f32[1024,128]{1,0:T(8,128)} async-done(((f32[1024,2048]{1,0:T(8,128)}), f32[1024,128]{1,0:T(8,128)}) %reduce-scatter.12.cloned.1.call-update) | async-done | bytes 524304 | tf_op jit(solution)/shard_map/reduce_scatter | solution.py:303
  2305.2 248.9 %reduce-scatter.10.cloned.1.call-done = f32[128,3,1024]{2,0,1:T(8,128)} async-done(((f32[2048,3,1024]{2,0,1:T(8,128)}), f32[128,3,1024]{2,0,1:T(8,128)}) %reduce-scatter.10.cloned.1.call-update) | async-done | bytes 1572880 | tf_op jit(solution)/shard_map/reduce_scatter | solution.py:301
  (269 shorter events, 238.5 us)
Async XLA Ops:
  7.2 457.5 %copy-start = (bf16[1,704,2048]{2,1,0:T(8,128)(2,1)S(1)}, bf16[1,704,2048]{2,1,0:T(8,128)(2,1)}, u32[]{:S(2)}) copy-start(bf16[1,704,2048]{2,1,0:T(8,128)(2,1)} %param.25) | copy-start | bytes 8650756
  7.2 110.7 %all-gather.6.cloned.1.call-start = ((), (), s32[]{:S(2)}) async-start(), calls=%async_computation.10 | async-start | bytes 13369344 | tf_op jit(solution)/shard_map/all_gather | solution.py:66
  9.7 161.8 %all-gather.8.cloned.1.call-start = ((), (), s32[]{:S(2)}) async-start(), calls=%async_computation.11 | async-start | bytes 4456448 | tf_op jit(solution)/shard_map/all_gather | solution.py:68
  10.5 227.1 %all-reduce.15.cloned.1.call-start = ((), (), s32[]{:S(2)}) async-start(), calls=%async_computation.12 | async-start | bytes 4194304 | tf_op jit(solution)/shard_map/psum | solution.py:102
  56.0 69.0 %copy-start.42 = (f32[256]{0:T(256)}, f32[256]{0:T(256)S(1)}, u32[]{:S(2)}) copy-start(f32[256]{0:T(256)S(1)} %fusion.87) | copy-start | bytes 3076
  56.1 68.9 %copy-start.33 = (f32[1,2048]{1,0:T(1,128)}, f32[1,2048]{1,0:T(1,128)S(1)}, u32[]{:S(2)}) copy-start(f32[1,2048]{1,0:T(1,128)S(1)} %get-tuple-element.130) | copy-start | bytes 24580
  56.2 183.7 %copy-start.35 = (f32[1,2048]{1,0:T(1,128)}, f32[1,2048]{1,0:T(1,128)S(1)}, u32[]{:S(2)}) copy-start(f32[1,2048]{1,0:T(1,128)S(1)} %get-tuple-element.129) | copy-start | bytes 24580
  128.9 47.4 %copy-start.29 = (bf16[8,128,256]{2,1,0:T(8,128)(2,1)}, bf16[8,128,256]{2,1,0:T(8,128)(2,1)S(1)}, u32[]{:S(2)}) copy-start(bf16[8,128,256]{2,1,0:T(8,128)(2,1)S(1)} %convolution_convert_fusion.2) | copy-start | bytes 1572868
  176.3 477.4 %all-gather.10.cloned.1.call-start = ((), (), s32[]{:S(2)}) async-start(), calls=%async_computation.13 | async-start | bytes 24510464 | tf_op jit(solution)/shard_map/all_gather | solution.py:71
  256.4 191.5 %all-to-all-start = ((bf16[16,96,2048]{2,1,0:T(8,128)(2,1)}), bf16[16,96,2048]{2,1,0:T(8,128)(2,1)}, u32[]{:S(2)}, u32[]{:S(2)}) async-start(bf16[16,96,2048]{2,1,0:T(8,128)(2,1)} %bitcast.271), calls=%async_computation | async-start | bytes 12582912 | tf_op jit(solution)/shard_map/all_to_all | solution.py:130
  262.1 473.0 %all-gather.12.cloned.1.call-start = ((), (), s32[]{:S(2)}) async-start(), calls=%async_computation.14 | async-start | bytes 12255232 | tf_op jit(solution)/shard_map/all_gather | solution.py:72
  471.7 228.3 %all-to-all-start.1 = ((bf16[16,96,2048]{2,1,0:T(8,128)(2,1)}), bf16[16,96,2048]{2,1,0:T(8,128)(2,1)}, u32[]{:S(2)}, u32[]{:S(2)}) async-start(bf16[16,96,2048]{2,1,0:T(8,128)(2,1)} %bitcast.280), calls=%async_computation.1 | async-start | bytes 12582912 | tf_op jit(solution)/shard_map/all_to_all | solution.py:139
  771.2 215.1 %slice-start.3 = ((s8[5767168]{0:T(1024)(128)(4,1)}), s8[4194304]{0:T(1024)(128)(4,1)S(1)}, s32[]{:S(2)}) async-start(s8[5767168]{0:T(1024)(128)(4,1)} %bitcast.315), calls=%async_computation.26 | async-start | bytes 8388608
  998.3 123.3 %copy-start.3 = (bf16[256,2048]{1,0:T(8,128)(2,1)S(1)}, bf16[256,2048]{1,0:T(8,128)(2,1)}, u32[]{:S(2)}) copy-start(bf16[256,2048]{1,0:T(8,128)(2,1)} %copy-done.2) | copy-start | bytes 3145732
  998.3 123.6 %copy-start.14 = (bf16[256,2048]{1,0:T(8,128)(2,1)S(1)}, bf16[256,2048]{1,0:T(8,128)(2,1)}, u32[]{:S(2)}) copy-start(bf16[256,2048]{1,0:T(8,128)(2,1)} %param.15) | copy-start | bytes 3145732
  998.3 138.7 %all-to-all-start.3 = ((bf16[16,96,2048]{2,1,0:T(8,128)(2,1)}), bf16[16,96,2048]{2,1,0:T(8,128)(2,1)}, u32[]{:S(2)}, u32[]{:S(2)}) async-start(bf16[16,96,2048]{2,1,0:T(8,128)(2,1)} %bitcast.281), calls=%async_computation.3 | async-start | bytes 12582912 | tf_op jit(solution)/shard_map/all_to_all | solution.py:204
  1004.0 276.0 %all-reduce.17.cloned.1.call-start = ((), (), s32[]{:S(2)}) async-start(), calls=%async_computation.15 | async-start | bytes 4194304 | tf_op jit(solution)/shard_map/psum | solution.py:232
  1188.4 223.0 %all-reduce.19.cloned.1.call-start = ((), (), s32[]{:S(2)}) async-start(), calls=%async_computation.22 | async-start | bytes 8388608 | tf_op jit(solution)/shard_map/psum | solution.py:152
  1189.1 90.9 %copy-start.36 = (f32[1,2048]{1,0:T(1,128)S(1)}, f32[1,2048]{1,0:T(1,128)}, u32[]{:S(2)}) copy-start(f32[1,2048]{1,0:T(1,128)} %copy-done.35) | copy-start | bytes 24580
  1189.1 90.8 %copy-start.45 = (f32[256]{0:T(256)S(1)}, f32[256]{0:T(256)}, u32[]{:S(2)}) copy-start(f32[256]{0:T(256)} %copy-done.44) | copy-start | bytes 3076
  1303.0 263.3 %reduce-scatter.20.cloned.1.call-start = ((), (), s32[]{:S(2)}) async-start(), calls=%async_computation.21 | async-start | bytes 1114112
  1307.5 103.8 %copy-start.9 = (bf16[256,2048]{1,0:T(8,128)(2,1)S(1)}, bf16[256,2048]{1,0:T(8,128)(2,1)}, u32[]{:S(2)}) copy-start(bf16[256,2048]{1,0:T(8,128)(2,1)} %param.14) | copy-start | bytes 3145732
  1307.5 103.8 %copy-start.34 = (f32[1,2048]{1,0:T(1,128)S(1)}, f32[1,2048]{1,0:T(1,128)}, u32[]{:S(2)}) copy-start(f32[1,2048]{1,0:T(1,128)} %copy-done.33) | copy-start | bytes 24580
  1307.5 103.8 %copy-start.43 = (f32[256]{0:T(256)S(1)}, f32[256]{0:T(256)}, u32[]{:S(2)}) copy-start(f32[256]{0:T(256)} %copy-done.42) | copy-start | bytes 3076
  1415.1 494.7 %reduce-scatter.16.cloned.1.call-start = ((), (), s32[]{:S(2)}) async-start(), calls=%async_computation.19 | async-start | bytes 49020928 | tf_op jit(solution)/shard_map/reduce_scatter | solution.py:306
  1435.4 529.5 %reduce-scatter.14.cloned.1.call-start = ((), (), s32[]{:S(2)}) async-start(), calls=%async_computation.18 | async-start | bytes 139264 | tf_op jit(solution)/shard_map/reduce_scatter | solution.py:304
  1436.4 759.7 %reduce-scatter.18.cloned.1.call-start = ((), (), s32[]{:S(2)}) async-start(), calls=%async_computation.20 | async-start | bytes 24510464 | tf_op jit(solution)/shard_map/reduce_scatter | solution.py:307
  1449.2 856.0 %reduce-scatter.12.cloned.1.call-start = ((), (), s32[]{:S(2)}) async-start(), calls=%async_computation.17 | async-start | bytes 8912896 | tf_op jit(solution)/shard_map/reduce_scatter | solution.py:303
  1456.5 1097.7 %reduce-scatter.10.cloned.1.call-start = ((), (), s32[]{:S(2)}) async-start(), calls=%async_computation.16 | async-start | bytes 26738688 | tf_op jit(solution)/shard_map/reduce_scatter | solution.py:301
  1482.6 78.5 %copy-start.47 = (f32[256]{0:T(256)S(1)}, f32[256]{0:T(256)}, u32[]{:S(2)}) copy-start(f32[256]{0:T(256)} %copy-done.46) | copy-start | bytes 3076
  1482.6 78.5 %copy-start.6 = (f32[256,2048]{1,0:T(8,128)S(1)}, f32[256,2048]{1,0:T(8,128)}, u32[]{:S(2)}) copy-start(f32[256,2048]{1,0:T(8,128)} %copy-done.4) | copy-start | bytes 6291460
  1566.3 987.8 %copy-start.1 = (bf16[1,704,2048]{2,1,0:T(8,128)(2,1)S(1)}, bf16[1,704,2048]{2,1,0:T(8,128)(2,1)}, u32[]{:S(2)}) copy-start(bf16[1,704,2048]{2,1,0:T(8,128)(2,1)} %param.25) | copy-start | bytes 8650756
  (45 other events, 178.7 us)
Sparse Core Ops, SparseCore 0:
  10.8 107.1 all-gather.5
  120.1 51.3 all-gather.7
  176.4 61.0 all-reduce.14
  239.6 244.5 all-gather.9
  486.4 214.5 all-gather.11
  1188.5 91.4 all-reduce.16
  1303.1 108.2 all-reduce.18
  1416.0 57.3 reduce-scatter.19
  1477.7 432.0 reduce-scatter.15
  1913.6 51.3 reduce-scatter.13
  1970.2 225.8 reduce-scatter.17
  2201.2 103.9 reduce-scatter.11
  2310.4 243.6 reduce-scatter.9
where the time goes:
time: 2570 us; the launch traced here: 2560 us
  waiting for transfers between devices  1500 us (58%)
  blocking collectives  568 us (22%)
  matrix products  209 us (8%)
  local copies, waits for them, and re-layouts  183 us (7%)
  other arithmetic  47.8 us (2%)
  starting transfers between devices  36.8 us (1%)
    reduce_scatter x1, waiting for transfers between devices, local(): lax.psum_scatter(shared_in_grad, 'expert', scatter_dimension=0, tiled=True)  342 us
    reduce_scatter x1, waiting for transfers between devices, local(): lax.psum_scatter(qkv_weight_grad, 'expert', scatter_dimension=0, tiled=True)  249 us
    reduce_scatter x1, waiting for transfers between devices, local(): lax.psum_scatter(shared_out_grad, 'expert', scatter_dimension=1, tiled=True)  231 us
    all_to_all x1, blocking collectives, local(): lax.all_to_all(slot_grad, 'expert', split_axis=0, concat_axis=0, tiled=True)  202 us
    all_to_all x1, waiting for transfers between devices, local(): lax.all_to_all(send_rows, 'expert', split_axis=0, concat_axis=0, tiled=True)  185 us
    all_gather x1, blocking collectives, local(): lax.all_gather(router_weight, 'expert', axis=0, tiled=True)  139 us
    all_gather x1, blocking collectives, local(): lax.all_gather(shared_gate, 'expert', axis=0, tiled=True)  118 us
    reduce_scatter x1, waiting for transfers between devices, local(): lax.psum_scatter(out_weight_grad, 'expert', scatter_dimension=1, tiled=True)  109 us
  transfers between devices with their start and end apart: 16, of which 11 were waited for; matrix products, arithmetic and copies ran while one was open for 11% of the time, Pallas kernels for 0%

commit v1 on v0

v1 whole, which is shorter than its diff:
```python
import jax
import jax.numpy as jnp
import numpy as np
from jax import lax
from jax.sharding import PartitionSpec as P

eps = 1e-06
theta_base = 1000000.0
neg_large = -1e30
bf16 = jnp.bfloat16
f32 = jnp.float32


def rms_norm(values, gain_row):
    factor = lax.rsqrt(jnp.mean(values * values, axis=-1, keepdims=True) + eps)
    return values * factor * gain_row


def rotary_tables(length, head_size):
    half_size = head_size // 2
    frequency = np.float32(theta_base) ** (
        -(np.arange(half_size, dtype=np.float32) * np.float32(2.0)) / np.float32(head_size)
    )
    angles = np.arange(length, dtype=np.float32)[:, None] * frequency[None, :].astype(np.float32)
    cosine = np.concatenate([np.cos(angles), np.cos(angles)], axis=-1)[None, :, None, :]
    sine = np.concatenate([np.sin(angles), np.sin(angles)], axis=-1)[None, :, None, :]
    return jnp.asarray(cosine, f32), jnp.asarray(sine, f32)


def rotary(values, cosine, sine):
    half_size = values.shape[-1] // 2
    turned = jnp.concatenate([-values[..., half_size:], values[..., :half_size]], axis=-1)
    return values * cosine + turned * sine


def rotary_back(grads, cosine, sine):
    half_size = grads.shape[-1] // 2
    scaled = grads * sine
    turned = jnp.concatenate([scaled[..., half_size:], -scaled[..., :half_size]], axis=-1)
    return grads * cosine + turned


def silu_product(gate_part, up_part):
    return jax.nn.silu(gate_part) * up_part


def silu_back(gate_part, up_part, grad):
    return jax.vjp(silu_product, gate_part, up_part)[1](grad)


def chip_ring(chips):
    columns = chips // 4
    if chips % 4 or columns < 2 or columns % 2:
        return list(range(chips))
    walk = [(0, 0)]
    for column in range(columns):
        rows = range(1, 4) if column % 2 == 0 else range(3, 0, -1)
        walk += [(row, column) for row in rows]
    walk += [(0, column) for column in range(columns - 1, 0, -1)]
    return [row * columns + column for row, column in walk]


def mm(left, right, contract_left=1, contract_right=0):
    return lax.dot_general(
        left,
        right,
        (((contract_left,), (contract_right,)), ((), ())),
        preferred_element_type=f32,
    )


class Ring:
    def __init__(self, devices):
        self.devices = devices
        self.chips = devices // 2
        order = chip_ring(self.chips)
        n = self.chips
        self.next = [
            (order[i] * 2 + c, order[(i + 1) % n] * 2 + c) for i in range(n) for c in range(2)
        ]
        self.prev = [(b, a) for a, b in self.next]
        self.core = [(e, e ^ 1) for e in range(devices)]
        half = n // 2
        offsets = [0]
        for k in range(1, half):
            offsets += [-k, k]
        self.offsets = offsets + [half]
        place = {chip: i for i, chip in enumerate(order)}
        self.chip_table = np.array(
            [
                [order[(place[e // 2] + o) % n] for o in self.offsets]
                for e in range(devices)
            ],
            np.int32,
        )
        self.seq_table = np.stack(
            [
                2 * self.chip_table + (np.arange(devices) % 2)[:, None],
                2 * self.chip_table + 1 - (np.arange(devices) % 2)[:, None],
            ],
            axis=-1,
        ).reshape(devices, devices)
        self.seq_inverse = np.argsort(self.seq_table, axis=1).astype(np.int32)

    def gather(self, block):
        half = self.chips // 2
        found = {0: block}
        ahead = back = block
        for k in range(1, half):
            ahead = lax.ppermute(ahead, "expert", self.next)
            back = lax.ppermute(back, "expert", self.prev)
            found[-k], found[k] = ahead, back
        cut = block.shape[0] // 2
        first = lax.ppermute(ahead[:cut], "expert", self.next)
        second = lax.ppermute(back[cut:], "expert", self.prev)
        found[half] = jnp.concatenate([first, second], axis=0)
        return found

    def reduce(self, terms):
        half = self.chips // 2

        def total(offset, more=()):
            out = None
            for term in list(terms[offset]) + list(more):
                out = term.astype(f32) if out is None else out + term.astype(f32)
            return out

        far = total(half).astype(bf16)
        cut = far.shape[0] // 2
        ahead = lax.ppermute(far[:cut], "expert", self.next)
        back = lax.ppermute(far[cut:], "expert", self.prev)
        for k in range(half - 1, 0, -1):
            mine, yours = total(k), total(-k)
            if k == half - 1:
                mine = jnp.concatenate([mine[:cut] + ahead.astype(f32), mine[cut:]], axis=0)
                yours = jnp.concatenate([yours[:cut], yours[cut:] + back.astype(f32)], axis=0)
            else:
                mine = mine + ahead.astype(f32)
                yours = yours + back.astype(f32)
            ahead = lax.ppermute(mine.astype(bf16), "expert", self.next)
            back = lax.ppermute(yours.astype(bf16), "expert", self.prev)
        return total(0, (ahead, back))

    def swap_core(self, block):
        return lax.ppermute(block, "expert", self.core)

    def gather_small(self, row, me):
        held = row[None]
        step = 1
        while step < self.devices:
            pairs = [(e, e ^ step) for e in range(self.devices)]
            other = lax.ppermute(held, "expert", pairs)
            upper = (me // step) % 2 == 1
            held = jnp.where(
                upper, jnp.concatenate([other, held]), jnp.concatenate([held, other])
            )
            step *= 2
        return held


def after(value, *others):
    return lax.optimization_barrier((value,) + others)[0]


def swap_tensor(block):
    return lax.ppermute(block, "tensor", [(0, 1), (1, 0)])


def sum_tensor(part):
    own = part.astype(bf16)
    return own.astype(f32) + swap_tensor(own).astype(f32)


def make_local(ring):
    devices, chips = ring.devices, ring.chips

    def local(
        tokens_in,
        cotangent,
        norm_gains,
        qkv_weight,
        qkv_bias,
        out_weight,
        router_weight,
        shared_gate,
        shared_in,
        shared_out,
        expert_in,
        expert_out,
        expert_ids,
        prefix_len,
    ):
        me = lax.axis_index("expert")
        core = me % 2
        length, width = tokens_in.shape
        top_count = expert_ids.shape[1]
        experts = router_weight.shape[1]
        capacity = length * top_count * 3 // (2 * experts)
        rows_dev = qkv_weight.shape[0]
        heads_t = qkv_bias.shape[1]
        heads = heads_t // 2
        hd_dev = qkv_bias.shape[2]
        head_size = hd_dev * devices
        half_cols = heads * head_size
        score_scale = head_size ** (-0.5)
        chip_of = jnp.asarray(ring.chip_table)[me]
        seq_of = jnp.asarray(ring.seq_table)[me]
        seq_inv = jnp.asarray(ring.seq_inverse)[me]

        def own_first(own, other):
            return jnp.where(
                core == 0,
                jnp.concatenate([own, other], axis=0),
                jnp.concatenate([other, own], axis=0),
            )

        pieces = [
            norm_gains.reshape(-1),
            qkv_bias.reshape(-1),
            router_weight.reshape(-1),
            shared_gate.reshape(-1),
            expert_ids.astype(bf16).reshape(-1),
            prefix_len.astype(bf16).reshape(-1),
        ]
        sizes = [p.shape[0] for p in pieces]
        total = sum(sizes)
        padded = -(-total // 1024) * 1024
        small = jnp.concatenate(pieces + [jnp.zeros((padded - total,), bf16)])
        small_all = ring.gather_small(small, me)
        cuts = np.cumsum([0] + sizes)
        found = [small_all[:, cuts[i] : cuts[i + 1]] for i in range(len(sizes))]
        gains_f = (
            found[0].reshape(devices, 2, rows_dev).transpose(1, 0, 2).reshape(2, width).astype(f32)
        )
        bias_all = (
            found[1].reshape(devices, 3, heads_t, hd_dev).transpose(1, 2, 0, 3)
            .reshape(3, 2, half_cols)
        )
        bias = lax.dynamic_index_in_dim(bias_all, core, 1, keepdims=False).astype(f32)
        router_w = found[2].reshape(width, experts)
        gate_vec = found[3].reshape(width)
        ids_all = found[4].reshape(devices, length, top_count).astype(jnp.int32)
        prefix_all = found[5].reshape(devices).astype(jnp.int32)
        prefix_pair = jnp.stack([prefix_all[me], prefix_all[me ^ 1]])

        def halve(weight, parts):
            halves = weight.reshape(rows_dev, parts, 2, half_cols)
            own = lax.dynamic_index_in_dim(halves, core, 2, keepdims=False)
            other = lax.dynamic_index_in_dim(halves, 1 - core, 2, keepdims=False)
            got = ring.swap_core(other.reshape(rows_dev, -1))
            return own_first(own.reshape(rows_dev, -1), got)

        def assemble(blocks):
            depth = 2 * rows_dev
            whole = jnp.zeros((width, blocks[0].shape[1]), bf16)
            for i, offset in enumerate(ring.offsets):
                whole = lax.dynamic_update_slice(whole, blocks[offset], (chip_of[i] * depth, 0))
            return whole

        qkv_blocks = ring.gather(halve(qkv_weight, 3))
        qkv_w = assemble(qkv_blocks)
        out_block = after(halve(out_weight.T, 1), qkv_blocks[chips // 2 - 1])
        out_w = assemble(ring.gather(out_block))

        units = shared_out.shape[0]
        unit_chip = units // chips
        sh_rows = jnp.concatenate(
            [
                shared_in.reshape(rows_dev, 2, chips, unit_chip),
                shared_out.T.reshape(rows_dev, 1, chips, unit_chip),
            ],
            axis=1,
        )
        sh_send = sh_rows.transpose(2, 0, 1, 3).reshape(chips, rows_dev, 3 * unit_chip)
        sh_send = after(sh_send, qkv_blocks[chips // 2])
        same_core = [[2 * i + c for i in range(chips)] for c in range(2)]
        sh_mine = lax.all_to_all(
            sh_send, "expert", split_axis=0, concat_axis=0, tiled=True, axis_index_groups=same_core
        )
        sh_other = ring.swap_core(sh_mine)
        sh_w = jnp.where(
            core == 0,
            jnp.stack([sh_mine, sh_other], axis=1),
            jnp.stack([sh_other, sh_mine], axis=1),
        ).reshape(width, 3 * unit_chip)
        sh_in = sh_w[:, : 2 * unit_chip]
        sh_out_t = sh_w[:, 2 * unit_chip :]

        up_own = ring.gather(after(cotangent, qkv_blocks[chips // 2]))
        up_other = {o: ring.swap_core(b) for o, b in up_own.items()}

        inputs = tokens_in.astype(f32)
        first_b = rms_norm(inputs, gains_f[0]).astype(bf16)
        first_pair = jnp.concatenate([first_b, ring.swap_core(first_b)], axis=0)
        cosine, sine = rotary_tables(length, head_size)
        projected = mm(first_pair, qkv_w) + bias.reshape(-1)[None]
        projected = projected.reshape(2, length, 3, heads, head_size)
        query_heads = rotary(projected[:, :, 0], cosine, sine).astype(bf16)
        key_heads = rotary(projected[:, :, 1], cosine, sine).astype(bf16)
        value_heads = projected[:, :, 2].astype(bf16)
        scores = (
            jnp.einsum("bqhd,bkhd->bhqk", query_heads, key_heads, preferred_element_type=f32)
            * score_scale
        )
        row_index = jnp.arange(length, dtype=jnp.int32)[None, :, None]
        col_index = jnp.arange(length, dtype=jnp.int32)[None, None, :]
        allowed = (col_index <= row_index) | (col_index < prefix_pair[:, None, None])
        scores = jnp.where(allowed[:, None], scores, neg_large)
        row_max = jnp.max(scores, axis=-1, keepdims=True)
        weights = jnp.exp(scores - row_max)
        probs = weights / jnp.sum(weights, axis=-1, keepdims=True)
        probs_low = probs.astype(bf16)
        mixed = jnp.einsum("bhqk,bkhd->bqhd", probs_low, value_heads, preferred_element_type=f32)
        mixed = mixed.reshape(2 * length, half_cols).astype(bf16)
        attn_part = mm(mixed, out_w, 1, 1)
        attn_got = ring.swap_core(attn_part[length:].astype(bf16))
        attn_out = sum_tensor(attn_part[:length] + attn_got.astype(f32))
        residual = inputs + attn_out
        second_b = rms_norm(residual, gains_f[1]).astype(bf16)

        rows_own = ring.gather(second_b)
        rows_other = {o: ring.swap_core(b) for o, b in rows_own.items()}

        logits = mm(second_b, router_w)
        expert_range = jnp.arange(experts, dtype=jnp.int32)
        route_match = expert_ids[:, :, None] == expert_range[None, None, :]
        chosen = jnp.sum(jnp.where(route_match, logits[:, None, :], 0.0), axis=-1)
        gate_weights = jax.nn.softmax(chosen, axis=-1)
        shared_sigma = jax.nn.sigmoid(
            jnp.sum(second_b.astype(f32) * gate_vec.astype(f32)[None], axis=-1)
        )
        gate_dense = jnp.sum(jnp.where(route_match, gate_weights[:, :, None], 0.0), axis=1)
        gate_send = jnp.stack(
            [gate_dense.T, jnp.broadcast_to(shared_sigma[None], (experts, length))], axis=1
        )
        gate_all = lax.all_to_all(gate_send, "expert", split_axis=0, concat_axis=0, tiled=True)
        gate_all = gate_all[seq_of]
        gate_tok, sigma_tok = gate_all[:, 0], gate_all[:, 1]

        match = jnp.any(ids_all[seq_of] == me, axis=-1)
        triangle = jnp.asarray(np.triu(np.ones((length, length), np.float32)), bf16)
        rank = mm(match.astype(bf16), triangle) - 1.0
        slots = jnp.arange(capacity, dtype=f32)[None, :, None]
        pick = (slots == rank[:, None, :]) & match[:, None, :]
        pick_b = pick.astype(bf16)
        gate_slot = jnp.sum(jnp.where(pick, gate_tok[:, None, :], 0.0), axis=-1)

        ex_in = expert_in[0].reshape(width, -1)
        ex_out = expert_out[0]
        part_units = ex_out.shape[0]
        near = [i for i, o in enumerate(ring.offsets) if 4 * abs(o) <= chips]
        far = [i for i, o in enumerate(ring.offsets) if 4 * abs(o) > chips]

        def forward(group):
            held = {}
            offs = [ring.offsets[i] for i in group]
            held["rows"] = jnp.concatenate(
                [
                    mm(pick_b[2 * i + c], (rows_own, rows_other)[c][ring.offsets[i]]).astype(bf16)
                    for i in group
                    for c in range(2)
                ],
                axis=0,
            )
            gate_up = mm(held["rows"], ex_in)
            held["gate"], held["up"] = gate_up[:, :part_units], gate_up[:, part_units:]
            held["hidden"] = silu_product(held["gate"], held["up"]).astype(bf16)
            held["produced"] = mm(held["hidden"], ex_out).astype(bf16)
            lo, hi = 2 * group[0], 2 * group[-1] + 2
            held["gates"] = gate_slot[lo:hi].reshape(-1, 1)
            weighted = (held["gates"] * held["produced"].astype(f32)).astype(bf16)
            held["tokens"] = jnp.concatenate([rows_own[o] for o in offs], axis=0)
            shared_gu = mm(held["tokens"], sh_in)
            held["sgate"], held["sup"] = shared_gu[:, :unit_chip], shared_gu[:, unit_chip:]
            held["shidden"] = silu_product(held["sgate"], held["sup"]).astype(bf16)
            held["shared"] = mm(held["shidden"], sh_out_t, 1, 1)
            held["sigma"] = sigma_tok.reshape(-1, 2, length)[group[0] : group[-1] + 1, 0].reshape(-1, 1)
            gated = held["sigma"] * held["shared"]
            own, other = {}, {}
            for j, i in enumerate(group):
                block = weighted[2 * j * capacity : (2 * j + 1) * capacity]
                routed = mm(pick_b[2 * i], block, 0, 0)
                own[offs[j]] = (routed + gated[j * length : (j + 1) * length]).astype(bf16)
                block = weighted[(2 * j + 1) * capacity : (2 * j + 2) * capacity]
                other[offs[j]] = mm(pick_b[2 * i + 1], block, 0, 0).astype(bf16)
            return held, own, other

        def backward(group, held):
            offs = [ring.offsets[i] for i in group]
            lo, hi = 2 * group[0], 2 * group[-1] + 2
            up_rows = jnp.concatenate(
                [
                    mm(pick_b[2 * i + c], (up_own, up_other)[c][ring.offsets[i]])
                    for i in group
                    for c in range(2)
                ],
                axis=0,
            )
            dots = jnp.sum(up_rows * held["produced"].astype(f32), axis=-1)
            dots = jnp.sum(
                jnp.where(pick[lo:hi], dots.reshape(-1, capacity)[:, :, None], 0.0), axis=1
            )
            slot_grad = (held["gates"] * up_rows).astype(bf16)
            hidden_grad = mm(slot_grad, ex_out, 1, 1)
            gate_grad, up_grad = silu_back(held["gate"], held["up"], hidden_grad)
            gu_grad = jnp.concatenate([gate_grad.astype(bf16), up_grad.astype(bf16)], axis=1)
            entry_grad = mm(gu_grad, ex_in, 1, 1).astype(bf16)
            upstream = jnp.concatenate([up_own[o] for o in offs], axis=0).astype(f32)
            sigma_dots = jnp.sum(upstream * held["shared"], axis=-1).reshape(-1, length)
            y_grad = (held["sigma"] * upstream).astype(bf16)
            shared_hidden_grad = mm(y_grad, sh_out_t)
            gate_grad, up_grad = silu_back(held["sgate"], held["sup"], shared_hidden_grad)
            shared_gu_grad = jnp.concatenate([gate_grad.astype(bf16), up_grad.astype(bf16)], axis=1)
            shared_back = mm(shared_gu_grad, sh_in, 1, 1)
            own, other = {}, {}
            for j, i in enumerate(group):
                block = entry_grad[2 * j * capacity : (2 * j + 1) * capacity]
                routed = mm(pick_b[2 * i], block, 0, 0)
                own[offs[j]] = (routed + shared_back[j * length : (j + 1) * length]).astype(bf16)
                block = entry_grad[(2 * j + 1) * capacity : (2 * j + 2) * capacity]
                other[offs[j]] = mm(pick_b[2 * i + 1], block, 0, 0).astype(bf16)
            later = (slot_grad, gu_grad, y_grad, shared_gu_grad)
            return own, other, dots, sigma_dots, later

        held_near, moe_near, moe_near_o = forward(near)
        held_far, moe_far, moe_far_o = forward(far)
        moe_own, moe_other = {**moe_near, **moe_far}, {**moe_near_o, **moe_far_o}

        back_far, back_far_o, dots_far, sdots_far, later_far = backward(far, held_far)
        back_near, back_near_o, dots_near, sdots_near, later_near = backward(near, held_near)
        back_own, back_other = {**back_near, **back_far}, {**back_near_o, **back_far_o}
        back_terms = {o: [b, ring.swap_core(back_other[o])] for o, b in back_own.items()}
        second_part = ring.reduce(back_terms)

        moe_terms = {o: [b, ring.swap_core(moe_other[o])] for o, b in moe_own.items()}
        moe_part = ring.reduce(moe_terms)
        output = (residual + sum_tensor(moe_part)).astype(bf16)

        dots = jnp.concatenate([dots_near, dots_far], axis=0)
        sdots = jnp.concatenate([sdots_near, sdots_far], axis=0)
        sdots = jnp.stack([sdots, jnp.zeros_like(sdots)], axis=1).reshape(devices, length)
        dot_send = jnp.stack([dots, sdots], axis=1)[seq_inv]
        dot_got = lax.all_to_all(dot_send, "expert", split_axis=0, concat_axis=0, tiled=True)
        dot_got = jnp.concatenate([dot_got[:, 0], jnp.sum(dot_got[:, 1], axis=0)[None]], axis=0)
        dot_got = dot_got + swap_tensor(dot_got)
        gate_grad_dense, sigma_grad = dot_got[:experts].T, dot_got[experts]
        row_term = jnp.sum(gate_dense * gate_grad_dense, axis=-1, keepdims=True)
        logit_grad = (gate_dense * (gate_grad_dense - row_term)).astype(bf16)
        gate_logit_grad = sigma_grad * shared_sigma * (1.0 - shared_sigma)

        second_grad = sum_tensor(second_part)
        second_grad = second_grad + mm(logit_grad, router_w, 1, 1)
        second_grad = second_grad + gate_logit_grad[:, None] * gate_vec.astype(f32)[None]
        upstream = cotangent.astype(f32)
        residual_norm_grad, gain_two_grad = jax.vjp(rms_norm, residual, gains_f[1])[1](second_grad)
        residual_grad = upstream + residual_norm_grad
        attn_grad = residual_grad.astype(bf16)
        attn_grad_pair = jnp.concatenate([attn_grad, ring.swap_core(attn_grad)], axis=0)

        depth = 2 * rows_dev

        def by_chip(left, right):
            return {
                offset: [
                    mm(lax.dynamic_slice_in_dim(left, chip_of[i] * depth, depth, 1), right, 0, 0)
                ]
                for i, offset in enumerate(ring.offsets)
            }

        out_grad = ring.reduce(by_chip(attn_grad_pair, mixed))
        mixed_grad = mm(attn_grad_pair, out_w).astype(bf16).reshape(2, length, heads, head_size)
        prob_grad = jnp.einsum(
            "bqhd,bkhd->bhqk", mixed_grad, value_heads, preferred_element_type=f32
        )
        row_term = jnp.sum(probs * prob_grad, axis=-1, keepdims=True)
        score_grad = (probs * (prob_grad - row_term)).astype(bf16)
        query_grad = (
            jnp.einsum("bhqk,bkhd->bqhd", score_grad, key_heads, preferred_element_type=f32)
            * score_scale
        )
        key_grad = (
            jnp.einsum("bhqk,bqhd->bkhd", score_grad, query_heads, preferred_element_type=f32)
            * score_scale
        )
        value_grad = jnp.einsum(
            "bhqk,bqhd->bkhd", probs_low, mixed_grad, preferred_element_type=f32
        )
        proj_grad = jnp.stack(
            [
                rotary_back(query_grad, cosine, sine).astype(bf16),
                rotary_back(key_grad, cosine, sine).astype(bf16),
                value_grad.astype(bf16),
            ],
            axis=2,
        ).reshape(2 * length, 3 * half_cols)
        qkv_grad = ring.reduce(by_chip(first_pair, proj_grad))
        bias_grad = jnp.sum(proj_grad.astype(f32), axis=0)
        first_part = mm(proj_grad, qkv_w, 1, 1)
        first_got = ring.swap_core(first_part[length:].astype(bf16))
        first_grad = sum_tensor(first_part[:length] + first_got.astype(f32))
        input_norm_grad, gain_one_grad = jax.vjp(rms_norm, inputs, gains_f[0])[1](first_grad)
        input_grad = (residual_grad + input_norm_grad).astype(bf16)

        def regroup(grad, parts):
            grad = grad.reshape(2, rows_dev, parts * half_cols)
            own = lax.dynamic_index_in_dim(grad, core, 0, keepdims=False)
            other = lax.dynamic_index_in_dim(grad, 1 - core, 0, keepdims=False)
            own = own.astype(bf16).reshape(rows_dev, parts, half_cols)
            got = ring.swap_core(other.astype(bf16)).reshape(rows_dev, parts, half_cols)
            both = jnp.where(
                core == 0, jnp.stack([own, got], axis=2), jnp.stack([got, own], axis=2)
            )
            return both.reshape(rows_dev, parts, 2 * half_cols).astype(f32)

        qkv_weight_grad = regroup(qkv_grad, 3)
        out_weight_grad = regroup(out_grad, 1)[:, 0].T

        def two(left, right):
            return mm(left[0], right[0], 0, 0) + mm(left[1], right[1], 0, 0)

        slot_grads, gu_grads, y_grads, sgu_grads = zip(later_near, later_far, strict=True)
        expert_out_grad = two((held_near["hidden"], held_far["hidden"]), slot_grads)[None]
        expert_in_grad = two((held_near["rows"], held_far["rows"]), gu_grads).reshape(
            1, width, 2, part_units
        )
        tokens = (held_near["tokens"], held_far["tokens"])
        sh_grad = jnp.concatenate(
            [
                two(tokens, sgu_grads).astype(bf16),
                two(y_grads, (held_near["shidden"], held_far["shidden"])).astype(bf16),
            ],
            axis=1,
        ).reshape(chips, 2, rows_dev, 3 * unit_chip)
        sh_own = lax.dynamic_index_in_dim(sh_grad, core, 1, keepdims=False)
        sh_give = lax.dynamic_index_in_dim(sh_grad, 1 - core, 1, keepdims=False)
        sh_sum = (sh_own.astype(f32) + ring.swap_core(sh_give).astype(f32)).astype(bf16)
        sh_back = lax.all_to_all(
            sh_sum, "expert", split_axis=0, concat_axis=0, tiled=True, axis_index_groups=same_core
        )
        sh_back = sh_back.reshape(chips, rows_dev, 3, unit_chip).transpose(1, 2, 0, 3)
        sh_back = sh_back.reshape(rows_dev, 3, units).astype(f32)
        shared_in_grad = sh_back[:, :2]
        shared_out_grad = sh_back[:, 2].T

        second_f = second_b.astype(f32)
        router_part = mm(second_b, logit_grad, 0, 0)
        shared_gate_part = jnp.sum(gate_logit_grad[:, None] * second_f, axis=0)
        early = jnp.concatenate(
            [router_part, shared_gate_part[:, None], gain_two_grad[:, None]], axis=1
        ).reshape(devices, rows_dev * (experts + 2))
        early = lax.all_to_all(early, "expert", split_axis=0, concat_axis=0, tiled=True)
        early = jnp.sum(early, axis=0).reshape(rows_dev, experts + 2)
        router_grad, shared_gate_grad = early[:, :experts], early[:, experts]
        bias_send = bias_grad.reshape(3 * heads, devices, hd_dev).transpose(1, 0, 2)
        late = jnp.concatenate(
            [gain_one_grad.reshape(devices, rows_dev), bias_send.reshape(devices, -1)], axis=1
        )
        late = lax.all_to_all(late, "expert", split_axis=0, concat_axis=0, tiled=True)
        gain_one = jnp.sum(late[:, :rows_dev], axis=0)
        bias_got = jnp.sum(late[:, rows_dev:].reshape(chips, 2, 3, heads, hd_dev), axis=0)
        qkv_bias_grad = bias_got.transpose(1, 0, 2, 3).reshape(3, heads_t, hd_dev)
        gains_grad = jnp.stack([gain_one, early[:, experts + 1]], axis=0)

        return (
            output,
            input_grad,
            gains_grad,
            qkv_weight_grad,
            qkv_bias_grad,
            out_weight_grad,
            router_grad,
            shared_gate_grad,
            shared_in_grad,
            shared_out_grad,
            expert_in_grad,
            expert_out_grad,
        )

    return local


def solution(mesh):
    ring = Ring(mesh.shape["expert"])
    return jax.shard_map(
        make_local(ring),
        mesh=mesh,
        in_specs=(
            P("expert", None),
            P("expert", None),
            P(None, "expert"),
            P("expert", None, "tensor"),
            P(None, "tensor", "expert"),
            P("tensor", "expert"),
            P("expert", None),
            P("expert"),
            P("expert", None, "tensor"),
            P("tensor", "expert"),
            P("expert", None, None, "tensor"),
            P("expert", "tensor", None),
            P("expert", None),
            P("expert"),
        ),
        out_specs=(
            P("expert", None),
            P("expert", None),
            P(None, "expert"),
            P("expert", None, "tensor"),
            P(None, "tensor", "expert"),
            P("tensor", "expert"),
            P("expert", None),
            P("expert"),
            P("expert", None, "tensor"),
            P("tensor", "expert"),
            P("expert", None, None, "tensor"),
            P("expert", "tensor", None),
        ),
        check_vma=False,
    )
```

time: 2570 us -> 1130 us (0.44)
  waiting for transfers between devices: 1500 us -> 356 us
  blocking collectives: 568 us -> 0 us
  matrix products: 209 us -> 334 us
  starting transfers between devices: 36.8 us -> 141 us
  other arithmetic: 47.8 us -> 85.5 us
    reduce_scatter x5 -> x0, waiting for transfers between devices: 981 us -> none  [the longest x1 342 us: local(): lax.psum_scatter(shared_in_grad, 'expert', scatter_dimension=0, tiled=True)]
    ppermute x0 -> x115, waiting for transfers between devices: none -> 347 us  [the longest x12 107 us: reduce(): back = lax.ppermute(yours.astype(bf16), 'expert', self.prev)]
    all_gather x4 -> x0, blocking collectives: 298 us -> none  [the longest x1 139 us: local(): lax.all_gather(router_weight, 'expert', axis=0, tiled=True)]
    psum x3 -> x0, waiting for transfers between devices: 228 us -> none  [the longest x1 99 us: local(): moe_out = lax.psum(moe_part, 'tensor')]
    all_to_all x1 -> x0, blocking collectives: 202 us -> none  [local(): lax.all_to_all(slot_grad, 'expert', split_axis=0, concat_axis=0, tiled=True)]
    all_to_all x3 -> x6, waiting for transfers between devices: 185 us -> 9.41 us  [the longest x1 5.11 us: local(): lax.all_to_all(dot_send, 'expert', split_axis=0, concat_axis=0, tiled=True)]
    dot_general x29 -> x117, matrix products: 209 us -> 330 us  [the longest x112 323 us: mm(): lax.dot_general(left, right, (((contract_left,), (contract_right,)), ((),...]
    ppermute x0 -> x115, starting transfers between devices: none -> 114 us  [the longest x12 26.8 us: reduce(): ahead = lax.ppermute(mine.astype(bf16), 'expert', self.next)]
  transfers between devices with their start and end apart: 16 -> 121, of which waited for: 11 -> 42; matrix products, arithmetic and copies ran while one was open for 11% -> 39% of each run, Pallas kernels for 0% -> 0%
where the time goes in v1:
time: 1130 us; the launch traced here: 1120 us
  waiting for transfers between devices  356 us (32%)
  matrix products  334 us (30%)
  local copies, waits for them, and re-layouts  197 us (17%)
  starting transfers between devices  141 us (12%)
  other arithmetic  85.5 us (8%)
    dot_general x112, matrix products, mm(): lax.dot_general(left, right, (((contract_left,), (contract_right,)), ((),...  323 us
    ppermute x12, waiting for transfers between devices, reduce(): back = lax.ppermute(yours.astype(bf16), 'expert', self.prev)  107 us
    ppermute x12, waiting for transfers between devices, gather(): back = lax.ppermute(back, 'expert', self.prev)  89.6 us
    ppermute x12, waiting for transfers between devices, reduce(): ahead = lax.ppermute(mine.astype(bf16), 'expert', self.next)  76.9 us
    unnamed x301, local copies, waits for them, and re-layouts  63.2 us
    ppermute x12, starting transfers between devices, reduce(): ahead = lax.ppermute(mine.astype(bf16), 'expert', self.next)  26.8 us
    select_n x2, local copies, waits for them, and re-layouts, local(): jnp.where(core == 0, jnp.stack([sh_mine, sh_other], axis=1), jnp.stack([s...  26.1 us
    ppermute x4, waiting for transfers between devices, gather(): first = lax.ppermute(ahead[:cut], 'expert', self.next)  25.8 us
  transfers between devices with their start and end apart: 121, of which 42 were waited for; matrix products, arithmetic and copies ran while one was open for 39% of the time, Pallas kernels for 0%

profile of v1, /device:TPU:0, one launch (start us, length us, event | category | flops | bytes accessed | tf_op | source)
XLA Modules:
  0.0 1123.4 jit_solution(1083705054023143732)
XLA Ops:
  63.8 8.5 collective-permute-done.6
  76.6 13.6 %collective-permute-done.8 = bf16[256,1536]{0,1:T(8,128)(2,1)S(1)} collective-permute-done((bf16[256,1536]{0,1:T(8,128)(2,1)}, bf16[256,1536]{0,1:T(8,128)(2,1)S(1)}, u32[]{:S(2)}, u32[]{:S(2)}) %collective-permute-start.8) | collective-permute-done | bytes 786464 | tf_op jit(solution)/shard_map/ppermute | solution.py:110
  98.5 10.1 collective-permute-done.11
  130.0 8.3 convolution_add_fusion.1
  211.5 44.8 %collective-permute-done.66 = bf16[256,2048]{1,0:T(8,128)(2,1)} collective-permute-done((bf16[256,2048]{1,0:T(8,128)(2,1)}, bf16[256,2048]{1,0:T(8,128)(2,1)}, u32[]{:S(2)}, u32[]{:S(2)}) %collective-permute-start.66) | collective-permute-done | bytes 1048608 | tf_op jit(solution)/shard_map/ppermute | solution.py:111
  258.7 13.3 %collective-permute-start.71 = (bf16[256,2048]{1,0:T(8,128)(2,1)}, bf16[256,2048]{1,0:T(8,128)(2,1)}, u32[]{:S(2)}, u32[]{:S(2)}) collective-permute-start(bf16[256,2048]{1,0:T(8,128)(2,1)} %collective-permute-done.64), channel_id=1, source_target_pairs={{0,8},{2,10},{8,16},{10,18},{16,24},{18,26},{24,28},{26,30},{28,20... | collective-permute-start | bytes 3145736 | tf_op jit(solution)/shard_map/ppermute | solution.py:110
  309.0 20.4 %collective-permute-done.75 = bf16[128,2048]{1,0:T(8,128)(2,1)S(1)} collective-permute-done((bf16[128,2048]{1,0:T(8,128)(2,1)S(1)}, bf16[128,2048]{1,0:T(8,128)(2,1)S(1)}, u32[]{:S(2)}, u32[]{:S(2)}) %collective-permute-start.75) | collective-permute-done | bytes 524320 | tf_op jit(solution)/shard_map/ppermute | solution.py:114
  342.7 18.0 %collective-permute-done.32 = bf16[256,2048]{1,0:T(8,128)(2,1)} collective-permute-done((bf16[256,2048]{1,0:T(8,128)(2,1)}, bf16[256,2048]{1,0:T(8,128)(2,1)}, u32[]{:S(2)}, u32[]{:S(2)}) %collective-permute-start.32) | collective-permute-done | bytes 1048608 | tf_op jit(solution)/shard_map/ppermute | solution.py:111
  376.4 9.3 collective-permute-done.40
  396.5 10.6 fusion.336
  425.3 15.3 %copy.285 = bf16[8,2,128,1056]{2,1,0,3:T(2,128)(2,1)} copy(bf16[8,2,128,1056]{2,3,0,1:T(8,128)(2,1)S(1)} %maximum_select_fusion) | data formatting | bytes 8650752 | tf_op jit(solution)/shard_map/jit(_where)/select_n | solution.py:281
  440.6 10.7 select_n.277
  574.8 11.0 fusion.12
  634.0 10.7 fusion.109
  685.7 11.1 reshape.494
  696.8 11.4 %convolution_add_fusion = f32[2048,1408]{0,1:T(8,128)} fusion(f32[2048,1408]{0,1:T(8,128)} %fusion.109, bf16[576,2048]{1,0:T(8,128)(2,1)S(1)} %copy-done.103, bf16[576,704]{1,0:T(8,128)(2,1)} %get-tuple-element.124, bf16[576,704]{1,0:T(8,128)(2,1)} %get-tuple-element.123), kind=kOutput, calls=%fused_computation.10 | convolution fusion | flops 3328016384 | bytes 27049984 | tf_op jit(solution)/shard_map/dot_general | solution.py:64
  708.2 9.0 constant_dynamic-slice_fusion.1
  737.2 10.7 collective-permute-done.47
  752.5 8.6 collective-permute-done.80
  773.1 14.7 %collective-permute-done.55 = bf16[256,2048]{1,0:T(8,128)(2,1)} collective-permute-done((bf16[256,2048]{1,0:T(8,128)(2,1)}, bf16[256,2048]{1,0:T(8,128)(2,1)}, u32[]{:S(2)}, u32[]{:S(2)}) %collective-permute-start.55) | collective-permute-done | bytes 1048608 | tf_op jit(solution)/shard_map/ppermute | solution.py:141
  790.5 30.1 %collective-permute-done.88 = bf16[256,2048]{1,0:T(8,128)(2,1)} collective-permute-done((bf16[256,2048]{1,0:T(8,128)(2,1)}, bf16[256,2048]{1,0:T(8,128)(2,1)}, u32[]{:S(2)}, u32[]{:S(2)}) %collective-permute-start.88) | collective-permute-done | bytes 1048608 | tf_op jit(solution)/shard_map/ppermute | solution.py:141
  822.8 8.9 collective-permute-done.81
  835.0 17.1 %collective-permute-done.48 = bf16[256,2048]{1,0:T(8,128)(2,1)S(1)} collective-permute-done((bf16[256,2048]{1,0:T(8,128)(2,1)S(1)}, bf16[256,2048]{1,0:T(8,128)(2,1)S(1)}, u32[]{:S(2)}, u32[]{:S(2)}) %collective-permute-start.48) | collective-permute-done | bytes 1048608 | tf_op jit(solution)/shard_map/ppermute | solution.py:140
  852.1 13.0 %collective-permute-start.82 = (bf16[256,2048]{1,0:T(8,128)(2,1)S(1)}, bf16[256,2048]{1,0:T(8,128)(2,1)S(1)}, u32[]{:S(2)}, u32[]{:S(2)}) collective-permute-start(bf16[256,2048]{1,0:T(8,128)(2,1)S(1)} %add_convert_fusion.6), channel_id=1, source_target_pairs={{0,8},{2,10},{8,16},{10,18},{16,24},{18,26},{24,28},{26,30},{28,20... | collective-permute-start | bytes 3145736 | tf_op jit(solution)/shard_map/ppermute | solution.py:140
  865.7 11.4 %collective-permute-done.89 = bf16[256,2048]{1,0:T(8,128)(2,1)S(1)} collective-permute-done((bf16[256,2048]{1,0:T(8,128)(2,1)S(1)}, bf16[256,2048]{1,0:T(8,128)(2,1)S(1)}, u32[]{:S(2)}, u32[]{:S(2)}) %collective-permute-start.89) | collective-permute-done | bytes 1048608 | tf_op jit(solution)/shard_map/ppermute | solution.py:141
  877.7 9.9 collective-permute-done.82
  891.7 11.5 %collective-permute-done.56 = bf16[256,2048]{1,0:T(8,128)(2,1)S(1)} collective-permute-done((bf16[256,2048]{1,0:T(8,128)(2,1)S(1)}, bf16[256,2048]{1,0:T(8,128)(2,1)S(1)}, u32[]{:S(2)}, u32[]{:S(2)}) %collective-permute-start.56) | collective-permute-done | bytes 1048608 | tf_op jit(solution)/shard_map/ppermute | solution.py:141
  905.5 9.6 collective-permute-done.49
  925.7 11.9 %collective-permute-done.83 = bf16[256,2048]{1,0:T(8,128)(2,1)S(1)} collective-permute-done((bf16[256,2048]{1,0:T(8,128)(2,1)S(1)}, bf16[256,2048]{1,0:T(8,128)(2,1)S(1)}, u32[]{:S(2)}, u32[]{:S(2)}) %collective-permute-start.83) | collective-permute-done | bytes 1048608 | tf_op jit(solution)/shard_map/ppermute | solution.py:140
  939.9 10.7 add_bitcast_fusion
  1046.8 13.2 %collective-permute-done.101 = bf16[256,1536]{1,0:T(8,128)(2,1)S(1)} collective-permute-done((bf16[256,1536]{1,0:T(8,128)(2,1)S(1)}, bf16[256,1536]{1,0:T(8,128)(2,1)S(1)}, u32[]{:S(2)}, u32[]{:S(2)}) %collective-permute-start.101) | collective-permute-done | bytes 786464 | tf_op jit(solution)/shard_map/ppermute | solution.py:141
  1069.7 13.9 %collective-permute-done.102 = bf16[256,1536]{1,0:T(8,128)(2,1)S(1)} collective-permute-done((bf16[256,1536]{1,0:T(8,128)(2,1)S(1)}, bf16[256,1536]{1,0:T(8,128)(2,1)S(1)}, u32[]{:S(2)}, u32[]{:S(2)}) %collective-permute-start.102) | collective-permute-done | bytes 786464 | tf_op jit(solution)/shard_map/ppermute | solution.py:141
  (861 shorter events, 682.2 us)
Async XLA Ops:
  7.8 67.7 %collective-permute-start.14 = (bf16[128,512]{0,1:T(8,128)(2,1)}, bf16[128,512]{0,1:T(8,128)(2,1)}, u32[]{:S(2)}, u32[]{:S(2)}) collective-permute-start(bf16[128,512]{0,1:T(8,128)(2,1)} %get-tuple-element.162), channel_id=1, source_target_pairs={{0,2},{2,0},{4,6},{6,4},{8,10},{10,8},{12,14},{14,12},{16,18},{18,... | collective-permute-start | bytes 393224 | tf_op jit(solution)/shard_map/ppermute | solution.py:145
  60.0 70.0 %collective-permute-start.4 = (bf16[256,2048]{1,0:T(8,128)(2,1)}, bf16[256,2048]{1,0:T(8,128)(2,1)}, u32[]{:S(2)}, u32[]{:S(2)}) collective-permute-start(bf16[256,2048]{1,0:T(8,128)(2,1)} %fusion.79), channel_id=1, source_target_pairs={{0,2},{2,0},{4,6},{6,4},{8,10},{10,8},{12,14},{14,12},{16,18},{18,... | collective-permute-start | bytes 3145736 | tf_op jit(solution)/shard_map/ppermute | solution.py:145
  117.9 48.0 %collective-permute-start.18 = (bf16[256,512]{0,1:T(8,128)(2,1)}, bf16[256,512]{0,1:T(8,128)(2,1)}, u32[]{:S(2)}, u32[]{:S(2)}) collective-permute-start(bf16[256,512]{0,1:T(8,128)(2,1)} %collective-permute-done.16), channel_id=1, source_target_pairs={{8,0},{10,2},{16,8},{18,10},{24,16},{26,18},{28,24},{30,26},{20,28... | collective-permute-start | bytes 786440 | tf_op jit(solution)/shard_map/ppermute | solution.py:111
  119.3 48.3 %collective-permute-start.17 = (bf16[256,512]{0,1:T(8,128)(2,1)S(1)}, bf16[256,512]{0,1:T(8,128)(2,1)}, u32[]{:S(2)}, u32[]{:S(2)}) collective-permute-start(bf16[256,512]{0,1:T(8,128)(2,1)S(1)} %collective-permute-done.15), channel_id=1, source_target_pairs={{0,8},{2,10},{8,16},{10,18},{16,24},{18,26},{24,28},{26,30},{28,20... | collective-permute-start | bytes 786440 | tf_op jit(solution)/shard_map/ppermute | solution.py:110
  126.8 69.4 %collective-permute-start.62 = (bf16[256,2048]{1,0:T(8,128)(2,1)}, bf16[256,2048]{1,0:T(8,128)(2,1)}, u32[]{:S(2)}, u32[]{:S(2)}) collective-permute-start(bf16[256,2048]{1,0:T(8,128)(2,1)} %param.21), channel_id=1, source_target_pairs={{8,0},{10,2},{16,8},{18,10},{24,16},{26,18},{28,24},{30,26},{20,28... | collective-permute-start | bytes 3145736 | tf_op jit(solution)/shard_map/ppermute | solution.py:111
  128.4 69.7 %collective-permute-start.60 = (bf16[256,2048]{1,0:T(8,128)(2,1)}, bf16[256,2048]{1,0:T(8,128)(2,1)}, u32[]{:S(2)}, u32[]{:S(2)}) collective-permute-start(bf16[256,2048]{1,0:T(8,128)(2,1)} %param.21), channel_id=1, source_target_pairs={{0,8},{2,10},{8,16},{10,18},{16,24},{18,26},{24,28},{26,30},{28,20... | collective-permute-start | bytes 3145736 | tf_op jit(solution)/shard_map/ppermute | solution.py:110
  130.0 68.3 %collective-permute-start.59 = (bf16[256,2048]{1,0:T(8,128)(2,1)}, bf16[256,2048]{1,0:T(8,128)(2,1)}, u32[]{:S(2)}, u32[]{:S(2)}) collective-permute-start(bf16[256,2048]{1,0:T(8,128)(2,1)} %param.21), channel_id=1, source_target_pairs={{0,2},{2,0},{4,6},{6,4},{8,10},{10,8},{12,14},{14,12},{16,18},{18,... | collective-permute-start | bytes 3145736 | tf_op jit(solution)/shard_map/ppermute | solution.py:145
  191.7 181.7 %all-to-all-start.1 = ((bf16[8,128,1056]{1,2,0:T(8,128)(2,1)}), bf16[8,128,1056]{1,2,0:T(8,128)(2,1)}, u32[]{:S(2)}, u32[]{:S(2)}) async-start(bf16[8,128,1056]{1,2,0:T(8,128)(2,1)} %bitcast.387), calls=%async_computation.1 | async-start | bytes 4325376 | tf_op jit(solution)/shard_map/all_to_all | solution.py:277
  196.2 60.0 %collective-permute-start.66 = (bf16[256,2048]{1,0:T(8,128)(2,1)}, bf16[256,2048]{1,0:T(8,128)(2,1)}, u32[]{:S(2)}, u32[]{:S(2)}) collective-permute-start(bf16[256,2048]{1,0:T(8,128)(2,1)} %collective-permute-done.62), channel_id=1, source_target_pairs={{8,0},{10,2},{16,8},{18,10},{24,16},{26,18},{28,24},{30,26},{20,28... | collective-permute-start | bytes 3145736 | tf_op jit(solution)/shard_map/ppermute | solution.py:111
  198.1 79.9 %collective-permute-start.63 = (bf16[256,2048]{1,0:T(8,128)(2,1)}, bf16[256,2048]{1,0:T(8,128)(2,1)S(1)}, u32[]{:S(2)}, u32[]{:S(2)}) collective-permute-start(bf16[256,2048]{1,0:T(8,128)(2,1)} %collective-permute-done.62), channel_id=1, source_target_pairs={{0,2},{2,0},{4,6},{6,4},{8,10},{10,8},{12,14},{14,12},{16,18},{18,... | collective-permute-start | bytes 3145736 | tf_op jit(solution)/shard_map/ppermute | solution.py:145
  198.1 58.3 %collective-permute-start.64 = (bf16[256,2048]{1,0:T(8,128)(2,1)}, bf16[256,2048]{1,0:T(8,128)(2,1)}, u32[]{:S(2)}, u32[]{:S(2)}) collective-permute-start(bf16[256,2048]{1,0:T(8,128)(2,1)} %collective-permute-done.60), channel_id=1, source_target_pairs={{0,8},{2,10},{8,16},{10,18},{16,24},{18,26},{24,28},{26,30},{28,20... | collective-permute-start | bytes 3145736 | tf_op jit(solution)/shard_map/ppermute | solution.py:110
  198.3 60.4 %collective-permute-start.61 = (bf16[256,2048]{1,0:T(8,128)(2,1)}, bf16[256,2048]{1,0:T(8,128)(2,1)S(1)}, u32[]{:S(2)}, u32[]{:S(2)}) collective-permute-start(bf16[256,2048]{1,0:T(8,128)(2,1)} %collective-permute-done.60), channel_id=1, source_target_pairs={{0,2},{2,0},{4,6},{6,4},{8,10},{10,8},{12,14},{14,12},{16,18},{18,... | collective-permute-start | bytes 3145736 | tf_op jit(solution)/shard_map/ppermute | solution.py:145
  209.9 72.0 %collective-permute-start.24 = (bf16[256,2048]{1,0:T(8,128)(2,1)S(1)}, bf16[256,2048]{1,0:T(8,128)(2,1)S(1)}, u32[]{:S(2)}, u32[]{:S(2)}) collective-permute-start(bf16[256,2048]{1,0:T(8,128)(2,1)S(1)} %fusion.90), channel_id=1, source_target_pairs={{0,1},{1,0},{2,3},{3,2},{4,5},{5,4},{6,7},{7,6},{8,9},{9,8},{10,11... | collective-permute-start | bytes 3145736 | tf_op jit(solution)/shard_map/ppermute | solution.py:166
  256.4 47.1 %collective-permute-start.67 = (bf16[256,2048]{1,0:T(8,128)(2,1)}, bf16[256,2048]{1,0:T(8,128)(2,1)}, u32[]{:S(2)}, u32[]{:S(2)}) collective-permute-start(bf16[256,2048]{1,0:T(8,128)(2,1)} %collective-permute-done.66), channel_id=1, source_target_pairs={{0,2},{2,0},{4,6},{6,4},{8,10},{10,8},{12,14},{14,12},{16,18},{18,... | collective-permute-start | bytes 3145736 | tf_op jit(solution)/shard_map/ppermute | solution.py:145
  284.2 48.6 %collective-permute-start.28 = (bf16[256,2048]{1,0:T(8,128)(2,1)}, bf16[256,2048]{1,0:T(8,128)(2,1)}, u32[]{:S(2)}, u32[]{:S(2)}) collective-permute-start(bf16[256,2048]{1,0:T(8,128)(2,1)} %get-tuple-element.114), channel_id=1, source_target_pairs={{8,0},{10,2},{16,8},{18,10},{24,16},{26,18},{28,24},{30,26},{20,28... | collective-permute-start | bytes 3145736 | tf_op jit(solution)/shard_map/ppermute | solution.py:111
  373.4 47.4 %collective-permute-start.34 = (bf16[8,128,1056]{1,2,0:T(8,128)(2,1)}, bf16[8,128,1056]{1,2,0:T(8,128)(2,1)}, u32[]{:S(2)}, u32[]{:S(2)}) collective-permute-start(bf16[8,128,1056]{1,2,0:T(8,128)(2,1)} %all-to-all-done.1), channel_id=1, source_target_pairs={{0,2},{2,0},{4,6},{6,4},{8,10},{10,8},{12,14},{14,12},{16,18},{18,... | collective-permute-start | bytes 6488072 | tf_op jit(solution)/shard_map/ppermute | solution.py:145
  387.6 83.3 %collective-permute-start.43 = (bf16[128,2048]{1,0:T(8,128)(2,1)}, bf16[128,2048]{1,0:T(8,128)(2,1)}, u32[]{:S(2)}, u32[]{:S(2)}) collective-permute-start(bf16[128,2048]{1,0:T(8,128)(2,1)} %slice.782), channel_id=1, source_target_pairs={{8,0},{10,2},{16,8},{18,10},{24,16},{26,18},{28,24},{30,26},{20,28... | collective-permute-start | bytes 1572872 | tf_op jit(solution)/shard_map/ppermute | solution.py:115
  389.8 78.9 %collective-permute-start.42 = (bf16[128,2048]{1,0:T(8,128)(2,1)}, bf16[128,2048]{1,0:T(8,128)(2,1)}, u32[]{:S(2)}, u32[]{:S(2)}) collective-permute-start(bf16[128,2048]{1,0:T(8,128)(2,1)} %slice.781), channel_id=1, source_target_pairs={{0,8},{2,10},{8,16},{10,18},{16,24},{18,26},{24,28},{26,30},{28,20... | collective-permute-start | bytes 1572872 | tf_op jit(solution)/shard_map/ppermute | solution.py:114
  414.3 78.1 %collective-permute-start.41 = (bf16[256,2048]{1,0:T(8,128)(2,1)}, bf16[256,2048]{1,0:T(8,128)(2,1)}, u32[]{:S(2)}, u32[]{:S(2)}) collective-permute-start(bf16[256,2048]{1,0:T(8,128)(2,1)} %collective-permute-done.40), channel_id=1, source_target_pairs={{0,2},{2,0},{4,6},{6,4},{8,10},{10,8},{12,14},{14,12},{16,18},{18,... | collective-permute-start | bytes 3145736 | tf_op jit(solution)/shard_map/ppermute | solution.py:145
  414.3 73.4 %collective-permute-start.39 = (bf16[256,2048]{1,0:T(8,128)(2,1)}, bf16[256,2048]{1,0:T(8,128)(2,1)}, u32[]{:S(2)}, u32[]{:S(2)}) collective-permute-start(bf16[256,2048]{1,0:T(8,128)(2,1)} %collective-permute-done.38), channel_id=1, source_target_pairs={{0,2},{2,0},{4,6},{6,4},{8,10},{10,8},{12,14},{14,12},{16,18},{18,... | collective-permute-start | bytes 3145736 | tf_op jit(solution)/shard_map/ppermute | solution.py:145
  671.5 233.9 %collective-permute-start.36 = (bf16[256,2048]{1,0:T(8,128)(2,1)}, bf16[256,2048]{1,0:T(8,128)(2,1)}, u32[]{:S(2)}, u32[]{:S(2)}) collective-permute-start(bf16[256,2048]{1,0:T(8,128)(2,1)} %convolution_convert_fusion.18), channel_id=1, source_target_pairs={{0,2},{2,0},{4,6},{6,4},{8,10},{10,8},{12,14},{14,12},{16,18},{18,... | collective-permute-start | bytes 3145736 | tf_op jit(solution)/shard_map/ppermute | solution.py:145
  671.5 101.4 %collective-permute-start.52 = (bf16[256,2048]{1,0:T(8,128)(2,1)}, bf16[256,2048]{1,0:T(8,128)(2,1)}, u32[]{:S(2)}, u32[]{:S(2)}) collective-permute-start(bf16[256,2048]{1,0:T(8,128)(2,1)} %convolution_convert_fusion.13), channel_id=1, source_target_pairs={{0,2},{2,0},{4,6},{6,4},{8,10},{10,8},{12,14},{14,12},{16,18},{18,... | collective-permute-start | bytes 3145736 | tf_op jit(solution)/shard_map/ppermute | solution.py:145
  672.0 53.3 %collective-permute-start.45 = (bf16[256,2048]{1,0:T(8,128)(2,1)}, bf16[256,2048]{1,0:T(8,128)(2,1)}, u32[]{:S(2)}, u32[]{:S(2)}) collective-permute-start(bf16[256,2048]{1,0:T(8,128)(2,1)} %convolution_convert_fusion.16), channel_id=1, source_target_pairs={{0,2},{2,0},{4,6},{6,4},{8,10},{10,8},{12,14},{14,12},{16,18},{18,... | collective-permute-start | bytes 3145736 | tf_op jit(solution)/shard_map/ppermute | solution.py:145
  672.1 55.4 %collective-permute-start.46 = (bf16[256,2048]{1,0:T(8,128)(2,1)}, bf16[256,2048]{1,0:T(8,128)(2,1)}, u32[]{:S(2)}, u32[]{:S(2)}) collective-permute-start(bf16[256,2048]{1,0:T(8,128)(2,1)} %convolution_convert_fusion.15), channel_id=1, source_target_pairs={{0,2},{2,0},{4,6},{6,4},{8,10},{10,8},{12,14},{14,12},{16,18},{18,... | collective-permute-start | bytes 3145736 | tf_op jit(solution)/shard_map/ppermute | solution.py:145
  672.6 57.3 %collective-permute-start.53 = (bf16[256,2048]{1,0:T(8,128)(2,1)}, bf16[256,2048]{1,0:T(8,128)(2,1)}, u32[]{:S(2)}, u32[]{:S(2)}) collective-permute-start(bf16[256,2048]{1,0:T(8,128)(2,1)} %convolution_convert_fusion.12), channel_id=1, source_target_pairs={{0,2},{2,0},{4,6},{6,4},{8,10},{10,8},{12,14},{14,12},{16,18},{18,... | collective-permute-start | bytes 3145736 | tf_op jit(solution)/shard_map/ppermute | solution.py:145
  765.5 55.0 %collective-permute-start.88 = (bf16[256,2048]{1,0:T(8,128)(2,1)}, bf16[256,2048]{1,0:T(8,128)(2,1)}, u32[]{:S(2)}, u32[]{:S(2)}) collective-permute-start(bf16[256,2048]{1,0:T(8,128)(2,1)} %pad_maximum_fusion.20), channel_id=1, source_target_pairs={{8,0},{10,2},{16,8},{18,10},{24,16},{26,18},{28,24},{30,26},{20,28... | collective-permute-start | bytes 3145736 | tf_op jit(solution)/shard_map/ppermute | solution.py:141
  768.4 201.6 %all-to-all-start.5 = ((bf16[8,128,1056]{1,2,0:T(8,128)(2,1)}), bf16[8,128,1056]{1,2,0:T(8,128)(2,1)}, u32[]{:S(2)}, u32[]{:S(2)}) async-start(bf16[8,128,1056]{1,2,0:T(8,128)(2,1)} %fusion.9), calls=%async_computation.5 | async-start | bytes 4325376 | tf_op jit(solution)/shard_map/all_to_all | solution.py:537
  773.0 49.7 %collective-permute-start.70 = (bf16[256,2048]{1,0:T(8,128)(2,1)}, bf16[256,2048]{1,0:T(8,128)(2,1)S(1)}, u32[]{:S(2)}, u32[]{:S(2)}) collective-permute-start(bf16[256,2048]{1,0:T(8,128)(2,1)} %convolution_convert_fusion.9), channel_id=1, source_target_pairs={{0,2},{2,0},{4,6},{6,4},{8,10},{10,8},{12,14},{14,12},{16,18},{18,... | collective-permute-start | bytes 3145736 | tf_op jit(solution)/shard_map/ppermute | solution.py:145
  790.4 44.5 %collective-permute-start.37 = (bf16[256,2048]{1,0:T(8,128)(2,1)S(1)}, bf16[256,2048]{1,0:T(8,128)(2,1)S(1)}, u32[]{:S(2)}, u32[]{:S(2)}) collective-permute-start(bf16[256,2048]{1,0:T(8,128)(2,1)S(1)} %copy-done.61), channel_id=1, source_target_pairs={{0,2},{2,0},{4,6},{6,4},{8,10},{10,8},{12,14},{14,12},{16,18},{18,... | collective-permute-start | bytes 3145736 | tf_op jit(solution)/shard_map/ppermute | solution.py:145
  831.7 45.4 %collective-permute-start.89 = (bf16[256,2048]{1,0:T(8,128)(2,1)S(1)}, bf16[256,2048]{1,0:T(8,128)(2,1)S(1)}, u32[]{:S(2)}, u32[]{:S(2)}) collective-permute-start(bf16[256,2048]{1,0:T(8,128)(2,1)S(1)} %add_convert_fusion.4), channel_id=1, source_target_pairs={{8,0},{10,2},{16,8},{18,10},{24,16},{26,18},{28,24},{30,26},{20,28... | collective-permute-start | bytes 3145736 | tf_op jit(solution)/shard_map/ppermute | solution.py:141
  905.4 47.5 %collective-permute-start.35 = (bf16[256,2048]{1,0:T(8,128)(2,1)S(1)}, bf16[256,2048]{1,0:T(8,128)(2,1)S(1)}, u32[]{:S(2)}, u32[]{:S(2)}) collective-permute-start(bf16[256,2048]{1,0:T(8,128)(2,1)S(1)} %copy-done.56), channel_id=1, source_target_pairs={{0,2},{2,0},{4,6},{6,4},{8,10},{10,8},{12,14},{14,12},{16,18},{18,... | collective-permute-start | bytes 3145736 | tf_op jit(solution)/shard_map/ppermute | solution.py:145
  959.3 150.9 %collective-permute-start.58 = (bf16[256,2048]{1,0:T(8,128)(2,1)}, bf16[256,2048]{1,0:T(8,128)(2,1)}, u32[]{:S(2)}, u32[]{:S(2)}) collective-permute-start(bf16[256,2048]{1,0:T(8,128)(2,1)} %add_convert_fusion.9), channel_id=1, source_target_pairs={{0,1},{1,0},{2,3},{3,2},{4,5},{5,4},{6,7},{7,6},{8,9},{9,8},{10,11... | collective-permute-start | bytes 3145736 | tf_op jit(solution)/shard_map/ppermute | solution.py:166
  (226 other events, 4350.0 us)

commit v2 on v1

v2 whole, which is shorter than its diff:
```python
import functools

import jax
import jax.numpy as jnp
import numpy as np
from jax import lax
from jax.experimental import pallas as pl
from jax.experimental.pallas import tpu as pltpu
from jax.sharding import PartitionSpec as P

eps = 1e-06
theta_base = 1000000.0
neg_large = -1e30
no_slot = -100000.0
bf16 = jnp.bfloat16
f32 = jnp.float32
in_vmem = pl.BlockSpec(memory_space=pltpu.VMEM)
in_smem = pl.BlockSpec(memory_space=pltpu.SMEM)
in_any = pl.BlockSpec(memory_space=pl.ANY)


def rms_norm(values, gain_row):
    factor = lax.rsqrt(jnp.mean(values * values, axis=-1, keepdims=True) + eps)
    return values * factor * gain_row


def rotary_tables(length, head_size):
    half_size = head_size // 2
    frequency = np.float32(theta_base) ** (
        -(np.arange(half_size, dtype=np.float32) * np.float32(2.0)) / np.float32(head_size)
    )
    angles = np.arange(length, dtype=np.float32)[:, None] * frequency[None, :].astype(np.float32)
    cosine = np.concatenate([np.cos(angles), np.cos(angles)], axis=-1)
    sine = np.concatenate([-np.sin(angles), np.sin(angles)], axis=-1)
    return jnp.asarray(cosine, f32), jnp.asarray(sine, f32)


def chip_ring(chips):
    columns = chips // 4
    if chips % 4 or columns < 2 or columns % 2:
        return list(range(chips))
    walk = [(0, 0)]
    for column in range(columns):
        rows = range(1, 4) if column % 2 == 0 else range(3, 0, -1)
        walk += [(row, column) for row in rows]
    walk += [(0, column) for column in range(columns - 1, 0, -1)]
    return [row * columns + column for row, column in walk]


def mm(left, right, contract_left=1, contract_right=0):
    return lax.dot_general(
        left,
        right,
        (((contract_left,), (contract_right,)), ((), ())),
        preferred_element_type=f32,
    )


def nt(left, right):
    return mm(left, right, 1, 1)


def tiles(total, size):
    return [(lo, min(size, total - lo)) for lo in range(0, total, size)]


def params():
    return pltpu.CompilerParams(vmem_limit_bytes=56 * 1024 * 1024)


def half_turn(values):
    return pltpu.roll(values, values.shape[1] // 2, 1)


def masked(scores, prefix_cut):
    length = scores.shape[0]
    row = lax.broadcasted_iota(jnp.int32, (length, length), 0)
    col = lax.broadcasted_iota(jnp.int32, (length, length), 1)
    return jnp.where((col <= row) | (col < prefix_cut), scores, neg_large)


def softmax_rows(scores):
    weights = jnp.exp(scores - jnp.max(scores, axis=-1, keepdims=True))
    return weights / jnp.sum(weights, axis=-1, keepdims=True)


def load_blocks(chip_ref, blocks, scratch, sem, parts):
    depth = blocks[0].shape[0] // parts
    copies = []
    for i, block in enumerate(blocks):
        start = pl.multiple_of(chip_ref[i] * depth, depth)
        for c in range(parts):
            copies.append(
                pltpu.make_async_copy(
                    block.at[pl.ds(c * depth, depth)],
                    scratch.at[c, pl.ds(start, depth)],
                    sem.at[i * parts + c],
                )
            )
    for copy in copies:
        copy.start()
    return copies


def attend_kernel(count, heads, scale, *refs):
    chip_ref, prefix_ref, own, other, bias, cosine, sine = refs[:7]
    blocks = refs[7 : 7 + count]
    query, key, value, mixed, weight, sem = refs[7 + count :]
    copies = load_blocks(chip_ref, blocks, weight, sem, 3)
    length, head_size = cosine.shape
    columns = heads * head_size
    for copy in copies:
        copy.wait()
    for c, out in enumerate((query, key, value)):
        for b, rows in enumerate((own, other)):
            for lo, size in tiles(columns, 2 * head_size):
                part = mm(rows[...], weight[c, :, lo : lo + size])
                part = part + bias[:, c * columns + lo : c * columns + lo + size]
                for at in range(0, size, head_size):
                    one = part[:, at : at + head_size]
                    if c < 2:
                        one = one * cosine[...] + half_turn(one) * sine[...]
                    out[b * length : (b + 1) * length, lo + at : lo + at + head_size] = one.astype(
                        bf16
                    )
    for b in range(2):
        rows = slice(b * length, (b + 1) * length)
        for h in range(heads):
            cols = slice(h * head_size, (h + 1) * head_size)
            scores = masked(nt(query[rows, cols], key[rows, cols]) * scale, prefix_ref[b])
            probs = softmax_rows(scores).astype(bf16)
            mixed[rows, cols] = mm(probs, value[rows, cols]).astype(bf16)


def project_kernel(count, *refs):
    chip_ref, mixed = refs[:2]
    blocks = refs[2 : 2 + count]
    own, other, weight, sem = refs[2 + count :]
    copies = load_blocks(chip_ref, blocks, weight, sem, 1)
    for copy in copies:
        copy.wait()
    length, width = own.shape
    for lo, size in tiles(width, 512):
        part = nt(mixed[...], weight[0, lo : lo + size, :])
        own[:, lo : lo + size] = part[:length].astype(own.dtype)
        other[:, lo : lo + size] = part[length:].astype(other.dtype)


def attend_back_kernel(count, heads, scale, *refs):
    chip_ref, prefix_ref, own, other, query, key, value, cosine, sine = refs[:9]
    blocks = refs[9 : 9 + count]
    grad, bias, weight, sem = refs[9 + count :]
    copies = load_blocks(chip_ref, blocks, weight, sem, 1)
    length, head_size = cosine.shape
    columns = heads * head_size
    for copy in copies:
        copy.wait()
    for b, up in enumerate((own, other)):
        rows = slice(b * length, (b + 1) * length)
        mixed_grad = mm(up[...], weight[0]).astype(bf16)
        for h in range(heads):
            cols = slice(h * head_size, (h + 1) * head_size)
            q, k, v = query[rows, cols], key[rows, cols], value[rows, cols]
            up_head = mixed_grad[:, cols]
            probs = softmax_rows(masked(nt(q, k) * scale, prefix_ref[b]))
            prob_grad = nt(up_head, v)
            row_term = jnp.sum(probs * prob_grad, axis=-1, keepdims=True)
            score_grad = (probs * (prob_grad - row_term)).astype(bf16)
            q_grad = mm(score_grad, k) * scale
            k_grad = mm(score_grad, q, 0, 0) * scale
            v_grad = mm(probs.astype(bf16), up_head, 0, 0)
            for c, one in enumerate((q_grad, k_grad, v_grad)):
                if c < 2:
                    one = one * cosine[...] - half_turn(one) * sine[...]
                one = one.astype(bf16)
                at = slice(c * columns + h * head_size, c * columns + (h + 1) * head_size)
                grad[rows, at] = one
                column_sum = jnp.sum(one.astype(f32), axis=0, keepdims=True)
                bias[:, at] = column_sum if b == 0 else bias[:, at] + column_sum


def project_back_kernel(count, *refs):
    chip_ref, grad = refs[:2]
    blocks = refs[2 : 2 + count]
    own, other, weight, sem = refs[2 + count :]
    copies = load_blocks(chip_ref, blocks, weight, sem, 3)
    for copy in copies:
        copy.wait()
    length, width = own.shape
    columns = grad.shape[1] // 3
    for lo, size in tiles(width, 512):
        part = nt(grad[:, :columns], weight[0, lo : lo + size, :])
        for c in range(1, 3):
            part = part + nt(grad[:, c * columns : (c + 1) * columns], weight[c, lo : lo + size, :])
        own[:, lo : lo + size] = part[:length].astype(own.dtype)
        other[:, lo : lo + size] = part[length:].astype(other.dtype)


def moe_kernel(index, first, plan, sizes, *refs):
    length, width, capacity, units, shared_units = sizes
    count = sum(len(p) for p in plan)
    half_ref, row_ref, col_ref = refs[:3]
    given = refs[3 : 3 + count]
    in_hbm, out_hbm, shared_hbm = refs[3 + count : 6 + count]
    rest = refs[6 + count + (0 if first else 8) :]
    kept = rest[:8]
    moe_own, moe_other, back_own, back_other, dots = rest[8:13]
    (tok, up, w_in, w_out, w_sh, rows, up_rows, slots, hidden, gu, y_grad, s_hidden, s_gu) = rest[
        13:26
    ]
    load_sem, weight_sem, keep_sem = rest[26:]

    loads = []
    for which, pieces in enumerate(plan):
        target = (tok, tok, up, up)[which]
        for start_zero, start_one, size in pieces:
            start = start_zero + half_ref[0] * (start_one - start_zero)
            start = pl.multiple_of(start + (which % 2) * length, 16)
            loads.append(
                pltpu.make_async_copy(
                    given[len(loads)], target.at[pl.ds(start, size)], load_sem.at[len(loads)]
                )
            )
    weights = [
        pltpu.make_async_copy(a, b, weight_sem.at[i])
        for i, (a, b) in enumerate(((in_hbm, w_in), (out_hbm, w_out), (shared_hbm, w_sh)))
    ]
    for copy in loads + weights:
        copy.start()

    def keep(slot, source):
        target = kept[slot]
        target = target.at[:, index] if len(target.shape) == 4 else target.at[index]
        copy = pltpu.make_async_copy(source, target, keep_sem.at[slot])
        copy.start()
        return copy

    rank_own, rank_other = row_ref[index, 0:1, :], row_ref[index, 1:2, :]
    slot = lax.broadcasted_iota(jnp.int32, (capacity, length), 0).astype(f32)
    pick_own, pick_other = slot == rank_own, slot == rank_other
    one_own = jnp.where(pick_own, 1.0, 0.0).astype(bf16)
    one_other = jnp.where(pick_other, 1.0, 0.0).astype(bf16)
    gate_own = jnp.sum(jnp.where(pick_own, row_ref[index, 2:3, :], 0.0), axis=1, keepdims=True)
    gate_other = jnp.sum(jnp.where(pick_other, row_ref[index, 3:4, :], 0.0), axis=1, keepdims=True)
    gates = jnp.concatenate([gate_own, gate_other], axis=0)
    lane = lax.broadcasted_iota(jnp.int32, (length, 2 * capacity), 1).astype(f32)
    place = jnp.concatenate(
        [
            jnp.where(lane == col_ref[index, :, 0:1], 1.0, 0.0).astype(bf16),
            jnp.where(lane == col_ref[index, :, 1:2] + float(capacity), 1.0, 0.0).astype(bf16),
        ],
        axis=0,
    )
    sigma = col_ref[index, :, 2:3]
    for copy in loads:
        copy.wait()
    kept_copies = [keep(4, tok.at[0:length])]

    wide = min(512, width)

    @pl.loop(0, width // wide)
    def _(n):
        cols = pl.ds(pl.multiple_of(n * wide, wide), wide)
        rows[0:capacity, cols] = mm(one_own, tok[0:length, cols]).astype(bf16)
        rows[capacity:, cols] = mm(one_other, tok[length:, cols]).astype(bf16)
        got = mm(one_own, up[0:length, cols])
        up_rows[0:capacity, cols] = got.astype(bf16)
        slots[0:capacity, cols] = (gate_own * got).astype(bf16)
        got = mm(one_other, up[length:, cols])
        up_rows[capacity:, cols] = got.astype(bf16)
        slots[capacity:, cols] = (gate_other * got).astype(bf16)
        y_grad[:, cols] = (sigma * up[0:length, cols].astype(f32)).astype(bf16)

    kept_copies += [keep(0, rows), keep(1, slots), keep(5, y_grad)]

    def gated(gate_part, up_part, grad):
        sig = 1.0 / (1.0 + jnp.exp(-gate_part))
        silu = gate_part * sig
        return (
            (silu * up_part).astype(bf16),
            (grad * up_part * (sig * (1.0 + gate_part * (1.0 - sig)))).astype(bf16),
            (grad * silu).astype(bf16),
        )

    weights[0].wait()
    weights[1].wait()
    for lo, size in tiles(units, 256):
        at = slice(lo, lo + size)
        gate_part = nt(rows[...], w_in[0, at, :])
        up_part = nt(rows[...], w_in[1, at, :])
        grad = nt(slots[...], w_out[at, :])
        hidden[:, at], gu[0, :, at], gu[1, :, at] = gated(gate_part, up_part, grad)
    kept_copies += [keep(2, hidden), keep(3, gu)]
    weights[2].wait()
    for lo, size in tiles(shared_units, 256):
        at = slice(lo, lo + size)
        gate_part = nt(tok[0:length, :], w_sh[0, at, :])
        up_part = nt(tok[0:length, :], w_sh[1, at, :])
        grad = nt(y_grad[...], w_sh[2, at, :])
        s_hidden[:, at], s_gu[0, :, at], s_gu[1, :, at] = gated(gate_part, up_part, grad)
    kept_copies += [keep(6, s_hidden), keep(7, s_gu)]

    def last(n, sums):
        slot_dots, sigma_dots = sums
        cols = pl.ds(pl.multiple_of(n * wide, wide), wide)
        made = mm(hidden[...], w_out[:, cols]).astype(bf16).astype(f32)
        slot_dots = slot_dots + jnp.sum(
            up_rows[:, cols].astype(f32) * made, axis=1, keepdims=True
        )
        routed = mm(place, (gates * made).astype(bf16))
        shared = mm(s_hidden[...], w_sh[2, :, cols])
        sigma_dots = sigma_dots + jnp.sum(
            up[0:length, cols].astype(f32) * shared, axis=1, keepdims=True
        )
        moe_own[:, cols] = (routed[:length] + sigma * shared).astype(bf16)
        moe_other[:, cols] = routed[length:].astype(bf16)
        entry = mm(gu[0], w_in[0, :, cols]) + mm(gu[1], w_in[1, :, cols])
        routed = mm(place, entry.astype(bf16))
        shared = mm(s_gu[0], w_sh[0, :, cols]) + mm(s_gu[1], w_sh[1, :, cols])
        back_own[:, cols] = (routed[:length] + shared).astype(bf16)
        back_other[:, cols] = routed[length:].astype(bf16)
        return slot_dots, sigma_dots

    slot_dots, sigma_dots = lax.fori_loop(
        0,
        width // wide,
        last,
        (jnp.zeros((2 * capacity, 1), f32), jnp.zeros((length, 1), f32)),
    )
    dots[0:1, :] = jnp.sum(jnp.where(pick_own, slot_dots[:capacity], 0.0), axis=0, keepdims=True)
    dots[1:2, :] = jnp.sum(jnp.where(pick_other, slot_dots[capacity:], 0.0), axis=0, keepdims=True)
    row = lax.broadcasted_iota(jnp.int32, (length, length), 0)
    col = lax.broadcasted_iota(jnp.int32, (length, length), 1)
    dots[2:3, :] = jnp.sum(jnp.where(row == col, sigma_dots, 0.0), axis=0, keepdims=True)
    dots[3:, :] = jnp.zeros((dots.shape[0] - 3, length), f32)
    for copy in kept_copies:
        copy.wait()


def moe_call(index, sizes, chips, pieces, half, row_aux, col_aux, weights, kept):
    length, width, capacity, units, shared_units = sizes
    plan = [[(a, b, piece.shape[0]) for piece, a, b in group] for group in pieces]
    arrays = [piece for group in pieces for piece, _, _ in group]
    first = kept is None
    kept_shapes = [
        jax.ShapeDtypeStruct(shape, bf16)
        for shape in (
            (chips, 2 * capacity, width),
            (chips, 2 * capacity, width),
            (chips, 2 * capacity, units),
            (2, chips, 2 * capacity, units),
            (chips, length, width),
            (chips, length, width),
            (chips, length, shared_units),
            (2, chips, length, shared_units),
        )
    ]
    block = jax.ShapeDtypeStruct((length, width), bf16)
    operands = [half, row_aux, col_aux, *arrays, *weights] + ([] if first else list(kept))
    aliases = {} if first else {len(operands) - 8 + i: i for i in range(8)}
    flops = 2 * 2 * capacity * width * units * 6 + 2 * length * width * shared_units * 6
    flops += 2 * 2 * length * 2 * capacity * width * 4
    out = pl.pallas_call(
        functools.partial(moe_kernel, index, first, plan, sizes),
        out_shape=kept_shapes + [block] * 4 + [jax.ShapeDtypeStruct((8, length), f32)],
        in_specs=[in_smem, in_vmem, in_vmem]
        + [in_any] * (len(arrays) + 3 + (0 if first else 8)),
        out_specs=[in_any] * 8 + [in_vmem] * 5,
        scratch_shapes=[
            pltpu.VMEM((2 * length, width), bf16),
            pltpu.VMEM((2 * length, width), bf16),
            pltpu.VMEM((2, units, width), bf16),
            pltpu.VMEM((units, width), bf16),
            pltpu.VMEM((3, shared_units, width), bf16),
            pltpu.VMEM((2 * capacity, width), bf16),
            pltpu.VMEM((2 * capacity, width), bf16),
            pltpu.VMEM((2 * capacity, width), bf16),
            pltpu.VMEM((2 * capacity, units), bf16),
            pltpu.VMEM((2, 2 * capacity, units), bf16),
            pltpu.VMEM((length, width), bf16),
            pltpu.VMEM((length, shared_units), bf16),
            pltpu.VMEM((2, length, shared_units), bf16),
            pltpu.SemaphoreType.DMA((len(arrays),)),
            pltpu.SemaphoreType.DMA((3,)),
            pltpu.SemaphoreType.DMA((8,)),
        ],
        input_output_aliases=aliases,
        compiler_params=params(),
        cost_estimate=pl.CostEstimate(
            flops=flops, bytes_accessed=32 * 1024 * 1024, transcendentals=0
        ),
        name=f"experts_{index}",
    )(*operands)
    return out[:8], out[8:12], out[12]


class Ring:
    def __init__(self, devices):
        self.devices = devices
        self.chips = devices // 2
        order = chip_ring(self.chips)
        n = self.chips
        self.next = [
            (order[i] * 2 + c, order[(i + 1) % n] * 2 + c) for i in range(n) for c in range(2)
        ]
        self.prev = [(b, a) for a, b in self.next]
        self.core = [(e, e ^ 1) for e in range(devices)]
        half = n // 2
        offsets = [0]
        for k in range(1, half):
            offsets += [-k, k]
        self.offsets = offsets + [half]
        place = {chip: i for i, chip in enumerate(order)}
        self.chip_table = np.array(
            [
                [order[(place[e // 2] + o) % n] for o in self.offsets]
                for e in range(devices)
            ],
            np.int32,
        )
        self.seq_table = np.stack(
            [
                2 * self.chip_table + (np.arange(devices) % 2)[:, None],
                2 * self.chip_table + 1 - (np.arange(devices) % 2)[:, None],
            ],
            axis=-1,
        ).reshape(devices, devices)
        self.seq_inverse = np.argsort(self.seq_table, axis=1).astype(np.int32)

    def gather(self, block):
        half = self.chips // 2
        found = {0: block}
        ahead = back = block
        for k in range(1, half):
            ahead = lax.ppermute(ahead, "expert", self.next)
            back = lax.ppermute(back, "expert", self.prev)
            found[-k], found[k] = ahead, back
        cut = block.shape[0] // 2
        first = lax.ppermute(ahead[:cut], "expert", self.next)
        second = lax.ppermute(back[cut:], "expert", self.prev)
        return {o: [b] for o, b in found.items()} | {half: [first, second]}

    def gather_whole(self, block):
        found = self.gather(block)
        return [
            found[o][0] if len(found[o]) == 1 else jnp.concatenate(found[o], axis=0)
            for o in self.offsets
        ]

    def reduce(self, terms):
        half = self.chips // 2

        def total(offset, more=()):
            out = None
            for term in list(terms[offset]) + list(more):
                out = term.astype(f32) if out is None else out + term.astype(f32)
            return out

        far = total(half).astype(bf16)
        cut = far.shape[0] // 2
        ahead = lax.ppermute(far[:cut], "expert", self.next)
        back = lax.ppermute(far[cut:], "expert", self.prev)
        for k in range(half - 1, 0, -1):
            mine, yours = total(k), total(-k)
            if k == half - 1:
                mine = jnp.concatenate([mine[:cut] + ahead.astype(f32), mine[cut:]], axis=0)
                yours = jnp.concatenate([yours[:cut], yours[cut:] + back.astype(f32)], axis=0)
            else:
                mine = mine + ahead.astype(f32)
                yours = yours + back.astype(f32)
            ahead = lax.ppermute(mine.astype(bf16), "expert", self.next)
            back = lax.ppermute(yours.astype(bf16), "expert", self.prev)
        return total(0, (ahead, back))

    def swap_core(self, block):
        return lax.ppermute(block, "expert", self.core)

    def gather_small(self, row, me):
        held = row[None]
        step = 1
        while step < self.devices:
            pairs = [(e, e ^ step) for e in range(self.devices)]
            other = lax.ppermute(held, "expert", pairs)
            upper = (me // step) % 2 == 1
            held = jnp.where(
                upper, jnp.concatenate([other, held]), jnp.concatenate([held, other])
            )
            step *= 2
        return held


def after(value, *others):
    return lax.optimization_barrier((value,) + others)[0]


def swap_tensor(block):
    return lax.ppermute(block, "tensor", [(0, 1), (1, 0)])


def sum_tensor(part):
    own = part.astype(bf16)
    return own.astype(f32) + swap_tensor(own).astype(f32)


def make_local(ring):
    devices, chips = ring.devices, ring.chips

    def local(
        tokens_in,
        cotangent,
        norm_gains,
        qkv_weight,
        qkv_bias,
        out_weight,
        router_weight,
        shared_gate,
        shared_in,
        shared_out,
        expert_in,
        expert_out,
        expert_ids,
        prefix_len,
    ):
        me = lax.axis_index("expert")
        core = me % 2
        half = lax.axis_index("tensor")
        length, width = tokens_in.shape
        top_count = expert_ids.shape[1]
        experts = router_weight.shape[1]
        capacity = length * top_count * 3 // (2 * experts)
        rows_dev = qkv_weight.shape[0]
        heads_t = qkv_bias.shape[1]
        heads = heads_t // 2
        hd_dev = qkv_bias.shape[2]
        head_size = hd_dev * devices
        half_cols = heads * head_size
        score_scale = head_size ** (-0.5)
        chip_of = jnp.asarray(ring.chip_table)[me]
        seq_of = jnp.asarray(ring.seq_table)[me]
        seq_inv = jnp.asarray(ring.seq_inverse)[me]

        pieces = [
            norm_gains.reshape(-1),
            qkv_bias.reshape(-1),
            router_weight.reshape(-1),
            shared_gate.reshape(-1),
            expert_ids.T.astype(bf16).reshape(-1),
            prefix_len.astype(bf16).reshape(-1),
        ]
        sizes = [p.shape[0] for p in pieces]
        total = sum(sizes)
        padded = -(-total // 1024) * 1024
        small = jnp.concatenate(pieces + [jnp.zeros((padded - total,), bf16)])
        small_all = ring.gather_small(small, me)
        cuts = np.cumsum([0] + sizes)
        found = [small_all[:, cuts[i] : cuts[i + 1]] for i in range(len(sizes))]
        gains_f = (
            found[0].reshape(devices, 2, rows_dev).transpose(1, 0, 2).reshape(2, width).astype(f32)
        )
        bias_all = (
            found[1].reshape(devices, 3, heads_t, hd_dev).transpose(1, 2, 0, 3)
            .reshape(3, 2, half_cols)
        )
        bias = lax.dynamic_index_in_dim(bias_all, core, 1, keepdims=False).astype(f32)
        router_w = found[2].reshape(width, experts)
        gate_vec = found[3].reshape(width)
        ids_all = found[4].reshape(devices, top_count, length).astype(jnp.int32)
        prefix_all = found[5].reshape(devices).astype(jnp.int32)
        prefix_pair = jnp.stack([prefix_all[me], prefix_all[me ^ 1]])

        depth = 2 * rows_dev

        def by_core(own, other, axis):
            return jnp.where(
                core == 0,
                jnp.concatenate([own, other], axis=axis),
                jnp.concatenate([other, own], axis=axis),
            )

        def halves(array, axis):
            size = array.shape[axis] // 2
            own = lax.dynamic_slice_in_dim(array, core * size, size, axis)
            return own, lax.dynamic_slice_in_dim(array, (1 - core) * size, size, axis)

        own, other = halves(qkv_weight.transpose(1, 0, 2), 2)
        qkv_blocks = ring.gather_whole(
            by_core(own, ring.swap_core(other), 1).reshape(3 * depth, half_cols)
        )
        own, other = halves(out_weight, 0)
        out_block = by_core(own.T, ring.swap_core(other).T, 0)
        out_blocks = ring.gather_whole(after(out_block, qkv_blocks[-1]))

        units = shared_out.shape[0]
        unit_chip = units // chips
        sh_send = jnp.concatenate(
            [
                shared_in.transpose(1, 2, 0).reshape(2, chips, unit_chip, rows_dev),
                shared_out.reshape(1, chips, unit_chip, rows_dev),
            ],
            axis=0,
        ).transpose(1, 0, 2, 3)
        sh_send = after(sh_send.reshape(chips, 3 * unit_chip, rows_dev), qkv_blocks[-1])
        same_core = [[2 * i + c for i in range(chips)] for c in range(2)]
        sh_mine = lax.all_to_all(
            sh_send, "expert", split_axis=0, concat_axis=0, tiled=True, axis_index_groups=same_core
        )
        sh_w = by_core(sh_mine[:, None], ring.swap_core(sh_mine)[:, None], 1)
        sh_w = sh_w.transpose(2, 0, 1, 3).reshape(3, unit_chip, width)

        half_length = length // 2
        up_half = lax.dynamic_slice_in_dim(cotangent, half * half_length, half_length, 0)
        up_ring = ring.gather(after(up_half, out_blocks[-1]))
        up_own, up_other = {}, {}
        for offset in ring.offsets:
            pieces, at = [], 0
            for piece in up_ring[offset]:
                pieces.append((piece, at, half_length + at))
                pieces.append((swap_tensor(piece), half_length + at, at))
                at += piece.shape[0]
            up_own[offset] = pieces
            up_other[offset] = [(ring.swap_core(p), a, b) for p, a, b in pieces]

        inputs = tokens_in.astype(f32)
        first_b = rms_norm(inputs, gains_f[0]).astype(bf16)
        first_o = ring.swap_core(first_b)
        cosine, sine = rotary_tables(length, head_size)
        pair_cols = jax.ShapeDtypeStruct((2 * length, half_cols), bf16)
        chip_arg = chip_of.astype(jnp.int32)

        def cost(flops, moved):
            return pl.CostEstimate(flops=flops, bytes_accessed=moved, transcendentals=0)

        query, key, value, mixed = pl.pallas_call(
            functools.partial(attend_kernel, chips, heads, score_scale),
            out_shape=[pair_cols] * 4,
            in_specs=[in_smem] * 2 + [in_vmem] * 5 + [in_any] * chips,
            out_specs=[in_vmem] * 4,
            scratch_shapes=[
                pltpu.VMEM((3, width, half_cols), bf16),
                pltpu.SemaphoreType.DMA((3 * chips,)),
            ],
            compiler_params=params(),
            cost_estimate=cost(2 * 2 * length * width * 3 * half_cols, 12 * 1024 * 1024),
            name="attend",
        )(chip_arg, prefix_pair, first_b, first_o, bias.reshape(1, -1), cosine, sine, *qkv_blocks)
        attn_own, attn_give = pl.pallas_call(
            functools.partial(project_kernel, chips),
            out_shape=[
                jax.ShapeDtypeStruct((length, width), f32),
                jax.ShapeDtypeStruct((length, width), bf16),
            ],
            in_specs=[in_smem, in_vmem] + [in_any] * chips,
            out_specs=[in_vmem] * 2,
            scratch_shapes=[
                pltpu.VMEM((1, width, half_cols), bf16),
                pltpu.SemaphoreType.DMA((chips,)),
            ],
            compiler_params=params(),
            cost_estimate=cost(2 * 2 * length * width * half_cols, 6 * 1024 * 1024),
            name="project",
        )(chip_arg, mixed, *out_blocks)
        attn_out = sum_tensor(attn_own + ring.swap_core(attn_give).astype(f32))
        residual = inputs + attn_out
        second_b = rms_norm(residual, gains_f[1]).astype(bf16)

        rows_own, rows_other = {}, {}
        for offset, pieces in ring.gather(second_b).items():
            starts = [sum(p.shape[0] for p in pieces[:j]) for j in range(len(pieces))]
            rows_own[offset] = [(p, a, a) for p, a in zip(pieces, starts, strict=True)]
            rows_other[offset] = [(ring.swap_core(p), a, a) for p, a, _ in rows_own[offset]]

        logits = mm(second_b, router_w)
        expert_range = jnp.arange(experts, dtype=jnp.int32)
        route_match = expert_ids[:, :, None] == expert_range[None, None, :]
        chosen = jnp.sum(jnp.where(route_match, logits[:, None, :], 0.0), axis=-1)
        gate_weights = jax.nn.softmax(chosen, axis=-1)
        shared_sigma = jax.nn.sigmoid(
            jnp.sum(second_b.astype(f32) * gate_vec.astype(f32)[None], axis=-1)
        )
        gate_dense = jnp.sum(jnp.where(route_match, gate_weights[:, :, None], 0.0), axis=1)
        gate_send = jnp.stack(
            [gate_dense.T, jnp.broadcast_to(shared_sigma[None], (experts, length))], axis=1
        )
        gate_all = lax.all_to_all(gate_send, "expert", split_axis=0, concat_axis=0, tiled=True)
        gate_all = gate_all[seq_of].reshape(chips, 2, 2, length)

        match = jnp.any(ids_all[seq_of] == me, axis=1)
        triangle = jnp.asarray(np.triu(np.ones((length, length), np.float32)), bf16)
        rank = jnp.where(match, mm(match.astype(bf16), triangle) - 1.0, no_slot)
        rank = rank.reshape(chips, 2, length)
        blank = jnp.zeros((chips, 3, length), f32)
        row_aux = jnp.concatenate([rank, gate_all[:, :, 0], gate_all[:, :1, 1], blank], axis=1)
        col_aux = jnp.concatenate(
            [rank, gate_all[:, :1, 1], jnp.zeros((chips, 5, length), f32)], axis=1
        ).transpose(0, 2, 1)

        ex_in = expert_in[0].transpose(1, 2, 0)
        ex_out = expert_out[0]
        part_units = ex_out.shape[0]
        sizes = (length, width, capacity, part_units, unit_chip)
        half_arg = half.astype(jnp.int32).reshape(1)
        kept = None
        moe, back, dot_rows = {}, {}, []
        for i, offset in enumerate(ring.offsets):
            pieces = [rows_own[offset], rows_other[offset], up_own[offset], up_other[offset]]
            kept, blocks, rows = moe_call(
                i, sizes, chips, pieces, half_arg, row_aux, col_aux, (ex_in, ex_out, sh_w), kept
            )
            moe[offset], back[offset] = blocks[:2], blocks[2:]
            dot_rows.append(rows)

        back_terms = {o: [a, ring.swap_core(b)] for o, (a, b) in back.items()}
        second_part = ring.reduce(back_terms)
        moe_terms = {o: [a, ring.swap_core(b)] for o, (a, b) in moe.items()}
        moe_part = ring.reduce(moe_terms)
        output = (residual + sum_tensor(moe_part)).astype(bf16)

        dots = jnp.stack(dot_rows, axis=0)
        sdots = jnp.concatenate([dots[:, 2:3], jnp.zeros_like(dots[:, 2:3])], axis=1)
        dot_send = jnp.stack([dots[:, :2], sdots], axis=2).reshape(devices, 2, length)[seq_inv]
        dot_got = lax.all_to_all(dot_send, "expert", split_axis=0, concat_axis=0, tiled=True)
        dot_got = jnp.concatenate([dot_got[:, 0], jnp.sum(dot_got[:, 1], axis=0)[None]], axis=0)
        dot_got = dot_got + swap_tensor(dot_got)
        gate_grad_dense, sigma_grad = dot_got[:experts].T, dot_got[experts]
        row_term = jnp.sum(gate_dense * gate_grad_dense, axis=-1, keepdims=True)
        logit_grad = (gate_dense * (gate_grad_dense - row_term)).astype(bf16)
        gate_logit_grad = sigma_grad * shared_sigma * (1.0 - shared_sigma)

        second_grad = sum_tensor(second_part)
        second_grad = second_grad + mm(logit_grad, router_w, 1, 1)
        second_grad = second_grad + gate_logit_grad[:, None] * gate_vec.astype(f32)[None]
        upstream = cotangent.astype(f32)
        residual_norm_grad, gain_two_grad = jax.vjp(rms_norm, residual, gains_f[1])[1](second_grad)
        residual_grad = upstream + residual_norm_grad
        attn_grad = residual_grad.astype(bf16)
        attn_grad_o = ring.swap_core(attn_grad)

        def by_chip(left, other, right):
            pair = jnp.concatenate([left, other], axis=0)
            return {
                offset: [
                    mm(lax.dynamic_slice_in_dim(pair, chip_of[i] * depth, depth, 1), right, 0, 0)
                ]
                for i, offset in enumerate(ring.offsets)
            }

        proj_grad, bias_grad = pl.pallas_call(
            functools.partial(attend_back_kernel, chips, heads, score_scale),
            out_shape=[
                jax.ShapeDtypeStruct((2 * length, 3 * half_cols), bf16),
                jax.ShapeDtypeStruct((1, 3 * half_cols), f32),
            ],
            in_specs=[in_smem] * 2 + [in_vmem] * 7 + [in_any] * chips,
            out_specs=[in_vmem] * 2,
            scratch_shapes=[
                pltpu.VMEM((1, width, half_cols), bf16),
                pltpu.SemaphoreType.DMA((chips,)),
            ],
            compiler_params=params(),
            cost_estimate=cost(2 * 2 * length * width * half_cols * 2, 8 * 1024 * 1024),
            name="attend_back",
        )(
            chip_arg,
            prefix_pair,
            attn_grad,
            attn_grad_o,
            query,
            key,
            value,
            cosine,
            sine,
            *out_blocks,
        )
        qkv_grad = ring.reduce(by_chip(first_b, first_o, proj_grad))
        out_grad = ring.reduce(by_chip(attn_grad, attn_grad_o, mixed))
        bias_grad = bias_grad[0]
        first_own, first_give = pl.pallas_call(
            functools.partial(project_back_kernel, chips),
            out_shape=[
                jax.ShapeDtypeStruct((length, width), f32),
                jax.ShapeDtypeStruct((length, width), bf16),
            ],
            in_specs=[in_smem, in_vmem] + [in_any] * chips,
            out_specs=[in_vmem] * 2,
            scratch_shapes=[
                pltpu.VMEM((3, width, half_cols), bf16),
                pltpu.SemaphoreType.DMA((3 * chips,)),
            ],
            compiler_params=params(),
            cost_estimate=cost(2 * 2 * length * width * 3 * half_cols, 12 * 1024 * 1024),
            name="project_back",
        )(chip_arg, proj_grad, *qkv_blocks)
        first_grad = sum_tensor(first_own + ring.swap_core(first_give).astype(f32))
        input_norm_grad, gain_one_grad = jax.vjp(rms_norm, inputs, gains_f[0])[1](first_grad)
        input_grad = (residual_grad + input_norm_grad).astype(bf16)

        def regroup(grad, parts):
            own, other = halves(grad, 0)
            own = own.astype(bf16).reshape(rows_dev, parts, half_cols)
            got = ring.swap_core(other.astype(bf16)).reshape(rows_dev, parts, half_cols)
            return by_core(own, got, 2).astype(f32)

        qkv_weight_grad = regroup(qkv_grad, 3)
        out_weight_grad = regroup(out_grad, 1)[:, 0].T

        rows_all, slots_all, hidden_all, gu_all, tok_all, y_all, s_hidden_all, s_gu_all = kept
        slot_count = chips * 2 * capacity
        rows_all = rows_all.reshape(slot_count, width)
        expert_out_grad = mm(
            hidden_all.reshape(slot_count, part_units), slots_all.reshape(slot_count, width), 0, 0
        )[None]
        expert_in_grad = mm(gu_all.reshape(2, slot_count, part_units), rows_all, 1, 0)
        expert_in_grad = expert_in_grad.transpose(2, 0, 1)[None]
        token_count = chips * length
        sh_in_grad = mm(
            s_gu_all.reshape(2, token_count, unit_chip), tok_all.reshape(token_count, width), 1, 0
        )
        sh_out_grad = mm(
            s_hidden_all.reshape(token_count, unit_chip), y_all.reshape(token_count, width), 0, 0
        )
        sh_grad = jnp.concatenate(
            [sh_in_grad.astype(bf16), sh_out_grad.astype(bf16)[None]], axis=0
        ).reshape(3 * unit_chip, chips, 2, rows_dev)
        sh_grad = sh_grad.transpose(2, 1, 0, 3)
        own, other = halves(sh_grad, 0)
        sh_sum = (own.astype(f32) + ring.swap_core(other).astype(f32)).astype(bf16)[0]
        sh_back = lax.all_to_all(
            sh_sum, "expert", split_axis=0, concat_axis=0, tiled=True, axis_index_groups=same_core
        )
        sh_back = sh_back.reshape(chips, 3, unit_chip, rows_dev).astype(f32)
        shared_in_grad = sh_back[:, :2].transpose(3, 1, 0, 2).reshape(rows_dev, 2, units)
        shared_out_grad = sh_back[:, 2].reshape(units, rows_dev)

        second_f = second_b.astype(f32)
        router_part = mm(second_b, logit_grad, 0, 0)
        shared_gate_part = jnp.sum(gate_logit_grad[:, None] * second_f, axis=0)
        early = jnp.concatenate(
            [router_part, shared_gate_part[:, None], gain_two_grad[:, None]], axis=1
        ).reshape(devices, rows_dev * (experts + 2))
        early = lax.all_to_all(early, "expert", split_axis=0, concat_axis=0, tiled=True)
        early = jnp.sum(early, axis=0).reshape(rows_dev, experts + 2)
        router_grad, shared_gate_grad = early[:, :experts], early[:, experts]
        bias_send = bias_grad.reshape(3 * heads, devices, hd_dev).transpose(1, 0, 2)
        late = jnp.concatenate(
            [gain_one_grad.reshape(devices, rows_dev), bias_send.reshape(devices, -1)], axis=1
        )
        late = lax.all_to_all(late, "expert", split_axis=0, concat_axis=0, tiled=True)
        gain_one = jnp.sum(late[:, :rows_dev], axis=0)
        bias_got = jnp.sum(late[:, rows_dev:].reshape(chips, 2, 3, heads, hd_dev), axis=0)
        qkv_bias_grad = bias_got.transpose(1, 0, 2, 3).reshape(3, heads_t, hd_dev)
        gains_grad = jnp.stack([gain_one, early[:, experts + 1]], axis=0)

        return (
            output,
            input_grad,
            gains_grad,
            qkv_weight_grad,
            qkv_bias_grad,
            out_weight_grad,
            router_grad,
            shared_gate_grad,
            shared_in_grad,
            shared_out_grad,
            expert_in_grad,
            expert_out_grad,
        )

    return local


def solution(mesh):
    ring = Ring(mesh.shape["expert"])
    return jax.shard_map(
        make_local(ring),
        mesh=mesh,
        in_specs=(
            P("expert", None),
            P("expert", None),
            P(None, "expert"),
            P("expert", None, "tensor"),
            P(None, "tensor", "expert"),
            P("tensor", "expert"),
            P("expert", None),
            P("expert"),
            P("expert", None, "tensor"),
            P("tensor", "expert"),
            P("expert", None, None, "tensor"),
            P("expert", "tensor", None),
            P("expert", None),
            P("expert"),
        ),
        out_specs=(
            P("expert", None),
            P("expert", None),
            P(None, "expert"),
            P("expert", None, "tensor"),
            P(None, "tensor", "expert"),
            P("tensor", "expert"),
            P("expert", None),
            P("expert"),
            P("expert", None, "tensor"),
            P("tensor", "expert"),
            P("expert", None, None, "tensor"),
            P("expert", "tensor", None),
        ),
        check_vma=False,
    )
```

time: 1130 us -> 918 us (0.81)
  matrix products: 334 us -> 54 us
  Pallas kernels: 0 us -> 203 us
  waiting for transfers between devices: 356 us -> 276 us
  local copies, waits for them, and re-layouts: 197 us -> 122 us
  starting transfers between devices: 141 us -> 177 us
  other arithmetic: 85.5 us -> 65.8 us
    dot_general x112 -> x24, matrix products: 323 us -> 54 us  [mm(): lax.dot_general(left, right, (((contract_left,), (contract_right,)), ((),...]
    pallas_call x0 -> x12, Pallas kernels: none -> 203 us  [the longest x8 168 us: moe_call(): pl.pallas_call(functools.partial(moe_kernel, index, first, plan, sizes),...]
    ppermute x12, waiting for transfers between devices: 89.6 us -> 1.02 us  [gather(): back = lax.ppermute(back, 'expert', self.prev)]
    ppermute x12, waiting for transfers between devices: 107 us -> 26.8 us  [reduce(): back = lax.ppermute(yours.astype(bf16), 'expert', self.prev)]
    ppermute x12, waiting for transfers between devices: 76.9 us -> 132 us  [reduce(): ahead = lax.ppermute(mine.astype(bf16), 'expert', self.next)]
    select_n x2 -> x0, local copies, waits for them, and re-layouts: 26.1 us -> none  [local(): jnp.where(core == 0, jnp.stack([sh_mine, sh_other], axis=1), jnp.stack([s...]
    unnamed x301 -> x279, local copies, waits for them, and re-layouts: 63.2 us -> 38 us
    ppermute x12, starting transfers between devices: 22.3 us -> 42 us  [gather(): ahead = lax.ppermute(ahead, 'expert', self.next)]
  transfers between devices with their start and end apart: 121 -> 141, of which waited for: 42 -> 35; matrix products, arithmetic and copies ran while one was open for 39% -> 24% of each run, Pallas kernels for 0% -> 22%
where the time goes in v2:
time: 918 us; the launch traced here: 907 us
  waiting for transfers between devices  276 us (30%)
  Pallas kernels  203 us (22%)
  starting transfers between devices  177 us (19%)
  local copies, waits for them, and re-layouts  122 us (13%)
  other arithmetic  65.8 us (7%)
  matrix products  54 us (6%)
  between operations  9.28 us (1%)
    pallas_call x8, Pallas kernels, moe_call(): pl.pallas_call(functools.partial(moe_kernel, index, first, plan, sizes),...  168 us
    ppermute x12, waiting for transfers between devices, reduce(): ahead = lax.ppermute(mine.astype(bf16), 'expert', self.next)  132 us
    dot_general x24, matrix products, mm(): lax.dot_general(left, right, (((contract_left,), (contract_right,)), ((),...  54 us
    ppermute x12, starting transfers between devices, reduce(): ahead = lax.ppermute(mine.astype(bf16), 'expert', self.next)  46.4 us
    ppermute x12, starting transfers between devices, gather(): ahead = lax.ppermute(ahead, 'expert', self.next)  42 us
    unnamed x279, local copies, waits for them, and re-layouts  38 us
    ppermute x12, waiting for transfers between devices, gather(): ahead = lax.ppermute(ahead, 'expert', self.next)  35.5 us
    ppermute x12, waiting for transfers between devices, reduce(): back = lax.ppermute(yours.astype(bf16), 'expert', self.prev)  26.8 us
  transfers between devices with their start and end apart: 141, of which 35 were waited for; matrix products, arithmetic and copies ran while one was open for 24% of the time, Pallas kernels for 22%

profile of v2, /device:TPU:0, one launch (start us, length us, event | category | flops | bytes accessed | tf_op | source)
XLA Modules:
  0.0 907.1 jit_solution(10745752309969751640)
XLA Ops:
  13.4 15.1 %collective-permute-done.1 = bf16[2,4096]{1,0:T(2,128)(2,1)S(1)} collective-permute-done((bf16[2,4096]{1,0:T(2,128)(2,1)S(1)}, bf16[2,4096]{1,0:T(2,128)(2,1)S(1)}, u32[]{:S(2)}, u32[]{:S(2)}) %collective-permute-start.1) | collective-permute-done | bytes 16416 | tf_op jit(solution)/shard_map/ppermute | solution.py:483
  36.9 11.0 %collective-permute-done.8.refs_10_.refs_5_ = bf16[768,512]{1,0:T(8,128)(2,1)} collective-permute-done((bf16[768,512]{1,0:T(8,128)(2,1)S(1)}, bf16[768,512]{1,0:T(8,128)(2,1)}, u32[]{:S(2)}, u32[]{:S(2)}) %collective-permute-start.8) | collective-permute-done | bytes 786464 | tf_op jit(solution)/shard_map/ppermute | solution.py:435
  56.4 9.9 %collective-permute-done.10.refs_12_.refs_7_ = bf16[768,512]{1,0:T(8,128)(2,1)S(1)} collective-permute-done((bf16[768,512]{1,0:T(8,128)(2,1)}, bf16[768,512]{1,0:T(8,128)(2,1)S(1)}, u32[]{:S(2)}, u32[]{:S(2)}) %collective-permute-start.10) | collective-permute-done | bytes 786464 | tf_op jit(solution)/shard_map/ppermute | solution.py:435
  119.2 9.9 %attend.1 = (bf16[512,512]{1,0:T(8,128)(2,1)}, bf16[512,512]{1,0:T(8,128)(2,1)}, bf16[512,512]{1,0:T(8,128)(2,1)}, bf16[512,512]{1,0:T(8,128)(2,1)}) custom-call(s32[8]{0:T(128)} %get-tuple-element.368.refs_0_, s32[2]{0:T(128)} %pad_add_fusion.refs_1_, bf16[256,2048]{1,0:T(8,128)(2,1)} %copy-done.5, bf16[256,2048]{1,0:T(8,128)(2,1)} %copy-done.10, ...), custom_call_target="tpu_custom_call" | custom-call | flops 3221225472 | bytes 12582912 | tf_op jit(solution)/shard_map/attend/pallas_call | solution.py:633
  129.1 12.5 %collective-permute-done.21 = bf16[128,512]{1,0:T(8,128)(2,1)S(1)} collective-permute-done((bf16[128,512]{1,0:T(8,128)(2,1)S(1)}, bf16[128,512]{1,0:T(8,128)(2,1)S(1)}, u32[]{:S(2)}, u32[]{:S(2)}) %collective-permute-start.21) | collective-permute-done | bytes 131104 | tf_op jit(solution)/shard_map/ppermute | solution.py:439
  148.9 15.0 %collective-permute-start.39 = (bf16[128,2048]{1,0:T(8,128)(2,1)}, bf16[128,2048]{1,0:T(8,128)(2,1)}, u32[]{:S(2)}, u32[]{:S(2)}) collective-permute-start(bf16[128,2048]{1,0:T(8,128)(2,1)} %constant_dynamic-slice_fusion.3.refs_5_), channel_id=1, source_target_pairs={{0,8},{2,10},{8,16},{10,18},{16,24},{18,26},{24,28},{26,30},{28,20... | collective-permute-start | bytes 1572872 | tf_op jit(solution)/shard_map/ppermute | solution.py:435
  214.4 15.1 %all-to-all-done = f32[16,2,256]{2,1,0:T(2,128)S(1)} async-done(((f32[16,2,256]{2,1,0:T(2,128)}), f32[16,2,256]{2,1,0:T(2,128)S(1)}, u32[]{:S(2)}, u32[]{:S(2)}) %all-to-all-start) | async-done | bytes 32800 | tf_op jit(solution)/shard_map/all_to_all | solution.py:684
  239.9 15.3 %copy.280 = bf16[1056,8,2,128]{3,2,1,0:T(2,128)(2,1)} copy(bf16[1056,8,2,128]{3,0,1,2:T(8,128)(2,1)S(1)} %fusion.7) | data formatting | bytes 8650752 | tf_op jit(solution)/shard_map/transpose | solution.py:608
  255.2 10.4 %reshape.377.refs_11_.refs_17_ = bf16[3,352,2048]{2,1,0:T(8,128)(2,1)} reshape(bf16[1056,8,2,128]{3,2,1,0:T(2,128)(2,1)} %copy.280) | data formatting | bytes 8650752 | tf_op jit(solution)/shard_map/reshape | solution.py:608
  268.3 22.2 %experts_0.1 = (bf16[8,192,2048]{2,1,0:T(8,128)(2,1)}, bf16[8,192,2048]{2,1,0:T(8,128)(2,1)}, bf16[8,192,704]{2,1,0:T(8,128)(2,1)}, bf16[2,8,192,704]{3,2,1,0:T(...) custom-call(s32[1]{0:T(128)} %bitcast.15.refs_0_, ...), custom_call_target="tpu_custom_call" | custom-call | flops 7147094016 | bytes 33554432 | tf_op jit(solution)/shard_map/experts_0/pallas_call | solution.py:363
  292.1 20.7 %experts_1.1 = (bf16[8,192,2048]{2,1,0:T(8,128)(2,1)}, bf16[8,192,2048]{2,1,0:T(8,128)(2,1)}, bf16[8,192,704]{2,1,0:T(8,128)(2,1)}, bf16[2,8,192,704]{3,2,1,0:T(...) custom-call(s32[1]{0:T(128)} %bitcast.15.refs_0_, ...), custom_call_target="tpu_custom_call", output_to_operand_aliasing={{0}: (12, {}), {1}: (13, {}), {2}: (14, {}), {3}: (15, {}),... | custom-call | flops 7147094016 | bytes 33554432 | tf_op jit(solution)/shard_map/experts_1/pallas_call | solution.py:363
  315.9 20.9 %experts_2.1 = (bf16[8,192,2048]{2,1,0:T(8,128)(2,1)}, bf16[8,192,2048]{2,1,0:T(8,128)(2,1)}, bf16[8,192,704]{2,1,0:T(8,128)(2,1)}, bf16[2,8,192,704]{3,2,1,0:T(...) custom-call(s32[1]{0:T(128)} %bitcast.15.refs_0_, ...), custom_call_target="tpu_custom_call", output_to_operand_aliasing={{0}: (12, {}), {1}: (13, {}), {2}: (14, {}), {3}: (15, {}),... | custom-call | flops 7147094016 | bytes 33554432 | tf_op jit(solution)/shard_map/experts_2/pallas_call | solution.py:363
  341.8 20.6 %experts_3.1 = (bf16[8,192,2048]{2,1,0:T(8,128)(2,1)}, bf16[8,192,2048]{2,1,0:T(8,128)(2,1)}, bf16[8,192,704]{2,1,0:T(8,128)(2,1)}, bf16[2,8,192,704]{3,2,1,0:T(...) custom-call(s32[1]{0:T(128)} %bitcast.15.refs_0_, ...), custom_call_target="tpu_custom_call", output_to_operand_aliasing={{0}: (12, {}), {1}: (13, {}), {2}: (14, {}), {3}: (15, {}),... | custom-call | flops 7147094016 | bytes 33554432 | tf_op jit(solution)/shard_map/experts_3/pallas_call | solution.py:363
  366.1 20.8 %experts_4.1 = (bf16[8,192,2048]{2,1,0:T(8,128)(2,1)}, bf16[8,192,2048]{2,1,0:T(8,128)(2,1)}, bf16[8,192,704]{2,1,0:T(8,128)(2,1)}, bf16[2,8,192,704]{3,2,1,0:T(...) custom-call(s32[1]{0:T(128)} %bitcast.15.refs_0_, ...), custom_call_target="tpu_custom_call", output_to_operand_aliasing={{0}: (12, {}), {1}: (13, {}), {2}: (14, {}), {3}: (15, {}),... | custom-call | flops 7147094016 | bytes 33554432 | tf_op jit(solution)/shard_map/experts_4/pallas_call | solution.py:363
  390.7 21.0 %experts_5.1 = (bf16[8,192,2048]{2,1,0:T(8,128)(2,1)}, bf16[8,192,2048]{2,1,0:T(8,128)(2,1)}, bf16[8,192,704]{2,1,0:T(8,128)(2,1)}, bf16[2,8,192,704]{3,2,1,0:T(...) custom-call(s32[1]{0:T(128)} %bitcast.15.refs_0_, ...), custom_call_target="tpu_custom_call", output_to_operand_aliasing={{0}: (12, {}), {1}: (13, {}), {2}: (14, {}), {3}: (15, {}),... | custom-call | flops 7147094016 | bytes 33554432 | tf_op jit(solution)/shard_map/experts_5/pallas_call | solution.py:363
  415.2 20.6 %experts_6.1 = (bf16[8,192,2048]{2,1,0:T(8,128)(2,1)}, bf16[8,192,2048]{2,1,0:T(8,128)(2,1)}, bf16[8,192,704]{2,1,0:T(8,128)(2,1)}, bf16[2,8,192,704]{3,2,1,0:T(...) custom-call(s32[1]{0:T(128)} %bitcast.15.refs_0_, ...), custom_call_target="tpu_custom_call", output_to_operand_aliasing={{0}: (12, {}), {1}: (13, {}), {2}: (14, {}), {3}: (15, {}),... | custom-call | flops 7147094016 | bytes 33554432 | tf_op jit(solution)/shard_map/experts_6/pallas_call | solution.py:363
  439.5 20.9 %experts_7.1 = (bf16[8,192,2048]{2,1,0:T(8,128)(2,1)}, bf16[8,192,2048]{2,1,0:T(8,128)(2,1)}, bf16[8,192,704]{2,1,0:T(8,128)(2,1)}, bf16[2,8,192,704]{3,2,1,0:T(...) custom-call(s32[1]{0:T(128)} %bitcast.15.refs_0_, ...), custom_call_target="tpu_custom_call", output_to_operand_aliasing={{0}: (18, {}), {1}: (19, {}), {2}: (20, {}), {3}: (21, {}),... | custom-call | flops 7147094016 | bytes 33554432 | tf_op jit(solution)/shard_map/experts_7/pallas_call | solution.py:363
  466.2 10.9 %convolution_bitcast_fusion = f32[1,704,2048]{2,1,0:T(8,128)} fusion(bf16[8,192,704]{2,1,0:T(8,128)(2,1)} %get-tuple-element.244, bf16[8,192,2048]{2,1,0:T(8,128)(2,1)} %get-tuple-element.245), kind=kOutput, calls=%fused_computation.51 | convolution fusion | flops 4429185024 | bytes 14221312 | tf_op jit(solution)/shard_map/dot_general | solution.py:51
  477.1 14.3 %fusion.4 = f32[1,2048,2,704]{1,3,2,0:T(8,128)} fusion(bf16[2,8,192,704]{3,2,1,0:T(8,128)(2,1)} %get-tuple-element.243, bf16[8,192,2048]{2,1,0:T(8,128)(2,1)S(1)} %copy-done), kind=kOutput, calls=%fused_computation.8 | convolution fusion | flops 8858370048 | bytes 22151168 | tf_op jit(solution)/shard_map/dot_general | solution.py:51
  505.8 10.8 %reshape.385 = bf16[1056,8,2,128]{3,2,1,0:T(2,128)(2,1)} reshape(bf16[3,352,2048]{2,1,0:T(8,128)(2,1)} %pad_maximum_fusion) | data formatting | bytes 8650752 | tf_op jit(solution)/shard_map/reshape | solution.py:823
  517.5 10.7 %constant_dynamic-slice_fusion.1 = (bf16[1056,8,1,128]{3,2,1,0:T(2,128)(2,1)S(1)}, bf16[1056,8,1,128]{3,2,1,0:T(2,128)(2,1)S(1)}) fusion(bf16[1056,8,2,128]{3,2,1,0:T(2,128)(2,1)} %reshape.385, s32[]{:T(128)S(6)} %select_n.229, s32[]{:T(128)S(6)} %select_n.259), kind=kLoop, calls=%fused_computation.227 | loop fusion | bytes 8650760 | tf_op jit(solution)/shard_map/dynamic_slice | solution.py:582
  542.1 10.8 %collective-permute-done.100 = bf16[128,2048]{1,0:T(8,128)(2,1)S(1)} collective-permute-done((bf16[128,2048]{1,0:T(8,128)(2,1)S(1)}, bf16[128,2048]{1,0:T(8,128)(2,1)S(1)}, u32[]{:S(2)}, u32[]{:S(2)}) %collective-permute-start.100) | collective-permute-done | bytes 524320 | tf_op jit(solution)/shard_map/ppermute | solution.py:461
  555.7 10.5 %collective-permute-done.83 = bf16[128,2048]{1,0:T(8,128)(2,1)S(1)} collective-permute-done((bf16[128,2048]{1,0:T(8,128)(2,1)S(1)}, bf16[128,2048]{1,0:T(8,128)(2,1)S(1)}, u32[]{:S(2)}, u32[]{:S(2)}) %collective-permute-start.83) | collective-permute-done | bytes 524320 | tf_op jit(solution)/shard_map/ppermute | solution.py:461
  569.1 20.8 %collective-permute-done.101 = bf16[256,2048]{1,0:T(8,128)(2,1)S(1)} collective-permute-done((bf16[256,2048]{1,0:T(8,128)(2,1)S(1)}, bf16[256,2048]{1,0:T(8,128)(2,1)S(1)}, u32[]{:S(2)}, u32[]{:S(2)}) %collective-permute-start.101) | collective-permute-done | bytes 1048608 | tf_op jit(solution)/shard_map/ppermute | solution.py:471
  605.7 14.0 %collective-permute-done.102 = bf16[256,2048]{1,0:T(8,128)(2,1)} collective-permute-done((bf16[256,2048]{1,0:T(8,128)(2,1)}, bf16[256,2048]{1,0:T(8,128)(2,1)}, u32[]{:S(2)}, u32[]{:S(2)}) %collective-permute-start.102) | collective-permute-done | bytes 1048608 | tf_op jit(solution)/shard_map/ppermute | solution.py:471
  633.2 45.8 %collective-permute-done.84 = bf16[256,2048]{1,0:T(8,128)(2,1)S(1)} collective-permute-done((bf16[256,2048]{1,0:T(8,128)(2,1)S(1)}, bf16[256,2048]{1,0:T(8,128)(2,1)S(1)}, u32[]{:S(2)}, u32[]{:S(2)}) %collective-permute-start.84) | collective-permute-done | bytes 1048608 | tf_op jit(solution)/shard_map/ppermute | solution.py:471
  680.2 15.4 %collective-permute-start.85 = (bf16[256,2048]{1,0:T(8,128)(2,1)S(1)}, bf16[256,2048]{1,0:T(8,128)(2,1)S(1)}, u32[]{:S(2)}, u32[]{:S(2)}) collective-permute-start(bf16[256,2048]{1,0:T(8,128)(2,1)S(1)} %add_convert_fusion.12), channel_id=1, source_target_pairs={{0,8},{2,10},{8,16},{10,18},{16,24},{18,26},{24,28},{26,30},{28,20... | collective-permute-start | bytes 3145736 | tf_op jit(solution)/shard_map/ppermute | solution.py:471
  701.5 12.2 %collective-permute-done.110 = bf16[256,2048]{1,0:T(8,128)(2,1)S(1)} collective-permute-done((bf16[256,2048]{1,0:T(8,128)(2,1)S(1)}, bf16[256,2048]{1,0:T(8,128)(2,1)S(1)}, u32[]{:S(2)}, u32[]{:S(2)}) %collective-permute-start.110) | collective-permute-done | bytes 1048608 | tf_op jit(solution)/shard_map/ppermute | solution.py:472
  724.6 13.0 %collective-permute-start.86 = (bf16[256,2048]{1,0:T(8,128)(2,1)}, bf16[256,2048]{1,0:T(8,128)(2,1)}, u32[]{:S(2)}, u32[]{:S(2)}) collective-permute-start(bf16[256,2048]{1,0:T(8,128)(2,1)} %add_convert_fusion.11), channel_id=1, source_target_pairs={{0,8},{2,10},{8,16},{10,18},{16,24},{18,26},{24,28},{26,30},{28,20... | collective-permute-start | bytes 3145736 | tf_op jit(solution)/shard_map/ppermute | solution.py:471
  787.6 10.9 %attend_back.1 = (bf16[512,1536]{1,0:T(8,128)(2,1)}, f32[1,1536]{1,0:T(1,128)}) custom-call(s32[8]{0:T(128)} %get-tuple-element.368.refs_0_, s32[2]{0:T(128)} %pad_add_fusion.refs_1_, bf16[256,2048]{1,0:T(8,128)(2,1)} %copy-done.3, bf16[256,2048]{1,0:T(8,128)(2,1)} %copy-done.8, bf16[512,512]{1,0:T(8,128)(2,1)} %get-tuple-element.231.refs_4_, ...), custom_call_target="tpu_custom_call" | custom-call | flops 2147483648 | bytes 8388608 | tf_op jit(solution)/shard_map/attend_back/pallas_call | solution.py:747
  835.6 13.3 %collective-permute-done.117 = bf16[256,1536]{1,0:T(8,128)(2,1)S(1)} collective-permute-done((bf16[256,1536]{1,0:T(8,128)(2,1)S(1)}, bf16[256,1536]{1,0:T(8,128)(2,1)S(1)}, u32[]{:S(2)}, u32[]{:S(2)}) %collective-permute-start.117) | collective-permute-done | bytes 786464 | tf_op jit(solution)/shard_map/ppermute | solution.py:471
  858.6 12.4 %collective-permute-done.118 = bf16[256,1536]{1,0:T(8,128)(2,1)S(1)} collective-permute-done((bf16[256,1536]{1,0:T(8,128)(2,1)S(1)}, bf16[256,1536]{1,0:T(8,128)(2,1)S(1)}, u32[]{:S(2)}, u32[]{:S(2)}) %collective-permute-start.118) | collective-permute-done | bytes 786464 | tf_op jit(solution)/shard_map/ppermute | solution.py:471
  (744 shorter events, 390.2 us)
Async XLA Ops:
  13.4 59.3 %collective-permute-start.14 = (bf16[512,128]{0,1:T(8,128)(2,1)}, bf16[512,128]{0,1:T(8,128)(2,1)S(1)}, u32[]{:S(2)}, u32[]{:S(2)}) collective-permute-start(bf16[512,128]{0,1:T(8,128)(2,1)} %copy.306), channel_id=1, source_target_pairs={{0,2},{2,0},{4,6},{6,4},{8,10},{10,8},{12,14},{14,12},{16,18},{18,... | collective-permute-start | bytes 393224 | tf_op jit(solution)/shard_map/ppermute | solution.py:476
  72.6 45.6 %collective-permute-start.4 = (bf16[256,2048]{1,0:T(8,128)(2,1)S(1)}, bf16[256,2048]{1,0:T(8,128)(2,1)S(1)}, u32[]{:S(2)}, u32[]{:S(2)}) collective-permute-start(bf16[256,2048]{1,0:T(8,128)(2,1)S(1)} %fusion.21.refs_2_), channel_id=1, source_target_pairs={{0,2},{2,0},{4,6},{6,4},{8,10},{10,8},{12,14},{14,12},{16,18},{18,... | collective-permute-start | bytes 3145736 | tf_op jit(solution)/shard_map/ppermute | solution.py:476
  105.4 89.4 %all-to-all-start.1 = ((bf16[8,1056,128]{2,1,0:T(8,128)(2,1)}), bf16[8,1056,128]{2,1,0:T(8,128)(2,1)}, u32[]{:S(2)}, u32[]{:S(2)}) async-start(bf16[8,1056,128]{2,1,0:T(8,128)(2,1)} %bitcast.224), calls=%async_computation.1 | async-start | bytes 4325376 | tf_op jit(solution)/shard_map/all_to_all | solution.py:604
  181.2 48.9 %collective-permute-start.27 = (bf16[128,2048]{1,0:T(8,128)(2,1)}, bf16[128,2048]{1,0:T(8,128)(2,1)}, u32[]{:S(2)}, u32[]{:S(2)}) collective-permute-start(bf16[128,2048]{1,0:T(8,128)(2,1)} %constant_dynamic-slice_fusion.3.refs_5_), channel_id=1, source_target_pairs={{0,2},{2,0},{4,6},{6,4},{8,10},{10,8},{12,14},{14,12},{16,18},{18,... | collective-permute-start | bytes 1572872 | tf_op jit(solution)/shard_map/ppermute | solution.py:476
  194.8 40.2 %collective-permute-start.29 = (bf16[8,1056,128]{2,1,0:T(8,128)(2,1)}, bf16[8,1056,128]{2,1,0:T(8,128)(2,1)}, u32[]{:S(2)}, u32[]{:S(2)}) collective-permute-start(bf16[8,1056,128]{2,1,0:T(8,128)(2,1)} %all-to-all-done.1), channel_id=1, source_target_pairs={{0,2},{2,0},{4,6},{6,4},{8,10},{10,8},{12,14},{14,12},{16,18},{18,... | collective-permute-start | bytes 6488072 | tf_op jit(solution)/shard_map/ppermute | solution.py:476
  232.4 35.8 %collective-permute-start.31 = (bf16[256,2048]{1,0:T(8,128)(2,1)S(1)}, bf16[256,2048]{1,0:T(8,128)(2,1)S(1)}, u32[]{:S(2)}, u32[]{:S(2)}) collective-permute-start(bf16[256,2048]{1,0:T(8,128)(2,1)S(1)} %get-tuple-element.338.refs_3_), channel_id=1, source_target_pairs={{8,0},{10,2},{16,8},{18,10},{24,16},{26,18},{28,24},{30,26},{20,28... | collective-permute-start | bytes 3145736 | tf_op jit(solution)/shard_map/ppermute | solution.py:436
  235.0 56.1 %collective-permute-start.38 = (bf16[256,2048]{1,0:T(8,128)(2,1)}, bf16[256,2048]{1,0:T(8,128)(2,1)S(1)}, u32[]{:S(2)}, u32[]{:S(2)}) collective-permute-start(bf16[256,2048]{1,0:T(8,128)(2,1)} %collective-permute-done.37.refs_3_), channel_id=1, source_target_pairs={{0,2},{2,0},{4,6},{6,4},{8,10},{10,8},{12,14},{14,12},{16,18},{18,... | collective-permute-start | bytes 3145736 | tf_op jit(solution)/shard_map/ppermute | solution.py:476
  266.1 49.7 %collective-permute-start.50 = (bf16[256,2048]{1,0:T(8,128)(2,1)}, bf16[256,2048]{1,0:T(8,128)(2,1)S(1)}, u32[]{:S(2)}, u32[]{:S(2)}) collective-permute-start(bf16[256,2048]{1,0:T(8,128)(2,1)} %collective-permute-done.37.refs_3_), channel_id=1, source_target_pairs={{0,8},{2,10},{8,16},{10,18},{16,24},{18,26},{24,28},{26,30},{28,20... | collective-permute-start | bytes 3145736 | tf_op jit(solution)/shard_map/ppermute | solution.py:435
  268.3 46.3 %collective-permute-start.32 = (bf16[256,2048]{1,0:T(8,128)(2,1)S(1)}, bf16[256,2048]{1,0:T(8,128)(2,1)S(1)}, u32[]{:S(2)}, u32[]{:S(2)}) collective-permute-start(bf16[256,2048]{1,0:T(8,128)(2,1)S(1)} %collective-permute-done.31.refs_3_), channel_id=1, source_target_pairs={{0,2},{2,0},{4,6},{6,4},{8,10},{10,8},{12,14},{14,12},{16,18},{18,... | collective-permute-start | bytes 3145736 | tf_op jit(solution)/shard_map/ppermute | solution.py:476
  291.1 46.8 %collective-permute-start.44 = (bf16[256,2048]{1,0:T(8,128)(2,1)S(1)}, bf16[256,2048]{1,0:T(8,128)(2,1)S(1)}, u32[]{:S(2)}, u32[]{:S(2)}) collective-permute-start(bf16[256,2048]{1,0:T(8,128)(2,1)S(1)} %collective-permute-done.31.refs_3_), channel_id=1, source_target_pairs={{8,0},{10,2},{16,8},{18,10},{24,16},{26,18},{28,24},{30,26},{20,28... | collective-permute-start | bytes 3145736 | tf_op jit(solution)/shard_map/ppermute | solution.py:436
  437.6 131.4 %collective-permute-start.97 = (bf16[256,2048]{1,0:T(8,128)(2,1)}, bf16[256,2048]{1,0:T(8,128)(2,1)}, u32[]{:S(2)}, u32[]{:S(2)}) collective-permute-start(bf16[256,2048]{1,0:T(8,128)(2,1)} %get-tuple-element.212), channel_id=1, source_target_pairs={{0,2},{2,0},{4,6},{6,4},{8,10},{10,8},{12,14},{14,12},{16,18},{18,... | collective-permute-start | bytes 3145736 | tf_op jit(solution)/shard_map/ppermute | solution.py:476
  438.0 154.7 %collective-permute-start.105 = (bf16[256,2048]{1,0:T(8,128)(2,1)}, bf16[256,2048]{1,0:T(8,128)(2,1)}, u32[]{:S(2)}, u32[]{:S(2)}) collective-permute-start(bf16[256,2048]{1,0:T(8,128)(2,1)} %get-tuple-element.220), channel_id=1, source_target_pairs={{0,2},{2,0},{4,6},{6,4},{8,10},{10,8},{12,14},{14,12},{16,18},{18,... | collective-permute-start | bytes 3145736 | tf_op jit(solution)/shard_map/ppermute | solution.py:476
  438.2 91.5 %collective-permute-start.98 = (bf16[256,2048]{1,0:T(8,128)(2,1)}, bf16[256,2048]{1,0:T(8,128)(2,1)}, u32[]{:S(2)}, u32[]{:S(2)}) collective-permute-start(bf16[256,2048]{1,0:T(8,128)(2,1)} %get-tuple-element.214), channel_id=1, source_target_pairs={{0,2},{2,0},{4,6},{6,4},{8,10},{10,8},{12,14},{14,12},{16,18},{18,... | collective-permute-start | bytes 3145736 | tf_op jit(solution)/shard_map/ppermute | solution.py:476
  438.5 93.2 %collective-permute-start.106 = (bf16[256,2048]{1,0:T(8,128)(2,1)}, bf16[256,2048]{1,0:T(8,128)(2,1)S(1)}, u32[]{:S(2)}, u32[]{:S(2)}) collective-permute-start(bf16[256,2048]{1,0:T(8,128)(2,1)} %get-tuple-element.222), channel_id=1, source_target_pairs={{0,2},{2,0},{4,6},{6,4},{8,10},{10,8},{12,14},{14,12},{16,18},{18,... | collective-permute-start | bytes 3145736 | tf_op jit(solution)/shard_map/ppermute | solution.py:476
  462.5 54.1 %all-to-all-start.2 = ((f32[16,2,256]{2,1,0:T(2,128)}), f32[16,2,256]{2,1,0:T(2,128)S(1)}, u32[]{:S(2)}, u32[]{:S(2)}) async-start(f32[16,2,256]{2,1,0:T(2,128)} %gather_fusion.2), calls=%async_computation.2 | async-start | bytes 65536 | tf_op jit(solution)/shard_map/all_to_all | solution.py:721
  531.8 65.6 %collective-permute-start.134 = (bf16[1,8,1056,128]{3,2,1,0:T(8,128)(2,1)S(1)}, bf16[1,8,1056,128]{3,2,1,0:T(8,128)(2,1)S(1)}, u32[]{:S(2)}, u32[]{:S(2)}) collective-permute-start(bf16[1,8,1056,128]{3,2,1,0:T(8,128)(2,1)S(1)} %bitcast.226), channel_id=1, source_target_pairs={{0,2},{2,0},{4,6},{6,4},{8,10},{10,8},{12,14},{14,12},{16,18},{18,... | collective-permute-start | bytes 6488072 | tf_op jit(solution)/shard_map/ppermute | solution.py:476
  569.0 36.6 %collective-permute-start.96 = (bf16[256,2048]{1,0:T(8,128)(2,1)}, bf16[256,2048]{1,0:T(8,128)(2,1)}, u32[]{:S(2)}, u32[]{:S(2)}) collective-permute-start(bf16[256,2048]{1,0:T(8,128)(2,1)} %get-tuple-element.210), channel_id=1, source_target_pairs={{0,2},{2,0},{4,6},{6,4},{8,10},{10,8},{12,14},{14,12},{16,18},{18,... | collective-permute-start | bytes 3145736 | tf_op jit(solution)/shard_map/ppermute | solution.py:476
  589.9 37.9 %collective-permute-start.104 = (bf16[256,2048]{1,0:T(8,128)(2,1)}, bf16[256,2048]{1,0:T(8,128)(2,1)}, u32[]{:S(2)}, u32[]{:S(2)}) collective-permute-start(bf16[256,2048]{1,0:T(8,128)(2,1)} %get-tuple-element.218), channel_id=1, source_target_pairs={{0,2},{2,0},{4,6},{6,4},{8,10},{10,8},{12,14},{14,12},{16,18},{18,... | collective-permute-start | bytes 3145736 | tf_op jit(solution)/shard_map/ppermute | solution.py:476
  592.7 103.5 %collective-permute-start.95 = (bf16[256,2048]{1,0:T(8,128)(2,1)}, bf16[256,2048]{1,0:T(8,128)(2,1)S(1)}, u32[]{:S(2)}, u32[]{:S(2)}) collective-permute-start(bf16[256,2048]{1,0:T(8,128)(2,1)} %get-tuple-element.208), channel_id=1, source_target_pairs={{0,2},{2,0},{4,6},{6,4},{8,10},{10,8},{12,14},{14,12},{16,18},{18,... | collective-permute-start | bytes 3145736 | tf_op jit(solution)/shard_map/ppermute | solution.py:476
  600.3 148.6 %all-to-all-start.5 = ((bf16[8,1056,128]{2,1,0:T(8,128)(2,1)}), bf16[8,1056,128]{2,1,0:T(8,128)(2,1)}, u32[]{:S(2)}, u32[]{:S(2)}) async-start(bf16[8,1056,128]{2,1,0:T(8,128)(2,1)} %fusion.20), calls=%async_computation.5 | async-start | bytes 4325376 | tf_op jit(solution)/shard_map/all_to_all | solution.py:827
  619.8 59.2 %collective-permute-start.84 = (bf16[256,2048]{1,0:T(8,128)(2,1)S(1)}, bf16[256,2048]{1,0:T(8,128)(2,1)S(1)}, u32[]{:S(2)}, u32[]{:S(2)}) collective-permute-start(bf16[256,2048]{1,0:T(8,128)(2,1)S(1)} %pad_maximum_fusion.1), channel_id=1, source_target_pairs={{0,8},{2,10},{8,16},{10,18},{16,24},{18,26},{24,28},{26,30},{28,20... | collective-permute-start | bytes 3145736 | tf_op jit(solution)/shard_map/ppermute | solution.py:471
  627.8 51.7 %collective-permute-start.88 = (bf16[256,2048]{1,0:T(8,128)(2,1)S(1)}, bf16[256,2048]{1,0:T(8,128)(2,1)S(1)}, u32[]{:S(2)}, u32[]{:S(2)}) collective-permute-start(bf16[256,2048]{1,0:T(8,128)(2,1)S(1)} %copy-done.118), channel_id=1, source_target_pairs={{0,2},{2,0},{4,6},{6,4},{8,10},{10,8},{12,14},{14,12},{16,18},{18,... | collective-permute-start | bytes 3145736 | tf_op jit(solution)/shard_map/ppermute | solution.py:476
  627.9 52.3 %collective-permute-start.91 = (bf16[256,2048]{1,0:T(8,128)(2,1)S(1)}, bf16[256,2048]{1,0:T(8,128)(2,1)S(1)}, u32[]{:S(2)}, u32[]{:S(2)}) collective-permute-start(bf16[256,2048]{1,0:T(8,128)(2,1)S(1)} %pad_maximum_fusion.2), channel_id=1, source_target_pairs={{8,0},{10,2},{16,8},{18,10},{24,16},{26,18},{28,24},{30,26},{20,28... | collective-permute-start | bytes 3145736 | tf_op jit(solution)/shard_map/ppermute | solution.py:472
  631.6 69.8 %collective-permute-start.103 = (bf16[256,2048]{1,0:T(8,128)(2,1)S(1)}, bf16[256,2048]{1,0:T(8,128)(2,1)S(1)}, u32[]{:S(2)}, u32[]{:S(2)}) collective-permute-start(bf16[256,2048]{1,0:T(8,128)(2,1)S(1)} %add_convert_fusion.4), channel_id=1, source_target_pairs={{0,8},{2,10},{8,16},{10,18},{16,24},{18,26},{24,28},{26,30},{28,20... | collective-permute-start | bytes 3145736 | tf_op jit(solution)/shard_map/ppermute | solution.py:471
  679.0 34.7 %collective-permute-start.110 = (bf16[256,2048]{1,0:T(8,128)(2,1)S(1)}, bf16[256,2048]{1,0:T(8,128)(2,1)S(1)}, u32[]{:S(2)}, u32[]{:S(2)}) collective-permute-start(bf16[256,2048]{1,0:T(8,128)(2,1)S(1)} %add_convert_fusion.2), channel_id=1, source_target_pairs={{8,0},{10,2},{16,8},{18,10},{24,16},{26,18},{28,24},{30,26},{20,28... | collective-permute-start | bytes 3145736 | tf_op jit(solution)/shard_map/ppermute | solution.py:472
  680.2 34.2 %collective-permute-start.43 = (bf16[256,2048]{1,0:T(8,128)(2,1)S(1)}, bf16[256,2048]{1,0:T(8,128)(2,1)S(1)}, u32[]{:S(2)}, u32[]{:S(2)}) collective-permute-start(bf16[256,2048]{1,0:T(8,128)(2,1)S(1)} %copy-done.117), channel_id=1, source_target_pairs={{0,2},{2,0},{4,6},{6,4},{8,10},{10,8},{12,14},{14,12},{16,18},{18,... | collective-permute-start | bytes 3145736 | tf_op jit(solution)/shard_map/ppermute | solution.py:476
  680.2 42.8 %collective-permute-start.85 = (bf16[256,2048]{1,0:T(8,128)(2,1)S(1)}, bf16[256,2048]{1,0:T(8,128)(2,1)S(1)}, u32[]{:S(2)}, u32[]{:S(2)}) collective-permute-start(bf16[256,2048]{1,0:T(8,128)(2,1)S(1)} %add_convert_fusion.12), channel_id=1, source_target_pairs={{0,8},{2,10},{8,16},{10,18},{16,24},{18,26},{24,28},{26,30},{28,20... | collective-permute-start | bytes 3145736 | tf_op jit(solution)/shard_map/ppermute | solution.py:471
  696.9 40.7 %collective-permute-start.87 = (bf16[256,2048]{1,0:T(8,128)(2,1)S(1)}, bf16[256,2048]{1,0:T(8,128)(2,1)S(1)}, u32[]{:S(2)}, u32[]{:S(2)}) collective-permute-start(bf16[256,2048]{1,0:T(8,128)(2,1)S(1)} %copy-done.116), channel_id=1, source_target_pairs={{0,2},{2,0},{4,6},{6,4},{8,10},{10,8},{12,14},{14,12},{16,18},{18,... | collective-permute-start | bytes 3145736 | tf_op jit(solution)/shard_map/ppermute | solution.py:476
  701.4 52.6 %collective-permute-start.30 = (bf16[256,2048]{1,0:T(8,128)(2,1)}, bf16[256,2048]{1,0:T(8,128)(2,1)}, u32[]{:S(2)}, u32[]{:S(2)}) collective-permute-start(bf16[256,2048]{1,0:T(8,128)(2,1)} %get-tuple-element.136), channel_id=1, source_target_pairs={{0,2},{2,0},{4,6},{6,4},{8,10},{10,8},{12,14},{14,12},{16,18},{18,... | collective-permute-start | bytes 3145736 | tf_op jit(solution)/shard_map/ppermute | solution.py:476
  724.6 36.3 %collective-permute-start.86 = (bf16[256,2048]{1,0:T(8,128)(2,1)}, bf16[256,2048]{1,0:T(8,128)(2,1)}, u32[]{:S(2)}, u32[]{:S(2)}) collective-permute-start(bf16[256,2048]{1,0:T(8,128)(2,1)} %add_convert_fusion.11), channel_id=1, source_target_pairs={{0,8},{2,10},{8,16},{10,18},{16,24},{18,26},{24,28},{26,30},{28,20... | collective-permute-start | bytes 3145736 | tf_op jit(solution)/shard_map/ppermute | solution.py:471
  744.4 38.5 %collective-permute-start.113 = (bf16[256,2048]{1,0:T(8,128)(2,1)S(1)}, bf16[256,2048]{1,0:T(8,128)(2,1)S(1)}, u32[]{:S(2)}, u32[]{:S(2)}) collective-permute-start(bf16[256,2048]{1,0:T(8,128)(2,1)S(1)} %fusion.125.refs_2_), channel_id=1, source_target_pairs={{0,2},{2,0},{4,6},{6,4},{8,10},{10,8},{12,14},{14,12},{16,18},{18,... | collective-permute-start | bytes 3145736 | tf_op jit(solution)/shard_map/ppermute | solution.py:476
  769.4 127.8 %collective-permute-start.94 = (bf16[256,2048]{1,0:T(8,128)(2,1)}, bf16[256,2048]{1,0:T(8,128)(2,1)}, u32[]{:S(2)}, u32[]{:S(2)}) collective-permute-start(bf16[256,2048]{1,0:T(8,128)(2,1)} %add_convert_fusion.8), channel_id=1, source_target_pairs={{0,1},{1,0},{2,3},{3,2},{4,5},{5,4},{6,7},{7,6},{8,9},{9,8},{10,11... | collective-permute-start | bytes 3145736 | tf_op jit(solution)/shard_map/ppermute | solution.py:497
  (237 other events, 3513.4 us)

commit v3 on v2

--- a/solution.py
+++ b/solution.py
@@ -64,8 +64,8 @@
     return [(lo, min(size, total - lo)) for lo in range(0, total, size)]
 
 
-def params():
-    return pltpu.CompilerParams(vmem_limit_bytes=56 * 1024 * 1024)
+def params(mebibytes=56):
+    return pltpu.CompilerParams(vmem_limit_bytes=mebibytes * 1024 * 1024)
 
 
 def half_turn(values):
@@ -84,17 +84,19 @@
     return weights / jnp.sum(weights, axis=-1, keepdims=True)
 
 
-def load_blocks(chip_ref, blocks, scratch, sem, parts):
-    depth = blocks[0].shape[0] // parts
+def load_blocks(chip_ref, blocks, scratch, sem, first, last):
+    whole = len(blocks) - 2
+    depth = blocks[0].shape[0] // 4
     copies = []
-    for i, block in enumerate(blocks):
+    for i in range(whole + 1):
         start = pl.multiple_of(chip_ref[i] * depth, depth)
-        for c in range(parts):
+        for c in range(first, last):
+            block, at = (blocks[i], c) if i < whole else (blocks[whole + c // 2], c % 2)
             copies.append(
                 pltpu.make_async_copy(
-                    block.at[pl.ds(c * depth, depth)],
-                    scratch.at[c, pl.ds(start, depth)],
-                    sem.at[i * parts + c],
+                    block.at[pl.ds(at * depth, depth)],
+                    scratch.at[c - first, pl.ds(start, depth)],
+                    sem.at[len(copies)],
                 )
             )
     for copy in copies:
@@ -106,7 +108,7 @@
     chip_ref, prefix_ref, own, other, bias, cosine, sine = refs[:7]
     blocks = refs[7 : 7 + count]
     query, key, value, mixed, weight, sem = refs[7 + count :]
-    copies = load_blocks(chip_ref, blocks, weight, sem, 3)
+    copies = load_blocks(chip_ref, blocks, weight, sem, 0, 3)
     length, head_size = cosine.shape
     columns = heads * head_size
     for copy in copies:
@@ -136,7 +138,7 @@
     chip_ref, mixed = refs[:2]
     blocks = refs[2 : 2 + count]
     own, other, weight, sem = refs[2 + count :]
-    copies = load_blocks(chip_ref, blocks, weight, sem, 1)
+    copies = load_blocks(chip_ref, blocks, weight, sem, 3, 4)
     for copy in copies:
         copy.wait()
     length, width = own.shape
@@ -150,7 +152,7 @@
     chip_ref, prefix_ref, own, other, query, key, value, cosine, sine = refs[:9]
     blocks = refs[9 : 9 + count]
     grad, bias, weight, sem = refs[9 + count :]
-    copies = load_blocks(chip_ref, blocks, weight, sem, 1)
+    copies = load_blocks(chip_ref, blocks, weight, sem, 3, 4)
     length, head_size = cosine.shape
     columns = heads * head_size
     for copy in copies:
@@ -183,7 +185,7 @@
     chip_ref, grad = refs[:2]
     blocks = refs[2 : 2 + count]
     own, other, weight, sem = refs[2 + count :]
-    copies = load_blocks(chip_ref, blocks, weight, sem, 3)
+    copies = load_blocks(chip_ref, blocks, weight, sem, 0, 3)
     for copy in copies:
         copy.wait()
     length, width = own.shape
@@ -196,82 +198,99 @@
         other[:, lo : lo + size] = part[length:].astype(other.dtype)
 
 
-def moe_kernel(index, first, plan, sizes, *refs):
+def moe_kernel(index, span, first, plan, sizes, *refs):
     length, width, capacity, units, shared_units = sizes
     count = sum(len(p) for p in plan)
+    own_rows, slab = span * length, 2 * span * capacity
     half_ref, row_ref, col_ref = refs[:3]
     given = refs[3 : 3 + count]
     in_hbm, out_hbm, shared_hbm = refs[3 + count : 6 + count]
     rest = refs[6 + count + (0 if first else 8) :]
-    kept = rest[:8]
-    moe_own, moe_other, back_own, back_other, dots = rest[8:13]
-    (tok, up, w_in, w_out, w_sh, rows, up_rows, slots, hidden, gu, y_grad, s_hidden, s_gu) = rest[
-        13:26
+    kept, outs, dots = rest[:8], rest[8 : 8 + 4 * span], rest[8 + 4 * span]
+    tok, up, rows, up_rows, slots, hidden, gu, y_grad, s_hidden, s_gu, made_out = rest[
+        9 + 4 * span : 20 + 4 * span
     ]
-    load_sem, weight_sem, keep_sem = rest[26:]
+    w_in, w_out, w_sh, load_sem, weight_sem, out_sem, keep_sem = rest[20 + 4 * span :]
+    wide = min(512, width)
+    columns = tiles(width, wide)
 
     loads = []
-    for which, pieces in enumerate(plan):
-        target = (tok, tok, up, up)[which]
-        for start_zero, start_one, size in pieces:
-            start = start_zero + half_ref[0] * (start_one - start_zero)
-            start = pl.multiple_of(start + (which % 2) * length, 16)
-            loads.append(
-                pltpu.make_async_copy(
-                    given[len(loads)], target.at[pl.ds(start, size)], load_sem.at[len(loads)]
+    for n, (lo, size_cols) in enumerate(columns):
+        cols, number = slice(lo, lo + size_cols), 0
+        loads.append([])
+        for which, pieces in enumerate(plan):
+            target, at = (tok, up)[which // (2 * span)], which % (2 * span) * length
+            for start_zero, start_one, size in pieces:
+                start = start_zero + half_ref[0] * (start_one - start_zero)
+                start = pl.multiple_of(start + at, 16)
+                copy = pltpu.make_async_copy(
+                    given[number].at[:, cols],
+                    target.at[pl.ds(start, size), cols],
+                    load_sem.at[n, number],
                 )
-            )
+                copy.start()
+                loads[-1].append(copy)
+                number += 1
+
     weights = [
         pltpu.make_async_copy(a, b, weight_sem.at[i])
-        for i, (a, b) in enumerate(((in_hbm, w_in), (out_hbm, w_out), (shared_hbm, w_sh)))
+        for i, (a, b) in enumerate(((shared_hbm, w_sh), (in_hbm, w_in), (out_hbm, w_out)))
     ]
-    for copy in loads + weights:
+    for copy in weights:
         copy.start()
 
     def keep(slot, source):
         target = kept[slot]
-        target = target.at[:, index] if len(target.shape) == 4 else target.at[index]
+        size = source.shape[-2]
+        first_row = index * (size // span)
+        if len(target.shape) == 3:
+            target = target.at[:, pl.ds(first_row, size)]
+        else:
+            target = target.at[pl.ds(first_row, size)]
         copy = pltpu.make_async_copy(source, target, keep_sem.at[slot])
         copy.start()
         return copy
 
-    rank_own, rank_other = row_ref[index, 0:1, :], row_ref[index, 1:2, :]
     slot = lax.broadcasted_iota(jnp.int32, (capacity, length), 0).astype(f32)
-    pick_own, pick_other = slot == rank_own, slot == rank_other
-    one_own = jnp.where(pick_own, 1.0, 0.0).astype(bf16)
-    one_other = jnp.where(pick_other, 1.0, 0.0).astype(bf16)
-    gate_own = jnp.sum(jnp.where(pick_own, row_ref[index, 2:3, :], 0.0), axis=1, keepdims=True)
-    gate_other = jnp.sum(jnp.where(pick_other, row_ref[index, 3:4, :], 0.0), axis=1, keepdims=True)
-    gates = jnp.concatenate([gate_own, gate_other], axis=0)
     lane = lax.broadcasted_iota(jnp.int32, (length, 2 * capacity), 1).astype(f32)
-    place = jnp.concatenate(
-        [
-            jnp.where(lane == col_ref[index, :, 0:1], 1.0, 0.0).astype(bf16),
-            jnp.where(lane == col_ref[index, :, 1:2] + float(capacity), 1.0, 0.0).astype(bf16),
-        ],
-        axis=0,
-    )
-    sigma = col_ref[index, :, 2:3]
-    for copy in loads:
-        copy.wait()
-    kept_copies = [keep(4, tok.at[0:length])]
-
-    wide = min(512, width)
-
-    @pl.loop(0, width // wide)
-    def _(n):
-        cols = pl.ds(pl.multiple_of(n * wide, wide), wide)
-        rows[0:capacity, cols] = mm(one_own, tok[0:length, cols]).astype(bf16)
-        rows[capacity:, cols] = mm(one_other, tok[length:, cols]).astype(bf16)
-        got = mm(one_own, up[0:length, cols])
-        up_rows[0:capacity, cols] = got.astype(bf16)
-        slots[0:capacity, cols] = (gate_own * got).astype(bf16)
-        got = mm(one_other, up[length:, cols])
-        up_rows[capacity:, cols] = got.astype(bf16)
-        slots[capacity:, cols] = (gate_other * got).astype(bf16)
-        y_grad[:, cols] = (sigma * up[0:length, cols].astype(f32)).astype(bf16)
-
-    kept_copies += [keep(0, rows), keep(1, slots), keep(5, y_grad)]
+    picks, ones, places, gates, sigmas = [], [], [], [], []
+    for j in range(span):
+        for c in range(2):
+            pick = slot == row_ref[index + j, c : c + 1, :]
+            picks.append(pick)
+            ones.append(jnp.where(pick, 1.0, 0.0).astype(bf16))
+            gate = jnp.where(pick, row_ref[index + j, 2 + c : 3 + c, :], 0.0)
+            gates.append(jnp.sum(gate, axis=1, keepdims=True))
+        places.append(
+            jnp.concatenate(
+                [
+                    jnp.where(
+                        lane == col_ref[index + j, :, c : c + 1] + float(c * capacity), 1.0, 0.0
+                    ).astype(bf16)
+                    for c in range(2)
+                ],
+                axis=0,
+            )
+        )
+        sigmas.append(col_ref[index + j, :, 2:3])
+    gate_all = jnp.concatenate(gates, axis=0)
+    sigma_all = jnp.concatenate(sigmas, axis=0)
+
+    for n, (lo, size) in enumerate(columns):
+        cols = slice(lo, lo + size)
+        for copy in loads[n]:
+            copy.wait()
+        for j in range(span):
+            for c in range(2):
+                source = slice((c * span + j) * length, (c * span + j + 1) * length)
+                target = slice((2 * j + c) * capacity, (2 * j + c + 1) * capacity)
+                rows[target, cols] = mm(ones[2 * j + c], tok[source, cols]).astype(bf16)
+                got = mm(ones[2 * j + c], up[source, cols])
+                up_rows[target, cols] = got.astype(bf16)
+                slots[target, cols] = (gates[2 * j + c] * got).astype(bf16)
+        y_grad[:, cols] = (sigma_all * up[0:own_rows, cols].astype(f32)).astype(bf16)
+
+    kept_copies = [keep(4, tok.at[0:own_rows]), keep(0, rows), keep(1, slots), keep(5, y_grad)]
 
     def gated(gate_part, up_part, grad):
         sig = 1.0 / (1.0 + jnp.exp(-gate_part))
@@ -283,7 +302,15 @@
         )
 
     weights[0].wait()
+    for lo, size in tiles(shared_units, 256):
+        at = slice(lo, lo + size)
+        gate_part = nt(tok[0:own_rows, :], w_sh[0, at, :])
+        up_part = nt(tok[0:own_rows, :], w_sh[1, at, :])
+        grad = nt(y_grad[...], w_sh[2, at, :])
+        s_hidden[:, at], s_gu[0, :, at], s_gu[1, :, at] = gated(gate_part, up_part, grad)
+    kept_copies += [keep(6, s_hidden), keep(7, s_gu)]
     weights[1].wait()
+    weights[2].wait()
     for lo, size in tiles(units, 256):
         at = slice(lo, lo + size)
         gate_part = nt(rows[...], w_in[0, at, :])
@@ -291,107 +318,157 @@
         grad = nt(slots[...], w_out[at, :])
         hidden[:, at], gu[0, :, at], gu[1, :, at] = gated(gate_part, up_part, grad)
     kept_copies += [keep(2, hidden), keep(3, gu)]
-    weights[2].wait()
-    for lo, size in tiles(shared_units, 256):
-        at = slice(lo, lo + size)
-        gate_part = nt(tok[0:length, :], w_sh[0, at, :])
-        up_part = nt(tok[0:length, :], w_sh[1, at, :])
-        grad = nt(y_grad[...], w_sh[2, at, :])
-        s_hidden[:, at], s_gu[0, :, at], s_gu[1, :, at] = gated(gate_part, up_part, grad)
-    kept_copies += [keep(6, s_hidden), keep(7, s_gu)]
-
-    def last(n, sums):
-        slot_dots, sigma_dots = sums
-        cols = pl.ds(pl.multiple_of(n * wide, wide), wide)
+
+    slot_dots, sigma_dots = jnp.zeros((slab, 1), f32), jnp.zeros((own_rows, 1), f32)
+    sent = []
+    for n, (lo, size) in enumerate(columns):
+        cols, turn = slice(lo, lo + size), n % 2
+        if n >= 2:
+            for copy in sent[n - 2]:
+                copy.wait()
         made = mm(hidden[...], w_out[:, cols]).astype(bf16).astype(f32)
         slot_dots = slot_dots + jnp.sum(
             up_rows[:, cols].astype(f32) * made, axis=1, keepdims=True
         )
-        routed = mm(place, (gates * made).astype(bf16))
+        made = (gate_all * made).astype(bf16)
         shared = mm(s_hidden[...], w_sh[2, :, cols])
         sigma_dots = sigma_dots + jnp.sum(
-            up[0:length, cols].astype(f32) * shared, axis=1, keepdims=True
-        )
-        moe_own[:, cols] = (routed[:length] + sigma * shared).astype(bf16)
-        moe_other[:, cols] = routed[length:].astype(bf16)
-        entry = mm(gu[0], w_in[0, :, cols]) + mm(gu[1], w_in[1, :, cols])
-        routed = mm(place, entry.astype(bf16))
-        shared = mm(s_gu[0], w_sh[0, :, cols]) + mm(s_gu[1], w_sh[1, :, cols])
-        back_own[:, cols] = (routed[:length] + shared).astype(bf16)
-        back_other[:, cols] = routed[length:].astype(bf16)
-        return slot_dots, sigma_dots
-
-    slot_dots, sigma_dots = lax.fori_loop(
-        0,
-        width // wide,
-        last,
-        (jnp.zeros((2 * capacity, 1), f32), jnp.zeros((length, 1), f32)),
-    )
-    dots[0:1, :] = jnp.sum(jnp.where(pick_own, slot_dots[:capacity], 0.0), axis=0, keepdims=True)
-    dots[1:2, :] = jnp.sum(jnp.where(pick_other, slot_dots[capacity:], 0.0), axis=0, keepdims=True)
+            up[0:own_rows, cols].astype(f32) * shared, axis=1, keepdims=True
+        )
+        shared = sigma_all * shared
+        entry = (mm(gu[0], w_in[0, :, cols]) + mm(gu[1], w_in[1, :, cols])).astype(bf16)
+        shared_back = mm(s_gu[0], w_sh[0, :, cols]) + mm(s_gu[1], w_sh[1, :, cols])
+        sent.append([])
+        for j in range(span):
+            mine = slice(j * length, (j + 1) * length)
+            theirs = slice(2 * j * capacity, 2 * (j + 1) * capacity)
+            routed = mm(places[j], made[theirs])
+            made_out[turn, 4 * j] = (routed[:length] + shared[mine]).astype(bf16)
+            made_out[turn, 4 * j + 1] = routed[length:].astype(bf16)
+            routed = mm(places[j], entry[theirs])
+            made_out[turn, 4 * j + 2] = (routed[:length] + shared_back[mine]).astype(bf16)
+            made_out[turn, 4 * j + 3] = routed[length:].astype(bf16)
+            for k in range(4 * j, 4 * j + 4):
+                pairs = [(made_out.at[turn, k], outs[k].at[:, cols])]
+                if k % 4 < 2:
+                    middle = length // 2
+                    pairs = [
+                        (
+                            made_out.at[turn, k, pl.ds(pl.multiple_of(h * middle, 16), middle)],
+                            outs[k].at[m * middle : (m + 1) * middle, cols],
+                        )
+                        for m, h in enumerate((half_ref[0], 1 - half_ref[0]))
+                    ]
+                for m, (source, target) in enumerate(pairs):
+                    copy = pltpu.make_async_copy(source, target, out_sem.at[turn, k, m])
+                    copy.start()
+                    sent[-1].append(copy)
     row = lax.broadcasted_iota(jnp.int32, (length, length), 0)
     col = lax.broadcasted_iota(jnp.int32, (length, length), 1)
-    dots[2:3, :] = jnp.sum(jnp.where(row == col, sigma_dots, 0.0), axis=0, keepdims=True)
-    dots[3:, :] = jnp.zeros((dots.shape[0] - 3, length), f32)
-    for copy in kept_copies:
+    for j in range(span):
+        for c in range(2):
+            part = slot_dots[(2 * j + c) * capacity : (2 * j + c + 1) * capacity]
+            part = jnp.where(picks[2 * j + c], part, 0.0)
+            dots[j, c : c + 1, :] = jnp.sum(part, axis=0, keepdims=True)
+        part = jnp.where(row == col, sigma_dots[j * length : (j + 1) * length], 0.0)
+        dots[j, 2:3, :] = jnp.sum(part, axis=0, keepdims=True)
+        dots[j, 3:, :] = jnp.zeros((dots.shape[1] - 3, length), f32)
+    for copy in kept_copies + [copy for group in sent[-2:] for copy in group]:
         copy.wait()
 
 
-def moe_call(index, sizes, chips, pieces, half, row_aux, col_aux, weights, kept):
+def moe_call(index, span, sizes, chips, pieces, half, row_aux, col_aux, weights, kept):
     length, width, capacity, units, shared_units = sizes
     plan = [[(a, b, piece.shape[0]) for piece, a, b in group] for group in pieces]
     arrays = [piece for group in pieces for piece, _, _ in group]
     first = kept is None
+    own_rows, slab = span * length, 2 * span * capacity
+    slots, tokens = chips * 2 * capacity, chips * length
     kept_shapes = [
         jax.ShapeDtypeStruct(shape, bf16)
         for shape in (
-            (chips, 2 * capacity, width),
-            (chips, 2 * capacity, width),
-            (chips, 2 * capacity, units),
-            (2, chips, 2 * capacity, units),
-            (chips, length, width),
-            (chips, length, width),
-            (chips, length, shared_units),
-            (2, chips, length, shared_units),
+            (slots, width),
+            (slots, width),
+            (slots, units),
+            (2, slots, units),
+            (tokens, width),
+            (tokens, width),
+            (tokens, shared_units),
+            (2, tokens, shared_units),
         )
     ]
     block = jax.ShapeDtypeStruct((length, width), bf16)
     operands = [half, row_aux, col_aux, *arrays, *weights] + ([] if first else list(kept))
     aliases = {} if first else {len(operands) - 8 + i: i for i in range(8)}
-    flops = 2 * 2 * capacity * width * units * 6 + 2 * length * width * shared_units * 6
-    flops += 2 * 2 * length * 2 * capacity * width * 4
+    flops = 2 * slab * width * units * 6 + 2 * own_rows * width * shared_units * 6
     out = pl.pallas_call(
-        functools.partial(moe_kernel, index, first, plan, sizes),
-        out_shape=kept_shapes + [block] * 4 + [jax.ShapeDtypeStruct((8, length), f32)],
+        functools.partial(moe_kernel, index, span, first, plan, sizes),
+        out_shape=kept_shapes
+        + [block] * (4 * span)
+        + [jax.ShapeDtypeStruct((span, 8, length), f32)],
         in_specs=[in_smem, in_vmem, in_vmem]
         + [in_any] * (len(arrays) + 3 + (0 if first else 8)),
-        out_specs=[in_any] * 8 + [in_vmem] * 5,
+        out_specs=[in_any] * (8 + 4 * span) + [in_vmem],
         scratch_shapes=[
-            pltpu.VMEM((2 * length, width), bf16),
-            pltpu.VMEM((2 * length, width), bf16),
+            pltpu.VMEM((2 * own_rows, width), bf16),
+            pltpu.VMEM((2 * own_rows, width), bf16),
+            pltpu.VMEM((slab, width), bf16),
+            pltpu.VMEM((slab, width), bf16),
+            pltpu.VMEM((slab, width), bf16),
+            pltpu.VMEM((slab, units), bf16),
+            pltpu.VMEM((2, slab, units), bf16),
+            pltpu.VMEM((own_rows, width), bf16),
+            pltpu.VMEM((own_rows, shared_units), bf16),
+            pltpu.VMEM((2, own_rows, shared_units), bf16),
+            pltpu.VMEM((2, 4 * span, length, min(512, width)), bf16),
             pltpu.VMEM((2, units, width), bf16),
             pltpu.VMEM((units, width), bf16),
             pltpu.VMEM((3, shared_units, width), bf16),
-            pltpu.VMEM((2 * capacity, width), bf16),
-            pltpu.VMEM((2 * capacity, width), bf16),
-            pltpu.VMEM((2 * capacity, width), bf16),
-            pltpu.VMEM((2 * capacity, units), bf16),
-            pltpu.VMEM((2, 2 * capacity, units), bf16),
-            pltpu.VMEM((length, width), bf16),
-            pltpu.VMEM((length, shared_units), bf16),
-            pltpu.VMEM((2, length, shared_units), bf16),
-            pltpu.SemaphoreType.DMA((len(arrays),)),
+            pltpu.SemaphoreType.DMA((len(tiles(width, min(512, width))), len(arrays))),
             pltpu.SemaphoreType.DMA((3,)),
+            pltpu.SemaphoreType.DMA((2, 4 * span, 2)),
             pltpu.SemaphoreType.DMA((8,)),
         ],
         input_output_aliases=aliases,
         compiler_params=params(),
         cost_estimate=pl.CostEstimate(
-            flops=flops, bytes_accessed=32 * 1024 * 1024, transcendentals=0
+            flops=flops, bytes_accessed=(16 + 12 * span) * 1024 * 1024, transcendentals=0
         ),
         name=f"experts_{index}",
     )(*operands)
-    return out[:8], out[8:12], out[12]
+    blocks = out[8 : 8 + 4 * span]
+    return out[:8], [blocks[4 * j : 4 * j + 4] for j in range(span)], out[8 + 4 * span]
+
+
+def spread_kernel(core_ref, own, other, out):
+    parts, units, _ = out.shape
+    count, _, rows = own.shape
+
+    def spread(first, second):
+        for i in range(count):
+            for c in range(parts):
+                at = slice(c * units, (c + 1) * units)
+                both = jnp.concatenate([first[i, at, :], second[i, at, :]], axis=1)
+                out[c, :, 2 * i * rows : 2 * (i + 1) * rows] = both
+
+    @pl.when(core_ref[0] == 0)
+    def _():
+        spread(own, other)
+
+    @pl.when(core_ref[0] == 1)
+    def _():
+        spread(other, own)
+
+
+def shared_grad_kernel(tok, y_grad, hidden, gu, out):
+    units = hidden.shape[1]
+    rows = out.shape[3]
+    for c in range(3):
+        left = gu[c] if c < 2 else hidden[...]
+        right = tok[...] if c < 2 else y_grad[...]
+        part = mm(left, right, 0, 0).astype(bf16)
+        for k in range(2):
+            out[k, 0, c * units : (c + 1) * units, :] = part[:, k * rows : (k + 1) * rows]
 
 
 class Ring:
@@ -427,50 +504,57 @@
         ).reshape(devices, devices)
         self.seq_inverse = np.argsort(self.seq_table, axis=1).astype(np.int32)
 
+    def step(self, ahead, back=None, last=False):
+        back = ahead if back is None else back
+        if last:
+            cut = ahead.shape[0] // 2
+            ahead, back = ahead[:cut], back[cut:]
+        return self.send_pair(ahead, back)
+
+    def send_pair(self, ahead, back):
+        return [
+            lax.ppermute(ahead, "expert", self.next),
+            lax.ppermute(back, "expert", self.prev),
+        ]
+
     def gather(self, block):
         half = self.chips // 2
-        found = {0: block}
-        ahead = back = block
+        found = {0: [block]}
+        pair = [block]
         for k in range(1, half):
-            ahead = lax.ppermute(ahead, "expert", self.next)
-            back = lax.ppermute(back, "expert", self.prev)
-            found[-k], found[k] = ahead, back
-        cut = block.shape[0] // 2
-        first = lax.ppermute(ahead[:cut], "expert", self.next)
-        second = lax.ppermute(back[cut:], "expert", self.prev)
-        return {o: [b] for o, b in found.items()} | {half: [first, second]}
-
-    def gather_whole(self, block):
-        found = self.gather(block)
-        return [
-            found[o][0] if len(found[o]) == 1 else jnp.concatenate(found[o], axis=0)
-            for o in self.offsets
-        ]
+            pair = self.step(*pair)
+            found[-k], found[k] = pair[:1], pair[1:]
+        found[half] = self.step(*pair, last=True)
+        return found
+
+    def add_up(self, terms):
+        out = None
+        for term in terms:
+            out = term.astype(f32) if out is None else out + term.astype(f32)
+        return out
+
+    def reduce_first(self, terms):
+        total = self.add_up(terms).astype(bf16)
+        return self.step(total, last=True)
+
+    def reduce_terms(self, ahead_terms, back_terms, sending, first):
+        mine, yours = self.add_up(ahead_terms), self.add_up(back_terms)
+        ahead, back = (part.astype(f32) for part in sending)
+        if first:
+            cut = ahead.shape[0]
+            mine = jnp.concatenate([mine[:cut] + ahead, mine[cut:]], axis=0)
+            yours = jnp.concatenate([yours[:cut], yours[cut:] + back], axis=0)
+        else:
+            mine, yours = mine + ahead, yours + back
+        return [mine.astype(bf16), yours.astype(bf16)]
 
     def reduce(self, terms):
         half = self.chips // 2
-
-        def total(offset, more=()):
-            out = None
-            for term in list(terms[offset]) + list(more):
-                out = term.astype(f32) if out is None else out + term.astype(f32)
-            return out
-
-        far = total(half).astype(bf16)
-        cut = far.shape[0] // 2
-        ahead = lax.ppermute(far[:cut], "expert", self.next)
-        back = lax.ppermute(far[cut:], "expert", self.prev)
+        sending = self.reduce_first(terms[half])
         for k in range(half - 1, 0, -1):
-            mine, yours = total(k), total(-k)
-            if k == half - 1:
-                mine = jnp.concatenate([mine[:cut] + ahead.astype(f32), mine[cut:]], axis=0)
-                yours = jnp.concatenate([yours[:cut], yours[cut:] + back.astype(f32)], axis=0)
-            else:
-                mine = mine + ahead.astype(f32)
-                yours = yours + back.astype(f32)
-            ahead = lax.ppermute(mine.astype(bf16), "expert", self.next)
-            back = lax.ppermute(yours.astype(bf16), "expert", self.prev)
-        return total(0, (ahead, back))
+            send = self.reduce_terms(terms[k], terms[-k], sending, k == half - 1)
+            sending = self.send_pair(*send)
+        return self.add_up([*terms[0], *sending])
 
     def swap_core(self, block):
         return lax.ppermute(block, "expert", self.core)
@@ -491,6 +575,10 @@
 
 def after(value, *others):
     return lax.optimization_barrier((value,) + others)[0]
+
+
+def hold(*values):
+    return list(lax.optimization_barrier(values))
 
 
 def swap_tensor(block):
@@ -568,6 +656,9 @@
         prefix_all = found[5].reshape(devices).astype(jnp.int32)
         prefix_pair = jnp.stack([prefix_all[me], prefix_all[me ^ 1]])
 
+        def cost(flops, moved):
+            return pl.CostEstimate(flops=flops, bytes_accessed=moved, transcendentals=0)
+
         depth = 2 * rows_dev
 
         def by_core(own, other, axis):
@@ -582,13 +673,19 @@
             own = lax.dynamic_slice_in_dim(array, core * size, size, axis)
             return own, lax.dynamic_slice_in_dim(array, (1 - core) * size, size, axis)
 
-        own, other = halves(qkv_weight.transpose(1, 0, 2), 2)
-        qkv_blocks = ring.gather_whole(
-            by_core(own, ring.swap_core(other), 1).reshape(3 * depth, half_cols)
-        )
-        own, other = halves(out_weight, 0)
-        out_block = by_core(own.T, ring.swap_core(other).T, 0)
-        out_blocks = ring.gather_whole(after(out_block, qkv_blocks[-1]))
+        qkv_own, qkv_other = halves(qkv_weight.transpose(1, 0, 2), 2)
+        out_own, out_other = halves(out_weight, 0)
+        own = jnp.concatenate([qkv_own, out_own.T[None]], axis=0)
+        other = jnp.concatenate([qkv_other, out_other.T[None]], axis=0)
+        block = by_core(own, ring.swap_core(other), 1).reshape(4 * depth, half_cols)
+        found = ring.gather(block)
+        attn_w = [piece for offset in ring.offsets for piece in found[offset]]
+
+        half_length = length // 2
+        steps = chips // 2
+        up_zero = lax.dynamic_slice_in_dim(cotangent, half * half_length, half_length, 0)
+        up_cross = {0: [swap_tensor(up_zero)]}
+        up_ring = {0: [up_zero], 1: ring.step(after(up_zero, attn_w[-3]), None)}
 
         units = shared_out.shape[0]
         unit_chip = units // chips
@@ -599,27 +696,11 @@
             ],
             axis=0,
         ).transpose(1, 0, 2, 3)
-        sh_send = after(sh_send.reshape(chips, 3 * unit_chip, rows_dev), qkv_blocks[-1])
+        sh_send = after(sh_send.reshape(chips, 3 * unit_chip, rows_dev), attn_w[-3])
         same_core = [[2 * i + c for i in range(chips)] for c in range(2)]
         sh_mine = lax.all_to_all(
             sh_send, "expert", split_axis=0, concat_axis=0, tiled=True, axis_index_groups=same_core
         )
-        sh_w = by_core(sh_mine[:, None], ring.swap_core(sh_mine)[:, None], 1)
-        sh_w = sh_w.transpose(2, 0, 1, 3).reshape(3, unit_chip, width)
-
-        half_length = length // 2
-        up_half = lax.dynamic_slice_in_dim(cotangent, half * half_length, half_length, 0)
-        up_ring = ring.gather(after(up_half, out_blocks[-1]))
-        up_own, up_other = {}, {}
-        for offset in ring.offsets:
-            pieces, at = [], 0
-            for piece in up_ring[offset]:
-                pieces.append((piece, at, half_length + at))
-                pieces.append((swap_tensor(piece), half_length + at, at))
-                at += piece.shape[0]
-            up_own[offset] = pieces
-            up_other[offset] = [(ring.swap_core(p), a, b) for p, a, b in pieces]
-
         inputs = tokens_in.astype(f32)
         first_b = rms_norm(inputs, gains_f[0]).astype(bf16)
         first_o = ring.swap_core(first_b)
@@ -627,13 +708,10 @@
         pair_cols = jax.ShapeDtypeStruct((2 * length, half_cols), bf16)
         chip_arg = chip_of.astype(jnp.int32)
 
-        def cost(flops, moved):
-            return pl.CostEstimate(flops=flops, bytes_accessed=moved, transcendentals=0)
-
         query, key, value, mixed = pl.pallas_call(
-            functools.partial(attend_kernel, chips, heads, score_scale),
+            functools.partial(attend_kernel, chips + 1, heads, score_scale),
             out_shape=[pair_cols] * 4,
-            in_specs=[in_smem] * 2 + [in_vmem] * 5 + [in_any] * chips,
+            in_specs=[in_smem] * 2 + [in_vmem] * 5 + [in_any] * (chips + 1),
             out_specs=[in_vmem] * 4,
             scratch_shapes=[
                 pltpu.VMEM((3, width, half_cols), bf16),
@@ -642,14 +720,14 @@
             compiler_params=params(),
             cost_estimate=cost(2 * 2 * length * width * 3 * half_cols, 12 * 1024 * 1024),
             name="attend",
-        )(chip_arg, prefix_pair, first_b, first_o, bias.reshape(1, -1), cosine, sine, *qkv_blocks)
+        )(chip_arg, prefix_pair, first_b, first_o, bias.reshape(1, -1), cosine, sine, *attn_w)
         attn_own, attn_give = pl.pallas_call(
-            functools.partial(project_kernel, chips),
+            functools.partial(project_kernel, chips + 1),
             out_shape=[
                 jax.ShapeDtypeStruct((length, width), f32),
                 jax.ShapeDtypeStruct((length, width), bf16),
             ],
-            in_specs=[in_smem, in_vmem] + [in_any] * chips,
+            in_specs=[in_smem, in_vmem] + [in_any] * (chips + 1),
             out_specs=[in_vmem] * 2,
             scratch_shapes=[
                 pltpu.VMEM((1, width, half_cols), bf16),
@@ -658,16 +736,12 @@
             compiler_params=params(),
             cost_estimate=cost(2 * 2 * length * width * half_cols, 6 * 1024 * 1024),
             name="project",
-        )(chip_arg, mixed, *out_blocks)
-        attn_out = sum_tensor(attn_own + ring.swap_core(attn_give).astype(f32))
+        )(chip_arg, mixed, *attn_w)
+        attn_own = (attn_own + ring.swap_core(attn_give).astype(f32)).astype(bf16)
+        attn_got = swap_tensor(attn_own)
+        attn_out = attn_own.astype(f32) + attn_got.astype(f32)
         residual = inputs + attn_out
         second_b = rms_norm(residual, gains_f[1]).astype(bf16)
-
-        rows_own, rows_other = {}, {}
-        for offset, pieces in ring.gather(second_b).items():
-            starts = [sum(p.shape[0] for p in pieces[:j]) for j in range(len(pieces))]
-            rows_own[offset] = [(p, a, a) for p, a in zip(pieces, starts, strict=True)]
-            rows_other[offset] = [(ring.swap_core(p), a, a) for p, a, _ in rows_own[offset]]
 
         logits = mm(second_b, router_w)
         expert_range = jnp.arange(experts, dtype=jnp.int32)
@@ -699,23 +773,154 @@
         part_units = ex_out.shape[0]
         sizes = (length, width, capacity, part_units, unit_chip)
         half_arg = half.astype(jnp.int32).reshape(1)
+        core_arg = core.astype(jnp.int32).reshape(1)
+        swap_core = ring.swap_core
+
+        def each(function, items):
+            return [function(item) for item in items]
+
+        second_b, up_ring[1], sh_mine = hold(second_b, up_ring[1], sh_mine)
+        rows_ring = {0: [second_b]}
+        up_ring_o = {0: each(swap_core, up_ring[0])}
+        up_cross_o = {}
         kept = None
-        moe, back, dot_rows = {}, {}, []
-        for i, offset in enumerate(ring.offsets):
-            pieces = [rows_own[offset], rows_other[offset], up_own[offset], up_other[offset]]
+        moe, back, moe_o, back_o, dot_rows = {}, {}, {}, {}, []
+        sh_w = None
+        for k in range(1, steps + 2):
+            last = k == steps + 1
+            now = []
+            if not last:
+                rows_ring[k] = ring.step(*rows_ring[k - 1], last=k == steps)
+                now.append(rows_ring[k])
+                if k < steps:
+                    up_ring[k + 1] = ring.step(*up_ring[k], last=k + 1 == steps)
+                    now.append(up_ring[k + 1])
+                up_cross[k] = each(swap_tensor, up_ring[k])
+                up_ring_o[k] = each(swap_core, up_ring[k])
+                now += [up_cross[k], up_ring_o[k]]
+            g = k - 1
+            rows_o = each(swap_core, rows_ring[g])
+            up_cross_o[g] = each(swap_core, up_cross[g])
+            if sh_w is None:
+                sh_w = pl.pallas_call(
+                    spread_kernel,
+                    out_shape=jax.ShapeDtypeStruct((3, unit_chip, width), bf16),
+                    in_specs=[in_smem, in_vmem, in_vmem],
+                    out_specs=in_vmem,
+                    compiler_params=params(),
+                    cost_estimate=cost(0, 16 * 1024 * 1024),
+                    name="spread",
+                )(core_arg, sh_mine, swap_core(sh_mine))
+
+            def in_place(pieces, crossed):
+                found = []
+                for chip in [pieces] if g == steps else [[p] for p in pieces]:
+                    at = 0
+                    found.append([])
+                    for piece in chip:
+                        first = (at, at) if crossed is None else (at, half_length + at)
+                        if crossed:
+                            first = first[::-1]
+                        found[-1].append((piece, *first))
+                        at += piece.shape[0]
+                return found
+
+            def joined(straight, crossed):
+                both = zip(in_place(straight, False), in_place(crossed, True), strict=True)
+                return [a + b for a, b in both]
+
+            index = 0 if g == 0 else 2 * g - 1
+            offsets = ring.offsets[index : index + (1 if g in (0, steps) else 2)]
+            pieces = (
+                in_place(rows_ring[g], None)
+                + in_place(rows_o, None)
+                + joined(up_ring[g], up_cross[g])
+                + joined(up_ring_o[g], up_cross_o[g])
+            )
             kept, blocks, rows = moe_call(
-                i, sizes, chips, pieces, half_arg, row_aux, col_aux, (ex_in, ex_out, sh_w), kept
+                index,
+                len(offsets),
+                sizes,
+                chips,
+                pieces,
+                half_arg,
+                row_aux,
+                col_aux,
+                (ex_in, ex_out, sh_w),
+                kept,
             )
-            moe[offset], back[offset] = blocks[:2], blocks[2:]
             dot_rows.append(rows)
-
-        back_terms = {o: [a, ring.swap_core(b)] for o, (a, b) in back.items()}
-        second_part = ring.reduce(back_terms)
-        moe_terms = {o: [a, ring.swap_core(b)] for o, (a, b) in moe.items()}
-        moe_part = ring.reduce(moe_terms)
-        output = (residual + sum_tensor(moe_part)).astype(bf16)
-
-        dots = jnp.stack(dot_rows, axis=0)
+            if not last:
+                *_, dot_rows[-1] = held = hold(*now, rows)
+                rows_ring[k] = held[0]
+                if k < steps:
+                    up_ring[k + 1] = held[1]
+                up_cross[k], up_ring_o[k] = held[-3:-1]
+            for o, (moe_own, moe_give, back_own, back_give) in zip(offsets, blocks, strict=True):
+                moe[o], back[o] = moe_own, back_own
+                back_o[o] = swap_core(back_give)
+                moe_o[o] = swap_core(moe_give)
+
+        rows_all, slots_all, hidden_all, gu_all, tok_all, y_all, s_hidden_all, s_gu_all = kept
+        slot_count = chips * 2 * capacity
+
+        def crossing(o):
+            mine = moe[o].astype(f32) + moe_o[o].astype(f32)
+            return swap_tensor(mine[half_length:].astype(bf16))
+
+        def moe_terms(o):
+            return [moe[o][:half_length], moe_o[o][:half_length], moe_cross[o]]
+
+        far = ring.offsets[-1]
+        moe_cross = {}
+        sending = ring.reduce_first([back[far], back_o[far]])
+        moe_cross[far] = crossing(far)
+        sending, moe_cross[far] = hold(sending, moe_cross[far])
+        for k in range(steps - 1, 0, -1):
+            send = ring.reduce_terms(
+                [back[k], back_o[k]], [back[-k], back_o[-k]], sending, k == steps - 1
+            )
+            number = steps - 1 - k
+            if number == 0:
+                gu_all, *send = hold(gu_all, *send)
+                expert_in_grad = mm(gu_all, rows_all, 1, 0).transpose(2, 0, 1)[None]
+                token = expert_in_grad[:, :1, :1, :1]
+            elif number == 1:
+                s_hidden_all, *send = hold(s_hidden_all, *send)
+                sh_grad = pl.pallas_call(
+                    shared_grad_kernel,
+                    grid=(chips,),
+                    out_shape=jax.ShapeDtypeStruct((2, chips, 3 * unit_chip, rows_dev), bf16),
+                    in_specs=[
+                        pl.BlockSpec((chips * length, depth), lambda n: (0, n)),
+                        pl.BlockSpec((chips * length, depth), lambda n: (0, n)),
+                        pl.BlockSpec((chips * length, unit_chip), lambda n: (0, 0)),
+                        pl.BlockSpec((2, chips * length, unit_chip), lambda n: (0, 0, 0)),
+                    ],
+                    out_specs=pl.BlockSpec((2, 1, 3 * unit_chip, rows_dev), lambda n: (0, n, 0, 0)),
+                    compiler_params=params(),
+                    cost_estimate=cost(
+                        2 * chips * length * width * 3 * unit_chip, 26 * 1024 * 1024
+                    ),
+                    name="shared_grad",
+                )(tok_all, y_all, s_hidden_all, s_gu_all)
+                token = sh_grad[:, :1, :1, :1]
+            elif number == 2:
+                hidden_all, *send = hold(hidden_all, *send)
+                expert_out_grad = mm(hidden_all, slots_all, 0, 0)[None]
+                token = expert_out_grad[:, :1, :1]
+            sending = ring.send_pair(*send)
+            moe_cross[k], moe_cross[-k] = crossing(k), crossing(-k)
+            sending, moe_cross[k], moe_cross[-k], token = hold(
+                sending, moe_cross[k], moe_cross[-k], token
+            )
+        second_part = ring.add_up([back[0], back_o[0], *sending]).astype(bf16)
+        moe_cross[0] = crossing(0)
+        second_got = swap_tensor(second_part)
+        sending = ring.reduce_first(moe_terms(far))
+        second_got, moe_cross[0], sending = hold(second_got, moe_cross[0], sending)
+
+        dots = jnp.concatenate(dot_rows, axis=0)
         sdots = jnp.concatenate([dots[:, 2:3], jnp.zeros_like(dots[:, 2:3])], axis=1)
         dot_send = jnp.stack([dots[:, :2], sdots], axis=2).reshape(devices, 2, length)[seq_inv]
         dot_got = lax.all_to_all(dot_send, "expert", split_axis=0, concat_axis=0, tiled=True)
@@ -726,7 +931,7 @@
         logit_grad = (gate_dense * (gate_grad_dense - row_term)).astype(bf16)
         gate_logit_grad = sigma_grad * shared_sigma * (1.0 - shared_sigma)
 
-        second_grad = sum_tensor(second_part)
+        second_grad = second_part.astype(f32) + second_got.astype(f32)
         second_grad = second_grad + mm(logit_grad, router_w, 1, 1)
         second_grad = second_grad + gate_logit_grad[:, None] * gate_vec.astype(f32)[None]
         upstream = cotangent.astype(f32)
@@ -734,6 +939,19 @@
         residual_grad = upstream + residual_norm_grad
         attn_grad = residual_grad.astype(bf16)
         attn_grad_o = ring.swap_core(attn_grad)
+
+        for k in range(steps - 1, 0, -1):
+            send = ring.reduce_terms(moe_terms(k), moe_terms(-k), sending, k == steps - 1)
+            sending = ring.send_pair(*send)
+        moe_half = ring.add_up([*moe_terms(0), *sending])
+        res_half = lax.dynamic_slice_in_dim(residual, half * half_length, half_length, 0)
+        out_half = (res_half + moe_half).astype(bf16)
+        out_got = swap_tensor(out_half)
+        output = jnp.where(
+            half == 0,
+            jnp.concatenate([out_half, out_got], axis=0),
+            jnp.concatenate([out_got, out_half], axis=0),
+        )
 
         def by_chip(left, other, right):
             pair = jnp.concatenate([left, other], axis=0)
@@ -745,12 +963,12 @@
             }
 
         proj_grad, bias_grad = pl.pallas_call(
-            functools.partial(attend_back_kernel, chips, heads, score_scale),
+            functools.partial(attend_back_kernel, chips + 1, heads, score_scale),
             out_shape=[
                 jax.ShapeDtypeStruct((2 * length, 3 * half_cols), bf16),
                 jax.ShapeDtypeStruct((1, 3 * half_cols), f32),
             ],
-            in_specs=[in_smem] * 2 + [in_vmem] * 7 + [in_any] * chips,
+            in_specs=[in_smem] * 2 + [in_vmem] * 7 + [in_any] * (chips + 1),
             out_specs=[in_vmem] * 2,
             scratch_shapes=[
                 pltpu.VMEM((1, width, half_cols), bf16),
@@ -769,18 +987,18 @@
             value,
             cosine,
             sine,
-            *out_blocks,
+            *attn_w,
         )
         qkv_grad = ring.reduce(by_chip(first_b, first_o, proj_grad))
         out_grad = ring.reduce(by_chip(attn_grad, attn_grad_o, mixed))
         bias_grad = bias_grad[0]
         first_own, first_give = pl.pallas_call(
-            functools.partial(project_back_kernel, chips),
+            functools.partial(project_back_kernel, chips + 1),
             out_shape=[
                 jax.ShapeDtypeStruct((length, width), f32),
                 jax.ShapeDtypeStruct((length, width), bf16),
             ],
-            in_specs=[in_smem, in_vmem] + [in_any] * chips,
+            in_specs=[in_smem, in_vmem] + [in_any] * (chips + 1),
             out_specs=[in_vmem] * 2,
             scratch_shapes=[
                 pltpu.VMEM((3, width, half_cols), bf16),
@@ -789,7 +1007,7 @@
             compiler_params=params(),
             cost_estimate=cost(2 * 2 * length * width * 3 * half_cols, 12 * 1024 * 1024),
             name="project_back",
-        )(chip_arg, proj_grad, *qkv_blocks)
+        )(chip_arg, proj_grad, *attn_w)
         first_grad = sum_tensor(first_own + ring.swap_core(first_give).astype(f32))
         input_norm_grad, gain_one_grad = jax.vjp(rms_norm, inputs, gains_f[0])[1](first_grad)
         input_grad = (residual_grad + input_norm_grad).astype(bf16)
@@ -803,25 +1021,6 @@
         qkv_weight_grad = regroup(qkv_grad, 3)
         out_weight_grad = regroup(out_grad, 1)[:, 0].T
 
-        rows_all, slots_all, hidden_all, gu_all, tok_all, y_all, s_hidden_all, s_gu_all = kept
-        slot_count = chips * 2 * capacity
-        rows_all = rows_all.reshape(slot_count, width)
-        expert_out_grad = mm(
-            hidden_all.reshape(slot_count, part_units), slots_all.reshape(slot_count, width), 0, 0
-        )[None]
-        expert_in_grad = mm(gu_all.reshape(2, slot_count, part_units), rows_all, 1, 0)
-        expert_in_grad = expert_in_grad.transpose(2, 0, 1)[None]
-        token_count = chips * length
-        sh_in_grad = mm(
-            s_gu_all.reshape(2, token_count, unit_chip), tok_all.reshape(token_count, width), 1, 0
-        )
-        sh_out_grad = mm(
-            s_hidden_all.reshape(token_count, unit_chip), y_all.reshape(token_count, width), 0, 0
-        )
-        sh_grad = jnp.concatenate(
-            [sh_in_grad.astype(bf16), sh_out_grad.astype(bf16)[None]], axis=0
-        ).reshape(3 * unit_chip, chips, 2, rows_dev)
-        sh_grad = sh_grad.transpose(2, 1, 0, 3)
         own, other = halves(sh_grad, 0)
         sh_sum = (own.astype(f32) + ring.swap_core(other).astype(f32)).astype(bf16)[0]
         sh_back = lax.all_to_all(

time: 918 us -> 807 us (0.88)
  local copies, waits for them, and re-layouts: 122 us -> 68 us
  Pallas kernels: 203 us -> 179 us
  other arithmetic: 65.8 us -> 86.8 us
  starting transfers between devices: 177 us -> 157 us
  waiting for transfers between devices: 276 us -> 259 us
  matrix products: 54 us -> 41.5 us
    ppermute x64 -> x56, waiting for transfers between devices: 235 us -> 81.4 us  [the longest x28 69.3 us: send_pair(): lax.ppermute(ahead, 'expert', self.next)]
    ppermute x14 -> x22, waiting for transfers between devices: 4.18 us -> 113 us  [swap_tensor(): return lax.ppermute(block, 'tensor', [(0, 1), (1, 0)])]
    ppermute x64 -> x56, starting transfers between devices: 119 us -> 86.7 us  [the longest x28 47.4 us: send_pair(): lax.ppermute(ahead, 'expert', self.next)]
    ppermute x4, waiting for transfers between devices: 19.6 us -> 47.6 us  [gather_small(): other = lax.ppermute(held, 'expert', pairs)]
    pallas_call x12 -> x11, Pallas kernels: 203 us -> 179 us  [the longest x5 121 us: moe_call(): pl.pallas_call(functools.partial(moe_kernel, index, span, first, plan, si...]
    reshape x2 -> x0, local copies, waits for them, and re-layouts: 21.1 us -> none  [the longest x1 10.8 us: local(): sh_grad = jnp.concatenate([sh_in_grad.astype(bf16), sh_out_grad.astype(bf...]
    transpose x1 -> x0, local copies, waits for them, and re-layouts: 15.3 us -> none  [local(): sh_w = sh_w.transpose(2, 0, 1, 3).reshape(3, unit_chip, width)]
    convert_element_type x10 -> x13, other arithmetic: 15.1 us -> 28.2 us  [the longest x8 20.6 us: reduce_terms(): return [mine.astype(bf16), yours.astype(bf16)]]
  transfers between devices with their start and end apart: 141 -> 140, of which waited for: 35 -> 40; matrix products, arithmetic and copies ran while one was open for 24% -> 22% of each run, Pallas kernels for 22% -> 22%
where the time goes in v3:
time: 807 us; the launch traced here: 801 us
  waiting for transfers between devices  259 us (32%)
  Pallas kernels  179 us (22%)
  starting transfers between devices  157 us (19%)
  other arithmetic  86.8 us (11%)
  local copies, waits for them, and re-layouts  68 us (8%)
  matrix products  41.5 us (5%)
  between operations  9.05 us (1%)
    pallas_call x5, Pallas kernels, moe_call(): pl.pallas_call(functools.partial(moe_kernel, index, span, first, plan, si...  121 us
    ppermute x22, waiting for transfers between devices, swap_tensor(): return lax.ppermute(block, 'tensor', [(0, 1), (1, 0)])  113 us
    ppermute x28, waiting for transfers between devices, send_pair(): lax.ppermute(ahead, 'expert', self.next)  69.3 us
    ppermute x4, waiting for transfers between devices, gather_small(): other = lax.ppermute(held, 'expert', pairs)  47.6 us
    ppermute x28, starting transfers between devices, send_pair(): lax.ppermute(ahead, 'expert', self.next)  47.4 us
    dot_general x22, matrix products, mm(): lax.dot_general(left, right, (((contract_left,), (contract_right,)), ((),...  41.5 us
    ppermute x28, starting transfers between devices, send_pair(): lax.ppermute(back, 'expert', self.prev)  39.3 us
    unnamed x307, local copies, waits for them, and re-layouts  28 us
  transfers between devices with their start and end apart: 140, of which 40 were waited for; matrix products, arithmetic and copies ran while one was open for 22% of the time, Pallas kernels for 22%

profile of v3, /device:TPU:0, one launch (start us, length us, event | category | flops | bytes accessed | tf_op | source)
XLA Modules:
  0.0 801.2 jit_solution(30720760793518010)
XLA Ops:
  10.7 21.6 %collective-permute-done.1 = bf16[2,4096]{1,0:T(2,128)(2,1)S(1)} collective-permute-done((bf16[2,4096]{1,0:T(2,128)(2,1)S(1)}, bf16[2,4096]{1,0:T(2,128)(2,1)S(1)}, u32[]{:S(2)}, u32[]{:S(2)}) %collective-permute-start.1) | collective-permute-done | bytes 16416 | tf_op jit(solution)/shard_map/ppermute | solution.py:567
  40.7 24.5 %collective-permute-done.3 = bf16[8,4096]{1,0:T(8,128)(2,1)S(1)} collective-permute-done((bf16[8,4096]{1,0:T(8,128)(2,1)S(1)}, bf16[8,4096]{1,0:T(8,128)(2,1)S(1)}, u32[]{:S(2)}, u32[]{:S(2)}) %collective-permute-start.3) | collective-permute-done | bytes 65568 | tf_op jit(solution)/shard_map/ppermute | solution.py:567
  76.8 10.4 %collective-permute-done.10.refs_12_.refs_7_.refs_14_ = bf16[1024,512]{1,0:T(8,128)(2,1)} collective-permute-done((bf16[1024,512]{1,0:T(8,128)(2,1)}, bf16[1024,512]{1,0:T(8,128)(2,1)}, u32[]{:S(2)}, u32[]{:S(2)}) %collective-permute-start.10) | collective-permute-done | bytes 1048608 | tf_op jit(solution)/shard_map/ppermute | solution.py:516
  104.3 9.9 %attend.1 = (bf16[512,512]{1,0:T(8,128)(2,1)}, bf16[512,512]{1,0:T(8,128)(2,1)}, bf16[512,512]{1,0:T(8,128)(2,1)}, bf16[512,512]{1,0:T(8,128)(2,1)}) custom-call(s32[8]{0:T(128)} %get-tuple-element.440.refs_0_, s32[2]{0:T(128)} %pad_add_fusion.refs_1_, bf16[256,2048]{1,0:T(8,128)(2,1)} %copy-done.7, bf16[256,2048]{1,0:T(8,128)(2,1)} %copy-done.10, ...), custom_call_target="tpu_custom_call" | custom-call | flops 3221225472 | bytes 12582912 | tf_op jit(solution)/shard_map/attend/pallas_call | solution.py:711
  131.4 19.5 %collective-permute-done.15 = bf16[256,2048]{1,0:T(8,128)(2,1)} collective-permute-done((bf16[256,2048]{1,0:T(8,128)(2,1)S(1)}, bf16[256,2048]{1,0:T(8,128)(2,1)}, u32[]{:S(2)}, u32[]{:S(2)}) %collective-permute-start.15) | collective-permute-done | bytes 1048608 | tf_op jit(solution)/shard_map/ppermute | solution.py:585
  166.7 8.7 %all-to-all-start = ((f32[16,2,256]{2,1,0:T(2,128)}), f32[16,2,256]{2,1,0:T(2,128)S(1)}, u32[]{:S(2)}, u32[]{:S(2)}) async-start(f32[16,2,256]{2,1,0:T(2,128)} %pad_maximum_fusion.10), calls=%async_computation | async-start | bytes 65536 | tf_op jit(solution)/shard_map/all_to_all | solution.py:758
  178.6 6.8 all-to-all-done
  198.7 18.4 %experts_0.1 = (bf16[1536,2048]{1,0:T(8,128)(2,1)}, bf16[1536,2048]{1,0:T(8,128)(2,1)}, bf16[1536,704]{1,0:T(8,128)(2,1)}, bf16[2,1536,704]{2,1,0:T(8,128)(2,1)}...) custom-call(s32[1]{0:T(128)} %bitcast.17.refs_0_, ...), custom_call_target="tpu_custom_call" | custom-call | flops 5536481280 | bytes 29360128 | tf_op jit(solution)/shard_map/experts_0/pallas_call | solution.py:404
  221.4 11.9 %collective-permute-done.35.refs_7_ = bf16[128,2048]{1,0:T(8,128)(2,1)S(1)} collective-permute-done((bf16[128,2048]{1,0:T(8,128)(2,1)}, bf16[128,2048]{1,0:T(8,128)(2,1)S(1)}, u32[]{:S(2)}, u32[]{:S(2)}) %collective-permute-start.35) | collective-permute-done | bytes 524320 | tf_op jit(solution)/shard_map/ppermute | solution.py:516
  234.0 9.8 %collective-permute-start.34 = (bf16[256,2048]{1,0:T(8,128)(2,1)S(1)}, bf16[256,2048]{1,0:T(8,128)(2,1)}, u32[]{:S(2)}, u32[]{:S(2)}) collective-permute-start(bf16[256,2048]{1,0:T(8,128)(2,1)S(1)} %collective-permute-done.26.refs_4_), channel_id=1, source_target_pairs={{8,0},{10,2},{16,8},{18,10},{24,16},{26,18},{28,24},{30,26},{20,28... | collective-permute-start | bytes 3145736 | tf_op jit(solution)/shard_map/ppermute | solution.py:517
  245.7 28.1 %experts_1.1 = (bf16[1536,2048]{1,0:T(8,128)(2,1)}, bf16[1536,2048]{1,0:T(8,128)(2,1)}, bf16[1536,704]{1,0:T(8,128)(2,1)}, bf16[2,1536,704]{2,1,0:T(8,128)(2,1)}...) custom-call(s32[1]{0:T(128)} %bitcast.17.refs_0_, ...), custom_call_target="tpu_custom_call", output_to_operand_aliasing={{0}: (18, {}), {1}: (19, {}), {2}: (20, {}), {3}: (21, {}),... | custom-call | flops 11072962560 | bytes 41943040 | tf_op jit(solution)/shard_map/experts_1/pallas_call | solution.py:404
  275.7 6.7 collective-permute-done.47.refs_7_
  283.0 7.0 collective-permute-done.48.refs_8_
  305.0 8.7 %collective-permute-done.50.refs_10_ = bf16[128,2048]{1,0:T(8,128)(2,1)} collective-permute-done((bf16[128,2048]{1,0:T(8,128)(2,1)S(1)}, bf16[128,2048]{1,0:T(8,128)(2,1)}, u32[]{:S(2)}, u32[]{:S(2)}) %collective-permute-start.50) | collective-permute-done | bytes 524320 | tf_op jit(solution)/shard_map/ppermute | solution.py:585
  316.3 28.0 %experts_3.1 = (bf16[1536,2048]{1,0:T(8,128)(2,1)}, bf16[1536,2048]{1,0:T(8,128)(2,1)}, bf16[1536,704]{1,0:T(8,128)(2,1)}, bf16[2,1536,704]{2,1,0:T(8,128)(2,1)}...) custom-call(s32[1]{0:T(128)} %bitcast.17.refs_0_, ...), custom_call_target="tpu_custom_call", output_to_operand_aliasing={{0}: (18, {}), {1}: (19, {}), {2}: (20, {}), {3}: (21, {}),... | custom-call | flops 11072962560 | bytes 41943040 | tf_op jit(solution)/shard_map/experts_3/pallas_call | solution.py:404
  366.2 28.2 %experts_5.1 = (bf16[1536,2048]{1,0:T(8,128)(2,1)}, bf16[1536,2048]{1,0:T(8,128)(2,1)}, bf16[1536,704]{1,0:T(8,128)(2,1)}, bf16[2,1536,704]{2,1,0:T(8,128)(2,1)}...) custom-call(s32[1]{0:T(128)} %bitcast.17.refs_0_, ...), custom_call_target="tpu_custom_call", output_to_operand_aliasing={{0}: (18, {}), {1}: (19, {}), {2}: (20, {}), {3}: (21, {}),... | custom-call | flops 11072962560 | bytes 41943040 | tf_op jit(solution)/shard_map/experts_5/pallas_call | solution.py:404
  400.4 18.7 %experts_7.1 = (bf16[1536,2048]{1,0:T(8,128)(2,1)}, bf16[1536,2048]{1,0:T(8,128)(2,1)}, bf16[1536,704]{1,0:T(8,128)(2,1)}, bf16[2,1536,704]{2,1,0:T(8,128)(2,1)}...) custom-call(s32[1]{0:T(128)} %bitcast.17.refs_0_, ...), custom_call_target="tpu_custom_call", output_to_operand_aliasing={{0}: (18, {}), {1}: (19, {}), {2}: (20, {}), {3}: (21, {}),... | custom-call | flops 5536481280 | bytes 29360128 | tf_op jit(solution)/shard_map/experts_7/pallas_call | solution.py:404
  447.8 6.4 collective-permute-done.78
  459.3 9.5 %collective-permute-done.85 = bf16[128,2048]{1,0:T(8,128)(2,1)S(1)} collective-permute-done((bf16[128,2048]{1,0:T(8,128)(2,1)S(1)}, bf16[128,2048]{1,0:T(8,128)(2,1)S(1)}, u32[]{:S(2)}, u32[]{:S(2)}) %collective-permute-start.85) | collective-permute-done | bytes 524320 | tf_op jit(solution)/shard_map/ppermute | solution.py:585
  470.4 10.7 %collective-permute-done.83 = bf16[128,2048]{1,0:T(8,128)(2,1)S(1)} collective-permute-done((bf16[128,2048]{1,0:T(8,128)(2,1)S(1)}, bf16[128,2048]{1,0:T(8,128)(2,1)S(1)}, u32[]{:S(2)}, u32[]{:S(2)}) %collective-permute-start.83) | collective-permute-done | bytes 524320 | tf_op jit(solution)/shard_map/ppermute | solution.py:585
  490.3 12.5 %fusion.2 = f32[1,2048,2,704]{1,3,2,0:T(8,128)} fusion(bf16[2,1536,704]{2,1,0:T(8,128)(2,1)S(1)} %bitcast.169, bf16[1536,2048]{1,0:T(8,128)(2,1)S(1)} %bitcast.160), kind=kOutput, calls=%fused_computation.5 | convolution fusion | flops 8858370048 | bytes 22151168 | tf_op jit(solution)/shard_map/dot_general | solution.py:51
  505.5 10.2 %collective-permute-done.90 = bf16[128,2048]{1,0:T(8,128)(2,1)S(1)} collective-permute-done((bf16[128,2048]{1,0:T(8,128)(2,1)S(1)}, bf16[128,2048]{1,0:T(8,128)(2,1)S(1)}, u32[]{:S(2)}, u32[]{:S(2)}) %collective-permute-start.90) | collective-permute-done | bytes 524320 | tf_op jit(solution)/shard_map/ppermute | solution.py:585
  525.5 17.1 %shared_grad.1 = bf16[2,8,1056,128]{3,2,1,0:T(8,128)(2,1)} custom-call(bf16[2048,2048]{1,0:T(8,128)(2,1)} %get-tuple-element.314.tok, bf16[2048,2048]{1,0:T(8,128)(2,1)} %get-tuple-element.315.y_grad, bf16[2048,352]{1,0:T(8,128)(2,1)} %get-tuple-element.316.hidden, bf16[2,2048,352]{2,1,0:T(8,128)(2,1)} %get-tuple-element.317.gu), custom_call_target="tpu_custom_call" | custom-call | flops 8858370048 | bytes 27262976 | tf_op jit(solution)/shard_map/shared_grad/pallas_call | solution.py:890
  554.6 6.5 convolution_bitcast_fusion
  564.6 19.7 %collective-permute-done.100 = bf16[256,2048]{1,0:T(8,128)(2,1)S(1)} collective-permute-done((bf16[256,2048]{1,0:T(8,128)(2,1)S(1)}, bf16[256,2048]{1,0:T(8,128)(2,1)S(1)}, u32[]{:S(2)}, u32[]{:S(2)}) %collective-permute-start.100) | collective-permute-done | bytes 1048608 | tf_op jit(solution)/shard_map/ppermute | solution.py:585
  633.2 10.9 %attend_back.1 = (bf16[512,1536]{1,0:T(8,128)(2,1)}, f32[1,1536]{1,0:T(1,128)}) custom-call(s32[8]{0:T(128)} %get-tuple-element.440.refs_0_, s32[2]{0:T(128)} %pad_add_fusion.refs_1_, bf16[256,2048]{1,0:T(8,128)(2,1)} %copy-done, bf16[256,2048]{1,0:T(8,128)(2,1)} %copy-done.4, bf16[512,512]{1,0:T(8,128)(2,1)} %get-tuple-element.307.refs_4_, ...), custom_call_target="tpu_custom_call" | custom-call | flops 2147483648 | bytes 8388608 | tf_op jit(solution)/shard_map/attend_back/pallas_call | solution.py:965
  651.8 9.5 %project_back.1 = (f32[256,2048]{1,0:T(8,128)}, bf16[256,2048]{1,0:T(8,128)(2,1)}) custom-call(s32[8]{0:T(128)} %get-tuple-element.440.refs_0_, bf16[512,1536]{1,0:T(8,128)(2,1)} %get-tuple-element.310.refs_1_, bf16[1024,512]{1,0:T(8,128)(2,1)} %bitcast.181, bf16[1024,512]{1,0:T(8,128)(2,1)} %copy-done.34, ...), custom_call_target="tpu_custom_call" | custom-call | flops 3221225472 | bytes 12582912 | tf_op jit(solution)/shard_map/project_back/pallas_call | solution.py:995
  668.5 10.3 %collective-permute-start.125 = (bf16[256,512]{1,0:T(8,128)(2,1)}, bf16[256,512]{1,0:T(8,128)(2,1)}, u32[]{:S(2)}, u32[]{:S(2)}) collective-permute-start(bf16[256,512]{1,0:T(8,128)(2,1)} %pad_maximum_fusion.7), channel_id=1, source_target_pairs={{0,8},{2,10},{8,16},{10,18},{16,24},{18,26},{24,28},{26,30},{28,20... | collective-permute-start | bytes 786440 | tf_op jit(solution)/shard_map/ppermute | solution.py:516
  697.3 9.4 %collective-permute-done.126 = bf16[256,512]{1,0:T(8,128)(2,1)S(1)} collective-permute-done((bf16[256,512]{1,0:T(8,128)(2,1)S(1)}, bf16[256,512]{1,0:T(8,128)(2,1)S(1)}, u32[]{:S(2)}, u32[]{:S(2)}) %collective-permute-start.126) | collective-permute-done | bytes 262176 | tf_op jit(solution)/shard_map/ppermute | solution.py:516
  720.8 12.1 %collective-permute-done.116 = bf16[256,1536]{1,0:T(8,128)(2,1)S(1)} collective-permute-done((bf16[256,1536]{1,0:T(8,128)(2,1)S(1)}, bf16[256,1536]{1,0:T(8,128)(2,1)S(1)}, u32[]{:S(2)}, u32[]{:S(2)}) %collective-permute-start.116) | collective-permute-done | bytes 786464 | tf_op jit(solution)/shard_map/ppermute | solution.py:516
  744.5 7.7 collective-permute-done.117
  759.6 7.4 collective-permute-done.110
  (770 shorter events, 365.5 us)
Async XLA Ops:
  97.8 56.5 %all-to-all-start.1 = ((bf16[8,1056,128]{2,1,0:T(8,128)(2,1)}), bf16[8,1056,128]{2,1,0:T(8,128)(2,1)}, u32[]{:S(2)}, u32[]{:S(2)}) async-start(bf16[8,1056,128]{2,1,0:T(8,128)(2,1)} %bitcast.182), calls=%async_computation.1 | async-start | bytes 4325376 | tf_op jit(solution)/shard_map/all_to_all | solution.py:701
  127.1 34.2 %collective-permute-start.19 = (bf16[128,2048]{1,0:T(8,128)(2,1)}, bf16[128,2048]{1,0:T(8,128)(2,1)}, u32[]{:S(2)}, u32[]{:S(2)}) collective-permute-start(bf16[128,2048]{1,0:T(8,128)(2,1)} %constant_dynamic-slice_fusion.2.refs_5_), channel_id=1, source_target_pairs={{0,1},{1,0},{2,3},{3,2},{4,5},{5,4},{6,7},{7,6},{8,9},{9,8},{10,11... | collective-permute-start | bytes 1572872 | tf_op jit(solution)/shard_map/ppermute | solution.py:585
  127.6 37.7 %collective-permute-start.20 = (bf16[128,2048]{1,0:T(8,128)(2,1)}, bf16[128,2048]{1,0:T(8,128)(2,1)}, u32[]{:S(2)}, u32[]{:S(2)}) collective-permute-start(bf16[128,2048]{1,0:T(8,128)(2,1)} %constant_dynamic-slice_fusion.2.refs_5_), channel_id=1, source_target_pairs={{0,2},{2,0},{4,6},{6,4},{8,10},{10,8},{12,14},{14,12},{16,18},{18,... | collective-permute-start | bytes 1572872 | tf_op jit(solution)/shard_map/ppermute | solution.py:560
  154.3 38.3 %collective-permute-start.22 = (bf16[8,1056,128]{2,1,0:T(8,128)(2,1)}, bf16[8,1056,128]{2,1,0:T(8,128)(2,1)}, u32[]{:S(2)}, u32[]{:S(2)}) collective-permute-start(bf16[8,1056,128]{2,1,0:T(8,128)(2,1)} %all-to-all-done.1.own), channel_id=1, source_target_pairs={{0,2},{2,0},{4,6},{6,4},{8,10},{10,8},{12,14},{14,12},{16,18},{18,... | collective-permute-start | bytes 6488072 | tf_op jit(solution)/shard_map/ppermute | solution.py:560
  233.3 40.5 %collective-permute-start.33 = (bf16[256,2048]{1,0:T(8,128)(2,1)S(1)}, bf16[256,2048]{1,0:T(8,128)(2,1)}, u32[]{:S(2)}, u32[]{:S(2)}) collective-permute-start(bf16[256,2048]{1,0:T(8,128)(2,1)S(1)} %collective-permute-done.25.refs_3_), channel_id=1, source_target_pairs={{0,8},{2,10},{8,16},{10,18},{16,24},{18,26},{24,28},{26,30},{28,20... | collective-permute-start | bytes 3145736 | tf_op jit(solution)/shard_map/ppermute | solution.py:516
  234.0 39.8 %collective-permute-start.34 = (bf16[256,2048]{1,0:T(8,128)(2,1)S(1)}, bf16[256,2048]{1,0:T(8,128)(2,1)}, u32[]{:S(2)}, u32[]{:S(2)}) collective-permute-start(bf16[256,2048]{1,0:T(8,128)(2,1)S(1)} %collective-permute-done.26.refs_4_), channel_id=1, source_target_pairs={{8,0},{10,2},{16,8},{18,10},{24,16},{26,18},{28,24},{30,26},{20,28... | collective-permute-start | bytes 3145736 | tf_op jit(solution)/shard_map/ppermute | solution.py:517
  275.1 40.5 %collective-permute-start.53 = (bf16[256,2048]{1,0:T(8,128)(2,1)}, bf16[256,2048]{1,0:T(8,128)(2,1)}, u32[]{:S(2)}, u32[]{:S(2)}) collective-permute-start(bf16[256,2048]{1,0:T(8,128)(2,1)} %collective-permute-done.33.refs_3_), channel_id=1, source_target_pairs={{0,2},{2,0},{4,6},{6,4},{8,10},{10,8},{12,14},{14,12},{16,18},{18,... | collective-permute-start | bytes 3145736 | tf_op jit(solution)/shard_map/ppermute | solution.py:560
  275.1 40.6 %collective-permute-start.54 = (bf16[256,2048]{1,0:T(8,128)(2,1)}, bf16[256,2048]{1,0:T(8,128)(2,1)}, u32[]{:S(2)}, u32[]{:S(2)}) collective-permute-start(bf16[256,2048]{1,0:T(8,128)(2,1)} %collective-permute-done.34.refs_4_), channel_id=1, source_target_pairs={{0,2},{2,0},{4,6},{6,4},{8,10},{10,8},{12,14},{14,12},{16,18},{18,... | collective-permute-start | bytes 3145736 | tf_op jit(solution)/shard_map/ppermute | solution.py:560
  305.0 42.2 %collective-permute-start.23 = (bf16[256,2048]{1,0:T(8,128)(2,1)}, bf16[256,2048]{1,0:T(8,128)(2,1)}, u32[]{:S(2)}, u32[]{:S(2)}) collective-permute-start(bf16[256,2048]{1,0:T(8,128)(2,1)} %get-tuple-element.175), channel_id=1, source_target_pairs={{0,2},{2,0},{4,6},{6,4},{8,10},{10,8},{12,14},{14,12},{16,18},{18,... | collective-permute-start | bytes 3145736 | tf_op jit(solution)/shard_map/ppermute | solution.py:560
  315.8 33.8 %collective-permute-start.96 = (bf16[256,2048]{1,0:T(8,128)(2,1)}, bf16[256,2048]{1,0:T(8,128)(2,1)}, u32[]{:S(2)}, u32[]{:S(2)}) collective-permute-start(bf16[256,2048]{1,0:T(8,128)(2,1)} %get-tuple-element.286), channel_id=1, source_target_pairs={{0,2},{2,0},{4,6},{6,4},{8,10},{10,8},{12,14},{14,12},{16,18},{18,... | collective-permute-start | bytes 3145736 | tf_op jit(solution)/shard_map/ppermute | solution.py:560
  359.5 36.1 %collective-permute-start.98 = (bf16[256,2048]{1,0:T(8,128)(2,1)}, bf16[256,2048]{1,0:T(8,128)(2,1)S(1)}, u32[]{:S(2)}, u32[]{:S(2)}) collective-permute-start(bf16[256,2048]{1,0:T(8,128)(2,1)} %get-tuple-element.288), channel_id=1, source_target_pairs={{0,2},{2,0},{4,6},{6,4},{8,10},{10,8},{12,14},{14,12},{16,18},{18,... | collective-permute-start | bytes 3145736 | tf_op jit(solution)/shard_map/ppermute | solution.py:560
  398.3 34.5 %collective-permute-start.89 = (bf16[256,2048]{1,0:T(8,128)(2,1)}, bf16[256,2048]{1,0:T(8,128)(2,1)}, u32[]{:S(2)}, u32[]{:S(2)}) collective-permute-start(bf16[256,2048]{1,0:T(8,128)(2,1)} %get-tuple-element.276), channel_id=1, source_target_pairs={{0,2},{2,0},{4,6},{6,4},{8,10},{10,8},{12,14},{14,12},{16,18},{18,... | collective-permute-start | bytes 3145736 | tf_op jit(solution)/shard_map/ppermute | solution.py:560
  399.1 84.6 %collective-permute-start.86 = (bf16[256,2048]{1,0:T(8,128)(2,1)}, bf16[256,2048]{1,0:T(8,128)(2,1)}, u32[]{:S(2)}, u32[]{:S(2)}) collective-permute-start(bf16[256,2048]{1,0:T(8,128)(2,1)} %get-tuple-element.271), channel_id=1, source_target_pairs={{0,2},{2,0},{4,6},{6,4},{8,10},{10,8},{12,14},{14,12},{16,18},{18,... | collective-permute-start | bytes 3145736 | tf_op jit(solution)/shard_map/ppermute | solution.py:560
  399.2 45.8 %collective-permute-start.84 = (bf16[256,2048]{1,0:T(8,128)(2,1)}, bf16[256,2048]{1,0:T(8,128)(2,1)}, u32[]{:S(2)}, u32[]{:S(2)}) collective-permute-start(bf16[256,2048]{1,0:T(8,128)(2,1)} %get-tuple-element.268), channel_id=1, source_target_pairs={{0,2},{2,0},{4,6},{6,4},{8,10},{10,8},{12,14},{14,12},{16,18},{18,... | collective-permute-start | bytes 3145736 | tf_op jit(solution)/shard_map/ppermute | solution.py:560
  399.6 37.2 %collective-permute-start.79 = (bf16[256,2048]{1,0:T(8,128)(2,1)}, bf16[256,2048]{1,0:T(8,128)(2,1)}, u32[]{:S(2)}, u32[]{:S(2)}) collective-permute-start(bf16[256,2048]{1,0:T(8,128)(2,1)} %get-tuple-element.261), channel_id=1, source_target_pairs={{0,2},{2,0},{4,6},{6,4},{8,10},{10,8},{12,14},{14,12},{16,18},{18,... | collective-permute-start | bytes 3145736 | tf_op jit(solution)/shard_map/ppermute | solution.py:560
  446.3 40.3 %collective-permute-start.72 = (bf16[256,2048]{1,0:T(8,128)(2,1)S(1)}, bf16[256,2048]{1,0:T(8,128)(2,1)S(1)}, u32[]{:S(2)}, u32[]{:S(2)}) collective-permute-start(bf16[256,2048]{1,0:T(8,128)(2,1)S(1)} %copy-done.136), channel_id=1, source_target_pairs={{0,2},{2,0},{4,6},{6,4},{8,10},{10,8},{12,14},{14,12},{16,18},{18,... | collective-permute-start | bytes 3145736 | tf_op jit(solution)/shard_map/ppermute | solution.py:560
  481.1 36.7 %collective-permute-start.93 = (bf16[256,2048]{1,0:T(8,128)(2,1)}, bf16[256,2048]{1,0:T(8,128)(2,1)}, u32[]{:S(2)}, u32[]{:S(2)}) collective-permute-start(bf16[256,2048]{1,0:T(8,128)(2,1)} %get-tuple-element.281), channel_id=1, source_target_pairs={{0,2},{2,0},{4,6},{6,4},{8,10},{10,8},{12,14},{14,12},{16,18},{18,... | collective-permute-start | bytes 3145736 | tf_op jit(solution)/shard_map/ppermute | solution.py:560
  481.7 39.0 %collective-permute-start.71 = (bf16[256,2048]{1,0:T(8,128)(2,1)}, bf16[256,2048]{1,0:T(8,128)(2,1)}, u32[]{:S(2)}, u32[]{:S(2)}) collective-permute-start(bf16[256,2048]{1,0:T(8,128)(2,1)} %get-tuple-element.248), channel_id=1, source_target_pairs={{0,2},{2,0},{4,6},{6,4},{8,10},{10,8},{12,14},{14,12},{16,18},{18,... | collective-permute-start | bytes 3145736 | tf_op jit(solution)/shard_map/ppermute | solution.py:560
  515.7 35.4 %collective-permute-start.24 = (bf16[256,2048]{1,0:T(8,128)(2,1)}, bf16[256,2048]{1,0:T(8,128)(2,1)S(1)}, u32[]{:S(2)}, u32[]{:S(2)}) collective-permute-start(bf16[256,2048]{1,0:T(8,128)(2,1)} %get-tuple-element.177), channel_id=1, source_target_pairs={{0,2},{2,0},{4,6},{6,4},{8,10},{10,8},{12,14},{14,12},{16,18},{18,... | collective-permute-start | bytes 3145736 | tf_op jit(solution)/shard_map/ppermute | solution.py:560
  587.8 37.0 %collective-permute-start.112 = (bf16[256,2048]{1,0:T(8,128)(2,1)S(1)}, bf16[256,2048]{1,0:T(8,128)(2,1)S(1)}, u32[]{:S(2)}, u32[]{:S(2)}) collective-permute-start(bf16[256,2048]{1,0:T(8,128)(2,1)S(1)} %fusion.115.refs_2_), channel_id=1, source_target_pairs={{0,2},{2,0},{4,6},{6,4},{8,10},{10,8},{12,14},{14,12},{16,18},{18,... | collective-permute-start | bytes 3145736 | tf_op jit(solution)/shard_map/ppermute | solution.py:560
  603.5 166.1 %all-to-all-start.5 = ((bf16[8,1056,128]{2,1,0:T(8,128)(2,1)}), bf16[8,1056,128]{2,1,0:T(8,128)(2,1)}, u32[]{:S(2)}, u32[]{:S(2)}) async-start(bf16[8,1056,128]{2,1,0:T(8,128)(2,1)} %fusion.12), calls=%async_computation.5 | async-start | bytes 4325376 | tf_op jit(solution)/shard_map/all_to_all | solution.py:1026
  616.4 45.6 %collective-permute-start.105 = (bf16[128,2048]{1,0:T(8,128)(2,1)}, bf16[128,2048]{1,0:T(8,128)(2,1)S(1)}, u32[]{:S(2)}, u32[]{:S(2)}) collective-permute-start(bf16[128,2048]{1,0:T(8,128)(2,1)} %add_convert_fusion.13), channel_id=1, source_target_pairs={{0,8},{2,10},{8,16},{10,18},{16,24},{18,26},{24,28},{26,30},{28,20... | collective-permute-start | bytes 1572872 | tf_op jit(solution)/shard_map/ppermute | solution.py:516
  624.8 55.7 %collective-permute-start.108 = (bf16[128,2048]{1,0:T(8,128)(2,1)}, bf16[128,2048]{1,0:T(8,128)(2,1)}, u32[]{:S(2)}, u32[]{:S(2)}) collective-permute-start(bf16[128,2048]{1,0:T(8,128)(2,1)} %add_convert_fusion.11), channel_id=1, source_target_pairs={{8,0},{10,2},{16,8},{18,10},{24,16},{26,18},{28,24},{30,26},{20,28... | collective-permute-start | bytes 1572872 | tf_op jit(solution)/shard_map/ppermute | solution.py:517
  625.9 40.8 %collective-permute-start.124 = (bf16[128,512]{1,0:T(8,128)(2,1)}, bf16[128,512]{1,0:T(8,128)(2,1)}, u32[]{:S(2)}, u32[]{:S(2)}) collective-permute-start(bf16[128,512]{1,0:T(8,128)(2,1)} %get-tuple-element.429), channel_id=1, source_target_pairs={{0,8},{2,10},{8,16},{10,18},{16,24},{18,26},{24,28},{26,30},{28,20... | collective-permute-start | bytes 393224 | tf_op jit(solution)/shard_map/ppermute | solution.py:516
  629.9 38.5 %collective-permute-start.128 = (bf16[128,512]{1,0:T(8,128)(2,1)}, bf16[128,512]{1,0:T(8,128)(2,1)}, u32[]{:S(2)}, u32[]{:S(2)}) collective-permute-start(bf16[128,512]{1,0:T(8,128)(2,1)} %get-tuple-element.430), channel_id=1, source_target_pairs={{8,0},{10,2},{16,8},{18,10},{24,16},{26,18},{28,24},{30,26},{20,28... | collective-permute-start | bytes 393224 | tf_op jit(solution)/shard_map/ppermute | solution.py:517
  647.2 45.3 %collective-permute-start.115 = (bf16[128,1536]{1,0:T(8,128)(2,1)}, bf16[128,1536]{1,0:T(8,128)(2,1)}, u32[]{:S(2)}, u32[]{:S(2)}) collective-permute-start(bf16[128,1536]{1,0:T(8,128)(2,1)} %get-tuple-element.421), channel_id=1, source_target_pairs={{0,8},{2,10},{8,16},{10,18},{16,24},{18,26},{24,28},{26,30},{28,20... | collective-permute-start | bytes 1179656 | tf_op jit(solution)/shard_map/ppermute | solution.py:516
  662.1 34.1 %collective-permute-start.119 = (bf16[128,1536]{1,0:T(8,128)(2,1)}, bf16[128,1536]{1,0:T(8,128)(2,1)}, u32[]{:S(2)}, u32[]{:S(2)}) collective-permute-start(bf16[128,1536]{1,0:T(8,128)(2,1)} %get-tuple-element.422), channel_id=1, source_target_pairs={{8,0},{10,2},{16,8},{18,10},{24,16},{26,18},{28,24},{30,26},{20,28... | collective-permute-start | bytes 1179656 | tf_op jit(solution)/shard_map/ppermute | solution.py:517
  666.8 51.2 %collective-permute-start.113 = (bf16[256,2048]{1,0:T(8,128)(2,1)}, bf16[256,2048]{1,0:T(8,128)(2,1)}, u32[]{:S(2)}, u32[]{:S(2)}) collective-permute-start(bf16[256,2048]{1,0:T(8,128)(2,1)} %get-tuple-element.312), channel_id=1, source_target_pairs={{0,2},{2,0},{4,6},{6,4},{8,10},{10,8},{12,14},{14,12},{16,18},{18,... | collective-permute-start | bytes 3145736 | tf_op jit(solution)/shard_map/ppermute | solution.py:560
  686.8 50.7 %collective-permute-start.106 = (bf16[128,2048]{1,0:T(8,128)(2,1)}, bf16[128,2048]{1,0:T(8,128)(2,1)S(1)}, u32[]{:S(2)}, u32[]{:S(2)}) collective-permute-start(bf16[128,2048]{1,0:T(8,128)(2,1)} %add_convert_fusion.12), channel_id=1, source_target_pairs={{0,8},{2,10},{8,16},{10,18},{16,24},{18,26},{24,28},{26,30},{28,20... | collective-permute-start | bytes 1572872 | tf_op jit(solution)/shard_map/ppermute | solution.py:516
  691.0 47.7 %collective-permute-start.109 = (bf16[128,2048]{1,0:T(8,128)(2,1)S(1)}, bf16[128,2048]{1,0:T(8,128)(2,1)S(1)}, u32[]{:S(2)}, u32[]{:S(2)}) collective-permute-start(bf16[128,2048]{1,0:T(8,128)(2,1)S(1)} %copy-done.93), channel_id=1, source_target_pairs={{8,0},{10,2},{16,8},{18,10},{24,16},{26,18},{28,24},{30,26},{20,28... | collective-permute-start | bytes 1572872 | tf_op jit(solution)/shard_map/ppermute | solution.py:517
  732.8 48.1 %collective-permute-start.114 = (bf16[256,2048]{1,0:T(8,128)(2,1)}, bf16[256,2048]{1,0:T(8,128)(2,1)}, u32[]{:S(2)}, u32[]{:S(2)}) collective-permute-start(bf16[256,2048]{1,0:T(8,128)(2,1)} %add_convert_fusion.1), channel_id=1, source_target_pairs={{0,1},{1,0},{2,3},{3,2},{4,5},{5,4},{6,7},{7,6},{8,9},{9,8},{10,11... | collective-permute-start | bytes 3145736 | tf_op jit(solution)/shard_map/ppermute | solution.py:585
  754.9 34.9 %collective-permute-start.118 = (bf16[256,1536]{1,0:T(8,128)(2,1)}, bf16[256,1536]{1,0:T(8,128)(2,1)}, u32[]{:S(2)}, u32[]{:S(2)}) collective-permute-start(bf16[256,1536]{1,0:T(8,128)(2,1)} %fusion.6), channel_id=1, source_target_pairs={{0,8},{2,10},{8,16},{10,18},{16,24},{18,26},{24,28},{26,30},{28,20... | collective-permute-start | bytes 2359304 | tf_op jit(solution)/shard_map/ppermute | solution.py:516
  (254 other events, 4279.6 us)

commit v4 on v3

--- a/solution.py
+++ b/solution.py
@@ -199,20 +199,34 @@
 
 
 def moe_kernel(index, span, first, plan, sizes, *refs):
-    length, width, capacity, units, shared_units = sizes
+    length, width, capacity, units, shared_units, experts, top_count = sizes
     count = sum(len(p) for p in plan)
     own_rows, slab = span * length, 2 * span * capacity
-    half_ref, row_ref, col_ref = refs[:3]
-    given = refs[3 : 3 + count]
-    in_hbm, out_hbm, shared_hbm = refs[3 + count : 6 + count]
-    rest = refs[6 + count + (0 if first else 8) :]
-    kept, outs, dots = rest[:8], rest[8 : 8 + 4 * span], rest[8 + 4 * span]
+    half_ref, row_hbm, col_hbm, router_hbm = refs[:4]
+    given = refs[4 : 4 + count]
+    in_hbm, out_hbm, shared_hbm = refs[4 + count : 7 + count]
+    rest = refs[7 + count + (0 if first else 8) :]
+    kept, owns, give, dots = rest[:8], rest[8 : 8 + span], rest[8 + span], rest[9 + span]
     tok, up, rows, up_rows, slots, hidden, gu, y_grad, s_hidden, s_gu, made_out = rest[
-        9 + 4 * span : 20 + 4 * span
+        10 + span : 21 + span
     ]
-    w_in, w_out, w_sh, load_sem, weight_sem, out_sem, keep_sem = rest[20 + 4 * span :]
+    w_in, w_out, w_sh, row_ref, col_ref, router = rest[21 + span : 27 + span]
+    load_sem, weight_sem, out_sem, keep_sem = rest[27 + span :]
     wide = min(512, width)
     columns = tiles(width, wide)
+
+    tables = [
+        pltpu.make_async_copy(a, b, weight_sem.at[3 + i])
+        for i, (a, b) in enumerate(
+            (
+                (row_hbm.at[pl.ds(index, span)], row_ref),
+                (col_hbm.at[pl.ds(index, span)], col_ref),
+                (router_hbm, router),
+            )
+        )
+    ]
+    for copy in tables:
+        copy.start()
 
     loads = []
     for n, (lo, size_cols) in enumerate(columns):
@@ -220,11 +234,11 @@
         loads.append([])
         for which, pieces in enumerate(plan):
             target, at = (tok, up)[which // (2 * span)], which % (2 * span) * length
-            for start_zero, start_one, size in pieces:
+            for first_row, size, start_zero, start_one in pieces:
                 start = start_zero + half_ref[0] * (start_one - start_zero)
                 start = pl.multiple_of(start + at, 16)
                 copy = pltpu.make_async_copy(
-                    given[number].at[:, cols],
+                    given[number].at[first_row : first_row + size, cols],
                     target.at[pl.ds(start, size), cols],
                     load_sem.at[n, number],
                 )
@@ -234,10 +248,18 @@
 
     weights = [
         pltpu.make_async_copy(a, b, weight_sem.at[i])
-        for i, (a, b) in enumerate(((shared_hbm, w_sh), (in_hbm, w_in), (out_hbm, w_out)))
+        for i, (a, b) in enumerate(
+            (
+                (shared_hbm, w_sh),
+                (in_hbm, w_in),
+                (out_hbm, w_out),
+            )
+        )
     ]
     for copy in weights:
         copy.start()
+    for copy in tables:
+        copy.wait()
 
     def keep(slot, source):
         target = kept[slot]
@@ -253,41 +275,59 @@
 
     slot = lax.broadcasted_iota(jnp.int32, (capacity, length), 0).astype(f32)
     lane = lax.broadcasted_iota(jnp.int32, (length, 2 * capacity), 1).astype(f32)
-    picks, ones, places, gates, sigmas = [], [], [], [], []
+    picks, ones, places = [], [], []
     for j in range(span):
+        place = []
         for c in range(2):
-            pick = slot == row_ref[index + j, c : c + 1, :]
+            pick = slot == row_ref[j, c : c + 1, :]
             picks.append(pick)
             ones.append(jnp.where(pick, 1.0, 0.0).astype(bf16))
-            gate = jnp.where(pick, row_ref[index + j, 2 + c : 3 + c, :], 0.0)
-            gates.append(jnp.sum(gate, axis=1, keepdims=True))
-        places.append(
-            jnp.concatenate(
-                [
-                    jnp.where(
-                        lane == col_ref[index + j, :, c : c + 1] + float(c * capacity), 1.0, 0.0
-                    ).astype(bf16)
-                    for c in range(2)
-                ],
-                axis=0,
-            )
-        )
-        sigmas.append(col_ref[index + j, :, 2:3])
-    gate_all = jnp.concatenate(gates, axis=0)
-    sigma_all = jnp.concatenate(sigmas, axis=0)
-
+            rank = col_ref[j, :, c : c + 1] + float(c * capacity)
+            place.append(jnp.where(lane == rank, 1.0, 0.0))
+        places.append(jnp.concatenate(place, axis=0))
+
+    logits = jnp.zeros((2 * own_rows, router.shape[1]), f32)
     for n, (lo, size) in enumerate(columns):
         cols = slice(lo, lo + size)
         for copy in loads[n]:
             copy.wait()
+        logits = logits + mm(tok[:, cols], router[cols, :])
         for j in range(span):
             for c in range(2):
                 source = slice((c * span + j) * length, (c * span + j + 1) * length)
                 target = slice((2 * j + c) * capacity, (2 * j + c + 1) * capacity)
                 rows[target, cols] = mm(ones[2 * j + c], tok[source, cols]).astype(bf16)
-                got = mm(ones[2 * j + c], up[source, cols])
-                up_rows[target, cols] = got.astype(bf16)
-                slots[target, cols] = (gates[2 * j + c] * got).astype(bf16)
+                up_rows[target, cols] = mm(ones[2 * j + c], up[source, cols]).astype(bf16)
+
+    expert = lax.broadcasted_iota(jnp.int32, (length, router.shape[1]), 1).astype(f32)
+    mine = expert == half_ref[1].astype(f32)
+    row = lax.broadcasted_iota(jnp.int32, (2 * capacity, 2 * capacity), 0)
+    col = lax.broadcasted_iota(jnp.int32, (2 * capacity, 2 * capacity), 1)
+    gates, sigmas = [], []
+    for j in range(span):
+        taken = []
+        for c in range(2):
+            part = logits[(c * span + j) * length : (c * span + j + 1) * length]
+            first_id = 2 + c * top_count
+            chosen = expert == col_ref[j, :, first_id : first_id + 1]
+            for k in range(first_id + 1, first_id + top_count):
+                chosen = chosen | (expert == col_ref[j, :, k : k + 1])
+            peak = jnp.max(jnp.where(chosen, part, neg_large), axis=1, keepdims=True)
+            weight = jnp.where(chosen, jnp.exp(part - peak), 0.0)
+            weight = weight / jnp.sum(weight, axis=1, keepdims=True)
+            taken.append(jnp.sum(jnp.where(mine, weight, 0.0), axis=1, keepdims=True))
+            if c == 0:
+                gate = expert == float(experts)
+                gate = jnp.sum(jnp.where(gate, part, 0.0), axis=1, keepdims=True)
+                sigmas.append(1.0 / (1.0 + jnp.exp(-gate)))
+        slot_gates = jnp.sum(places[j] * jnp.concatenate(taken, axis=0), axis=0, keepdims=True)
+        gates.append(jnp.sum(jnp.where(row == col, slot_gates, 0.0), axis=1, keepdims=True))
+        places[j] = places[j].astype(bf16)
+    gate_all = jnp.concatenate(gates, axis=0)
+    sigma_all = jnp.concatenate(sigmas, axis=0)
+    for lo, size in columns:
+        cols = slice(lo, lo + size)
+        slots[:, cols] = (gate_all * up_rows[:, cols].astype(f32)).astype(bf16)
         y_grad[:, cols] = (sigma_all * up[0:own_rows, cols].astype(f32)).astype(bf16)
 
     kept_copies = [keep(4, tok.at[0:own_rows]), keep(0, rows), keep(1, slots), keep(5, y_grad)]
@@ -348,19 +388,18 @@
             routed = mm(places[j], entry[theirs])
             made_out[turn, 4 * j + 2] = (routed[:length] + shared_back[mine]).astype(bf16)
             made_out[turn, 4 * j + 3] = routed[length:].astype(bf16)
-            for k in range(4 * j, 4 * j + 4):
-                pairs = [(made_out.at[turn, k], outs[k].at[:, cols])]
-                if k % 4 < 2:
-                    middle = length // 2
-                    pairs = [
-                        (
-                            made_out.at[turn, k, pl.ds(pl.multiple_of(h * middle, 16), middle)],
-                            outs[k].at[m * middle : (m + 1) * middle, cols],
-                        )
-                        for m, h in enumerate((half_ref[0], 1 - half_ref[0]))
+            middle = length // 2
+            for k in range(4):
+                target, base = (owns[j], 0) if k % 2 == 0 else (give, 2 * j * length)
+                base += (length, 0)[k // 2]
+                for m, h in enumerate((half_ref[0], 1 - half_ref[0])):
+                    source = made_out.at[
+                        turn, 4 * j + k, pl.ds(pl.multiple_of(h * middle, 16), middle)
                     ]
-                for m, (source, target) in enumerate(pairs):
-                    copy = pltpu.make_async_copy(source, target, out_sem.at[turn, k, m])
+                    at = base + m * middle
+                    copy = pltpu.make_async_copy(
+                        source, target.at[at : at + middle, cols], out_sem.at[turn, 4 * j + k, m]
+                    )
                     copy.start()
                     sent[-1].append(copy)
     row = lax.broadcasted_iota(jnp.int32, (length, length), 0)
@@ -377,10 +416,10 @@
         copy.wait()
 
 
-def moe_call(index, span, sizes, chips, pieces, half, row_aux, col_aux, weights, kept):
-    length, width, capacity, units, shared_units = sizes
-    plan = [[(a, b, piece.shape[0]) for piece, a, b in group] for group in pieces]
-    arrays = [piece for group in pieces for piece, _, _ in group]
+def moe_call(index, span, sizes, chips, pieces, where, row_aux, col_aux, router, weights, kept):
+    length, width, capacity, units, shared_units = sizes[:5]
+    plan = [[place for _, place in group] for group in pieces]
+    arrays = [piece for group in pieces for piece, _ in group]
     first = kept is None
     own_rows, slab = span * length, 2 * span * capacity
     slots, tokens = chips * 2 * capacity, chips * length
@@ -397,18 +436,21 @@
             (2, tokens, shared_units),
         )
     ]
-    block = jax.ShapeDtypeStruct((length, width), bf16)
-    operands = [half, row_aux, col_aux, *arrays, *weights] + ([] if first else list(kept))
+    own = jax.ShapeDtypeStruct((2 * length, width), bf16)
+    give = jax.ShapeDtypeStruct((2 * own_rows, width), bf16)
+    operands = [where, row_aux, col_aux, router, *arrays, *weights]
+    operands += [] if first else list(kept)
     aliases = {} if first else {len(operands) - 8 + i: i for i in range(8)}
     flops = 2 * slab * width * units * 6 + 2 * own_rows * width * shared_units * 6
     out = pl.pallas_call(
         functools.partial(moe_kernel, index, span, first, plan, sizes),
         out_shape=kept_shapes
-        + [block] * (4 * span)
+        + [own] * span
+        + [give]
         + [jax.ShapeDtypeStruct((span, 8, length), f32)],
-        in_specs=[in_smem, in_vmem, in_vmem]
+        in_specs=[in_smem] + [in_any] * 3
         + [in_any] * (len(arrays) + 3 + (0 if first else 8)),
-        out_specs=[in_any] * (8 + 4 * span) + [in_vmem],
+        out_specs=[in_any] * (9 + span) + [in_vmem],
         scratch_shapes=[
             pltpu.VMEM((2 * own_rows, width), bf16),
             pltpu.VMEM((2 * own_rows, width), bf16),
@@ -424,20 +466,22 @@
             pltpu.VMEM((2, units, width), bf16),
             pltpu.VMEM((units, width), bf16),
             pltpu.VMEM((3, shared_units, width), bf16),
+            pltpu.VMEM((span, *row_aux.shape[1:]), f32),
+            pltpu.VMEM((span, *col_aux.shape[1:]), f32),
+            pltpu.VMEM(router.shape, bf16),
             pltpu.SemaphoreType.DMA((len(tiles(width, min(512, width))), len(arrays))),
-            pltpu.SemaphoreType.DMA((3,)),
+            pltpu.SemaphoreType.DMA((6,)),
             pltpu.SemaphoreType.DMA((2, 4 * span, 2)),
             pltpu.SemaphoreType.DMA((8,)),
         ],
         input_output_aliases=aliases,
         compiler_params=params(),
         cost_estimate=pl.CostEstimate(
-            flops=flops, bytes_accessed=(16 + 12 * span) * 1024 * 1024, transcendentals=0
+            flops=flops // 64, bytes_accessed=span * 512 * 1024, transcendentals=0
         ),
         name=f"experts_{index}",
     )(*operands)
-    blocks = out[8 : 8 + 4 * span]
-    return out[:8], [blocks[4 * j : 4 * j + 4] for j in range(span)], out[8 + 4 * span]
+    return out[:8], out[8 : 8 + span], out[8 + span], out[9 + span]
 
 
 def spread_kernel(core_ref, own, other, out):
@@ -517,16 +561,6 @@
             lax.ppermute(back, "expert", self.prev),
         ]
 
-    def gather(self, block):
-        half = self.chips // 2
-        found = {0: [block]}
-        pair = [block]
-        for k in range(1, half):
-            pair = self.step(*pair)
-            found[-k], found[k] = pair[:1], pair[1:]
-        found[half] = self.step(*pair, last=True)
-        return found
-
     def add_up(self, terms):
         out = None
         for term in terms:
@@ -559,22 +593,19 @@
     def swap_core(self, block):
         return lax.ppermute(block, "expert", self.core)
 
-    def gather_small(self, row, me):
-        held = row[None]
-        step = 1
-        while step < self.devices:
-            pairs = [(e, e ^ step) for e in range(self.devices)]
-            other = lax.ppermute(held, "expert", pairs)
-            upper = (me // step) % 2 == 1
-            held = jnp.where(
-                upper, jnp.concatenate([other, held]), jnp.concatenate([held, other])
-            )
-            step *= 2
-        return held
+    def double_small(self, held, me, step):
+        pairs = [(e, e ^ step) for e in range(self.devices)]
+        other = lax.ppermute(held, "expert", pairs)
+        upper = (me // step) % 2 == 1
+        return jnp.where(upper, jnp.concatenate([other, held]), jnp.concatenate([held, other]))
 
 
 def after(value, *others):
     return lax.optimization_barrier((value,) + others)[0]
+
+
+def after_all(values, *others):
+    return lax.optimization_barrier((list(values),) + others)[0]
 
 
 def hold(*values):
@@ -639,7 +670,45 @@
         total = sum(sizes)
         padded = -(-total // 1024) * 1024
         small = jnp.concatenate(pieces + [jnp.zeros((padded - total,), bf16)])
-        small_all = ring.gather_small(small, me)
+        swap_core = ring.swap_core
+
+        def cost(flops, moved):
+            return pl.CostEstimate(
+                flops=flops // 64, bytes_accessed=moved // 64, transcendentals=0
+            )
+
+        depth = 2 * rows_dev
+
+        def by_core(own, other, axis):
+            return jnp.where(
+                core == 0,
+                jnp.concatenate([own, other], axis=axis),
+                jnp.concatenate([other, own], axis=axis),
+            )
+
+        def halves(array, axis):
+            size = array.shape[axis] // 2
+            own = lax.dynamic_slice_in_dim(array, core * size, size, axis)
+            return own, lax.dynamic_slice_in_dim(array, (1 - core) * size, size, axis)
+
+        qkv_own, qkv_other = halves(qkv_weight.transpose(1, 0, 2), 2)
+        out_own, out_other = halves(out_weight, 0)
+        own = jnp.concatenate([qkv_own, out_own.T[None]], axis=0)
+        other = jnp.concatenate([qkv_other, out_other.T[None]], axis=0)
+        block = by_core(own, ring.swap_core(other), 1).reshape(4 * depth, half_cols)
+        half_length = length // 2
+        steps = chips // 2
+        up_zero = lax.dynamic_slice_in_dim(cotangent, half * half_length, half_length, 0)
+        small_all = small[None]
+        for k in range(devices.bit_length() - 1):
+            small_all = ring.double_small(small_all, me, 1 << k)
+        pair = ring.step(block)
+        attn_w = [block]
+        for k in range(1, steps + 1):
+            if k > 1:
+                pair = ring.step(*pair, last=k == steps)
+            attn_w += pair
+
         cuts = np.cumsum([0] + sizes)
         found = [small_all[:, cuts[i] : cuts[i + 1]] for i in range(len(sizes))]
         gains_f = (
@@ -656,36 +725,23 @@
         prefix_all = found[5].reshape(devices).astype(jnp.int32)
         prefix_pair = jnp.stack([prefix_all[me], prefix_all[me ^ 1]])
 
-        def cost(flops, moved):
-            return pl.CostEstimate(flops=flops, bytes_accessed=moved, transcendentals=0)
-
-        depth = 2 * rows_dev
-
-        def by_core(own, other, axis):
-            return jnp.where(
-                core == 0,
-                jnp.concatenate([own, other], axis=axis),
-                jnp.concatenate([other, own], axis=axis),
-            )
-
-        def halves(array, axis):
-            size = array.shape[axis] // 2
-            own = lax.dynamic_slice_in_dim(array, core * size, size, axis)
-            return own, lax.dynamic_slice_in_dim(array, (1 - core) * size, size, axis)
-
-        qkv_own, qkv_other = halves(qkv_weight.transpose(1, 0, 2), 2)
-        out_own, out_other = halves(out_weight, 0)
-        own = jnp.concatenate([qkv_own, out_own.T[None]], axis=0)
-        other = jnp.concatenate([qkv_other, out_other.T[None]], axis=0)
-        block = by_core(own, ring.swap_core(other), 1).reshape(4 * depth, half_cols)
-        found = ring.gather(block)
-        attn_w = [piece for offset in ring.offsets for piece in found[offset]]
-
-        half_length = length // 2
-        steps = chips // 2
-        up_zero = lax.dynamic_slice_in_dim(cotangent, half * half_length, half_length, 0)
-        up_cross = {0: [swap_tensor(up_zero)]}
-        up_ring = {0: [up_zero], 1: ring.step(after(up_zero, attn_w[-3]), None)}
+
+        match = jnp.any(ids_all[seq_of] == me, axis=1)
+        triangle = jnp.asarray(np.triu(np.ones((length, length), np.float32)), bf16)
+        rank = jnp.where(match, mm(match.astype(bf16), triangle) - 1.0, no_slot)
+        rank = rank.reshape(chips, 2, length)
+        row_aux = jnp.concatenate([rank, jnp.zeros((chips, 6, length), f32)], axis=1)
+        ids_ring = ids_all[seq_of].reshape(chips, 2 * top_count, length).astype(f32)
+        blank = jnp.zeros((chips, -(2 + 2 * top_count) % 8, length), f32)
+        col_aux = jnp.concatenate([rank, ids_ring, blank], axis=1).transpose(0, 2, 1)
+        router_all = jnp.concatenate(
+            [
+                router_w,
+                gate_vec[:, None],
+                jnp.zeros((width, -(experts + 1) % 128), bf16),
+            ],
+            axis=1,
+        )
 
         units = shared_out.shape[0]
         unit_chip = units // chips
@@ -696,11 +752,12 @@
             ],
             axis=0,
         ).transpose(1, 0, 2, 3)
-        sh_send = after(sh_send.reshape(chips, 3 * unit_chip, rows_dev), attn_w[-3])
+        sh_send = sh_send.reshape(chips, 3 * unit_chip, rows_dev)
+
+        up_cross = {0: swap_tensor(up_zero)}
+        attn_w[-4:-2], sh_send, up_cross[0] = hold(attn_w[-4:-2], sh_send, up_cross[0])
+        up_next = ring.step(after(up_zero, attn_w[-3]))
         same_core = [[2 * i + c for i in range(chips)] for c in range(2)]
-        sh_mine = lax.all_to_all(
-            sh_send, "expert", split_axis=0, concat_axis=0, tiled=True, axis_index_groups=same_core
-        )
         inputs = tokens_in.astype(f32)
         first_b = rms_norm(inputs, gains_f[0]).astype(bf16)
         first_o = ring.swap_core(first_b)
@@ -721,6 +778,10 @@
             cost_estimate=cost(2 * 2 * length * width * 3 * half_cols, 12 * 1024 * 1024),
             name="attend",
         )(chip_arg, prefix_pair, first_b, first_o, bias.reshape(1, -1), cosine, sine, *attn_w)
+        mixed, up_next = hold(mixed, up_next)
+        sh_mine = lax.all_to_all(
+            after(sh_send, up_next[0]), "expert", split_axis=0, concat_axis=0, tiled=True, axis_index_groups=same_core
+        )
         attn_own, attn_give = pl.pallas_call(
             functools.partial(project_kernel, chips + 1),
             out_shape=[
@@ -743,6 +804,19 @@
         residual = inputs + attn_out
         second_b = rms_norm(residual, gains_f[1]).astype(bf16)
 
+        second_b, up_next, sh_mine, row_aux, col_aux, router_all = hold(
+            second_b, up_next, sh_mine, row_aux, col_aux, router_all
+        )
+        pair = {
+            0: [
+                jnp.concatenate([second_b, up_next[0]], axis=0),
+                jnp.concatenate([up_next[1], second_b], axis=0),
+            ]
+        }
+        pair_o = {0: [swap_core(pair[0][0]), swap_core(up_next[1])]}
+        up_zero_o = swap_core(up_zero)
+        cross_o = {}
+
         logits = mm(second_b, router_w)
         expert_range = jnp.arange(experts, dtype=jnp.int32)
         route_match = expert_ids[:, :, None] == expert_range[None, None, :]
@@ -752,186 +826,235 @@
             jnp.sum(second_b.astype(f32) * gate_vec.astype(f32)[None], axis=-1)
         )
         gate_dense = jnp.sum(jnp.where(route_match, gate_weights[:, :, None], 0.0), axis=1)
-        gate_send = jnp.stack(
-            [gate_dense.T, jnp.broadcast_to(shared_sigma[None], (experts, length))], axis=1
-        )
-        gate_all = lax.all_to_all(gate_send, "expert", split_axis=0, concat_axis=0, tiled=True)
-        gate_all = gate_all[seq_of].reshape(chips, 2, 2, length)
-
-        match = jnp.any(ids_all[seq_of] == me, axis=1)
-        triangle = jnp.asarray(np.triu(np.ones((length, length), np.float32)), bf16)
-        rank = jnp.where(match, mm(match.astype(bf16), triangle) - 1.0, no_slot)
-        rank = rank.reshape(chips, 2, length)
-        blank = jnp.zeros((chips, 3, length), f32)
-        row_aux = jnp.concatenate([rank, gate_all[:, :, 0], gate_all[:, :1, 1], blank], axis=1)
-        col_aux = jnp.concatenate(
-            [rank, gate_all[:, :1, 1], jnp.zeros((chips, 5, length), f32)], axis=1
-        ).transpose(0, 2, 1)
-
         ex_in = expert_in[0].transpose(1, 2, 0)
         ex_out = expert_out[0]
         part_units = ex_out.shape[0]
-        sizes = (length, width, capacity, part_units, unit_chip)
-        half_arg = half.astype(jnp.int32).reshape(1)
+        sizes = (length, width, capacity, part_units, unit_chip, experts, top_count)
+        half_arg = jnp.stack([half, me]).astype(jnp.int32)
         core_arg = core.astype(jnp.int32).reshape(1)
-        swap_core = ring.swap_core
-
-        def each(function, items):
-            return [function(item) for item in items]
-
-        second_b, up_ring[1], sh_mine = hold(second_b, up_ring[1], sh_mine)
-        rows_ring = {0: [second_b]}
-        up_ring_o = {0: each(swap_core, up_ring[0])}
-        up_cross_o = {}
+
+        sh_w = pl.pallas_call(
+            spread_kernel,
+            out_shape=jax.ShapeDtypeStruct((3, unit_chip, width), bf16),
+            in_specs=[in_smem, in_vmem, in_vmem],
+            out_specs=in_vmem,
+            compiler_params=params(),
+            cost_estimate=cost(0, 16 * 1024 * 1024),
+            name="spread",
+        )(core_arg, sh_mine, swap_core(sh_mine))
+
+        def row_pieces(found, own_zero, g):
+            full, part = length, length // 2
+            if g == 0:
+                return [[(own_zero, (0, full, 0, 0))]]
+            if g == steps:
+                ahead, back = found[g]
+                return [[(ahead, (0, part, 0, 0)), (back, (0, part, part, part))]]
+            return [[(found[g][0], (0, full, 0, 0))], [(found[g][1], (half_length, full, 0, 0))]]
+
+        def up_pieces(found, own_zero, crossed, g):
+            whole, part = half_length, half_length // 2
+            if g == 0:
+                straight = [[(own_zero, (0, whole, 0, whole))]]
+            elif g == steps:
+                ahead, back = found[g - 1]
+                straight = [
+                    [
+                        (ahead, (length, part, 0, whole)),
+                        (back, (part, part, part, whole + part)),
+                    ]
+                ]
+            else:
+                ahead, back = found[g - 1]
+                straight = [
+                    [(ahead, (length, whole, 0, whole))],
+                    [(back, (0, whole, 0, whole))],
+                ]
+            for j, chip in enumerate(straight):
+                chip.append((crossed, (j * whole, whole, whole, 0)))
+            return straight
+
         kept = None
-        moe, back, moe_o, back_o, dot_rows = {}, {}, {}, {}, []
-        sh_w = None
+        own_terms, give_terms, dot_rows = {}, {}, []
+        terms, crossed = {}, {}
+
+        def receive(g):
+            index, count = (0, 1) if g == 0 else (2 * g - 1, 1 if g == steps else 2)
+            crossing = []
+            for j in range(count):
+                own, got, at = own_terms[g][j], give_got[g], 2 * j * length
+                parts = []
+                for i in range(4):
+                    lo, hi = i * half_length, (i + 1) * half_length
+                    parts.append([own[lo:hi], got[at + lo : at + hi]])
+                terms[ring.offsets[index + j]] = [parts[0], parts[2]]
+                crossing.append(ring.add_up(parts[1]).astype(bf16))
+                out_gives.setdefault(g, []).append(parts[3])
+            return crossing[0] if count == 1 else jnp.concatenate(crossing, axis=0)
+
+        def receive_outs(g):
+            parts = [ring.add_up(part).astype(bf16) for part in out_gives[g]]
+            return parts[0] if len(parts) == 1 else jnp.concatenate(parts, axis=0)
+
+        def place_crossed(which, g, got):
+            index, count = (0, 1) if g == 0 else (2 * g - 1, 1 if g == steps else 2)
+            for j in range(count):
+                crossed[which, ring.offsets[index + j]] = got[
+                    j * half_length : (j + 1) * half_length
+                ]
+
+        out_gives, give_got = {}, {}
         for k in range(1, steps + 2):
-            last = k == steps + 1
+            g = k - 1
             now = []
-            if not last:
-                rows_ring[k] = ring.step(*rows_ring[k - 1], last=k == steps)
-                now.append(rows_ring[k])
-                if k < steps:
-                    up_ring[k + 1] = ring.step(*up_ring[k], last=k + 1 == steps)
-                    now.append(up_ring[k + 1])
-                up_cross[k] = each(swap_tensor, up_ring[k])
-                up_ring_o[k] = each(swap_core, up_ring[k])
-                now += [up_cross[k], up_ring_o[k]]
-            g = k - 1
-            rows_o = each(swap_core, rows_ring[g])
-            up_cross_o[g] = each(swap_core, up_cross[g])
-            if sh_w is None:
-                sh_w = pl.pallas_call(
-                    spread_kernel,
-                    out_shape=jax.ShapeDtypeStruct((3, unit_chip, width), bf16),
-                    in_specs=[in_smem, in_vmem, in_vmem],
-                    out_specs=in_vmem,
-                    compiler_params=params(),
-                    cost_estimate=cost(0, 16 * 1024 * 1024),
-                    name="spread",
-                )(core_arg, sh_mine, swap_core(sh_mine))
-
-            def in_place(pieces, crossed):
-                found = []
-                for chip in [pieces] if g == steps else [[p] for p in pieces]:
-                    at = 0
-                    found.append([])
-                    for piece in chip:
-                        first = (at, at) if crossed is None else (at, half_length + at)
-                        if crossed:
-                            first = first[::-1]
-                        found[-1].append((piece, *first))
-                        at += piece.shape[0]
-                return found
-
-            def joined(straight, crossed):
-                both = zip(in_place(straight, False), in_place(crossed, True), strict=True)
-                return [a + b for a, b in both]
-
-            index = 0 if g == 0 else 2 * g - 1
-            offsets = ring.offsets[index : index + (1 if g in (0, steps) else 2)]
+            if k <= steps:
+                ahead, back = pair[g]
+                cut = half_length // 2
+                if k == steps:
+                    ahead, back = ahead[: length // 2], back[half_length + length // 2 :]
+                pair[k] = ring.send_pair(ahead, back)
+                first, second = pair[g][0][length:], pair[g][1][:half_length]
+                if k == steps:
+                    first, second = first[:cut], second[cut:]
+                up_cross[k] = swap_tensor(jnp.concatenate([first, second], axis=0))
+                now = [pair[k], up_cross[k]]
+            if g > 0:
+                pair_o[g] = [swap_core(x) for x in pair[g]]
+            if g > 0:
+                cross_o[g] = swap_core(after(up_cross[g], *pair_o[g]))
+            else:
+                cross_o[g] = swap_core(up_cross[g])
+            if g >= 1:
+                give_got[g - 1] = swap_core(after(give_terms[g - 1], cross_o[g]))
+                now.append(give_got[g - 1])
+            if g >= 2:
+                grads = receive(g - 2)
+                grads, pair_o[g] = hold(grads, pair_o[g])
+                now.append(swap_tensor(grads))
             pieces = (
-                in_place(rows_ring[g], None)
-                + in_place(rows_o, None)
-                + joined(up_ring[g], up_cross[g])
-                + joined(up_ring_o[g], up_cross_o[g])
+                row_pieces(pair, second_b, g)
+                + row_pieces(pair_o, pair_o[0][0], g)
+                + up_pieces(pair, up_zero, up_cross[g], g)
+                + up_pieces(pair_o, up_zero_o, cross_o[g], g)
             )
-            kept, blocks, rows = moe_call(
-                index,
-                len(offsets),
+            span = 1 if g in (0, steps) else 2
+            kept, own_terms[g], give_terms[g], rows = moe_call(
+                0 if g == 0 else 2 * g - 1,
+                span,
                 sizes,
                 chips,
                 pieces,
                 half_arg,
                 row_aux,
                 col_aux,
+                router_all,
                 (ex_in, ex_out, sh_w),
                 kept,
             )
             dot_rows.append(rows)
-            if not last:
-                *_, dot_rows[-1] = held = hold(*now, rows)
-                rows_ring[k] = held[0]
-                if k < steps:
-                    up_ring[k + 1] = held[1]
-                up_cross[k], up_ring_o[k] = held[-3:-1]
-            for o, (moe_own, moe_give, back_own, back_give) in zip(offsets, blocks, strict=True):
-                moe[o], back[o] = moe_own, back_own
-                back_o[o] = swap_core(back_give)
-                moe_o[o] = swap_core(moe_give)
+            *now, dot_rows[-1], give_terms[g] = hold(*now, rows, give_terms[g])
+            if k <= steps:
+                pair[k], up_cross[k], *now = now
+            if g >= 1:
+                give_got[g - 1] = now[0]
+            if g >= 2:
+                place_crossed(0, g - 2, now[1])
 
         rows_all, slots_all, hidden_all, gu_all, tok_all, y_all, s_hidden_all, s_gu_all = kept
-        slot_count = chips * 2 * capacity
-
-        def crossing(o):
-            mine = moe[o].astype(f32) + moe_o[o].astype(f32)
-            return swap_tensor(mine[half_length:].astype(bf16))
-
-        def moe_terms(o):
-            return [moe[o][:half_length], moe_o[o][:half_length], moe_cross[o]]
-
+        give_got[steps] = swap_core(give_terms[steps])
+        near_far = receive(steps - 1)
+        near_far, give_got[steps] = hold(near_far, give_got[steps])
+        grads = receive(steps)
+        s_hidden_all, grads = hold(s_hidden_all, grads)
         far = ring.offsets[-1]
-        moe_cross = {}
-        sending = ring.reduce_first([back[far], back_o[far]])
-        moe_cross[far] = crossing(far)
-        sending, moe_cross[far] = hold(sending, moe_cross[far])
+        grads = swap_tensor(grads)
+        sh_grad = pl.pallas_call(
+            shared_grad_kernel,
+            grid=(chips,),
+            out_shape=jax.ShapeDtypeStruct((2, chips, 3 * unit_chip, rows_dev), bf16),
+            in_specs=[
+                pl.BlockSpec((chips * length, depth), lambda n: (0, n)),
+                pl.BlockSpec((chips * length, depth), lambda n: (0, n)),
+                pl.BlockSpec((chips * length, unit_chip), lambda n: (0, 0)),
+                pl.BlockSpec((2, chips * length, unit_chip), lambda n: (0, 0, 0)),
+            ],
+            out_specs=pl.BlockSpec((2, 1, 3 * unit_chip, rows_dev), lambda n: (0, n, 0, 0)),
+            compiler_params=params(),
+            cost_estimate=cost(2 * chips * length * width * 3 * unit_chip, 26 * 1024 * 1024),
+            name="shared_grad",
+        )(tok_all, y_all, s_hidden_all, s_gu_all)
+        near_got = swap_tensor(near_far)
+        grads, sh_grad = hold(grads, sh_grad)
+        place_crossed(0, steps, grads)
+
+        def ring_terms(which, o):
+            return [*terms[o][which], crossed[which, o]]
+
+        sending = ring.reduce_first(ring_terms(0, far))
+        own, other = halves(sh_grad, 0)
+        sh_got = swap_core(other)
+        gu_all = after(gu_all, grads)
+        sh_sum = (own.astype(f32) + sh_got.astype(f32)).astype(bf16)[0]
+        expert_in_grad = mm(gu_all, rows_all, 1, 0).transpose(2, 0, 1)[None]
+        near_got, sending, sh_sum, expert_in_grad = hold(
+            near_got, sending, sh_sum, expert_in_grad
+        )
+        place_crossed(0, steps - 1, near_got)
+        out_sent = {}
         for k in range(steps - 1, 0, -1):
             send = ring.reduce_terms(
-                [back[k], back_o[k]], [back[-k], back_o[-k]], sending, k == steps - 1
+                ring_terms(0, k), ring_terms(0, -k), sending, k == steps - 1
             )
-            number = steps - 1 - k
-            if number == 0:
-                gu_all, *send = hold(gu_all, *send)
-                expert_in_grad = mm(gu_all, rows_all, 1, 0).transpose(2, 0, 1)[None]
-                token = expert_in_grad[:, :1, :1, :1]
-            elif number == 1:
-                s_hidden_all, *send = hold(s_hidden_all, *send)
-                sh_grad = pl.pallas_call(
-                    shared_grad_kernel,
-                    grid=(chips,),
-                    out_shape=jax.ShapeDtypeStruct((2, chips, 3 * unit_chip, rows_dev), bf16),
-                    in_specs=[
-                        pl.BlockSpec((chips * length, depth), lambda n: (0, n)),
-                        pl.BlockSpec((chips * length, depth), lambda n: (0, n)),
-                        pl.BlockSpec((chips * length, unit_chip), lambda n: (0, 0)),
-                        pl.BlockSpec((2, chips * length, unit_chip), lambda n: (0, 0, 0)),
-                    ],
-                    out_specs=pl.BlockSpec((2, 1, 3 * unit_chip, rows_dev), lambda n: (0, n, 0, 0)),
-                    compiler_params=params(),
-                    cost_estimate=cost(
-                        2 * chips * length * width * 3 * unit_chip, 26 * 1024 * 1024
-                    ),
-                    name="shared_grad",
-                )(tok_all, y_all, s_hidden_all, s_gu_all)
-                token = sh_grad[:, :1, :1, :1]
-            elif number == 2:
-                hidden_all, *send = hold(hidden_all, *send)
+            now = []
+            if k == steps - 1:
+                hidden_all, send, far_outs = hold(hidden_all, send, receive_outs(steps))
                 expert_out_grad = mm(hidden_all, slots_all, 0, 0)[None]
-                token = expert_out_grad[:, :1, :1]
+                out_sent[steps] = swap_tensor(far_outs)
+                dots = jnp.concatenate(after_all(dot_rows, send[0]), axis=0)
+                sdots = jnp.concatenate([dots[:, 2:3], jnp.zeros_like(dots[:, 2:3])], axis=1)
+                dot_send = jnp.stack([dots[:, :2], sdots], axis=2)
+                dot_send = dot_send.reshape(devices, 2, length)[seq_inv]
+                dot_got = lax.all_to_all(
+                    dot_send, "expert", split_axis=0, concat_axis=0, tiled=True
+                )
+                dot_got = jnp.concatenate(
+                    [dot_got[:, 0], jnp.sum(dot_got[:, 1], axis=0)[None]], axis=0
+                )
+                now = [out_sent[steps], dot_got, expert_out_grad]
             sending = ring.send_pair(*send)
-            moe_cross[k], moe_cross[-k] = crossing(k), crossing(-k)
-            sending, moe_cross[k], moe_cross[-k], token = hold(
-                sending, moe_cross[k], moe_cross[-k], token
+            sending, *now = hold(sending, *now)
+            if k == steps - 1:
+                out_sent[steps], dot_got, expert_out_grad = now
+        place_crossed(1, steps, out_sent[steps])
+        dot_got = dot_got + swap_tensor(dot_got)
+        second_half = ring.add_up([*ring_terms(0, 0), *sending]).astype(bf16)
+        sh_back = lax.all_to_all(
+            after(sh_sum, second_half),
+            "expert",
+            split_axis=0,
+            concat_axis=0,
+            tiled=True,
+            axis_index_groups=same_core,
+        )
+        second_got = swap_tensor(second_half)
+        out_sending = ring.reduce_first(ring_terms(1, far))
+        second_got, out_sending = hold(second_got, out_sending)
+
+        def both_halves(own, other):
+            return jnp.where(
+                half == 0,
+                jnp.concatenate([own, other], axis=0),
+                jnp.concatenate([other, own], axis=0),
             )
-        second_part = ring.add_up([back[0], back_o[0], *sending]).astype(bf16)
-        moe_cross[0] = crossing(0)
-        second_got = swap_tensor(second_part)
-        sending = ring.reduce_first(moe_terms(far))
-        second_got, moe_cross[0], sending = hold(second_got, moe_cross[0], sending)
-
-        dots = jnp.concatenate(dot_rows, axis=0)
-        sdots = jnp.concatenate([dots[:, 2:3], jnp.zeros_like(dots[:, 2:3])], axis=1)
-        dot_send = jnp.stack([dots[:, :2], sdots], axis=2).reshape(devices, 2, length)[seq_inv]
-        dot_got = lax.all_to_all(dot_send, "expert", split_axis=0, concat_axis=0, tiled=True)
-        dot_got = jnp.concatenate([dot_got[:, 0], jnp.sum(dot_got[:, 1], axis=0)[None]], axis=0)
-        dot_got = dot_got + swap_tensor(dot_got)
+
+        second_part = both_halves(second_half, second_got)
+
         gate_grad_dense, sigma_grad = dot_got[:experts].T, dot_got[experts]
         row_term = jnp.sum(gate_dense * gate_grad_dense, axis=-1, keepdims=True)
         logit_grad = (gate_dense * (gate_grad_dense - row_term)).astype(bf16)
         gate_logit_grad = sigma_grad * shared_sigma * (1.0 - shared_sigma)
 
-        second_grad = second_part.astype(f32) + second_got.astype(f32)
+        second_grad = second_part.astype(f32)
         second_grad = second_grad + mm(logit_grad, router_w, 1, 1)
         second_grad = second_grad + gate_logit_grad[:, None] * gate_vec.astype(f32)[None]
         upstream = cotangent.astype(f32)
@@ -940,26 +1063,13 @@
         attn_grad = residual_grad.astype(bf16)
         attn_grad_o = ring.swap_core(attn_grad)
 
-        for k in range(steps - 1, 0, -1):
-            send = ring.reduce_terms(moe_terms(k), moe_terms(-k), sending, k == steps - 1)
-            sending = ring.send_pair(*send)
-        moe_half = ring.add_up([*moe_terms(0), *sending])
-        res_half = lax.dynamic_slice_in_dim(residual, half * half_length, half_length, 0)
-        out_half = (res_half + moe_half).astype(bf16)
-        out_got = swap_tensor(out_half)
-        output = jnp.where(
-            half == 0,
-            jnp.concatenate([out_half, out_got], axis=0),
-            jnp.concatenate([out_got, out_half], axis=0),
-        )
-
-        def by_chip(left, other, right):
-            pair = jnp.concatenate([left, other], axis=0)
+        def by_chip(left, right, wanted=tuple(ring.offsets)):
             return {
                 offset: [
-                    mm(lax.dynamic_slice_in_dim(pair, chip_of[i] * depth, depth, 1), right, 0, 0)
+                    mm(lax.dynamic_slice_in_dim(left, chip_of[i] * depth, depth, 1), right, 0, 0)
                 ]
                 for i, offset in enumerate(ring.offsets)
+                if offset in wanted
             }
 
         proj_grad, bias_grad = pl.pallas_call(
@@ -989,8 +1099,26 @@
             sine,
             *attn_w,
         )
-        qkv_grad = ring.reduce(by_chip(first_b, first_o, proj_grad))
-        out_grad = ring.reduce(by_chip(attn_grad, attn_grad_o, mixed))
+        crossing = swap_tensor(receive_outs(steps - 1))
+        first_pair = jnp.concatenate([first_b, first_o], axis=0)
+        attn_grad_pair = jnp.concatenate([attn_grad, attn_grad_o], axis=0)
+        out_parts = by_chip(attn_grad_pair, mixed)
+        far_out = out_parts[steps][0].astype(bf16)
+        far_out, proj_grad, sh_back = hold(far_out, proj_grad, sh_back)
+        far_part = by_chip(first_pair, proj_grad, [steps])[steps][0].astype(bf16)
+        far_part = jnp.concatenate([far_part, far_out], axis=1)
+        cut = depth // 2
+        proj_grad, ahead, back = hold(proj_grad, far_part[:cut], far_part[cut:])
+        going = ring.send_pair(ahead, back)
+        qkv_parts = by_chip(first_pair, proj_grad, ring.offsets[:-1])
+        attn_parts = {
+            o: [
+                jnp.concatenate(
+                    [qkv_parts[o][0].astype(bf16), out_parts[o][0].astype(bf16)], axis=1
+                )
+            ]
+            for o in qkv_parts
+        }
         bias_grad = bias_grad[0]
         first_own, first_give = pl.pallas_call(
             functools.partial(project_back_kernel, chips + 1),
@@ -1008,27 +1136,11 @@
             cost_estimate=cost(2 * 2 * length * width * 3 * half_cols, 12 * 1024 * 1024),
             name="project_back",
         )(chip_arg, proj_grad, *attn_w)
-        first_grad = sum_tensor(first_own + ring.swap_core(first_give).astype(f32))
-        input_norm_grad, gain_one_grad = jax.vjp(rms_norm, inputs, gains_f[0])[1](first_grad)
-        input_grad = (residual_grad + input_norm_grad).astype(bf16)
-
-        def regroup(grad, parts):
-            own, other = halves(grad, 0)
-            own = own.astype(bf16).reshape(rows_dev, parts, half_cols)
-            got = ring.swap_core(other.astype(bf16)).reshape(rows_dev, parts, half_cols)
-            return by_core(own, got, 2).astype(f32)
-
-        qkv_weight_grad = regroup(qkv_grad, 3)
-        out_weight_grad = regroup(out_grad, 1)[:, 0].T
-
-        own, other = halves(sh_grad, 0)
-        sh_sum = (own.astype(f32) + ring.swap_core(other).astype(f32)).astype(bf16)[0]
-        sh_back = lax.all_to_all(
-            sh_sum, "expert", split_axis=0, concat_axis=0, tiled=True, axis_index_groups=same_core
-        )
-        sh_back = sh_back.reshape(chips, 3, unit_chip, rows_dev).astype(f32)
-        shared_in_grad = sh_back[:, :2].transpose(3, 1, 0, 2).reshape(rows_dev, 2, units)
-        shared_out_grad = sh_back[:, 2].reshape(units, rows_dev)
+        first_own = (first_own + swap_core(first_give).astype(f32)).astype(bf16)
+        def send_outs(k, going):
+            return ring.send_pair(
+                *ring.reduce_terms(ring_terms(1, k), ring_terms(1, -k), going, k == steps - 1)
+            )
 
         second_f = second_b.astype(f32)
         router_part = mm(second_b, logit_grad, 0, 0)
@@ -1036,16 +1148,69 @@
         early = jnp.concatenate(
             [router_part, shared_gate_part[:, None], gain_two_grad[:, None]], axis=1
         ).reshape(devices, rows_dev * (experts + 2))
-        early = lax.all_to_all(early, "expert", split_axis=0, concat_axis=0, tiled=True)
+
+        def send_next(k, going):
+            return ring.send_pair(
+                *ring.reduce_terms(attn_parts[k], attn_parts[-k], going, k == steps - 1)
+            )
+
+        pieces = [attn_parts[o][0] for o in ring.offsets[:-1]]
+        going, crossing, first_own, pieces = hold(going, crossing, first_own, pieces)
+        for o, piece in zip(ring.offsets[:-1], pieces, strict=True):
+            attn_parts[o] = [piece]
+        place_crossed(1, steps - 1, crossing)
+        for k in range(steps - 1, -1, -1):
+            if k > 0:
+                going = send_next(k, going)
+                out_sending = send_outs(k, out_sending)
+            now = []
+            if k > 0:
+                now.append(swap_tensor(receive_outs(k - 1)))
+            if k == steps - 2:
+                now.append(swap_tensor(first_own))
+            if k == 0:
+                res_half = lax.dynamic_slice_in_dim(residual, half * half_length, half_length, 0)
+                out_half = ring.add_up([res_half, *ring_terms(1, 0), *out_sending]).astype(bf16)
+                output = both_halves(out_half, swap_tensor(out_half))
+                break
+            if k == 2:
+                now.append(sh_back)
+            going, out_sending, *now = hold(going, out_sending, *now)
+            place_crossed(1, k - 1, now[0])
+            if k == 2:
+                sh_back = now[-1]
+            if k == steps - 2:
+                first_got = now[1]
+        attn_grads = ring.add_up([*attn_parts[0], *going])
+        first_grad = first_own.astype(f32) + first_got.astype(f32)
+        input_norm_grad, gain_one_grad = jax.vjp(rms_norm, inputs, gains_f[0])[1](first_grad)
+        input_grad = (residual_grad + input_norm_grad).astype(bf16)
+
+        own, other = halves(attn_grads.astype(bf16), 0)
+        both = by_core(
+            own.reshape(rows_dev, 4, half_cols),
+            swap_core(other).reshape(rows_dev, 4, half_cols),
+            2,
+        ).astype(f32)
+        qkv_weight_grad = both[:, :3]
+        out_weight_grad = both[:, 3].T
+
+        sh_back = sh_back.reshape(chips, 3, unit_chip, rows_dev).astype(f32)
+        shared_in_grad = sh_back[:, :2].transpose(3, 1, 0, 2).reshape(rows_dev, 2, units)
+        shared_out_grad = sh_back[:, 2].reshape(units, rows_dev)
+
+        bias_send = bias_grad.reshape(3 * heads, devices, hd_dev).transpose(1, 0, 2)
+        late = jnp.concatenate(
+            [gain_one_grad.reshape(devices, rows_dev), bias_send.reshape(devices, -1), early],
+            axis=1,
+        )
+        late = lax.all_to_all(late, "expert", split_axis=0, concat_axis=0, tiled=True)
+        gain_one = jnp.sum(late[:, :rows_dev], axis=0)
+        count = 3 * heads * hd_dev
+        early = late[:, rows_dev + count :]
         early = jnp.sum(early, axis=0).reshape(rows_dev, experts + 2)
         router_grad, shared_gate_grad = early[:, :experts], early[:, experts]
-        bias_send = bias_grad.reshape(3 * heads, devices, hd_dev).transpose(1, 0, 2)
-        late = jnp.concatenate(
-            [gain_one_grad.reshape(devices, rows_dev), bias_send.reshape(devices, -1)], axis=1
-        )
-        late = lax.all_to_all(late, "expert", split_axis=0, concat_axis=0, tiled=True)
-        gain_one = jnp.sum(late[:, :rows_dev], axis=0)
-        bias_got = jnp.sum(late[:, rows_dev:].reshape(chips, 2, 3, heads, hd_dev), axis=0)
+        bias_got = jnp.sum(late[:, rows_dev : rows_dev + count].reshape(chips, 2, 3, heads, hd_dev), axis=0)
         qkv_bias_grad = bias_got.transpose(1, 0, 2, 3).reshape(3, heads_t, hd_dev)
         gains_grad = jnp.stack([gain_one, early[:, experts + 1]], axis=0)
 

time: 807 us -> 765 us (0.948)
  starting transfers between devices: 157 us -> 107 us
  other arithmetic: 86.8 us -> 104 us
  waiting for transfers between devices: 259 us -> 243 us
    ppermute x22 -> x20, waiting for transfers between devices: 113 us -> 35.2 us  [swap_tensor(): return lax.ppermute(block, 'tensor', [(0, 1), (1, 0)])]
    ppermute x52 -> x29, waiting for transfers between devices: 4.56 us -> 30.3 us  [swap_core(): return lax.ppermute(block, 'expert', self.core)]
    ppermute x28 -> x21, starting transfers between devices: 47.4 us -> 21.8 us  [send_pair(): lax.ppermute(ahead, 'expert', self.next)]
    convert_element_type x4 -> x15, other arithmetic: 6.74 us -> 32.2 us  [the longest x8 24.2 us: receive_outs(): parts = [ring.add_up(part).astype(bf16) for part in out_gives[g]]]
    ppermute x28 -> x21, waiting for transfers between devices: 69.3 us -> 93.9 us  [send_pair(): lax.ppermute(ahead, 'expert', self.next)]
    another operation x18 -> x7, other arithmetic: 18.1 us -> 2.1 us
    all_to_all x4 -> x2, waiting for transfers between devices: 9.05 us -> 25 us  [the longest x1 17.8 us: local(): lax.all_to_all(after(sh_send, up_next[0]), 'expert', split_axis=0, concat...]
    concatenate x2 -> x20, other arithmetic: 0.7 us -> 16.4 us  [the longest x3 4.62 us: receive_outs(): return parts[0] if len(parts) == 1 else jnp.concatenate(parts, axis=0)]
  transfers between devices with their start and end apart: 140 -> 99, of which waited for: 40 -> 46; matrix products, arithmetic and copies ran while one was open for 22% -> 24% of each run, Pallas kernels for 22% -> 24%
where the time goes in v4:
time: 765 us; the launch traced here: 755 us
  waiting for transfers between devices  243 us (32%)
  Pallas kernels  187 us (24%)
  starting transfers between devices  107 us (14%)
  other arithmetic  104 us (14%)
  local copies, waits for them, and re-layouts  63.3 us (8%)
  matrix products  41.8 us (5%)
  between operations  8.93 us (1%)
    pallas_call x5, Pallas kernels, moe_call(): pl.pallas_call(functools.partial(moe_kernel, index, span, first, plan, si...  129 us
    ppermute x21, waiting for transfers between devices, send_pair(): lax.ppermute(ahead, 'expert', self.next)  93.9 us
    ppermute x4, waiting for transfers between devices, double_small(): other = lax.ppermute(held, 'expert', pairs)  44.2 us
    dot_general x22, matrix products, mm(): lax.dot_general(left, right, (((contract_left,), (contract_right,)), ((),...  41.8 us
    ppermute x20, waiting for transfers between devices, swap_tensor(): return lax.ppermute(block, 'tensor', [(0, 1), (1, 0)])  35.2 us
    ppermute x21, starting transfers between devices, send_pair(): lax.ppermute(back, 'expert', self.prev)  34.2 us
    ppermute x29, waiting for transfers between devices, swap_core(): return lax.ppermute(block, 'expert', self.core)  30.3 us
    unnamed x228, local copies, waits for them, and re-layouts  24.9 us
  transfers between devices with their start and end apart: 99, of which 46 were waited for; matrix products, arithmetic and copies ran while one was open for 24% of the time, Pallas kernels for 24%

profile of v4, /device:TPU:0, one launch (start us, length us, event | category | flops | bytes accessed | tf_op | source)
XLA Modules:
  0.0 755.3 jit_solution(13926727747266206371)
XLA Ops:
  14.1 18.2 %collective-permute-done.1 = bf16[2,4096]{1,0:T(2,128)(2,1)S(1)} collective-permute-done((bf16[2,4096]{1,0:T(2,128)(2,1)S(1)}, bf16[2,4096]{1,0:T(2,128)(2,1)S(1)}, u32[]{:S(2)}, u32[]{:S(2)}) %collective-permute-start.1) | collective-permute-done | bytes 16416 | tf_op jit(solution)/shard_map/ppermute | solution.py:598
  40.6 24.5 %collective-permute-done.3 = bf16[8,4096]{1,0:T(8,128)(2,1)S(1)} collective-permute-done((bf16[8,4096]{1,0:T(8,128)(2,1)S(1)}, bf16[8,4096]{1,0:T(8,128)(2,1)S(1)}, u32[]{:S(2)}, u32[]{:S(2)}) %collective-permute-start.3) | collective-permute-done | bytes 65568 | tf_op jit(solution)/shard_map/ppermute | solution.py:598
  74.6 13.1 %collective-permute-done.10.refs_12_.refs_7_.refs_14_ = bf16[1024,512]{1,0:T(8,128)(2,1)} collective-permute-done((bf16[1024,512]{1,0:T(8,128)(2,1)}, bf16[1024,512]{1,0:T(8,128)(2,1)}, u32[]{:S(2)}, u32[]{:S(2)}) %collective-permute-start.10) | collective-permute-done | bytes 1048608 | tf_op jit(solution)/shard_map/ppermute | solution.py:560
  101.1 8.5 %collective-permute-done.13.refs_14_.refs_9_.refs_16_ = bf16[512,512]{1,0:T(8,128)(2,1)S(1)} collective-permute-done((bf16[512,512]{1,0:T(8,128)(2,1)}, bf16[512,512]{1,0:T(8,128)(2,1)S(1)}, u32[]{:S(2)}, u32[]{:S(2)}) %collective-permute-start.13) | collective-permute-done | bytes 524320 | tf_op jit(solution)/shard_map/ppermute | solution.py:560
  110.9 9.9 %attend.1 = (bf16[512,512]{1,0:T(8,128)(2,1)}, bf16[512,512]{1,0:T(8,128)(2,1)}, bf16[512,512]{1,0:T(8,128)(2,1)}, bf16[512,512]{1,0:T(8,128)(2,1)}) custom-call(s32[8]{0:T(128)} %get-tuple-element.537.refs_0_, s32[2]{0:T(128)} %pad_add_fusion.refs_1_, bf16[256,2048]{1,0:T(8,128)(2,1)} %copy-done.2, bf16[256,2048]{1,0:T(8,128)(2,1)} %copy-done.6, ...), custom_call_target="tpu_custom_call" | custom-call | flops 50331648 | bytes 196608 | tf_op jit(solution)/shard_map/attend/pallas_call | solution.py:768
  120.8 5.5 project.1
  126.4 4.7 all-to-all-start
  140.6 20.0 %collective-permute-done.18 = bf16[256,2048]{1,0:T(8,128)(2,1)} collective-permute-done((bf16[256,2048]{1,0:T(8,128)(2,1)S(1)}, bf16[256,2048]{1,0:T(8,128)(2,1)}, u32[]{:S(2)}, u32[]{:S(2)}) %collective-permute-start.18) | collective-permute-done | bytes 1048608 | tf_op jit(solution)/shard_map/ppermute | solution.py:616
  163.9 17.8 %all-to-all-done.own = bf16[8,1056,128]{2,1,0:T(8,128)(2,1)} async-done(((bf16[8,1056,128]{2,1,0:T(8,128)(2,1)}), bf16[8,1056,128]{2,1,0:T(8,128)(2,1)}, u32[]{:S(2)}, u32[]{:S(2)}) %all-to-all-start) | async-done | bytes 2162720 | tf_op jit(solution)/shard_map/all_to_all | solution.py:782
  193.0 5.0 spread.1.refs_12_.refs_18_.refs_16_
  199.2 19.1 %experts_0.1 = (bf16[1536,2048]{1,0:T(8,128)(2,1)}, bf16[1536,2048]{1,0:T(8,128)(2,1)}, bf16[1536,704]{1,0:T(8,128)(2,1)}, bf16[2,1536,704]{2,1,0:T(8,128)(2,1)}...) custom-call(s32[2]{0:T(128)} %pad_add_fusion.1.refs_0_, ...), custom_call_target="tpu_custom_call" | custom-call | flops 86507520 | bytes 524288 | tf_op jit(solution)/shard_map/experts_0/pallas_call | solution.py:445
  218.3 4.9 collective-permute-done.23.refs_4_.refs_8_
  233.3 9.7 %collective-permute-start.27 = (bf16[384,2048]{1,0:T(8,128)(2,1)S(1)}, bf16[384,2048]{1,0:T(8,128)(2,1)S(1)}, u32[]{:S(2)}, u32[]{:S(2)}) collective-permute-start(bf16[384,2048]{1,0:T(8,128)(2,1)S(1)} %collective-permute-done.24.refs_5_.refs_10_), channel_id=1, source_target_pairs={{8,0},{10,2},{16,8},{18,10},{24,16},{26,18},{28,24},{30,26},{20,28... | collective-permute-start | bytes 4718600 | tf_op jit(solution)/shard_map/ppermute | solution.py:561
  248.0 30.0 %experts_1.1 = (bf16[1536,2048]{1,0:T(8,128)(2,1)}, bf16[1536,2048]{1,0:T(8,128)(2,1)}, bf16[1536,704]{1,0:T(8,128)(2,1)}, bf16[2,1536,704]{2,1,0:T(8,128)(2,1)}...) custom-call(s32[2]{0:T(128)} %pad_add_fusion.1.refs_0_, ...), custom_call_target="tpu_custom_call", output_to_operand_aliasing={{0}: (19, {}), {1}: (20, {}), {2}: (21, {}), {3}: (22, {}),... | custom-call | flops 173015040 | bytes 1048576 | tf_op jit(solution)/shard_map/experts_1/pallas_call | solution.py:445
  295.4 30.0 %experts_3.1 = (bf16[1536,2048]{1,0:T(8,128)(2,1)}, bf16[1536,2048]{1,0:T(8,128)(2,1)}, bf16[1536,704]{1,0:T(8,128)(2,1)}, bf16[2,1536,704]{2,1,0:T(8,128)(2,1)}...) custom-call(s32[2]{0:T(128)} %pad_add_fusion.1.refs_0_, ...), custom_call_target="tpu_custom_call", output_to_operand_aliasing={{0}: (19, {}), {1}: (20, {}), {2}: (21, {}), {3}: (22, {}),... | custom-call | flops 173015040 | bytes 1048576 | tf_op jit(solution)/shard_map/experts_3/pallas_call | solution.py:445
  344.8 30.4 %experts_5.1 = (bf16[1536,2048]{1,0:T(8,128)(2,1)}, bf16[1536,2048]{1,0:T(8,128)(2,1)}, bf16[1536,704]{1,0:T(8,128)(2,1)}, bf16[2,1536,704]{2,1,0:T(8,128)(2,1)}...) custom-call(s32[2]{0:T(128)} %pad_add_fusion.1.refs_0_, ...), custom_call_target="tpu_custom_call", output_to_operand_aliasing={{0}: (19, {}), {1}: (20, {}), {2}: (21, {}), {3}: (22, {}),... | custom-call | flops 173015040 | bytes 1048576 | tf_op jit(solution)/shard_map/experts_5/pallas_call | solution.py:445
  385.5 19.6 %experts_7.1 = (bf16[1536,2048]{1,0:T(8,128)(2,1)}, bf16[1536,2048]{1,0:T(8,128)(2,1)}, bf16[1536,704]{1,0:T(8,128)(2,1)}, bf16[2,1536,704]{2,1,0:T(8,128)(2,1)}...) custom-call(s32[2]{0:T(128)} %pad_add_fusion.1.refs_0_, ...), custom_call_target="tpu_custom_call", output_to_operand_aliasing={{0}: (17, {}), {1}: (18, {}), {2}: (19, {}), {3}: (20, {}),... | custom-call | flops 86507520 | bytes 524288 | tf_op jit(solution)/shard_map/experts_7/pallas_call | solution.py:445
  420.2 17.3 %shared_grad.1 = bf16[2,8,1056,128]{3,2,1,0:T(8,128)(2,1)} custom-call(bf16[2048,2048]{1,0:T(8,128)(2,1)} %get-tuple-element.325.tok, bf16[2048,2048]{1,0:T(8,128)(2,1)} %get-tuple-element.326.y_grad, bf16[2048,352]{1,0:T(8,128)(2,1)} %get-tuple-element.327.hidden, bf16[2,2048,352]{2,1,0:T(8,128)(2,1)} %get-tuple-element.328.gu), custom_call_target="tpu_custom_call" | custom-call | flops 138412032 | bytes 425984 | tf_op jit(solution)/shard_map/shared_grad/pallas_call | solution.py:971
  443.2 13.7 %fusion.2 = f32[1,2048,2,704]{1,3,2,0:T(8,128)} fusion(bf16[2,1536,704]{2,1,0:T(8,128)(2,1)} %get-tuple-element.333, bf16[1536,2048]{1,0:T(8,128)(2,1)S(1)} %bitcast.166), kind=kOutput, calls=%fused_computation.4 | convolution fusion | flops 8858370048 | bytes 22151168 | tf_op jit(solution)/shard_map/dot_general | solution.py:51
  474.9 10.9 %convolution_bitcast_fusion = f32[1,704,2048]{2,1,0:T(8,128)} fusion(bf16[1536,704]{1,0:T(8,128)(2,1)} %get-tuple-element.350, bf16[1536,2048]{1,0:T(8,128)(2,1)} %get-tuple-element.351), kind=kOutput, calls=%fused_computation.43 | convolution fusion | flops 4429185024 | bytes 14221312 | tf_op jit(solution)/shard_map/dot_general | solution.py:51
  493.6 10.5 %collective-permute-done.64 = bf16[128,2048]{1,0:T(8,128)(2,1)S(1)} collective-permute-done((bf16[128,2048]{1,0:T(8,128)(2,1)S(1)}, bf16[128,2048]{1,0:T(8,128)(2,1)S(1)}, u32[]{:S(2)}, u32[]{:S(2)}) %collective-permute-start.64) | collective-permute-done | bytes 524320 | tf_op jit(solution)/shard_map/ppermute | solution.py:560
  516.7 6.8 collective-permute-done.66
  527.6 4.7 all-to-all-start.2
  551.1 10.8 %attend_back.1 = (bf16[512,1536]{1,0:T(8,128)(2,1)}, f32[1,1536]{1,0:T(1,128)}) custom-call(s32[8]{0:T(128)} %get-tuple-element.537.refs_0_, s32[2]{0:T(128)} %pad_add_fusion.refs_1_, bf16[256,2048]{1,0:T(8,128)(2,1)} %copy-done.4, bf16[256,2048]{1,0:T(8,128)(2,1)} %copy-done.8, bf16[512,512]{1,0:T(8,128)(2,1)} %get-tuple-element.361.refs_4_, ...), custom_call_target="tpu_custom_call" | custom-call | flops 33554432 | bytes 131072 | tf_op jit(solution)/shard_map/attend_back/pallas_call | solution.py:1075
  569.2 7.2 all-to-all-done.2
  579.1 9.6 %project_back.1 = (f32[256,2048]{1,0:T(8,128)}, bf16[256,2048]{1,0:T(8,128)(2,1)}) custom-call(s32[8]{0:T(128)} %get-tuple-element.537.refs_0_, bf16[512,1536]{1,0:T(8,128)(2,1)} %get-tuple-element.371.refs_1_, bf16[1024,512]{1,0:T(8,128)(2,1)} %bitcast.182, bf16[1024,512]{1,0:T(8,128)(2,1)} %copy-done.22, ...), custom_call_target="tpu_custom_call" | custom-call | flops 50331648 | bytes 196608 | tf_op jit(solution)/shard_map/project_back/pallas_call | solution.py:1123
  617.4 5.7 collective-permute-done.80
  623.5 25.3 %collective-permute-done.79 = bf16[128,2048]{1,0:T(8,128)(2,1)} collective-permute-done((bf16[128,2048]{1,0:T(8,128)(2,1)}, bf16[128,2048]{1,0:T(8,128)(2,1)}, u32[]{:S(2)}, u32[]{:S(2)}) %collective-permute-start.79) | collective-permute-done | bytes 524320 | tf_op jit(solution)/shard_map/ppermute | solution.py:560
  666.4 22.7 %collective-permute-done.84 = bf16[128,2048]{1,0:T(8,128)(2,1)} collective-permute-done((bf16[128,2048]{1,0:T(8,128)(2,1)}, bf16[128,2048]{1,0:T(8,128)(2,1)}, u32[]{:S(2)}, u32[]{:S(2)}) %collective-permute-start.84) | collective-permute-done | bytes 524320 | tf_op jit(solution)/shard_map/ppermute | solution.py:560
  709.5 4.8 fusion.15
  720.0 5.7 copy.209
  725.7 4.6 all-to-all-done.3
  (618 shorter events, 315.5 us)
Async XLA Ops:
  12.6 62.0 %collective-permute-start.12 = (bf16[128,2048]{1,0:T(8,128)(2,1)}, bf16[128,2048]{1,0:T(8,128)(2,1)}, u32[]{:S(2)}, u32[]{:S(2)}) collective-permute-start(bf16[128,2048]{1,0:T(8,128)(2,1)} %constant_dynamic-slice_fusion.5.refs_6_), channel_id=1, source_target_pairs={{0,1},{1,0},{2,3},{3,2},{4,5},{5,4},{6,7},{7,6},{8,9},{9,8},{10,11... | collective-permute-start | bytes 1572872 | tf_op jit(solution)/shard_map/ppermute | solution.py:616
  67.6 33.4 %collective-permute-start.4 = (bf16[256,2048]{1,0:T(8,128)(2,1)S(1)}, bf16[256,2048]{1,0:T(8,128)(2,1)S(1)}, u32[]{:S(2)}, u32[]{:S(2)}) collective-permute-start(bf16[256,2048]{1,0:T(8,128)(2,1)S(1)} %fusion.9.refs_2_), channel_id=1, source_target_pairs={{0,2},{2,0},{4,6},{6,4},{8,10},{10,8},{12,14},{14,12},{16,18},{18,... | collective-permute-start | bytes 3145736 | tf_op jit(solution)/shard_map/ppermute | solution.py:594
  126.4 55.2 %all-to-all-start = ((bf16[8,1056,128]{2,1,0:T(8,128)(2,1)}), bf16[8,1056,128]{2,1,0:T(8,128)(2,1)}, u32[]{:S(2)}, u32[]{:S(2)}) async-start(bf16[8,1056,128]{2,1,0:T(8,128)(2,1)} %bitcast.21), calls=%async_computation | async-start | bytes 4325376 | tf_op jit(solution)/shard_map/all_to_all | solution.py:782
  186.5 36.7 %collective-permute-start.23 = (bf16[384,2048]{1,0:T(8,128)(2,1)S(1)}, bf16[384,2048]{1,0:T(8,128)(2,1)S(1)}, u32[]{:S(2)}, u32[]{:S(2)}) collective-permute-start(bf16[384,2048]{1,0:T(8,128)(2,1)S(1)} %constant_dynamic-update-slice_fusion.refs_8_), channel_id=1, source_target_pairs={{0,8},{2,10},{8,16},{10,18},{16,24},{18,26},{24,28},{26,30},{28,20... | collective-permute-start | bytes 4718600 | tf_op jit(solution)/shard_map/ppermute | solution.py:560
  186.5 37.0 %collective-permute-start.24 = (bf16[384,2048]{1,0:T(8,128)(2,1)}, bf16[384,2048]{1,0:T(8,128)(2,1)S(1)}, u32[]{:S(2)}, u32[]{:S(2)}) collective-permute-start(bf16[384,2048]{1,0:T(8,128)(2,1)} %get-tuple-element.520.refs_10_), channel_id=1, source_target_pairs={{8,0},{10,2},{16,8},{18,10},{24,16},{26,18},{28,24},{30,26},{20,28... | collective-permute-start | bytes 4718600 | tf_op jit(solution)/shard_map/ppermute | solution.py:561
  231.8 46.4 %collective-permute-start.32 = (bf16[512,2048]{1,0:T(8,128)(2,1)}, bf16[512,2048]{1,0:T(8,128)(2,1)}, u32[]{:S(2)}, u32[]{:S(2)}) collective-permute-start(bf16[512,2048]{1,0:T(8,128)(2,1)} %get-tuple-element.237), channel_id=1, source_target_pairs={{0,2},{2,0},{4,6},{6,4},{8,10},{10,8},{12,14},{14,12},{16,18},{18,... | collective-permute-start | bytes 6291464 | tf_op jit(solution)/shard_map/ppermute | solution.py:594
  231.9 46.1 %collective-permute-start.26 = (bf16[384,2048]{1,0:T(8,128)(2,1)S(1)}, bf16[384,2048]{1,0:T(8,128)(2,1)S(1)}, u32[]{:S(2)}, u32[]{:S(2)}) collective-permute-start(bf16[384,2048]{1,0:T(8,128)(2,1)S(1)} %collective-permute-done.23.refs_4_.refs_8_), channel_id=1, source_target_pairs={{0,8},{2,10},{8,16},{10,18},{16,24},{18,26},{24,28},{26,30},{28,20... | collective-permute-start | bytes 4718600 | tf_op jit(solution)/shard_map/ppermute | solution.py:560
  233.3 44.9 %collective-permute-start.27 = (bf16[384,2048]{1,0:T(8,128)(2,1)S(1)}, bf16[384,2048]{1,0:T(8,128)(2,1)S(1)}, u32[]{:S(2)}, u32[]{:S(2)}) collective-permute-start(bf16[384,2048]{1,0:T(8,128)(2,1)S(1)} %collective-permute-done.24.refs_5_.refs_10_), channel_id=1, source_target_pairs={{8,0},{10,2},{16,8},{18,10},{24,16},{26,18},{28,24},{30,26},{20,28... | collective-permute-start | bytes 4718600 | tf_op jit(solution)/shard_map/ppermute | solution.py:561
  244.2 33.8 %collective-permute-start.28 = (bf16[256,2048]{1,0:T(8,128)(2,1)}, bf16[256,2048]{1,0:T(8,128)(2,1)}, u32[]{:S(2)}, u32[]{:S(2)}) collective-permute-start(bf16[256,2048]{1,0:T(8,128)(2,1)} %pad_maximum_fusion.1), channel_id=1, source_target_pairs={{0,1},{1,0},{2,3},{3,2},{4,5},{5,4},{6,7},{7,6},{8,9},{9,8},{10,11... | collective-permute-start | bytes 3145736 | tf_op jit(solution)/shard_map/ppermute | solution.py:616
  286.8 40.4 %collective-permute-start.40 = (bf16[1024,2048]{1,0:T(8,128)(2,1)}, bf16[1024,2048]{1,0:T(8,128)(2,1)}, u32[]{:S(2)}, u32[]{:S(2)}) collective-permute-start(bf16[1024,2048]{1,0:T(8,128)(2,1)} %get-tuple-element.254), channel_id=1, source_target_pairs={{0,2},{2,0},{4,6},{6,4},{8,10},{10,8},{12,14},{14,12},{16,18},{18,... | collective-permute-start | bytes 12582920 | tf_op jit(solution)/shard_map/ppermute | solution.py:594
  287.0 38.4 %collective-permute-start.34 = (bf16[384,2048]{1,0:T(8,128)(2,1)S(1)}, bf16[384,2048]{1,0:T(8,128)(2,1)S(1)}, u32[]{:S(2)}, u32[]{:S(2)}) collective-permute-start(bf16[384,2048]{1,0:T(8,128)(2,1)S(1)} %collective-permute-done.26.refs_4_.refs_8_), channel_id=1, source_target_pairs={{0,8},{2,10},{8,16},{10,18},{16,24},{18,26},{24,28},{26,30},{28,20... | collective-permute-start | bytes 4718600 | tf_op jit(solution)/shard_map/ppermute | solution.py:560
  288.7 36.8 %collective-permute-start.35 = (bf16[384,2048]{1,0:T(8,128)(2,1)S(1)}, bf16[384,2048]{1,0:T(8,128)(2,1)S(1)}, u32[]{:S(2)}, u32[]{:S(2)}) collective-permute-start(bf16[384,2048]{1,0:T(8,128)(2,1)S(1)} %collective-permute-done.27.refs_5_.refs_10_), channel_id=1, source_target_pairs={{8,0},{10,2},{16,8},{18,10},{24,16},{26,18},{28,24},{30,26},{20,28... | collective-permute-start | bytes 4718600 | tf_op jit(solution)/shard_map/ppermute | solution.py:561
  290.7 34.6 %collective-permute-start.36 = (bf16[256,2048]{1,0:T(8,128)(2,1)}, bf16[256,2048]{1,0:T(8,128)(2,1)}, u32[]{:S(2)}, u32[]{:S(2)}) collective-permute-start(bf16[256,2048]{1,0:T(8,128)(2,1)} %pad_maximum_fusion.2), channel_id=1, source_target_pairs={{0,1},{1,0},{2,3},{3,2},{4,5},{5,4},{6,7},{7,6},{8,9},{9,8},{10,11... | collective-permute-start | bytes 3145736 | tf_op jit(solution)/shard_map/ppermute | solution.py:616
  335.7 40.2 %collective-permute-start.48 = (bf16[1024,2048]{1,0:T(8,128)(2,1)}, bf16[1024,2048]{1,0:T(8,128)(2,1)}, u32[]{:S(2)}, u32[]{:S(2)}) collective-permute-start(bf16[1024,2048]{1,0:T(8,128)(2,1)} %get-tuple-element.276), channel_id=1, source_target_pairs={{0,2},{2,0},{4,6},{6,4},{8,10},{10,8},{12,14},{14,12},{16,18},{18,... | collective-permute-start | bytes 12582920 | tf_op jit(solution)/shard_map/ppermute | solution.py:594
  339.4 36.5 %collective-permute-start.49 = (bf16[256,2048]{1,0:T(8,128)(2,1)S(1)}, bf16[256,2048]{1,0:T(8,128)(2,1)}, u32[]{:S(2)}, u32[]{:S(2)}) collective-permute-start(bf16[256,2048]{1,0:T(8,128)(2,1)S(1)} %pad_maximum_fusion.3), channel_id=1, source_target_pairs={{0,1},{1,0},{2,3},{3,2},{4,5},{5,4},{6,7},{7,6},{8,9},{9,8},{10,11... | collective-permute-start | bytes 3145736 | tf_op jit(solution)/shard_map/ppermute | solution.py:616
  341.9 34.0 %collective-permute-start.44 = (bf16[128,2048]{1,0:T(8,128)(2,1)S(1)}, bf16[128,2048]{1,0:T(8,128)(2,1)S(1)}, u32[]{:S(2)}, u32[]{:S(2)}) collective-permute-start(bf16[128,2048]{1,0:T(8,128)(2,1)S(1)} %pad_maximum_fusion.20), channel_id=1, source_target_pairs={{0,1},{1,0},{2,3},{3,2},{4,5},{5,4},{6,7},{7,6},{8,9},{9,8},{10,11... | collective-permute-start | bytes 1572872 | tf_op jit(solution)/shard_map/ppermute | solution.py:616
  342.6 33.3 %collective-permute-start.42 = (bf16[128,2048]{1,0:T(8,128)(2,1)}, bf16[128,2048]{1,0:T(8,128)(2,1)S(1)}, u32[]{:S(2)}, u32[]{:S(2)}) collective-permute-start(bf16[128,2048]{1,0:T(8,128)(2,1)} %slice.466), channel_id=1, source_target_pairs={{0,8},{2,10},{8,16},{10,18},{16,24},{18,26},{24,28},{26,30},{28,20... | collective-permute-start | bytes 1572872 | tf_op jit(solution)/shard_map/ppermute | solution.py:560
  419.5 39.4 %collective-permute-start.56 = (bf16[256,2048]{1,0:T(8,128)(2,1)}, bf16[256,2048]{1,0:T(8,128)(2,1)}, u32[]{:S(2)}, u32[]{:S(2)}) collective-permute-start(bf16[256,2048]{1,0:T(8,128)(2,1)} %pad_maximum_fusion.5), channel_id=1, source_target_pairs={{0,1},{1,0},{2,3},{3,2},{4,5},{5,4},{6,7},{7,6},{8,9},{9,8},{10,11... | collective-permute-start | bytes 3145736 | tf_op jit(solution)/shard_map/ppermute | solution.py:616
  527.6 48.8 %all-to-all-start.2 = ((bf16[8,1056,128]{2,1,0:T(8,128)(2,1)}), bf16[8,1056,128]{2,1,0:T(8,128)(2,1)}, u32[]{:S(2)}, u32[]{:S(2)}) async-start(bf16[8,1056,128]{2,1,0:T(8,128)(2,1)} %fusion.8), calls=%async_computation.2 | async-start | bytes 4325376 | tf_op jit(solution)/shard_map/all_to_all | solution.py:1031
  547.0 54.3 %collective-permute-start.75 = (bf16[256,2048]{1,0:T(8,128)(2,1)}, bf16[256,2048]{1,0:T(8,128)(2,1)}, u32[]{:S(2)}, u32[]{:S(2)}) collective-permute-start(bf16[256,2048]{1,0:T(8,128)(2,1)} %pad_maximum_fusion.6), channel_id=1, source_target_pairs={{0,1},{1,0},{2,3},{3,2},{4,5},{5,4},{6,7},{7,6},{8,9},{9,8},{10,11... | collective-permute-start | bytes 3145736 | tf_op jit(solution)/shard_map/ppermute | solution.py:616
  549.6 67.2 %collective-permute-start.81 = (bf16[256,2048]{1,0:T(8,128)(2,1)}, bf16[256,2048]{1,0:T(8,128)(2,1)}, u32[]{:S(2)}, u32[]{:S(2)}) collective-permute-start(bf16[256,2048]{1,0:T(8,128)(2,1)} %pad_maximum_fusion.16), channel_id=1, source_target_pairs={{0,1},{1,0},{2,3},{3,2},{4,5},{5,4},{6,7},{7,6},{8,9},{9,8},{10,11... | collective-permute-start | bytes 3145736 | tf_op jit(solution)/shard_map/ppermute | solution.py:616
  610.9 38.0 %collective-permute-start.78 = (bf16[256,2048]{1,0:T(8,128)(2,1)}, bf16[256,2048]{1,0:T(8,128)(2,1)}, u32[]{:S(2)}, u32[]{:S(2)}) collective-permute-start(bf16[256,2048]{1,0:T(8,128)(2,1)} %pad_maximum_fusion.15), channel_id=1, source_target_pairs={{8,0},{10,2},{16,8},{18,10},{24,16},{26,18},{28,24},{30,26},{20,28... | collective-permute-start | bytes 3145736 | tf_op jit(solution)/shard_map/ppermute | solution.py:561
  613.4 35.4 %collective-permute-start.77 = (bf16[256,2048]{1,0:T(8,128)(2,1)}, bf16[256,2048]{1,0:T(8,128)(2,1)}, u32[]{:S(2)}, u32[]{:S(2)}) collective-permute-start(bf16[256,2048]{1,0:T(8,128)(2,1)} %pad_maximum_fusion.14), channel_id=1, source_target_pairs={{0,8},{2,10},{8,16},{10,18},{16,24},{18,26},{24,28},{26,30},{28,20... | collective-permute-start | bytes 3145736 | tf_op jit(solution)/shard_map/ppermute | solution.py:560
  615.1 33.8 %collective-permute-start.79 = (bf16[128,2048]{1,0:T(8,128)(2,1)}, bf16[128,2048]{1,0:T(8,128)(2,1)}, u32[]{:S(2)}, u32[]{:S(2)}) collective-permute-start(bf16[128,2048]{1,0:T(8,128)(2,1)} %pad_maximum_fusion.23), channel_id=1, source_target_pairs={{0,8},{2,10},{8,16},{10,18},{16,24},{18,26},{24,28},{26,30},{28,20... | collective-permute-start | bytes 1572872 | tf_op jit(solution)/shard_map/ppermute | solution.py:560
  616.8 43.9 %collective-permute-start.86 = (bf16[256,2048]{1,0:T(8,128)(2,1)S(1)}, bf16[256,2048]{1,0:T(8,128)(2,1)S(1)}, u32[]{:S(2)}, u32[]{:S(2)}) collective-permute-start(bf16[256,2048]{1,0:T(8,128)(2,1)S(1)} %pad_maximum_fusion.17), channel_id=1, source_target_pairs={{0,1},{1,0},{2,3},{3,2},{4,5},{5,4},{6,7},{7,6},{8,9},{9,8},{10,11... | collective-permute-start | bytes 3145736 | tf_op jit(solution)/shard_map/ppermute | solution.py:616
  623.0 42.9 %collective-permute-start.87 = (bf16[256,2048]{1,0:T(8,128)(2,1)S(1)}, bf16[256,2048]{1,0:T(8,128)(2,1)}, u32[]{:S(2)}, u32[]{:S(2)}) collective-permute-start(bf16[256,2048]{1,0:T(8,128)(2,1)S(1)} %add_convert_fusion.6), channel_id=1, source_target_pairs={{0,1},{1,0},{2,3},{3,2},{4,5},{5,4},{6,7},{7,6},{8,9},{9,8},{10,11... | collective-permute-start | bytes 3145736 | tf_op jit(solution)/shard_map/ppermute | solution.py:616
  651.4 37.7 %collective-permute-start.83 = (bf16[256,2048]{1,0:T(8,128)(2,1)}, bf16[256,2048]{1,0:T(8,128)(2,1)}, u32[]{:S(2)}, u32[]{:S(2)}) collective-permute-start(bf16[256,2048]{1,0:T(8,128)(2,1)} %add_convert_fusion.4), channel_id=1, source_target_pairs={{8,0},{10,2},{16,8},{18,10},{24,16},{26,18},{28,24},{30,26},{20,28... | collective-permute-start | bytes 3145736 | tf_op jit(solution)/shard_map/ppermute | solution.py:561
  654.6 34.5 %collective-permute-start.82 = (bf16[256,2048]{1,0:T(8,128)(2,1)}, bf16[256,2048]{1,0:T(8,128)(2,1)}, u32[]{:S(2)}, u32[]{:S(2)}) collective-permute-start(bf16[256,2048]{1,0:T(8,128)(2,1)} %add_convert_fusion.5), channel_id=1, source_target_pairs={{0,8},{2,10},{8,16},{10,18},{16,24},{18,26},{24,28},{26,30},{28,20... | collective-permute-start | bytes 3145736 | tf_op jit(solution)/shard_map/ppermute | solution.py:560
  665.9 66.8 %collective-permute-start.92 = (bf16[128,2048]{1,0:T(8,128)(2,1)}, bf16[128,2048]{1,0:T(8,128)(2,1)}, u32[]{:S(2)}, u32[]{:S(2)}) collective-permute-start(bf16[128,2048]{1,0:T(8,128)(2,1)} %get-tuple-element.509), channel_id=1, source_target_pairs={{0,1},{1,0},{2,3},{3,2},{4,5},{5,4},{6,7},{7,6},{8,9},{9,8},{10,11... | collective-permute-start | bytes 1572872 | tf_op jit(solution)/shard_map/ppermute | solution.py:616
  693.1 39.6 %collective-permute-start.90 = (bf16[128,2048]{1,0:T(8,128)(2,1)}, bf16[128,2048]{1,0:T(8,128)(2,1)}, u32[]{:S(2)}, u32[]{:S(2)}) collective-permute-start(bf16[128,2048]{1,0:T(8,128)(2,1)} %get-tuple-element.504), channel_id=1, source_target_pairs={{0,8},{2,10},{8,16},{10,18},{16,24},{18,26},{24,28},{26,30},{28,20... | collective-permute-start | bytes 1572872 | tf_op jit(solution)/shard_map/ppermute | solution.py:560
  694.2 38.5 %collective-permute-start.91 = (bf16[128,2048]{1,0:T(8,128)(2,1)}, bf16[128,2048]{1,0:T(8,128)(2,1)}, u32[]{:S(2)}, u32[]{:S(2)}) collective-permute-start(bf16[128,2048]{1,0:T(8,128)(2,1)} %get-tuple-element.503), channel_id=1, source_target_pairs={{8,0},{10,2},{16,8},{18,10},{24,16},{26,18},{28,24},{30,26},{20,28... | collective-permute-start | bytes 1572872 | tf_op jit(solution)/shard_map/ppermute | solution.py:561
  697.7 35.0 %collective-permute-start.89 = (bf16[256,2048]{1,0:T(8,128)(2,1)}, bf16[256,2048]{1,0:T(8,128)(2,1)}, u32[]{:S(2)}, u32[]{:S(2)}) collective-permute-start(bf16[256,2048]{1,0:T(8,128)(2,1)} %add_convert_fusion.2), channel_id=1, source_target_pairs={{8,0},{10,2},{16,8},{18,10},{24,16},{26,18},{28,24},{30,26},{20,28... | collective-permute-start | bytes 3145736 | tf_op jit(solution)/shard_map/ppermute | solution.py:561
  (174 other events, 2102.0 us)

commit v5 on v4

--- a/solution.py
+++ b/solution.py
@@ -756,7 +756,7 @@
 
         up_cross = {0: swap_tensor(up_zero)}
         attn_w[-4:-2], sh_send, up_cross[0] = hold(attn_w[-4:-2], sh_send, up_cross[0])
-        up_next = ring.step(after(up_zero, attn_w[-3]))
+        up_next = ring.step(after(up_zero, *attn_w[-2:]))
         same_core = [[2 * i + c for i in range(chips)] for c in range(2)]
         inputs = tokens_in.astype(f32)
         first_b = rms_norm(inputs, gains_f[0]).astype(bf16)
@@ -778,9 +778,13 @@
             cost_estimate=cost(2 * 2 * length * width * 3 * half_cols, 12 * 1024 * 1024),
             name="attend",
         )(chip_arg, prefix_pair, first_b, first_o, bias.reshape(1, -1), cosine, sine, *attn_w)
-        mixed, up_next = hold(mixed, up_next)
         sh_mine = lax.all_to_all(
-            after(sh_send, up_next[0]), "expert", split_axis=0, concat_axis=0, tiled=True, axis_index_groups=same_core
+            after(sh_send, *attn_w[-2:]),
+            "expert",
+            split_axis=0,
+            concat_axis=0,
+            tiled=True,
+            axis_index_groups=same_core,
         )
         attn_own, attn_give = pl.pallas_call(
             functools.partial(project_kernel, chips + 1),
@@ -800,6 +804,7 @@
         )(chip_arg, mixed, *attn_w)
         attn_own = (attn_own + ring.swap_core(attn_give).astype(f32)).astype(bf16)
         attn_got = swap_tensor(attn_own)
+        attn_got, sh_mine, up_next = hold(attn_got, sh_mine, up_next)
         attn_out = attn_own.astype(f32) + attn_got.astype(f32)
         residual = inputs + attn_out
         second_b = rms_norm(residual, gains_f[1]).astype(bf16)
@@ -927,7 +932,7 @@
             if g >= 1:
                 give_got[g - 1] = swap_core(after(give_terms[g - 1], cross_o[g]))
                 now.append(give_got[g - 1])
-            if g >= 2:
+            if g >= 3:
                 grads = receive(g - 2)
                 grads, pair_o[g] = hold(grads, pair_o[g])
                 now.append(swap_tensor(grads))
@@ -957,13 +962,12 @@
                 pair[k], up_cross[k], *now = now
             if g >= 1:
                 give_got[g - 1] = now[0]
-            if g >= 2:
+            if g >= 3:
                 place_crossed(0, g - 2, now[1])
 
         rows_all, slots_all, hidden_all, gu_all, tok_all, y_all, s_hidden_all, s_gu_all = kept
         give_got[steps] = swap_core(give_terms[steps])
         near_far = receive(steps - 1)
-        near_far, give_got[steps] = hold(near_far, give_got[steps])
         grads = receive(steps)
         s_hidden_all, grads = hold(s_hidden_all, grads)
         far = ring.offsets[-1]
@@ -990,15 +994,17 @@
         def ring_terms(which, o):
             return [*terms[o][which], crossed[which, o]]
 
+        zero_got = swap_tensor(after(receive(0), grads))
         sending = ring.reduce_first(ring_terms(0, far))
         own, other = halves(sh_grad, 0)
         sh_got = swap_core(other)
         gu_all = after(gu_all, grads)
         sh_sum = (own.astype(f32) + sh_got.astype(f32)).astype(bf16)[0]
         expert_in_grad = mm(gu_all, rows_all, 1, 0).transpose(2, 0, 1)[None]
-        near_got, sending, sh_sum, expert_in_grad = hold(
-            near_got, sending, sh_sum, expert_in_grad
-        )
+        near_got, zero_got, sending, sh_sum, expert_in_grad = hold(
+            near_got, zero_got, sending, sh_sum, expert_in_grad
+        )
+        place_crossed(0, 0, zero_got)
         place_crossed(0, steps - 1, near_got)
         out_sent = {}
         for k in range(steps - 1, 0, -1):
@@ -1120,6 +1126,32 @@
             for o in qkv_parts
         }
         bias_grad = bias_grad[0]
+        def send_outs(k, going):
+            return ring.send_pair(
+                *ring.reduce_terms(ring_terms(1, k), ring_terms(1, -k), going, k == steps - 1)
+            )
+
+        second_f = second_b.astype(f32)
+        router_part = mm(second_b, logit_grad, 0, 0)
+        shared_gate_part = jnp.sum(gate_logit_grad[:, None] * second_f, axis=0)
+        early = jnp.concatenate(
+            [router_part, shared_gate_part[:, None], gain_two_grad[:, None]], axis=1
+        ).reshape(devices, rows_dev * (experts + 2))
+
+        def send_next(k, going):
+            return ring.send_pair(
+                *ring.reduce_terms(attn_parts[k], attn_parts[-k], going, k == steps - 1)
+            )
+
+        pieces = [attn_parts[o][0] for o in ring.offsets[:-1]]
+        going, crossing, proj_grad, pieces = hold(going, crossing, proj_grad, pieces)
+        for o, piece in zip(ring.offsets[:-1], pieces, strict=True):
+            attn_parts[o] = [piece]
+        place_crossed(1, steps - 1, crossing)
+        send = ring.reduce_terms(
+            attn_parts[steps - 1], attn_parts[1 - steps], going, steps > 1
+        )
+        proj_grad, *send = hold(proj_grad, *send)
         first_own, first_give = pl.pallas_call(
             functools.partial(project_back_kernel, chips + 1),
             out_shape=[
@@ -1137,31 +1169,9 @@
             name="project_back",
         )(chip_arg, proj_grad, *attn_w)
         first_own = (first_own + swap_core(first_give).astype(f32)).astype(bf16)
-        def send_outs(k, going):
-            return ring.send_pair(
-                *ring.reduce_terms(ring_terms(1, k), ring_terms(1, -k), going, k == steps - 1)
-            )
-
-        second_f = second_b.astype(f32)
-        router_part = mm(second_b, logit_grad, 0, 0)
-        shared_gate_part = jnp.sum(gate_logit_grad[:, None] * second_f, axis=0)
-        early = jnp.concatenate(
-            [router_part, shared_gate_part[:, None], gain_two_grad[:, None]], axis=1
-        ).reshape(devices, rows_dev * (experts + 2))
-
-        def send_next(k, going):
-            return ring.send_pair(
-                *ring.reduce_terms(attn_parts[k], attn_parts[-k], going, k == steps - 1)
-            )
-
-        pieces = [attn_parts[o][0] for o in ring.offsets[:-1]]
-        going, crossing, first_own, pieces = hold(going, crossing, first_own, pieces)
-        for o, piece in zip(ring.offsets[:-1], pieces, strict=True):
-            attn_parts[o] = [piece]
-        place_crossed(1, steps - 1, crossing)
         for k in range(steps - 1, -1, -1):
             if k > 0:
-                going = send_next(k, going)
+                going = ring.send_pair(*send) if k == steps - 1 else send_next(k, going)
                 out_sending = send_outs(k, out_sending)
             now = []
             if k > 0:
@@ -1210,7 +1220,8 @@
         early = late[:, rows_dev + count :]
         early = jnp.sum(early, axis=0).reshape(rows_dev, experts + 2)
         router_grad, shared_gate_grad = early[:, :experts], early[:, experts]
-        bias_got = jnp.sum(late[:, rows_dev : rows_dev + count].reshape(chips, 2, 3, heads, hd_dev), axis=0)
+        bias_got = late[:, rows_dev : rows_dev + count].reshape(chips, 2, 3, heads, hd_dev)
+        bias_got = jnp.sum(bias_got, axis=0)
         qkv_bias_grad = bias_got.transpose(1, 0, 2, 3).reshape(3, heads_t, hd_dev)
         gains_grad = jnp.stack([gain_one, early[:, experts + 1]], axis=0)
 

time: 765 us -> 751 us (0.982)
  waiting for transfers between devices: 243 us -> 232 us
    ppermute x21, waiting for transfers between devices: 93.9 us -> 120 us  [send_pair(): lax.ppermute(ahead, 'expert', self.next)]
    ppermute x4, waiting for transfers between devices: 44.2 us -> 23.8 us  [double_small(): other = lax.ppermute(held, 'expert', pairs)]
    ppermute x20, waiting for transfers between devices: 35.2 us -> 14.9 us  [swap_tensor(): return lax.ppermute(block, 'tensor', [(0, 1), (1, 0)])]
    all_to_all x1, waiting for transfers between devices: 17.8 us -> 0.01 us  [local(): lax.all_to_all(after(sh_send, *attn_w[-2:]), 'expert', split_axis=0, conc...]
    ppermute x21, waiting for transfers between devices: 9.95 us -> 26.2 us  [send_pair(): lax.ppermute(back, 'expert', self.prev)]
    convert_element_type x0 -> x4, other arithmetic: none -> 8.13 us  [receive(): crossing.append(ring.add_up(parts[1]).astype(bf16))]
    convert_element_type x8 -> x5, other arithmetic: 24.2 us -> 18.4 us  [receive_outs(): parts = [ring.add_up(part).astype(bf16) for part in out_gives[g]]]
    unnamed x228 -> x252, local copies, waits for them, and re-layouts: 24.9 us -> 28.4 us
  transfers between devices with their start and end apart: 99 -> 99, of which waited for: 46 -> 45; matrix products, arithmetic and copies ran while one was open for 24% -> 22% of each run, Pallas kernels for 24% -> 25%
where the time goes in v5:
time: 751 us; the launch traced here: 741 us
  waiting for transfers between devices  232 us (31%)
  Pallas kernels  187 us (25%)
  starting transfers between devices  113 us (15%)
  other arithmetic  97 us (13%)
  local copies, waits for them, and re-layouts  62.3 us (8%)
  matrix products  41.2 us (5%)
  between operations  9.02 us (1%)
    pallas_call x5, Pallas kernels, moe_call(): pl.pallas_call(functools.partial(moe_kernel, index, span, first, plan, si...  129 us
    ppermute x21, waiting for transfers between devices, send_pair(): lax.ppermute(ahead, 'expert', self.next)  120 us
    dot_general x22, matrix products, mm(): lax.dot_general(left, right, (((contract_left,), (contract_right,)), ((),...  41.2 us
    ppermute x29, waiting for transfers between devices, swap_core(): return lax.ppermute(block, 'expert', self.core)  32.6 us
    ppermute x21, starting transfers between devices, send_pair(): lax.ppermute(back, 'expert', self.prev)  31.8 us
    unnamed x252, local copies, waits for them, and re-layouts  28.4 us
    ppermute x21, starting transfers between devices, send_pair(): lax.ppermute(ahead, 'expert', self.next)  27.1 us
    ppermute x21, waiting for transfers between devices, send_pair(): lax.ppermute(back, 'expert', self.prev)  26.2 us
  transfers between devices with their start and end apart: 99, of which 45 were waited for; matrix products, arithmetic and copies ran while one was open for 22% of the time, Pallas kernels for 25%

profile of v5, /device:TPU:0, one launch (start us, length us, event | category | flops | bytes accessed | tf_op | source)
XLA Modules:
  0.0 741.2 jit_solution(12067627936247443270)
XLA Ops:
  16.5 15.6 %collective-permute-done.6.refs_8_.refs_3_.refs_10_ = bf16[1024,512]{1,0:T(8,128)(2,1)S(1)} collective-permute-done((bf16[1024,512]{1,0:T(8,128)(2,1)S(1)}, bf16[1024,512]{1,0:T(8,128)(2,1)S(1)}, u32[]{:S(2)}, u32[]{:S(2)}) %collective-permute-start.6) | collective-permute-done | bytes 1048608 | tf_op jit(solution)/shard_map/ppermute | solution.py:560
  36.3 22.6 %collective-permute-done.2 = bf16[4,4096]{1,0:T(4,128)(2,1)S(1)} collective-permute-done((bf16[4,4096]{1,0:T(4,128)(2,1)S(1)}, bf16[4,4096]{1,0:T(4,128)(2,1)S(1)}, u32[]{:S(2)}, u32[]{:S(2)}) %collective-permute-start.2) | collective-permute-done | bytes 32800 | tf_op jit(solution)/shard_map/ppermute | solution.py:598
  63.9 4.8 copy.191
  68.8 16.1 %collective-permute-done.10.refs_12_.refs_7_.refs_14_ = bf16[1024,512]{1,0:T(8,128)(2,1)S(1)} collective-permute-done((bf16[1024,512]{1,0:T(8,128)(2,1)}, bf16[1024,512]{1,0:T(8,128)(2,1)S(1)}, u32[]{:S(2)}, u32[]{:S(2)}) %collective-permute-start.10) | collective-permute-done | bytes 1048608 | tf_op jit(solution)/shard_map/ppermute | solution.py:560
  91.0 5.3 collective-permute-done.13.refs_14_.refs_9_.refs_16_
  110.6 9.9 %attend.1 = (bf16[512,512]{1,0:T(8,128)(2,1)}, bf16[512,512]{1,0:T(8,128)(2,1)}, bf16[512,512]{1,0:T(8,128)(2,1)}, bf16[512,512]{1,0:T(8,128)(2,1)}) custom-call(s32[8]{0:T(128)} %get-tuple-element.543.refs_0_, s32[2]{0:T(128)} %pad_add_fusion.refs_1_, bf16[256,2048]{1,0:T(8,128)(2,1)} %copy-done.1, bf16[256,2048]{1,0:T(8,128)(2,1)} %copy-done.5, ...), custom_call_target="tpu_custom_call" | custom-call | flops 50331648 | bytes 196608 | tf_op jit(solution)/shard_map/attend/pallas_call | solution.py:768
  120.6 5.5 project.1
  139.1 10.3 %collective-permute-done.17 = bf16[128,2048]{1,0:T(8,128)(2,1)} collective-permute-done((bf16[128,2048]{1,0:T(8,128)(2,1)}, bf16[128,2048]{1,0:T(8,128)(2,1)}, u32[]{:S(2)}, u32[]{:S(2)}) %collective-permute-start.17) | collective-permute-done | bytes 524320 | tf_op jit(solution)/shard_map/ppermute | solution.py:560
  149.3 8.7 %collective-permute-done.18 = bf16[128,2048]{1,0:T(8,128)(2,1)} collective-permute-done((bf16[128,2048]{1,0:T(8,128)(2,1)}, bf16[128,2048]{1,0:T(8,128)(2,1)}, u32[]{:S(2)}, u32[]{:S(2)}) %collective-permute-start.18) | collective-permute-done | bytes 524320 | tf_op jit(solution)/shard_map/ppermute | solution.py:561
  165.4 6.3 collective-permute-start.23
  176.1 5.0 spread.1.refs_12_.refs_18_.refs_16_
  182.3 19.2 %experts_0.1 = (bf16[1536,2048]{1,0:T(8,128)(2,1)}, bf16[1536,2048]{1,0:T(8,128)(2,1)}, bf16[1536,704]{1,0:T(8,128)(2,1)}, bf16[2,1536,704]{2,1,0:T(8,128)(2,1)}...) custom-call(s32[2]{0:T(128)} %pad_add_fusion.1.refs_0_, ...), custom_call_target="tpu_custom_call" | custom-call | flops 86507520 | bytes 524288 | tf_op jit(solution)/shard_map/experts_0/pallas_call | solution.py:445
  217.3 9.7 %collective-permute-start.27 = (bf16[384,2048]{1,0:T(8,128)(2,1)S(1)}, bf16[384,2048]{1,0:T(8,128)(2,1)S(1)}, u32[]{:S(2)}, u32[]{:S(2)}) collective-permute-start(bf16[384,2048]{1,0:T(8,128)(2,1)S(1)} %collective-permute-done.24.refs_5_.refs_10_), channel_id=1, source_target_pairs={{8,0},{10,2},{16,8},{18,10},{24,16},{26,18},{28,24},{30,26},{20,28... | collective-permute-start | bytes 4718600 | tf_op jit(solution)/shard_map/ppermute | solution.py:561
  232.0 30.0 %experts_1.1 = (bf16[1536,2048]{1,0:T(8,128)(2,1)}, bf16[1536,2048]{1,0:T(8,128)(2,1)}, bf16[1536,704]{1,0:T(8,128)(2,1)}, bf16[2,1536,704]{2,1,0:T(8,128)(2,1)}...) custom-call(s32[2]{0:T(128)} %pad_add_fusion.1.refs_0_, ...), custom_call_target="tpu_custom_call", output_to_operand_aliasing={{0}: (19, {}), {1}: (20, {}), {2}: (21, {}), {3}: (22, {}),... | custom-call | flops 173015040 | bytes 1048576 | tf_op jit(solution)/shard_map/experts_1/pallas_call | solution.py:445
  276.1 30.2 %experts_3.1 = (bf16[1536,2048]{1,0:T(8,128)(2,1)}, bf16[1536,2048]{1,0:T(8,128)(2,1)}, bf16[1536,704]{1,0:T(8,128)(2,1)}, bf16[2,1536,704]{2,1,0:T(8,128)(2,1)}...) custom-call(s32[2]{0:T(128)} %pad_add_fusion.1.refs_0_, ...), custom_call_target="tpu_custom_call", output_to_operand_aliasing={{0}: (19, {}), {1}: (20, {}), {2}: (21, {}), {3}: (22, {}),... | custom-call | flops 173015040 | bytes 1048576 | tf_op jit(solution)/shard_map/experts_3/pallas_call | solution.py:445
  325.1 30.3 %experts_5.1 = (bf16[1536,2048]{1,0:T(8,128)(2,1)}, bf16[1536,2048]{1,0:T(8,128)(2,1)}, bf16[1536,704]{1,0:T(8,128)(2,1)}, bf16[2,1536,704]{2,1,0:T(8,128)(2,1)}...) custom-call(s32[2]{0:T(128)} %pad_add_fusion.1.refs_0_, ...), custom_call_target="tpu_custom_call", output_to_operand_aliasing={{0}: (19, {}), {1}: (20, {}), {2}: (21, {}), {3}: (22, {}),... | custom-call | flops 173015040 | bytes 1048576 | tf_op jit(solution)/shard_map/experts_5/pallas_call | solution.py:445
  365.7 19.6 %experts_7.1 = (bf16[1536,2048]{1,0:T(8,128)(2,1)}, bf16[1536,2048]{1,0:T(8,128)(2,1)}, bf16[1536,704]{1,0:T(8,128)(2,1)}, bf16[2,1536,704]{2,1,0:T(8,128)(2,1)}...) custom-call(s32[2]{0:T(128)} %pad_add_fusion.1.refs_0_, ...), custom_call_target="tpu_custom_call", output_to_operand_aliasing={{0}: (17, {}), {1}: (18, {}), {2}: (19, {}), {3}: (20, {}),... | custom-call | flops 86507520 | bytes 524288 | tf_op jit(solution)/shard_map/experts_7/pallas_call | solution.py:445
  402.2 17.2 %shared_grad.1 = bf16[2,8,1056,128]{3,2,1,0:T(8,128)(2,1)} custom-call(bf16[2048,2048]{1,0:T(8,128)(2,1)} %get-tuple-element.317.tok, bf16[2048,2048]{1,0:T(8,128)(2,1)} %get-tuple-element.318.y_grad, bf16[2048,352]{1,0:T(8,128)(2,1)} %get-tuple-element.319.hidden, bf16[2,2048,352]{2,1,0:T(8,128)(2,1)} %get-tuple-element.320.gu), custom_call_target="tpu_custom_call" | custom-call | flops 138412032 | bytes 425984 | tf_op jit(solution)/shard_map/shared_grad/pallas_call | solution.py:975
  428.1 13.7 %fusion.2 = f32[1,2048,2,704]{1,3,2,0:T(8,128)} fusion(bf16[2,1536,704]{2,1,0:T(8,128)(2,1)} %get-tuple-element.326, bf16[1536,2048]{1,0:T(8,128)(2,1)S(1)} %bitcast.166), kind=kOutput, calls=%fused_computation.4 | convolution fusion | flops 8858370048 | bytes 22151168 | tf_op jit(solution)/shard_map/dot_general | solution.py:51
  461.3 10.8 %convolution_bitcast_fusion = f32[1,704,2048]{2,1,0:T(8,128)} fusion(bf16[1536,704]{1,0:T(8,128)(2,1)} %get-tuple-element.347, bf16[1536,2048]{1,0:T(8,128)(2,1)} %get-tuple-element.348), kind=kOutput, calls=%fused_computation.43 | convolution fusion | flops 4429185024 | bytes 14221312 | tf_op jit(solution)/shard_map/dot_general | solution.py:51
  473.7 4.8 add_convert_fusion.16
  482.5 9.1 %collective-permute-done.64 = bf16[128,2048]{1,0:T(8,128)(2,1)S(1)} collective-permute-done((bf16[128,2048]{1,0:T(8,128)(2,1)S(1)}, bf16[128,2048]{1,0:T(8,128)(2,1)S(1)}, u32[]{:S(2)}, u32[]{:S(2)}) %collective-permute-start.64) | collective-permute-done | bytes 524320 | tf_op jit(solution)/shard_map/ppermute | solution.py:560
  503.0 8.4 %collective-permute-done.66 = bf16[128,2048]{1,0:T(8,128)(2,1)S(1)} collective-permute-done((bf16[128,2048]{1,0:T(8,128)(2,1)S(1)}, bf16[128,2048]{1,0:T(8,128)(2,1)S(1)}, u32[]{:S(2)}, u32[]{:S(2)}) %collective-permute-start.66) | collective-permute-done | bytes 524320 | tf_op jit(solution)/shard_map/ppermute | solution.py:560
  540.3 10.8 %attend_back.1 = (bf16[512,1536]{1,0:T(8,128)(2,1)}, f32[1,1536]{1,0:T(1,128)}) custom-call(s32[8]{0:T(128)} %get-tuple-element.543.refs_0_, s32[2]{0:T(128)} %pad_add_fusion.refs_1_, bf16[256,2048]{1,0:T(8,128)(2,1)} %copy-done.3, bf16[256,2048]{1,0:T(8,128)(2,1)} %copy-done.7, bf16[512,512]{1,0:T(8,128)(2,1)} %get-tuple-element.358.refs_4_, ...), custom_call_target="tpu_custom_call" | custom-call | flops 33554432 | bytes 131072 | tf_op jit(solution)/shard_map/attend_back/pallas_call | solution.py:1081
  558.4 6.4 all-to-all-done.2
  581.8 9.4 %project_back.1 = (f32[256,2048]{1,0:T(8,128)}, bf16[256,2048]{1,0:T(8,128)(2,1)}) custom-call(s32[8]{0:T(128)} %get-tuple-element.543.refs_0_, bf16[512,1536]{1,0:T(8,128)(2,1)} %get-tuple-element.387.refs_1_, bf16[1024,512]{1,0:T(8,128)(2,1)} %bitcast.182, bf16[1024,512]{1,0:T(8,128)(2,1)} %copy-done.22, ...), custom_call_target="tpu_custom_call" | custom-call | flops 50331648 | bytes 196608 | tf_op jit(solution)/shard_map/project_back/pallas_call | solution.py:1155
  600.0 8.7 %collective-permute-done.79 = bf16[128,2048]{1,0:T(8,128)(2,1)S(1)} collective-permute-done((bf16[128,2048]{1,0:T(8,128)(2,1)S(1)}, bf16[128,2048]{1,0:T(8,128)(2,1)S(1)}, u32[]{:S(2)}, u32[]{:S(2)}) %collective-permute-start.79) | collective-permute-done | bytes 524320 | tf_op jit(solution)/shard_map/ppermute | solution.py:561
  609.2 22.9 %collective-permute-done.78 = bf16[128,2048]{1,0:T(8,128)(2,1)S(1)} collective-permute-done((bf16[128,2048]{1,0:T(8,128)(2,1)S(1)}, bf16[128,2048]{1,0:T(8,128)(2,1)S(1)}, u32[]{:S(2)}, u32[]{:S(2)}) %collective-permute-start.78) | collective-permute-done | bytes 524320 | tf_op jit(solution)/shard_map/ppermute | solution.py:560
  644.1 27.0 %collective-permute-done.83 = bf16[128,2048]{1,0:T(8,128)(2,1)} collective-permute-done((bf16[128,2048]{1,0:T(8,128)(2,1)}, bf16[128,2048]{1,0:T(8,128)(2,1)}, u32[]{:S(2)}, u32[]{:S(2)}) %collective-permute-start.83) | collective-permute-done | bytes 524320 | tf_op jit(solution)/shard_map/ppermute | solution.py:560
  692.3 4.8 fusion.15
  702.9 5.7 copy.209
  708.5 7.7 %all-to-all-done.3 = f32[16,1,2528]{2,1,0:T(1,128)S(1)} async-done(((f32[16,1,2528]{2,1,0:T(1,128)}), f32[16,1,2528]{2,1,0:T(1,128)S(1)}, u32[]{:S(2)}, u32[]{:S(2)}) %all-to-all-start.3) | async-done | bytes 161824 | tf_op jit(solution)/shard_map/all_to_all | solution.py:1217
  (643 shorter events, 315.8 us)
Async XLA Ops:
  15.0 76.0 %collective-permute-start.12 = (bf16[128,2048]{1,0:T(8,128)(2,1)}, bf16[128,2048]{1,0:T(8,128)(2,1)}, u32[]{:S(2)}, u32[]{:S(2)}) collective-permute-start(bf16[128,2048]{1,0:T(8,128)(2,1)} %constant_dynamic-slice_fusion.5.refs_6_), channel_id=1, source_target_pairs={{0,1},{1,0},{2,3},{3,2},{4,5},{5,4},{6,7},{7,6},{8,9},{9,8},{10,11... | collective-permute-start | bytes 1572872 | tf_op jit(solution)/shard_map/ppermute | solution.py:616
  100.5 57.5 %all-to-all-start = ((bf16[8,1056,128]{2,1,0:T(8,128)(2,1)}), bf16[8,1056,128]{2,1,0:T(8,128)(2,1)}, u32[]{:S(2)}, u32[]{:S(2)}) async-start(bf16[8,1056,128]{2,1,0:T(8,128)(2,1)} %bitcast.186), calls=%async_computation | async-start | bytes 4325376 | tf_op jit(solution)/shard_map/all_to_all | solution.py:781
  165.4 40.2 %collective-permute-start.23 = (bf16[384,2048]{1,0:T(8,128)(2,1)S(1)}, bf16[384,2048]{1,0:T(8,128)(2,1)S(1)}, u32[]{:S(2)}, u32[]{:S(2)}) collective-permute-start(bf16[384,2048]{1,0:T(8,128)(2,1)S(1)} %constant_dynamic-update-slice_fusion.refs_8_), channel_id=1, source_target_pairs={{0,8},{2,10},{8,16},{10,18},{16,24},{18,26},{24,28},{26,30},{28,20... | collective-permute-start | bytes 4718600 | tf_op jit(solution)/shard_map/ppermute | solution.py:560
  171.7 36.3 %collective-permute-start.24 = (bf16[384,2048]{1,0:T(8,128)(2,1)}, bf16[384,2048]{1,0:T(8,128)(2,1)S(1)}, u32[]{:S(2)}, u32[]{:S(2)}) collective-permute-start(bf16[384,2048]{1,0:T(8,128)(2,1)} %get-tuple-element.526.refs_10_), channel_id=1, source_target_pairs={{8,0},{10,2},{16,8},{18,10},{24,16},{26,18},{28,24},{30,26},{20,28... | collective-permute-start | bytes 4718600 | tf_op jit(solution)/shard_map/ppermute | solution.py:561
  216.3 45.9 %collective-permute-start.32 = (bf16[512,2048]{1,0:T(8,128)(2,1)}, bf16[512,2048]{1,0:T(8,128)(2,1)}, u32[]{:S(2)}, u32[]{:S(2)}) collective-permute-start(bf16[512,2048]{1,0:T(8,128)(2,1)} %get-tuple-element.238), channel_id=1, source_target_pairs={{0,2},{2,0},{4,6},{6,4},{8,10},{10,8},{12,14},{14,12},{16,18},{18,... | collective-permute-start | bytes 6291464 | tf_op jit(solution)/shard_map/ppermute | solution.py:594
  216.5 45.6 %collective-permute-start.26 = (bf16[384,2048]{1,0:T(8,128)(2,1)S(1)}, bf16[384,2048]{1,0:T(8,128)(2,1)S(1)}, u32[]{:S(2)}, u32[]{:S(2)}) collective-permute-start(bf16[384,2048]{1,0:T(8,128)(2,1)S(1)} %collective-permute-done.23.refs_4_.refs_8_), channel_id=1, source_target_pairs={{0,8},{2,10},{8,16},{10,18},{16,24},{18,26},{24,28},{26,30},{28,20... | collective-permute-start | bytes 4718600 | tf_op jit(solution)/shard_map/ppermute | solution.py:560
  217.3 44.9 %collective-permute-start.27 = (bf16[384,2048]{1,0:T(8,128)(2,1)S(1)}, bf16[384,2048]{1,0:T(8,128)(2,1)S(1)}, u32[]{:S(2)}, u32[]{:S(2)}) collective-permute-start(bf16[384,2048]{1,0:T(8,128)(2,1)S(1)} %collective-permute-done.24.refs_5_.refs_10_), channel_id=1, source_target_pairs={{8,0},{10,2},{16,8},{18,10},{24,16},{26,18},{28,24},{30,26},{20,28... | collective-permute-start | bytes 4718600 | tf_op jit(solution)/shard_map/ppermute | solution.py:561
  228.2 33.8 %collective-permute-start.28 = (bf16[256,2048]{1,0:T(8,128)(2,1)}, bf16[256,2048]{1,0:T(8,128)(2,1)}, u32[]{:S(2)}, u32[]{:S(2)}) collective-permute-start(bf16[256,2048]{1,0:T(8,128)(2,1)} %pad_maximum_fusion.1), channel_id=1, source_target_pairs={{0,1},{1,0},{2,3},{3,2},{4,5},{5,4},{6,7},{7,6},{8,9},{9,8},{10,11... | collective-permute-start | bytes 3145736 | tf_op jit(solution)/shard_map/ppermute | solution.py:616
  270.8 37.8 %collective-permute-start.40 = (bf16[1024,2048]{1,0:T(8,128)(2,1)}, bf16[1024,2048]{1,0:T(8,128)(2,1)}, u32[]{:S(2)}, u32[]{:S(2)}) collective-permute-start(bf16[1024,2048]{1,0:T(8,128)(2,1)} %get-tuple-element.255), channel_id=1, source_target_pairs={{0,2},{2,0},{4,6},{6,4},{8,10},{10,8},{12,14},{14,12},{16,18},{18,... | collective-permute-start | bytes 12582920 | tf_op jit(solution)/shard_map/ppermute | solution.py:594
  270.9 36.7 %collective-permute-start.34 = (bf16[384,2048]{1,0:T(8,128)(2,1)S(1)}, bf16[384,2048]{1,0:T(8,128)(2,1)S(1)}, u32[]{:S(2)}, u32[]{:S(2)}) collective-permute-start(bf16[384,2048]{1,0:T(8,128)(2,1)S(1)} %collective-permute-done.26.refs_4_.refs_8_), channel_id=1, source_target_pairs={{0,8},{2,10},{8,16},{10,18},{16,24},{18,26},{24,28},{26,30},{28,20... | collective-permute-start | bytes 4718600 | tf_op jit(solution)/shard_map/ppermute | solution.py:560
  271.8 36.8 %collective-permute-start.35 = (bf16[384,2048]{1,0:T(8,128)(2,1)S(1)}, bf16[384,2048]{1,0:T(8,128)(2,1)S(1)}, u32[]{:S(2)}, u32[]{:S(2)}) collective-permute-start(bf16[384,2048]{1,0:T(8,128)(2,1)S(1)} %collective-permute-done.27.refs_5_.refs_10_), channel_id=1, source_target_pairs={{8,0},{10,2},{16,8},{18,10},{24,16},{26,18},{28,24},{30,26},{20,28... | collective-permute-start | bytes 4718600 | tf_op jit(solution)/shard_map/ppermute | solution.py:561
  317.1 40.1 %collective-permute-start.47 = (bf16[1024,2048]{1,0:T(8,128)(2,1)}, bf16[1024,2048]{1,0:T(8,128)(2,1)}, u32[]{:S(2)}, u32[]{:S(2)}) collective-permute-start(bf16[1024,2048]{1,0:T(8,128)(2,1)} %get-tuple-element.285), channel_id=1, source_target_pairs={{0,2},{2,0},{4,6},{6,4},{8,10},{10,8},{12,14},{14,12},{16,18},{18,... | collective-permute-start | bytes 12582920 | tf_op jit(solution)/shard_map/ppermute | solution.py:594
  320.5 36.7 %collective-permute-start.48 = (bf16[256,2048]{1,0:T(8,128)(2,1)}, bf16[256,2048]{1,0:T(8,128)(2,1)}, u32[]{:S(2)}, u32[]{:S(2)}) collective-permute-start(bf16[256,2048]{1,0:T(8,128)(2,1)} %pad_maximum_fusion.3), channel_id=1, source_target_pairs={{0,1},{1,0},{2,3},{3,2},{4,5},{5,4},{6,7},{7,6},{8,9},{9,8},{10,11... | collective-permute-start | bytes 3145736 | tf_op jit(solution)/shard_map/ppermute | solution.py:616
  322.3 34.9 %collective-permute-start.46 = (bf16[128,2048]{1,0:T(8,128)(2,1)S(1)}, bf16[128,2048]{1,0:T(8,128)(2,1)S(1)}, u32[]{:S(2)}, u32[]{:S(2)}) collective-permute-start(bf16[128,2048]{1,0:T(8,128)(2,1)S(1)} %pad_maximum_fusion.20), channel_id=1, source_target_pairs={{0,1},{1,0},{2,3},{3,2},{4,5},{5,4},{6,7},{7,6},{8,9},{9,8},{10,11... | collective-permute-start | bytes 1572872 | tf_op jit(solution)/shard_map/ppermute | solution.py:616
  322.8 34.3 %collective-permute-start.44 = (bf16[128,2048]{1,0:T(8,128)(2,1)S(1)}, bf16[128,2048]{1,0:T(8,128)(2,1)S(1)}, u32[]{:S(2)}, u32[]{:S(2)}) collective-permute-start(bf16[128,2048]{1,0:T(8,128)(2,1)S(1)} %slice.467), channel_id=1, source_target_pairs={{0,8},{2,10},{8,16},{10,18},{16,24},{18,26},{24,28},{26,30},{28,20... | collective-permute-start | bytes 1572872 | tf_op jit(solution)/shard_map/ppermute | solution.py:560
  323.6 33.6 %collective-permute-start.45 = (bf16[128,2048]{1,0:T(8,128)(2,1)S(1)}, bf16[128,2048]{1,0:T(8,128)(2,1)S(1)}, u32[]{:S(2)}, u32[]{:S(2)}) collective-permute-start(bf16[128,2048]{1,0:T(8,128)(2,1)S(1)} %slice.468), channel_id=1, source_target_pairs={{8,0},{10,2},{16,8},{18,10},{24,16},{26,18},{28,24},{30,26},{20,28... | collective-permute-start | bytes 1572872 | tf_op jit(solution)/shard_map/ppermute | solution.py:561
  401.7 42.1 %collective-permute-start.54 = (bf16[256,2048]{1,0:T(8,128)(2,1)}, bf16[256,2048]{1,0:T(8,128)(2,1)}, u32[]{:S(2)}, u32[]{:S(2)}) collective-permute-start(bf16[256,2048]{1,0:T(8,128)(2,1)} %pad_maximum_fusion.5), channel_id=1, source_target_pairs={{0,1},{1,0},{2,3},{3,2},{4,5},{5,4},{6,7},{7,6},{8,9},{9,8},{10,11... | collective-permute-start | bytes 3145736 | tf_op jit(solution)/shard_map/ppermute | solution.py:616
  515.9 48.9 %all-to-all-start.2 = ((bf16[8,1056,128]{2,1,0:T(8,128)(2,1)}), bf16[8,1056,128]{2,1,0:T(8,128)(2,1)}, u32[]{:S(2)}, u32[]{:S(2)}) async-start(bf16[8,1056,128]{2,1,0:T(8,128)(2,1)} %fusion.8), calls=%async_computation.2 | async-start | bytes 4325376 | tf_op jit(solution)/shard_map/all_to_all | solution.py:1037
  535.0 43.4 %collective-permute-start.75 = (bf16[256,2048]{1,0:T(8,128)(2,1)}, bf16[256,2048]{1,0:T(8,128)(2,1)}, u32[]{:S(2)}, u32[]{:S(2)}) collective-permute-start(bf16[256,2048]{1,0:T(8,128)(2,1)} %pad_maximum_fusion.6), channel_id=1, source_target_pairs={{0,1},{1,0},{2,3},{3,2},{4,5},{5,4},{6,7},{7,6},{8,9},{9,8},{10,11... | collective-permute-start | bytes 3145736 | tf_op jit(solution)/shard_map/ppermute | solution.py:616
  537.6 61.0 %collective-permute-start.80 = (bf16[256,2048]{1,0:T(8,128)(2,1)}, bf16[256,2048]{1,0:T(8,128)(2,1)}, u32[]{:S(2)}, u32[]{:S(2)}) collective-permute-start(bf16[256,2048]{1,0:T(8,128)(2,1)} %pad_maximum_fusion.16), channel_id=1, source_target_pairs={{0,1},{1,0},{2,3},{3,2},{4,5},{5,4},{6,7},{7,6},{8,9},{9,8},{10,11... | collective-permute-start | bytes 3145736 | tf_op jit(solution)/shard_map/ppermute | solution.py:616
  595.3 36.8 %collective-permute-start.76 = (bf16[256,2048]{1,0:T(8,128)(2,1)}, bf16[256,2048]{1,0:T(8,128)(2,1)S(1)}, u32[]{:S(2)}, u32[]{:S(2)}) collective-permute-start(bf16[256,2048]{1,0:T(8,128)(2,1)} %pad_maximum_fusion.14), channel_id=1, source_target_pairs={{0,8},{2,10},{8,16},{10,18},{16,24},{18,26},{24,28},{26,30},{28,20... | collective-permute-start | bytes 3145736 | tf_op jit(solution)/shard_map/ppermute | solution.py:560
  596.0 36.0 %collective-permute-start.77 = (bf16[256,2048]{1,0:T(8,128)(2,1)}, bf16[256,2048]{1,0:T(8,128)(2,1)S(1)}, u32[]{:S(2)}, u32[]{:S(2)}) collective-permute-start(bf16[256,2048]{1,0:T(8,128)(2,1)} %pad_maximum_fusion.15), channel_id=1, source_target_pairs={{8,0},{10,2},{16,8},{18,10},{24,16},{26,18},{28,24},{30,26},{20,28... | collective-permute-start | bytes 3145736 | tf_op jit(solution)/shard_map/ppermute | solution.py:561
  597.5 34.6 %collective-permute-start.78 = (bf16[128,2048]{1,0:T(8,128)(2,1)S(1)}, bf16[128,2048]{1,0:T(8,128)(2,1)S(1)}, u32[]{:S(2)}, u32[]{:S(2)}) collective-permute-start(bf16[128,2048]{1,0:T(8,128)(2,1)S(1)} %pad_maximum_fusion.23), channel_id=1, source_target_pairs={{0,8},{2,10},{8,16},{10,18},{16,24},{18,26},{24,28},{26,30},{28,20... | collective-permute-start | bytes 1572872 | tf_op jit(solution)/shard_map/ppermute | solution.py:560
  599.5 41.6 %collective-permute-start.85 = (bf16[256,2048]{1,0:T(8,128)(2,1)S(1)}, bf16[256,2048]{1,0:T(8,128)(2,1)S(1)}, u32[]{:S(2)}, u32[]{:S(2)}) collective-permute-start(bf16[256,2048]{1,0:T(8,128)(2,1)S(1)} %copy-done.70), channel_id=1, source_target_pairs={{0,1},{1,0},{2,3},{3,2},{4,5},{5,4},{6,7},{7,6},{8,9},{9,8},{10,11... | collective-permute-start | bytes 3145736 | tf_op jit(solution)/shard_map/ppermute | solution.py:616
  608.7 62.9 %collective-permute-start.87 = (bf16[256,2048]{1,0:T(8,128)(2,1)S(1)}, bf16[256,2048]{1,0:T(8,128)(2,1)S(1)}, u32[]{:S(2)}, u32[]{:S(2)}) collective-permute-start(bf16[256,2048]{1,0:T(8,128)(2,1)S(1)} %add_convert_fusion.4), channel_id=1, source_target_pairs={{0,1},{1,0},{2,3},{3,2},{4,5},{5,4},{6,7},{7,6},{8,9},{9,8},{10,11... | collective-permute-start | bytes 3145736 | tf_op jit(solution)/shard_map/ppermute | solution.py:616
  633.4 38.2 %collective-permute-start.82 = (bf16[256,2048]{1,0:T(8,128)(2,1)}, bf16[256,2048]{1,0:T(8,128)(2,1)}, u32[]{:S(2)}, u32[]{:S(2)}) collective-permute-start(bf16[256,2048]{1,0:T(8,128)(2,1)} %add_convert_fusion.5), channel_id=1, source_target_pairs={{8,0},{10,2},{16,8},{18,10},{24,16},{26,18},{28,24},{30,26},{20,28... | collective-permute-start | bytes 3145736 | tf_op jit(solution)/shard_map/ppermute | solution.py:561
  635.1 36.5 %collective-permute-start.81 = (bf16[256,2048]{1,0:T(8,128)(2,1)}, bf16[256,2048]{1,0:T(8,128)(2,1)}, u32[]{:S(2)}, u32[]{:S(2)}) collective-permute-start(bf16[256,2048]{1,0:T(8,128)(2,1)} %add_convert_fusion.6), channel_id=1, source_target_pairs={{0,8},{2,10},{8,16},{10,18},{16,24},{18,26},{24,28},{26,30},{28,20... | collective-permute-start | bytes 3145736 | tf_op jit(solution)/shard_map/ppermute | solution.py:560
  671.1 47.6 %collective-permute-start.92 = (bf16[128,2048]{1,0:T(8,128)(2,1)}, bf16[128,2048]{1,0:T(8,128)(2,1)}, u32[]{:S(2)}, u32[]{:S(2)}) collective-permute-start(bf16[128,2048]{1,0:T(8,128)(2,1)} %get-tuple-element.512), channel_id=1, source_target_pairs={{0,1},{1,0},{2,3},{3,2},{4,5},{5,4},{6,7},{7,6},{8,9},{9,8},{10,11... | collective-permute-start | bytes 1572872 | tf_op jit(solution)/shard_map/ppermute | solution.py:616
  675.9 42.8 %collective-permute-start.90 = (bf16[128,2048]{1,0:T(8,128)(2,1)}, bf16[128,2048]{1,0:T(8,128)(2,1)}, u32[]{:S(2)}, u32[]{:S(2)}) collective-permute-start(bf16[128,2048]{1,0:T(8,128)(2,1)} %get-tuple-element.507), channel_id=1, source_target_pairs={{0,8},{2,10},{8,16},{10,18},{16,24},{18,26},{24,28},{26,30},{28,20... | collective-permute-start | bytes 1572872 | tf_op jit(solution)/shard_map/ppermute | solution.py:560
  677.6 41.0 %collective-permute-start.91 = (bf16[128,2048]{1,0:T(8,128)(2,1)}, bf16[128,2048]{1,0:T(8,128)(2,1)}, u32[]{:S(2)}, u32[]{:S(2)}) collective-permute-start(bf16[128,2048]{1,0:T(8,128)(2,1)} %get-tuple-element.506), channel_id=1, source_target_pairs={{8,0},{10,2},{16,8},{18,10},{24,16},{26,18},{28,24},{30,26},{20,28... | collective-permute-start | bytes 1572872 | tf_op jit(solution)/shard_map/ppermute | solution.py:561
  680.8 37.9 %collective-permute-start.89 = (bf16[256,2048]{1,0:T(8,128)(2,1)}, bf16[256,2048]{1,0:T(8,128)(2,1)}, u32[]{:S(2)}, u32[]{:S(2)}) collective-permute-start(bf16[256,2048]{1,0:T(8,128)(2,1)} %add_convert_fusion.2), channel_id=1, source_target_pairs={{8,0},{10,2},{16,8},{18,10},{24,16},{26,18},{28,24},{30,26},{20,28... | collective-permute-start | bytes 3145736 | tf_op jit(solution)/shard_map/ppermute | solution.py:561
  684.9 33.8 %collective-permute-start.88 = (bf16[256,2048]{1,0:T(8,128)(2,1)}, bf16[256,2048]{1,0:T(8,128)(2,1)}, u32[]{:S(2)}, u32[]{:S(2)}) collective-permute-start(bf16[256,2048]{1,0:T(8,128)(2,1)} %add_convert_fusion.3), channel_id=1, source_target_pairs={{0,8},{2,10},{8,16},{10,18},{16,24},{18,26},{24,28},{26,30},{28,20... | collective-permute-start | bytes 3145736 | tf_op jit(solution)/shard_map/ppermute | solution.py:560
  (187 other events, 2113.1 us)

commit v6 on v5

--- a/solution.py
+++ b/solution.py
@@ -1013,8 +1013,7 @@
             )
             now = []
             if k == steps - 1:
-                hidden_all, send, far_outs = hold(hidden_all, send, receive_outs(steps))
-                expert_out_grad = mm(hidden_all, slots_all, 0, 0)[None]
+                send, far_outs = hold(send, receive_outs(steps))
                 out_sent[steps] = swap_tensor(far_outs)
                 dots = jnp.concatenate(after_all(dot_rows, send[0]), axis=0)
                 sdots = jnp.concatenate([dots[:, 2:3], jnp.zeros_like(dots[:, 2:3])], axis=1)
@@ -1026,11 +1025,11 @@
                 dot_got = jnp.concatenate(
                     [dot_got[:, 0], jnp.sum(dot_got[:, 1], axis=0)[None]], axis=0
                 )
-                now = [out_sent[steps], dot_got, expert_out_grad]
+                now = [out_sent[steps], dot_got]
             sending = ring.send_pair(*send)
             sending, *now = hold(sending, *now)
             if k == steps - 1:
-                out_sent[steps], dot_got, expert_out_grad = now
+                out_sent[steps], dot_got = now
         place_crossed(1, steps, out_sent[steps])
         dot_got = dot_got + swap_tensor(dot_got)
         second_half = ring.add_up([*ring_terms(0, 0), *sending]).astype(bf16)
@@ -1151,7 +1150,8 @@
         send = ring.reduce_terms(
             attn_parts[steps - 1], attn_parts[1 - steps], going, steps > 1
         )
-        proj_grad, *send = hold(proj_grad, *send)
+        proj_grad, hidden_all, *send = hold(proj_grad, hidden_all, *send)
+        expert_out_grad = mm(hidden_all, slots_all, 0, 0)[None]
         first_own, first_give = pl.pallas_call(
             functools.partial(project_back_kernel, chips + 1),
             out_shape=[
@@ -1185,8 +1185,12 @@
                 break
             if k == 2:
                 now.append(sh_back)
+            if k == steps - 1:
+                now.append(expert_out_grad)
             going, out_sending, *now = hold(going, out_sending, *now)
             place_crossed(1, k - 1, now[0])
+            if k == steps - 1:
+                expert_out_grad = now[-1]
             if k == 2:
                 sh_back = now[-1]
             if k == steps - 2:

time: 751 us -> 743 us (0.989)
    ppermute x21, waiting for transfers between devices: 26.2 us -> 18.6 us  [send_pair(): lax.ppermute(back, 'expert', self.prev)]
    unnamed x252 -> x258, local copies, waits for them, and re-layouts: 28.4 us -> 28.7 us
  transfers between devices with their start and end apart: 99 -> 99, of which waited for: 45 -> 44; matrix products, arithmetic and copies ran while one was open for 22% -> 22% of each run, Pallas kernels for 25% -> 25%
where the time goes in v6:
time: 743 us; the launch traced here: 738 us
  waiting for transfers between devices  232 us (31%)
  Pallas kernels  187 us (25%)
  starting transfers between devices  111 us (15%)
  other arithmetic  99.1 us (13%)
  local copies, waits for them, and re-layouts  62.5 us (8%)
  matrix products  36.6 us (5%)
  between operations  8.72 us (1%)
    pallas_call x5, Pallas kernels, moe_call(): pl.pallas_call(functools.partial(moe_kernel, index, span, first, plan, si...  129 us
    ppermute x21, waiting for transfers between devices, send_pair(): lax.ppermute(ahead, 'expert', self.next)  120 us
    dot_general x22, matrix products, mm(): lax.dot_general(left, right, (((contract_left,), (contract_right,)), ((),...  36.6 us
    ppermute x29, waiting for transfers between devices, swap_core(): return lax.ppermute(block, 'expert', self.core)  32.7 us
    ppermute x21, starting transfers between devices, send_pair(): lax.ppermute(back, 'expert', self.prev)  30.7 us
    unnamed x258, local copies, waits for them, and re-layouts  28.7 us
    ppermute x21, starting transfers between devices, send_pair(): lax.ppermute(ahead, 'expert', self.next)  27.5 us
    ppermute x20, starting transfers between devices, swap_tensor(): return lax.ppermute(block, 'tensor', [(0, 1), (1, 0)])  24.5 us
  transfers between devices with their start and end apart: 99, of which 44 were waited for; matrix products, arithmetic and copies ran while one was open for 22% of the time, Pallas kernels for 25%

profile of v6, /device:TPU:0, one launch (start us, length us, event | category | flops | bytes accessed | tf_op | source)
XLA Modules:
  0.0 737.6 jit_solution(3203640128171172253)
XLA Ops:
  16.5 15.7 %collective-permute-done.6.refs_8_.refs_3_.refs_10_ = bf16[1024,512]{1,0:T(8,128)(2,1)S(1)} collective-permute-done((bf16[1024,512]{1,0:T(8,128)(2,1)S(1)}, bf16[1024,512]{1,0:T(8,128)(2,1)S(1)}, u32[]{:S(2)}, u32[]{:S(2)}) %collective-permute-start.6) | collective-permute-done | bytes 1048608 | tf_op jit(solution)/shard_map/ppermute | solution.py:560
  36.3 22.6 %collective-permute-done.2 = bf16[4,4096]{1,0:T(4,128)(2,1)S(1)} collective-permute-done((bf16[4,4096]{1,0:T(4,128)(2,1)S(1)}, bf16[4,4096]{1,0:T(4,128)(2,1)S(1)}, u32[]{:S(2)}, u32[]{:S(2)}) %collective-permute-start.2) | collective-permute-done | bytes 32800 | tf_op jit(solution)/shard_map/ppermute | solution.py:598
  63.9 4.8 copy.191
  68.9 16.1 %collective-permute-done.10.refs_12_.refs_7_.refs_14_ = bf16[1024,512]{1,0:T(8,128)(2,1)S(1)} collective-permute-done((bf16[1024,512]{1,0:T(8,128)(2,1)}, bf16[1024,512]{1,0:T(8,128)(2,1)S(1)}, u32[]{:S(2)}, u32[]{:S(2)}) %collective-permute-start.10) | collective-permute-done | bytes 1048608 | tf_op jit(solution)/shard_map/ppermute | solution.py:560
  91.0 5.3 collective-permute-done.13.refs_14_.refs_9_.refs_16_
  110.6 9.9 %attend.1 = (bf16[512,512]{1,0:T(8,128)(2,1)}, bf16[512,512]{1,0:T(8,128)(2,1)}, bf16[512,512]{1,0:T(8,128)(2,1)}, bf16[512,512]{1,0:T(8,128)(2,1)}) custom-call(s32[8]{0:T(128)} %get-tuple-element.543.refs_0_, s32[2]{0:T(128)} %pad_add_fusion.refs_1_, bf16[256,2048]{1,0:T(8,128)(2,1)} %copy-done.1, bf16[256,2048]{1,0:T(8,128)(2,1)} %copy-done.5, ...), custom_call_target="tpu_custom_call" | custom-call | flops 50331648 | bytes 196608 | tf_op jit(solution)/shard_map/attend/pallas_call | solution.py:768
  120.5 5.5 project.1
  139.0 10.3 %collective-permute-done.17 = bf16[128,2048]{1,0:T(8,128)(2,1)} collective-permute-done((bf16[128,2048]{1,0:T(8,128)(2,1)}, bf16[128,2048]{1,0:T(8,128)(2,1)}, u32[]{:S(2)}, u32[]{:S(2)}) %collective-permute-start.17) | collective-permute-done | bytes 524320 | tf_op jit(solution)/shard_map/ppermute | solution.py:560
  149.3 8.7 %collective-permute-done.18 = bf16[128,2048]{1,0:T(8,128)(2,1)} collective-permute-done((bf16[128,2048]{1,0:T(8,128)(2,1)}, bf16[128,2048]{1,0:T(8,128)(2,1)}, u32[]{:S(2)}, u32[]{:S(2)}) %collective-permute-start.18) | collective-permute-done | bytes 524320 | tf_op jit(solution)/shard_map/ppermute | solution.py:561
  165.4 6.2 collective-permute-start.23
  176.0 5.0 spread.1.refs_12_.refs_18_.refs_16_
  182.2 19.2 %experts_0.1 = (bf16[1536,2048]{1,0:T(8,128)(2,1)}, bf16[1536,2048]{1,0:T(8,128)(2,1)}, bf16[1536,704]{1,0:T(8,128)(2,1)}, bf16[2,1536,704]{2,1,0:T(8,128)(2,1)}...) custom-call(s32[2]{0:T(128)} %pad_add_fusion.1.refs_0_, ...), custom_call_target="tpu_custom_call" | custom-call | flops 86507520 | bytes 524288 | tf_op jit(solution)/shard_map/experts_0/pallas_call | solution.py:445
  217.3 9.7 %collective-permute-start.27 = (bf16[384,2048]{1,0:T(8,128)(2,1)S(1)}, bf16[384,2048]{1,0:T(8,128)(2,1)S(1)}, u32[]{:S(2)}, u32[]{:S(2)}) collective-permute-start(bf16[384,2048]{1,0:T(8,128)(2,1)S(1)} %collective-permute-done.24.refs_5_.refs_10_), channel_id=1, source_target_pairs={{8,0},{10,2},{16,8},{18,10},{24,16},{26,18},{28,24},{30,26},{20,28... | collective-permute-start | bytes 4718600 | tf_op jit(solution)/shard_map/ppermute | solution.py:561
  232.0 30.1 %experts_1.1 = (bf16[1536,2048]{1,0:T(8,128)(2,1)}, bf16[1536,2048]{1,0:T(8,128)(2,1)}, bf16[1536,704]{1,0:T(8,128)(2,1)}, bf16[2,1536,704]{2,1,0:T(8,128)(2,1)}...) custom-call(s32[2]{0:T(128)} %pad_add_fusion.1.refs_0_, ...), custom_call_target="tpu_custom_call", output_to_operand_aliasing={{0}: (19, {}), {1}: (20, {}), {2}: (21, {}), {3}: (22, {}),... | custom-call | flops 173015040 | bytes 1048576 | tf_op jit(solution)/shard_map/experts_1/pallas_call | solution.py:445
  276.0 30.2 %experts_3.1 = (bf16[1536,2048]{1,0:T(8,128)(2,1)}, bf16[1536,2048]{1,0:T(8,128)(2,1)}, bf16[1536,704]{1,0:T(8,128)(2,1)}, bf16[2,1536,704]{2,1,0:T(8,128)(2,1)}...) custom-call(s32[2]{0:T(128)} %pad_add_fusion.1.refs_0_, ...), custom_call_target="tpu_custom_call", output_to_operand_aliasing={{0}: (19, {}), {1}: (20, {}), {2}: (21, {}), {3}: (22, {}),... | custom-call | flops 173015040 | bytes 1048576 | tf_op jit(solution)/shard_map/experts_3/pallas_call | solution.py:445
  325.0 30.2 %experts_5.1 = (bf16[1536,2048]{1,0:T(8,128)(2,1)}, bf16[1536,2048]{1,0:T(8,128)(2,1)}, bf16[1536,704]{1,0:T(8,128)(2,1)}, bf16[2,1536,704]{2,1,0:T(8,128)(2,1)}...) custom-call(s32[2]{0:T(128)} %pad_add_fusion.1.refs_0_, ...), custom_call_target="tpu_custom_call", output_to_operand_aliasing={{0}: (19, {}), {1}: (20, {}), {2}: (21, {}), {3}: (22, {}),... | custom-call | flops 173015040 | bytes 1048576 | tf_op jit(solution)/shard_map/experts_5/pallas_call | solution.py:445
  365.6 19.7 %experts_7.1 = (bf16[1536,2048]{1,0:T(8,128)(2,1)}, bf16[1536,2048]{1,0:T(8,128)(2,1)}, bf16[1536,704]{1,0:T(8,128)(2,1)}, bf16[2,1536,704]{2,1,0:T(8,128)(2,1)}...) custom-call(s32[2]{0:T(128)} %pad_add_fusion.1.refs_0_, ...), custom_call_target="tpu_custom_call", output_to_operand_aliasing={{0}: (17, {}), {1}: (18, {}), {2}: (19, {}), {3}: (20, {}),... | custom-call | flops 86507520 | bytes 524288 | tf_op jit(solution)/shard_map/experts_7/pallas_call | solution.py:445
  402.2 17.2 %shared_grad.1 = bf16[2,8,1056,128]{3,2,1,0:T(8,128)(2,1)} custom-call(bf16[2048,2048]{1,0:T(8,128)(2,1)} %get-tuple-element.317.tok, bf16[2048,2048]{1,0:T(8,128)(2,1)} %get-tuple-element.318.y_grad, bf16[2048,352]{1,0:T(8,128)(2,1)} %get-tuple-element.319.hidden, bf16[2,2048,352]{2,1,0:T(8,128)(2,1)} %get-tuple-element.320.gu), custom_call_target="tpu_custom_call" | custom-call | flops 138412032 | bytes 425984 | tf_op jit(solution)/shard_map/shared_grad/pallas_call | solution.py:975
  428.0 13.7 %fusion.2 = f32[1,2048,2,704]{1,3,2,0:T(8,128)} fusion(bf16[2,1536,704]{2,1,0:T(8,128)(2,1)} %get-tuple-element.326, bf16[1536,2048]{1,0:T(8,128)(2,1)S(1)} %bitcast.166), kind=kOutput, calls=%fused_computation.4 | convolution fusion | flops 8858370048 | bytes 22151168 | tf_op jit(solution)/shard_map/dot_general | solution.py:51
  460.1 6.8 all-to-all-done.1
  467.1 4.9 add_convert_fusion.16
  475.9 10.0 %collective-permute-done.64 = bf16[128,2048]{1,0:T(8,128)(2,1)S(1)} collective-permute-done((bf16[128,2048]{1,0:T(8,128)(2,1)S(1)}, bf16[128,2048]{1,0:T(8,128)(2,1)S(1)}, u32[]{:S(2)}, u32[]{:S(2)}) %collective-permute-start.64) | collective-permute-done | bytes 524320 | tf_op jit(solution)/shard_map/ppermute | solution.py:560
  497.5 7.9 %collective-permute-done.66 = bf16[128,2048]{1,0:T(8,128)(2,1)S(1)} collective-permute-done((bf16[128,2048]{1,0:T(8,128)(2,1)S(1)}, bf16[128,2048]{1,0:T(8,128)(2,1)S(1)}, u32[]{:S(2)}, u32[]{:S(2)}) %collective-permute-start.66) | collective-permute-done | bytes 524320 | tf_op jit(solution)/shard_map/ppermute | solution.py:560
  534.5 10.8 %attend_back.1 = (bf16[512,1536]{1,0:T(8,128)(2,1)}, f32[1,1536]{1,0:T(1,128)}) custom-call(s32[8]{0:T(128)} %get-tuple-element.543.refs_0_, s32[2]{0:T(128)} %pad_add_fusion.refs_1_, bf16[256,2048]{1,0:T(8,128)(2,1)} %copy-done.3, bf16[256,2048]{1,0:T(8,128)(2,1)} %copy-done.7, bf16[512,512]{1,0:T(8,128)(2,1)} %get-tuple-element.355.refs_4_, ...), custom_call_target="tpu_custom_call" | custom-call | flops 33554432 | bytes 131072 | tf_op jit(solution)/shard_map/attend_back/pallas_call | solution.py:1080
  552.7 7.7 %all-to-all-done.2 = bf16[8,1056,128]{2,1,0:T(8,128)(2,1)} async-done(((bf16[8,1056,128]{2,1,0:T(8,128)(2,1)}), bf16[8,1056,128]{2,1,0:T(8,128)(2,1)}, u32[]{:S(2)}, u32[]{:S(2)}) %all-to-all-start.2) | async-done | bytes 2162720 | tf_op jit(solution)/shard_map/all_to_all | solution.py:1036
  579.0 9.6 %project_back.1 = (f32[256,2048]{1,0:T(8,128)}, bf16[256,2048]{1,0:T(8,128)(2,1)}) custom-call(s32[8]{0:T(128)} %get-tuple-element.543.refs_0_, bf16[512,1536]{1,0:T(8,128)(2,1)} %get-tuple-element.387.refs_1_, bf16[1024,512]{1,0:T(8,128)(2,1)} %bitcast.184, bf16[1024,512]{1,0:T(8,128)(2,1)} %copy-done.23, ...), custom_call_target="tpu_custom_call" | custom-call | flops 50331648 | bytes 196608 | tf_op jit(solution)/shard_map/project_back/pallas_call | solution.py:1155
  594.6 6.5 convolution_bitcast_fusion
  606.5 22.8 %collective-permute-done.78 = bf16[128,2048]{1,0:T(8,128)(2,1)S(1)} collective-permute-done((bf16[128,2048]{1,0:T(8,128)(2,1)S(1)}, bf16[128,2048]{1,0:T(8,128)(2,1)S(1)}, u32[]{:S(2)}, u32[]{:S(2)}) %collective-permute-start.78) | collective-permute-done | bytes 524320 | tf_op jit(solution)/shard_map/ppermute | solution.py:560
  641.5 26.9 %collective-permute-done.83 = bf16[128,2048]{1,0:T(8,128)(2,1)} collective-permute-done((bf16[128,2048]{1,0:T(8,128)(2,1)}, bf16[128,2048]{1,0:T(8,128)(2,1)}, u32[]{:S(2)}, u32[]{:S(2)}) %collective-permute-start.83) | collective-permute-done | bytes 524320 | tf_op jit(solution)/shard_map/ppermute | solution.py:560
  689.1 4.8 fusion.15
  699.6 5.7 copy.209
  705.3 7.6 %all-to-all-done.3 = f32[16,1,2528]{2,1,0:T(1,128)S(1)} async-done(((f32[16,1,2528]{2,1,0:T(1,128)}), f32[16,1,2528]{2,1,0:T(1,128)S(1)}, u32[]{:S(2)}, u32[]{:S(2)}) %all-to-all-start.3) | async-done | bytes 161824 | tf_op jit(solution)/shard_map/all_to_all | solution.py:1221
  (649 shorter events, 316.9 us)
Async XLA Ops:
  15.0 76.0 %collective-permute-start.12 = (bf16[128,2048]{1,0:T(8,128)(2,1)}, bf16[128,2048]{1,0:T(8,128)(2,1)}, u32[]{:S(2)}, u32[]{:S(2)}) collective-permute-start(bf16[128,2048]{1,0:T(8,128)(2,1)} %constant_dynamic-slice_fusion.5.refs_6_), channel_id=1, source_target_pairs={{0,1},{1,0},{2,3},{3,2},{4,5},{5,4},{6,7},{7,6},{8,9},{9,8},{10,11... | collective-permute-start | bytes 1572872 | tf_op jit(solution)/shard_map/ppermute | solution.py:616
  100.5 57.5 %all-to-all-start = ((bf16[8,1056,128]{2,1,0:T(8,128)(2,1)}), bf16[8,1056,128]{2,1,0:T(8,128)(2,1)}, u32[]{:S(2)}, u32[]{:S(2)}) async-start(bf16[8,1056,128]{2,1,0:T(8,128)(2,1)} %bitcast.188), calls=%async_computation | async-start | bytes 4325376 | tf_op jit(solution)/shard_map/all_to_all | solution.py:781
  165.4 40.2 %collective-permute-start.23 = (bf16[384,2048]{1,0:T(8,128)(2,1)S(1)}, bf16[384,2048]{1,0:T(8,128)(2,1)S(1)}, u32[]{:S(2)}, u32[]{:S(2)}) collective-permute-start(bf16[384,2048]{1,0:T(8,128)(2,1)S(1)} %constant_dynamic-update-slice_fusion.refs_8_), channel_id=1, source_target_pairs={{0,8},{2,10},{8,16},{10,18},{16,24},{18,26},{24,28},{26,30},{28,20... | collective-permute-start | bytes 4718600 | tf_op jit(solution)/shard_map/ppermute | solution.py:560
  171.6 36.3 %collective-permute-start.24 = (bf16[384,2048]{1,0:T(8,128)(2,1)}, bf16[384,2048]{1,0:T(8,128)(2,1)S(1)}, u32[]{:S(2)}, u32[]{:S(2)}) collective-permute-start(bf16[384,2048]{1,0:T(8,128)(2,1)} %get-tuple-element.526.refs_10_), channel_id=1, source_target_pairs={{8,0},{10,2},{16,8},{18,10},{24,16},{26,18},{28,24},{30,26},{20,28... | collective-permute-start | bytes 4718600 | tf_op jit(solution)/shard_map/ppermute | solution.py:561
  216.3 45.9 %collective-permute-start.32 = (bf16[512,2048]{1,0:T(8,128)(2,1)}, bf16[512,2048]{1,0:T(8,128)(2,1)}, u32[]{:S(2)}, u32[]{:S(2)}) collective-permute-start(bf16[512,2048]{1,0:T(8,128)(2,1)} %get-tuple-element.238), channel_id=1, source_target_pairs={{0,2},{2,0},{4,6},{6,4},{8,10},{10,8},{12,14},{14,12},{16,18},{18,... | collective-permute-start | bytes 6291464 | tf_op jit(solution)/shard_map/ppermute | solution.py:594
  216.4 45.7 %collective-permute-start.26 = (bf16[384,2048]{1,0:T(8,128)(2,1)S(1)}, bf16[384,2048]{1,0:T(8,128)(2,1)S(1)}, u32[]{:S(2)}, u32[]{:S(2)}) collective-permute-start(bf16[384,2048]{1,0:T(8,128)(2,1)S(1)} %collective-permute-done.23.refs_4_.refs_8_), channel_id=1, source_target_pairs={{0,8},{2,10},{8,16},{10,18},{16,24},{18,26},{24,28},{26,30},{28,20... | collective-permute-start | bytes 4718600 | tf_op jit(solution)/shard_map/ppermute | solution.py:560
  217.3 44.9 %collective-permute-start.27 = (bf16[384,2048]{1,0:T(8,128)(2,1)S(1)}, bf16[384,2048]{1,0:T(8,128)(2,1)S(1)}, u32[]{:S(2)}, u32[]{:S(2)}) collective-permute-start(bf16[384,2048]{1,0:T(8,128)(2,1)S(1)} %collective-permute-done.24.refs_5_.refs_10_), channel_id=1, source_target_pairs={{8,0},{10,2},{16,8},{18,10},{24,16},{26,18},{28,24},{30,26},{20,28... | collective-permute-start | bytes 4718600 | tf_op jit(solution)/shard_map/ppermute | solution.py:561
  228.2 33.9 %collective-permute-start.28 = (bf16[256,2048]{1,0:T(8,128)(2,1)}, bf16[256,2048]{1,0:T(8,128)(2,1)}, u32[]{:S(2)}, u32[]{:S(2)}) collective-permute-start(bf16[256,2048]{1,0:T(8,128)(2,1)} %pad_maximum_fusion.1), channel_id=1, source_target_pairs={{0,1},{1,0},{2,3},{3,2},{4,5},{5,4},{6,7},{7,6},{8,9},{9,8},{10,11... | collective-permute-start | bytes 3145736 | tf_op jit(solution)/shard_map/ppermute | solution.py:616
  270.8 37.8 %collective-permute-start.40 = (bf16[1024,2048]{1,0:T(8,128)(2,1)}, bf16[1024,2048]{1,0:T(8,128)(2,1)}, u32[]{:S(2)}, u32[]{:S(2)}) collective-permute-start(bf16[1024,2048]{1,0:T(8,128)(2,1)} %get-tuple-element.255), channel_id=1, source_target_pairs={{0,2},{2,0},{4,6},{6,4},{8,10},{10,8},{12,14},{14,12},{16,18},{18,... | collective-permute-start | bytes 12582920 | tf_op jit(solution)/shard_map/ppermute | solution.py:594
  270.9 36.7 %collective-permute-start.34 = (bf16[384,2048]{1,0:T(8,128)(2,1)S(1)}, bf16[384,2048]{1,0:T(8,128)(2,1)S(1)}, u32[]{:S(2)}, u32[]{:S(2)}) collective-permute-start(bf16[384,2048]{1,0:T(8,128)(2,1)S(1)} %collective-permute-done.26.refs_4_.refs_8_), channel_id=1, source_target_pairs={{0,8},{2,10},{8,16},{10,18},{16,24},{18,26},{24,28},{26,30},{28,20... | collective-permute-start | bytes 4718600 | tf_op jit(solution)/shard_map/ppermute | solution.py:560
  271.7 36.8 %collective-permute-start.35 = (bf16[384,2048]{1,0:T(8,128)(2,1)S(1)}, bf16[384,2048]{1,0:T(8,128)(2,1)S(1)}, u32[]{:S(2)}, u32[]{:S(2)}) collective-permute-start(bf16[384,2048]{1,0:T(8,128)(2,1)S(1)} %collective-permute-done.27.refs_5_.refs_10_), channel_id=1, source_target_pairs={{8,0},{10,2},{16,8},{18,10},{24,16},{26,18},{28,24},{30,26},{20,28... | collective-permute-start | bytes 4718600 | tf_op jit(solution)/shard_map/ppermute | solution.py:561
  274.5 31.6 %collective-permute-start.36 = (bf16[256,2048]{1,0:T(8,128)(2,1)}, bf16[256,2048]{1,0:T(8,128)(2,1)}, u32[]{:S(2)}, u32[]{:S(2)}) collective-permute-start(bf16[256,2048]{1,0:T(8,128)(2,1)} %pad_maximum_fusion.2), channel_id=1, source_target_pairs={{0,1},{1,0},{2,3},{3,2},{4,5},{5,4},{6,7},{7,6},{8,9},{9,8},{10,11... | collective-permute-start | bytes 3145736 | tf_op jit(solution)/shard_map/ppermute | solution.py:616
  317.1 40.1 %collective-permute-start.47 = (bf16[1024,2048]{1,0:T(8,128)(2,1)}, bf16[1024,2048]{1,0:T(8,128)(2,1)}, u32[]{:S(2)}, u32[]{:S(2)}) collective-permute-start(bf16[1024,2048]{1,0:T(8,128)(2,1)} %get-tuple-element.285), channel_id=1, source_target_pairs={{0,2},{2,0},{4,6},{6,4},{8,10},{10,8},{12,14},{14,12},{16,18},{18,... | collective-permute-start | bytes 12582920 | tf_op jit(solution)/shard_map/ppermute | solution.py:594
  320.5 36.7 %collective-permute-start.48 = (bf16[256,2048]{1,0:T(8,128)(2,1)}, bf16[256,2048]{1,0:T(8,128)(2,1)}, u32[]{:S(2)}, u32[]{:S(2)}) collective-permute-start(bf16[256,2048]{1,0:T(8,128)(2,1)} %pad_maximum_fusion.3), channel_id=1, source_target_pairs={{0,1},{1,0},{2,3},{3,2},{4,5},{5,4},{6,7},{7,6},{8,9},{9,8},{10,11... | collective-permute-start | bytes 3145736 | tf_op jit(solution)/shard_map/ppermute | solution.py:616
  322.2 34.9 %collective-permute-start.46 = (bf16[128,2048]{1,0:T(8,128)(2,1)S(1)}, bf16[128,2048]{1,0:T(8,128)(2,1)S(1)}, u32[]{:S(2)}, u32[]{:S(2)}) collective-permute-start(bf16[128,2048]{1,0:T(8,128)(2,1)S(1)} %pad_maximum_fusion.20), channel_id=1, source_target_pairs={{0,1},{1,0},{2,3},{3,2},{4,5},{5,4},{6,7},{7,6},{8,9},{9,8},{10,11... | collective-permute-start | bytes 1572872 | tf_op jit(solution)/shard_map/ppermute | solution.py:616
  322.8 34.3 %collective-permute-start.44 = (bf16[128,2048]{1,0:T(8,128)(2,1)S(1)}, bf16[128,2048]{1,0:T(8,128)(2,1)S(1)}, u32[]{:S(2)}, u32[]{:S(2)}) collective-permute-start(bf16[128,2048]{1,0:T(8,128)(2,1)S(1)} %slice.467), channel_id=1, source_target_pairs={{0,8},{2,10},{8,16},{10,18},{16,24},{18,26},{24,28},{26,30},{28,20... | collective-permute-start | bytes 1572872 | tf_op jit(solution)/shard_map/ppermute | solution.py:560
  323.6 33.5 %collective-permute-start.45 = (bf16[128,2048]{1,0:T(8,128)(2,1)S(1)}, bf16[128,2048]{1,0:T(8,128)(2,1)S(1)}, u32[]{:S(2)}, u32[]{:S(2)}) collective-permute-start(bf16[128,2048]{1,0:T(8,128)(2,1)S(1)} %slice.468), channel_id=1, source_target_pairs={{8,0},{10,2},{16,8},{18,10},{24,16},{26,18},{28,24},{30,26},{20,28... | collective-permute-start | bytes 1572872 | tf_op jit(solution)/shard_map/ppermute | solution.py:561
  401.6 42.0 %collective-permute-start.54 = (bf16[256,2048]{1,0:T(8,128)(2,1)}, bf16[256,2048]{1,0:T(8,128)(2,1)}, u32[]{:S(2)}, u32[]{:S(2)}) collective-permute-start(bf16[256,2048]{1,0:T(8,128)(2,1)} %pad_maximum_fusion.5), channel_id=1, source_target_pairs={{0,1},{1,0},{2,3},{3,2},{4,5},{5,4},{6,7},{7,6},{8,9},{9,8},{10,11... | collective-permute-start | bytes 3145736 | tf_op jit(solution)/shard_map/ppermute | solution.py:616
  510.5 49.9 %all-to-all-start.2 = ((bf16[8,1056,128]{2,1,0:T(8,128)(2,1)}), bf16[8,1056,128]{2,1,0:T(8,128)(2,1)}, u32[]{:S(2)}, u32[]{:S(2)}) async-start(bf16[8,1056,128]{2,1,0:T(8,128)(2,1)} %fusion.8), calls=%async_computation.2 | async-start | bytes 4325376 | tf_op jit(solution)/shard_map/all_to_all | solution.py:1036
  529.3 46.3 %collective-permute-start.75 = (bf16[256,2048]{1,0:T(8,128)(2,1)}, bf16[256,2048]{1,0:T(8,128)(2,1)}, u32[]{:S(2)}, u32[]{:S(2)}) collective-permute-start(bf16[256,2048]{1,0:T(8,128)(2,1)} %pad_maximum_fusion.6), channel_id=1, source_target_pairs={{0,1},{1,0},{2,3},{3,2},{4,5},{5,4},{6,7},{7,6},{8,9},{9,8},{10,11... | collective-permute-start | bytes 3145736 | tf_op jit(solution)/shard_map/ppermute | solution.py:616
  531.9 71.1 %collective-permute-start.80 = (bf16[256,2048]{1,0:T(8,128)(2,1)}, bf16[256,2048]{1,0:T(8,128)(2,1)}, u32[]{:S(2)}, u32[]{:S(2)}) collective-permute-start(bf16[256,2048]{1,0:T(8,128)(2,1)} %pad_maximum_fusion.16), channel_id=1, source_target_pairs={{0,1},{1,0},{2,3},{3,2},{4,5},{5,4},{6,7},{7,6},{8,9},{9,8},{10,11... | collective-permute-start | bytes 3145736 | tf_op jit(solution)/shard_map/ppermute | solution.py:616
  592.5 36.7 %collective-permute-start.76 = (bf16[256,2048]{1,0:T(8,128)(2,1)}, bf16[256,2048]{1,0:T(8,128)(2,1)S(1)}, u32[]{:S(2)}, u32[]{:S(2)}) collective-permute-start(bf16[256,2048]{1,0:T(8,128)(2,1)} %pad_maximum_fusion.14), channel_id=1, source_target_pairs={{0,8},{2,10},{8,16},{10,18},{16,24},{18,26},{24,28},{26,30},{28,20... | collective-permute-start | bytes 3145736 | tf_op jit(solution)/shard_map/ppermute | solution.py:560
  593.3 36.0 %collective-permute-start.77 = (bf16[256,2048]{1,0:T(8,128)(2,1)}, bf16[256,2048]{1,0:T(8,128)(2,1)S(1)}, u32[]{:S(2)}, u32[]{:S(2)}) collective-permute-start(bf16[256,2048]{1,0:T(8,128)(2,1)} %pad_maximum_fusion.15), channel_id=1, source_target_pairs={{8,0},{10,2},{16,8},{18,10},{24,16},{26,18},{28,24},{30,26},{20,28... | collective-permute-start | bytes 3145736 | tf_op jit(solution)/shard_map/ppermute | solution.py:561
  603.9 34.4 %collective-permute-start.85 = (bf16[256,2048]{1,0:T(8,128)(2,1)S(1)}, bf16[256,2048]{1,0:T(8,128)(2,1)S(1)}, u32[]{:S(2)}, u32[]{:S(2)}) collective-permute-start(bf16[256,2048]{1,0:T(8,128)(2,1)S(1)} %copy-done.72), channel_id=1, source_target_pairs={{0,1},{1,0},{2,3},{3,2},{4,5},{5,4},{6,7},{7,6},{8,9},{9,8},{10,11... | collective-permute-start | bytes 3145736 | tf_op jit(solution)/shard_map/ppermute | solution.py:616
  606.0 63.0 %collective-permute-start.87 = (bf16[256,2048]{1,0:T(8,128)(2,1)S(1)}, bf16[256,2048]{1,0:T(8,128)(2,1)S(1)}, u32[]{:S(2)}, u32[]{:S(2)}) collective-permute-start(bf16[256,2048]{1,0:T(8,128)(2,1)S(1)} %add_convert_fusion.4), channel_id=1, source_target_pairs={{0,1},{1,0},{2,3},{3,2},{4,5},{5,4},{6,7},{7,6},{8,9},{9,8},{10,11... | collective-permute-start | bytes 3145736 | tf_op jit(solution)/shard_map/ppermute | solution.py:616
  630.6 38.3 %collective-permute-start.82 = (bf16[256,2048]{1,0:T(8,128)(2,1)}, bf16[256,2048]{1,0:T(8,128)(2,1)}, u32[]{:S(2)}, u32[]{:S(2)}) collective-permute-start(bf16[256,2048]{1,0:T(8,128)(2,1)} %add_convert_fusion.5), channel_id=1, source_target_pairs={{8,0},{10,2},{16,8},{18,10},{24,16},{26,18},{28,24},{30,26},{20,28... | collective-permute-start | bytes 3145736 | tf_op jit(solution)/shard_map/ppermute | solution.py:561
  632.3 36.6 %collective-permute-start.81 = (bf16[256,2048]{1,0:T(8,128)(2,1)}, bf16[256,2048]{1,0:T(8,128)(2,1)}, u32[]{:S(2)}, u32[]{:S(2)}) collective-permute-start(bf16[256,2048]{1,0:T(8,128)(2,1)} %add_convert_fusion.6), channel_id=1, source_target_pairs={{0,8},{2,10},{8,16},{10,18},{16,24},{18,26},{24,28},{26,30},{28,20... | collective-permute-start | bytes 3145736 | tf_op jit(solution)/shard_map/ppermute | solution.py:560
  668.4 46.9 %collective-permute-start.92 = (bf16[128,2048]{1,0:T(8,128)(2,1)}, bf16[128,2048]{1,0:T(8,128)(2,1)}, u32[]{:S(2)}, u32[]{:S(2)}) collective-permute-start(bf16[128,2048]{1,0:T(8,128)(2,1)} %get-tuple-element.512), channel_id=1, source_target_pairs={{0,1},{1,0},{2,3},{3,2},{4,5},{5,4},{6,7},{7,6},{8,9},{9,8},{10,11... | collective-permute-start | bytes 1572872 | tf_op jit(solution)/shard_map/ppermute | solution.py:616
  673.2 42.0 %collective-permute-start.90 = (bf16[128,2048]{1,0:T(8,128)(2,1)}, bf16[128,2048]{1,0:T(8,128)(2,1)}, u32[]{:S(2)}, u32[]{:S(2)}) collective-permute-start(bf16[128,2048]{1,0:T(8,128)(2,1)} %get-tuple-element.507), channel_id=1, source_target_pairs={{0,8},{2,10},{8,16},{10,18},{16,24},{18,26},{24,28},{26,30},{28,20... | collective-permute-start | bytes 1572872 | tf_op jit(solution)/shard_map/ppermute | solution.py:560
  674.6 40.6 %collective-permute-start.91 = (bf16[128,2048]{1,0:T(8,128)(2,1)}, bf16[128,2048]{1,0:T(8,128)(2,1)}, u32[]{:S(2)}, u32[]{:S(2)}) collective-permute-start(bf16[128,2048]{1,0:T(8,128)(2,1)} %get-tuple-element.506), channel_id=1, source_target_pairs={{8,0},{10,2},{16,8},{18,10},{24,16},{26,18},{28,24},{30,26},{20,28... | collective-permute-start | bytes 1572872 | tf_op jit(solution)/shard_map/ppermute | solution.py:561
  677.9 37.3 %collective-permute-start.89 = (bf16[256,2048]{1,0:T(8,128)(2,1)}, bf16[256,2048]{1,0:T(8,128)(2,1)}, u32[]{:S(2)}, u32[]{:S(2)}) collective-permute-start(bf16[256,2048]{1,0:T(8,128)(2,1)} %add_convert_fusion.2), channel_id=1, source_target_pairs={{8,0},{10,2},{16,8},{18,10},{24,16},{26,18},{28,24},{30,26},{20,28... | collective-permute-start | bytes 3145736 | tf_op jit(solution)/shard_map/ppermute | solution.py:561
  681.5 33.7 %collective-permute-start.88 = (bf16[256,2048]{1,0:T(8,128)(2,1)}, bf16[256,2048]{1,0:T(8,128)(2,1)}, u32[]{:S(2)}, u32[]{:S(2)}) collective-permute-start(bf16[256,2048]{1,0:T(8,128)(2,1)} %add_convert_fusion.3), channel_id=1, source_target_pairs={{0,8},{2,10},{8,16},{10,18},{16,24},{18,26},{24,28},{26,30},{28,20... | collective-permute-start | bytes 3145736 | tf_op jit(solution)/shard_map/ppermute | solution.py:560
  (189 other events, 2176.1 us)
